TPU v7x, 32 devices: a whole 2x2x4 slice. The times are simulated.
32 devices in a mesh: blk: 8 (over z, x), sub: 4 (over y, core).
Axes of the slice: x: 2, y: 2, z: 4, core: 2. Of those that a mesh axis runs over, the one named last changes fastest.
Arguments:
- source: float32 [5, 32, 64, 2048], P(None, 'sub', None, 'blk'), may hold values from -30 to 30
- inv_diag: float32 [5, 32, 64, 2048], P(None, 'sub', None, 'blk'), may hold values from 0.1 to 0.25
- coupling: float32 [8, 6, 5, 5], P('blk'), may hold values from -0.6 to 0.6
- face_map: int32 [8, 2], replicated, may hold values from 0 to 7, as said below
- wall_jac: float32 [3, 5, 2, 32, 2048], P(None, None, None, 'sub', 'blk'), may hold values from -6 to 6
- ffd_weight: float32 [8, 32, 2048], P(None, 'sub', 'blk'), may hold values from 0.05 to 0.5
- cp_ids: int32 [8, 32, 2048], P(None, 'sub', 'blk'), may hold values from -1 to 12287, as said below
Outputs:
- adjoint: float32 [5, 32, 64, 2048], P(None, 'sub', None, 'blk')
- cp_sens: float32 [3, 12288], P(None, ('blk', 'sub'))
Inputs may be any that keep to these rules, and one draw needn't show every extreme that they name: face_map[b, 0] is the block whose last chordwise cells meet block b's first ones; face_map[b, 1] the block whose first cells meet b's last ones; the second column is the inverse permutation of the first. `cp_ids`: -1 marks an unused slot; any other value is a control point, held by any device; the share of used slots differs from block to block.
All inputs are finite; a program needn't handle non-finite values.
Results may differ from a plain program's by a relative error of at most 0.0001.
Values sent between devices are 32-bit elements; how exact they have to be, the bound alone decides.
No kernel may reach another device: no remote copies, remote signals or barrier semaphores. Data moves between devices by JAX's collectives and lax.ppermute only.
A program may use at most 192 MiB of HBM per device.

v0:
```python
import jax
import jax.numpy as jnp
from jax import lax
from jax.sharding import PartitionSpec as P

SWEEPS = 3
CP_DEV = 384


def with_halo(block, sides, width):
    for axis, dim in sides:
        count = lax.axis_size(axis)
        forward = [(i, i + 1) for i in range(count - 1)]
        backward = [(target, source) for source, target in forward]
        low = lax.ppermute(
            lax.slice_in_dim(block, block.shape[dim] - width, None, axis=dim), axis, forward
        )
        high = lax.ppermute(lax.slice_in_dim(block, 0, width, axis=dim), axis, backward)
        block = jnp.concatenate([low, block, high], axis=dim)
    return block


def couple(matrix, field):
    return jnp.einsum("uv,vsni->usni", matrix, field, precision=lax.Precision.HIGHEST)


def relax_piece(adjoint, source, inv_diag, couplings, low_source, high_source):
    padded = with_halo(adjoint, (("sub", 1),), 1)
    chord_ends = jnp.stack([adjoint[..., 0], adjoint[..., -1]], 0)[None]
    all_ends = lax.all_gather(chord_ends, "blk", axis=0, tiled=True)
    low_face = lax.dynamic_index_in_dim(all_ends, low_source, 0, keepdims=False)[1]
    high_face = lax.dynamic_index_in_dim(all_ends, high_source, 0, keepdims=False)[0]
    zero_layer = jnp.zeros((adjoint.shape[0], adjoint.shape[1], 1, adjoint.shape[3]), jnp.float32)
    span_low = padded[:, :-2]
    span_high = padded[:, 2:]
    normal_low = jnp.concatenate([zero_layer, adjoint[:, :, :-1]], 2)
    normal_high = jnp.concatenate([adjoint[:, :, 1:], zero_layer], 2)
    chord_low = jnp.concatenate([low_face[..., None], adjoint[..., :-1]], 3)
    chord_high = jnp.concatenate([adjoint[..., 1:], high_face[..., None]], 3)
    summed = source
    neighbours = [span_low, span_high, normal_low, normal_high, chord_low, chord_high]
    for direction in range(6):
        summed = summed + couple(couplings[direction], neighbours[direction])
    return inv_diag * summed


def body(source, inv_diag, coupling, face_map, wall_jac, ffd_weight, cp_ids):
    couplings = coupling[0]
    block_index = lax.axis_index("blk")
    low_source = face_map[block_index, 0]
    high_source = face_map[block_index, 1]
    adjoint = inv_diag * source
    for sweep_index in range(SWEEPS):
        adjoint = relax_piece(adjoint, source, inv_diag, couplings, low_source, high_source)
    wall_sens = jnp.einsum(
        "cvksi,vski->csi", wall_jac, adjoint[:, :, 0:2, :], precision=lax.Precision.HIGHEST
    )
    contrib = (ffd_weight[None] * wall_sens[:, None]).reshape(3, -1)
    n_blocks = lax.axis_size("blk")
    n_spans = lax.axis_size("sub")
    points_all = CP_DEV * n_blocks * n_spans
    slots = jnp.where(cp_ids < 0, points_all, cp_ids).reshape(-1)

    def one_row(values):
        return jax.ops.segment_sum(values, slots, num_segments=points_all + 1)[:points_all]

    partial_sums = jax.vmap(one_row)(contrib)
    cp_sens = lax.psum_scatter(partial_sums, ("blk", "sub"), scatter_dimension=1, tiled=True)
    return (adjoint, cp_sens)


def solution(mesh):
    in_specs = (
        P(None, "sub", None, "blk"),
        P(None, "sub", None, "blk"),
        P("blk", None, None, None),
        P(),
        P(None, None, None, "sub", "blk"),
        P(None, "sub", "blk"),
        P(None, "sub", "blk"),
    )
    out_specs = (P(None, "sub", None, "blk"), P(None, ("blk", "sub")))
    return jax.shard_map(body, mesh=mesh, in_specs=in_specs, out_specs=out_specs, check_vma=False)
```

profile of v0, /device:TPU:0, one launch (start us, length us, event | category | flops | bytes accessed | tf_op | source)
XLA Modules:
  0.0 545.1 jit_solution(7254180310625874276)
XLA Ops:
  7.2 5.9 %copy_multiply_fusion = f32[5,8,64,256]{3,0,2,1:T(8,128)S(1)} fusion(f32[5,8,64,256]{3,2,1,0:T(8,128)} %param.8, f32[5,8,64,256]{3,2,1,0:T(8,128)} %param.7), kind=kLoop, calls=%fused_computation.4 | loop fusion | flops 655360 | bytes 7864320 | tf_op jit(solution)/shard_map/mul | solution.py:52
  13.1 2.0 copy-done
  16.1 3.1 collective-permute-start
  23.7 4.4 fusion.123
  28.1 4.7 fusion.122
  32.8 2.1 copy.94
  35.4 32.4 %all-gather = f32[16,5,8,64]{3,2,1,0:T(8,128)S(1)} all-gather(f32[2,5,8,64]{3,2,1,0:T(8,128)S(1)} %pad_maximum_fusion), channel_id=2, replica_groups=mesh['blk'=8,'sub'=4] {'blk'}, dimensions={0}, use_global_device_ids=true | all-gather | bytes 184320 | tf_op jit(solution)/shard_map/all_gather | solution.py:30
  70.2 2.0 copy.98
  72.6 7.9 %fusion.73 = f32[8,64,256,5]{2,3,1,0:T(8,128)} fusion(f32[5,8,64,256]{3,0,2,1:T(8,128)} %copy-done, f32[1,1,5,5]{3,2,1,0:T(8,128)S(1)} %copy.132), kind=kOutput, calls=%fused_computation.82 | convolution fusion | flops 38707200 | bytes 6750308 | tf_op jit(solution)/shard_map/uv,vsni->usni/dot_general | solution.py:24
  80.6 7.8 %fusion.75 = f32[8,64,256,5]{2,3,1,0:T(8,128)} fusion(f32[5,8,64,256]{3,0,2,1:T(8,128)} %copy-done, f32[1,1,5,5]{3,2,1,0:T(8,128)S(1)} %copy.131), kind=kOutput, calls=%fused_computation.84 | convolution fusion | flops 38707200 | bytes 6750308 | tf_op jit(solution)/shard_map/uv,vsni->usni/dot_general | solution.py:24
  88.6 9.3 %fusion.41 = f32[8,64,256,5]{2,3,1,0:T(8,128)} fusion(f32[5,8,64,255]{3,0,2,1:T(8,128)} %get-tuple-element.24, f32[5,8,64,1]{3,0,2,1:T(8,128)S(1)} %copy.96, f32[1,1,5,5]{3,2,1,0:T(8,128)S(1)} %copy.133), kind=kOutput, calls=%fused_computation.50 | convolution fusion | flops 39976960 | bytes 5242980 | tf_op jit(solution)/shard_map/uv,vsni->usni/dot_general | solution.py:24
  97.9 6.8 %fusion.45 = f32[8,64,256,5]{2,3,1,0:T(8,128)} fusion(f32[5,8,64,1]{3,0,2,1:T(8,128)S(1)} %copy-done.15, f32[5,8,64,255]{3,0,2,1:T(8,128)S(1)} %copy-done.12, f32[1,1,5,5]{3,2,1,0:T(8,128)S(1)} %copy.134), kind=kOutput, calls=%fused_computation.54 | convolution fusion | flops 39976960 | bytes 5242980 | tf_op jit(solution)/shard_map/uv,vsni->usni/dot_general | solution.py:24
  104.7 7.0 %fusion.2 = f32[8,64,256,5]{2,3,1,0:T(8,128)} fusion(f32[5,8,64,256]{3,0,2,1:T(8,128)S(1)} %copy-done.2, f32[5,1,64,256]{3,0,2,1:T(8,128)} %collective-permute-done, f32[1,1,5,5]{3,2,1,0:T(8,128)S(1)} %copy.129), kind=kOutput, calls=%fused_computation.11 | convolution fusion | flops 40058880 | bytes 5570660 | tf_op jit(solution)/shard_map/uv,vsni->usni/dot_general | solution.py:24
  111.7 13.5 %copy_multiply_fusion.1 = f32[5,8,64,256]{3,0,2,1:T(8,128)S(1)} fusion(f32[5,8,64,256]{3,2,1,0:T(8,128)S(1)} %copy-done.7, f32[5,8,64,256]{3,2,1,0:T(8,128)S(1)} %copy-done.8, f32[8,64,256,5]{2,3,1,0:T(8,128)} %fusion.45, f32[8,64,256,5]{2,3,1,0:T(8,128)} %fusion.41, f32[8,64,256,5]{2,3,1,0:T(8,128)} %fusion.73, f32[8,64,256,5]{2,3,1,0:T(8,128)} %fusion.75, ...), kind=kOutput, calls=%fused_computation.5 | convolution fusion | flops 44646400 | bytes 23920740 | tf_op jit(solution)/shard_map/uv,vsni->usni/dot_general | solution.py:24
  126.3 4.7 fusion.119
  131.0 2.7 fusion.120
  133.7 5.2 fusion.69
  138.9 5.2 fusion.71
  145.4 2.0 copy.102
  147.5 2.0 copy.103
  149.5 31.1 %all-gather.1 = f32[16,5,8,64]{3,2,1,0:T(8,128)S(1)} all-gather(f32[2,5,8,64]{3,2,1,0:T(8,128)S(1)} %pad_maximum_fusion.1), channel_id=3, replica_groups=mesh['blk'=8,'sub'=4] {'blk'}, dimensions={0}, use_global_device_ids=true | all-gather | bytes 184320 | tf_op jit(solution)/shard_map/all_gather | solution.py:30
  180.6 2.0 copy.104
  182.6 2.0 copy.105
  185.9 9.2 %fusion.49 = f32[8,64,256,5]{2,3,1,0:T(8,128)} fusion(f32[5,8,64,255]{3,0,2,1:T(8,128)} %get-tuple-element.18, f32[5,8,64,1]{3,0,2,1:T(8,128)} %copy.104, f32[1,1,5,5]{3,2,1,0:T(8,128)S(1)} %copy.133), kind=kOutput, calls=%fused_computation.58 | convolution fusion | flops 39976960 | bytes 5242980 | tf_op jit(solution)/shard_map/uv,vsni->usni/dot_general | solution.py:24
  195.1 7.0 %fusion.53 = f32[8,64,256,5]{2,3,1,0:T(8,128)} fusion(f32[5,8,64,1]{3,0,2,1:T(8,128)S(1)} %copy-done.17, f32[5,8,64,255]{3,0,2,1:T(8,128)S(1)} %copy-done.14, f32[1,1,5,5]{3,2,1,0:T(8,128)S(1)} %copy.134), kind=kOutput, calls=%fused_computation.62 | convolution fusion | flops 39976960 | bytes 5242980 | tf_op jit(solution)/shard_map/uv,vsni->usni/dot_general | solution.py:24
  202.1 5.3 fusion.10
  207.4 13.3 %copy_multiply_fusion.2 = f32[5,8,64,256]{3,0,2,1:T(8,128)S(1)} fusion(f32[5,8,64,256]{3,2,1,0:T(8,128)S(1)} %copy-done.7, f32[5,8,64,256]{3,2,1,0:T(8,128)S(1)} %copy-done.9, f32[8,64,256,5]{2,3,1,0:T(8,128)} %fusion.53, f32[8,64,256,5]{2,3,1,0:T(8,128)} %fusion.49, f32[8,64,256,5]{2,3,1,0:T(8,128)} %fusion.69, f32[8,64,256,5]{2,3,1,0:T(8,128)} %fusion.71, ...), kind=kOutput, calls=%fused_computation.6 | convolution fusion | flops 44646400 | bytes 23920740 | tf_op jit(solution)/shard_map/uv,vsni->usni/dot_general | solution.py:24
  221.9 4.7 fusion.116
  226.6 2.7 fusion.117
  229.3 5.6 %fusion.65 = f32[8,64,256,5]{2,3,1,0:T(8,128)} fusion(f32[5,8,64,256]{3,0,2,1:T(8,128)S(1)} %copy_multiply_fusion.2, f32[1,1,5,5]{3,2,1,0:T(8,128)S(1)} %copy.132), kind=kOutput, calls=%fused_computation.74 | convolution fusion | flops 38707200 | bytes 6754304 | tf_op jit(solution)/shard_map/uv,vsni->usni/dot_general | solution.py:24
  234.9 5.2 fusion.67
  240.1 3.1 collective-permute-start.4
  243.1 2.0 copy.108
  245.2 2.0 copy.109
  247.2 30.9 %all-gather.2 = f32[16,5,8,64]{3,2,1,0:T(8,128)S(1)} all-gather(f32[2,5,8,64]{3,2,1,0:T(8,128)S(1)} %pad_maximum_fusion.2), channel_id=4, replica_groups=mesh['blk'=8,'sub'=4] {'blk'}, dimensions={0}, use_global_device_ids=true | all-gather | bytes 184320 | tf_op jit(solution)/shard_map/all_gather | solution.py:30
  278.2 2.0 copy.110
  280.2 2.0 copy.111
  283.5 9.2 %fusion.57 = f32[8,64,256,5]{2,3,1,0:T(8,128)} fusion(f32[5,8,64,255]{3,0,2,1:T(8,128)} %get-tuple-element.12, f32[5,8,64,1]{3,0,2,1:T(8,128)} %copy.110, f32[1,1,5,5]{3,2,1,0:T(8,128)S(1)} %copy.133), kind=kOutput, calls=%fused_computation.66 | convolution fusion | flops 39976960 | bytes 5242980 | tf_op jit(solution)/shard_map/uv,vsni->usni/dot_general | solution.py:24
  292.7 6.9 %fusion.61 = f32[8,64,256,5]{2,3,1,0:T(8,128)} fusion(f32[5,8,64,1]{3,0,2,1:T(8,128)S(1)} %copy-done.16, f32[5,8,64,255]{3,0,2,1:T(8,128)S(1)} %copy-done.13, f32[1,1,5,5]{3,2,1,0:T(8,128)S(1)} %copy.134), kind=kOutput, calls=%fused_computation.70 | convolution fusion | flops 39976960 | bytes 5242980 | tf_op jit(solution)/shard_map/uv,vsni->usni/dot_general | solution.py:24
  299.6 5.3 fusion.18
  305.0 13.4 %copy_multiply_fusion.3 = f32[5,8,64,256]{3,0,2,1:T(8,128)S(1)} fusion(f32[5,8,64,256]{3,2,1,0:T(8,128)S(1)} %copy-done.7, f32[5,8,64,256]{3,2,1,0:T(8,128)S(1)} %copy-done.10, f32[8,64,256,5]{2,3,1,0:T(8,128)} %fusion.61, f32[8,64,256,5]{2,3,1,0:T(8,128)} %fusion.57, f32[8,64,256,5]{2,3,1,0:T(8,128)} %fusion.65, f32[8,64,256,5]{2,3,1,0:T(8,128)} %fusion.67, ...), kind=kOutput, calls=%fused_computation.7 | convolution fusion | flops 44646400 | bytes 23920740 | tf_op jit(solution)/shard_map/uv,vsni->usni/dot_general | solution.py:24
  318.4 2.0 copy-done.11
  320.8 4.6 bitcast_multiply_fusion
  325.5 83.0 %scatter_custom_fusion = f32[3,12289]{0,1:T(8,128)} fusion(s32[16384]{0:T(1024)S(1)} %bitcast.152, f32[3,16384]{0,1:T(8,128)} %bitcast_multiply_fusion, f32[]{:T(128)} %constant.25.clone.1), kind=kCustom, calls=%fused_computation.1 | custom fusion | flops 49152 | bytes 344080 | tf_op jit(solution)/shard_map/vmap()/scatter-add | solution.py:65
  408.4 4.7 slice.231
  413.2 4.5 copy.113
  417.7 118.7 %reduce-scatter.2.cloned.1.call-done = f32[3,384]{0,1:T(8,128)} async-done(((f32[3,12288]{0,1:T(8,128)}), f32[3,384]{0,1:T(8,128)}) %reduce-scatter.2.cloned.1.call-update) | async-done | bytes 4624 | tf_op jit(solution)/shard_map/reduce_scatter | solution.py:68
  536.4 1.6 copy.114
  (82 shorter events, 12.0 us)
Async XLA Ops:
  7.2 13.4 %copy-start.22 = (s32[8,2]{0,1:T(2,128)S(1)}, s32[8,2]{0,1:T(2,128)}, u32[]{:S(2)}) copy-start(s32[8,2]{0,1:T(2,128)} %param.10) | copy-start | bytes 196
  7.2 529.2 %reduce-scatter.2.cloned.1.call-start = ((), (), s32[]{:S(2)}) async-start(), calls=%async_computation.1 | async-start | bytes 6488064 | tf_op jit(solution)/shard_map/reduce_scatter | solution.py:68
  13.1 2.0 copy-start
  16.1 88.6 %collective-permute-start = (f32[5,1,64,256]{3,0,2,1:T(8,128)}, f32[5,1,64,256]{3,0,2,1:T(8,128)}, u32[]{:S(2)}, u32[]{:S(2)}) collective-permute-start(f32[5,1,64,256]{3,0,2,1:T(8,128)} %get-tuple-element.23), channel_id=1, source_target_pairs={{0,1},{1,2},{2,3},{4,5},{5,6},{6,7},{8,9},{9,10},{10,11},{12,13},{... | collective-permute-start | bytes 983048 | tf_op jit(solution)/shard_map/ppermute | solution.py:15
  19.2 92.4 %collective-permute-start.1 = (f32[5,1,64,256]{3,0,2,1:T(8,128)}, f32[5,1,64,256]{3,0,2,1:T(8,128)S(1)}, u32[]{:S(2)}, u32[]{:S(2)}) collective-permute-start(f32[5,1,64,256]{3,0,2,1:T(8,128)} %get-tuple-element.22), channel_id=1, source_target_pairs={{1,0},{2,1},{3,2},{5,4},{6,5},{7,6},{9,8},{10,9},{11,10},{13,12},{... | collective-permute-start | bytes 983048 | tf_op jit(solution)/shard_map/ppermute | solution.py:18
  23.7 4.4 copy-start.1
  32.8 37.0 %copy-start.18 = (f32[1,6,5,5]{1,0,3,2:T(1,128)S(1)}, f32[1,6,5,5]{1,0,3,2:T(1,128)}, u32[]{:S(2)}) copy-start(f32[1,6,5,5]{1,0,3,2:T(1,128)} %param.9) | copy-start | bytes 1804
  80.4 8.1 %copy-start.20 = (f32[8,8,256]{2,1,0:T(8,128)S(1)}, f32[8,8,256]{2,1,0:T(8,128)}, u32[]{:S(2)}) copy-start(f32[8,8,256]{2,1,0:T(8,128)} %param.12) | copy-start | bytes 196612
  80.6 8.0 %copy-start.21 = (s32[8,8,256]{2,1,0:T(8,128)S(1)}, s32[8,8,256]{2,1,0:T(8,128)}, u32[]{:S(2)}) copy-start(s32[8,8,256]{2,1,0:T(8,128)} %param.13) | copy-start | bytes 196612
  88.6 9.3 %copy-start.12 = (f32[5,8,64,255]{3,0,2,1:T(8,128)S(1)}, f32[5,8,64,255]{3,0,2,1:T(8,128)}, u32[]{:S(2)}) copy-start(f32[5,8,64,255]{3,0,2,1:T(8,128)} %get-tuple-element.25) | copy-start | bytes 7833604
  88.6 9.3 %copy-start.15 = (f32[5,8,64,1]{3,0,2,1:T(8,128)S(1)}, f32[5,8,64,1]{3,0,2,1:T(8,128)}, u32[]{:S(2)}) copy-start(f32[5,8,64,1]{3,0,2,1:T(8,128)} %copy.98) | copy-start | bytes 30724
  97.9 6.8 %copy-start.2 = (f32[5,8,64,256]{3,0,2,1:T(8,128)S(1)}, f32[5,8,64,256]{3,0,2,1:T(8,128)}, u32[]{:S(2)}) copy-start(f32[5,8,64,256]{3,0,2,1:T(8,128)} %copy-done) | copy-start | bytes 7864324
  104.7 7.0 %copy-start.7 = (f32[5,8,64,256]{3,2,1,0:T(8,128)S(1)}, f32[5,8,64,256]{3,2,1,0:T(8,128)}, u32[]{:S(2)}) copy-start(f32[5,8,64,256]{3,2,1,0:T(8,128)} %param.8) | copy-start | bytes 7864324
  104.7 7.0 %copy-start.8 = (f32[5,8,64,256]{3,2,1,0:T(8,128)S(1)}, f32[5,8,64,256]{3,2,1,0:T(8,128)}, u32[]{:S(2)}) copy-start(f32[5,8,64,256]{3,2,1,0:T(8,128)} %param.7) | copy-start | bytes 7864324
  125.2 13.7 %copy-start.5 = (f32[5,8,64,256]{3,0,2,1:T(8,128)}, f32[5,8,64,256]{3,0,2,1:T(8,128)S(1)}, u32[]{:S(2)}) copy-start(f32[5,8,64,256]{3,0,2,1:T(8,128)S(1)} %copy_multiply_fusion.1) | copy-start | bytes 7864324
  144.1 58.0 %collective-permute-start.2 = (f32[5,1,64,256]{3,0,2,1:T(8,128)}, f32[5,1,64,256]{3,0,2,1:T(8,128)S(1)}, u32[]{:S(2)}, u32[]{:S(2)}) collective-permute-start(f32[5,1,64,256]{3,0,2,1:T(8,128)} %get-tuple-element.17), channel_id=1, source_target_pairs={{0,1},{1,2},{2,3},{4,5},{5,6},{6,7},{8,9},{9,10},{10,11},{12,13},{... | collective-permute-start | bytes 983048 | tf_op jit(solution)/shard_map/ppermute | solution.py:15
  184.6 22.8 %collective-permute-start.3 = (f32[5,1,64,256]{3,0,2,1:T(8,128)}, f32[5,1,64,256]{3,0,2,1:T(8,128)S(1)}, u32[]{:S(2)}, u32[]{:S(2)}) collective-permute-start(f32[5,1,64,256]{3,0,2,1:T(8,128)} %get-tuple-element.16), channel_id=1, source_target_pairs={{1,0},{2,1},{3,2},{5,4},{6,5},{7,6},{9,8},{10,9},{11,10},{13,12},{... | collective-permute-start | bytes 983048 | tf_op jit(solution)/shard_map/ppermute | solution.py:18
  185.9 9.2 %copy-start.14 = (f32[5,8,64,255]{3,0,2,1:T(8,128)S(1)}, f32[5,8,64,255]{3,0,2,1:T(8,128)}, u32[]{:S(2)}) copy-start(f32[5,8,64,255]{3,0,2,1:T(8,128)} %get-tuple-element.19) | copy-start | bytes 7833604
  185.9 9.2 %copy-start.17 = (f32[5,8,64,1]{3,0,2,1:T(8,128)S(1)}, f32[5,8,64,1]{3,0,2,1:T(8,128)}, u32[]{:S(2)}) copy-start(f32[5,8,64,1]{3,0,2,1:T(8,128)} %copy.105) | copy-start | bytes 30724
  195.1 7.0 %copy-start.6 = (f32[5,8,64,256]{3,0,2,1:T(8,128)S(1)}, f32[5,8,64,256]{3,0,2,1:T(8,128)}, u32[]{:S(2)}) copy-start(f32[5,8,64,256]{3,0,2,1:T(8,128)} %copy-done.5) | copy-start | bytes 7864324
  202.1 5.3 copy-start.9
  220.8 14.1 %copy-start.3 = (f32[5,8,64,256]{3,0,2,1:T(8,128)}, f32[5,8,64,256]{3,0,2,1:T(8,128)S(1)}, u32[]{:S(2)}) copy-start(f32[5,8,64,256]{3,0,2,1:T(8,128)S(1)} %copy_multiply_fusion.2) | copy-start | bytes 7864324
  240.1 59.6 %collective-permute-start.4 = (f32[5,1,64,256]{3,0,2,1:T(8,128)}, f32[5,1,64,256]{3,0,2,1:T(8,128)S(1)}, u32[]{:S(2)}, u32[]{:S(2)}) collective-permute-start(f32[5,1,64,256]{3,0,2,1:T(8,128)} %get-tuple-element.11), channel_id=1, source_target_pairs={{0,1},{1,2},{2,3},{4,5},{5,6},{6,7},{8,9},{9,10},{10,11},{12,13},{... | collective-permute-start | bytes 983048 | tf_op jit(solution)/shard_map/ppermute | solution.py:15
  282.2 22.8 %collective-permute-start.5 = (f32[5,1,64,256]{3,0,2,1:T(8,128)}, f32[5,1,64,256]{3,0,2,1:T(8,128)S(1)}, u32[]{:S(2)}, u32[]{:S(2)}) collective-permute-start(f32[5,1,64,256]{3,0,2,1:T(8,128)} %get-tuple-element.10), channel_id=1, source_target_pairs={{1,0},{2,1},{3,2},{5,4},{6,5},{7,6},{9,8},{10,9},{11,10},{13,12},{... | collective-permute-start | bytes 983048 | tf_op jit(solution)/shard_map/ppermute | solution.py:18
  283.5 9.2 %copy-start.13 = (f32[5,8,64,255]{3,0,2,1:T(8,128)S(1)}, f32[5,8,64,255]{3,0,2,1:T(8,128)}, u32[]{:S(2)}) copy-start(f32[5,8,64,255]{3,0,2,1:T(8,128)} %get-tuple-element.13) | copy-start | bytes 7833604
  283.5 9.2 %copy-start.16 = (f32[5,8,64,1]{3,0,2,1:T(8,128)S(1)}, f32[5,8,64,1]{3,0,2,1:T(8,128)}, u32[]{:S(2)}) copy-start(f32[5,8,64,1]{3,0,2,1:T(8,128)} %copy.111) | copy-start | bytes 30724
  292.7 6.9 %copy-start.4 = (f32[5,8,64,256]{3,0,2,1:T(8,128)S(1)}, f32[5,8,64,256]{3,0,2,1:T(8,128)}, u32[]{:S(2)}) copy-start(f32[5,8,64,256]{3,0,2,1:T(8,128)} %copy-done.3) | copy-start | bytes 7864324
  299.6 5.3 copy-start.10
  305.0 15.5 %copy-start.19 = (f32[3,5,2,8,256]{4,3,2,1,0:T(8,128)S(1)}, f32[3,5,2,8,256]{4,3,2,1,0:T(8,128)}, u32[]{:S(2)}) copy-start(f32[3,5,2,8,256]{4,3,2,1,0:T(8,128)} %param.11) | copy-start | bytes 737284
  318.4 2.0 copy-start.11
Sparse Core Ops, SparseCore 0:
  413.3 123.0 reduce-scatter.1
where the time goes:
time: 549 us; the launch traced here: 545 us
  matrix products  143 us (26%)
  waiting for transfers between devices  119 us (22%)
  blocking collectives  94.3 us (17%)
  other arithmetic  93.5 us (17%)
  local copies, waits for them, and re-layouts  65.8 us (12%)
  between operations  18.4 us (3%)
  starting transfers between devices  11.4 us (2%)
    dot_general x18, matrix products, couple(): jnp.einsum('uv,vsni->usni', matrix, field, precision=lax.Precision.HIGHEST)  143 us
    reduce_scatter x1, waiting for transfers between devices, body(): lax.psum_scatter(partial_sums, ('blk', 'sub'), scatter_dimension=1, tiled...  119 us
    all_gather x3, blocking collectives, relax_piece(): all_ends = lax.all_gather(chord_ends, 'blk', axis=0, tiled=True)  94.3 us
    scatter-add x1, other arithmetic, one_row(): jax.ops.segment_sum(values, slots, num_segments=points_all + 1)[:points_all]  83 us
    slice x9, local copies, waits for them, and re-layouts, relax_piece(): chord_ends = jnp.stack([adjoint[..., 0], adjoint[..., -1]], 0)[None]  20.6 us
    slice x3, local copies, waits for them, and re-layouts, relax_piece(): chord_low = jnp.concatenate([low_face[..., None], adjoint[..., :-1]], 3)  14.1 us
    unnamed x58, local copies, waits for them, and re-layouts  11.1 us
  transfers between devices with their start and end apart: 7, of which 1 were waited for; matrix products, arithmetic and copies ran while one was open for 22% of the time, Pallas kernels for 0%

commit v1 on v0

v1 whole, which is shorter than its diff:
```python
import functools

import jax
import jax.numpy as jnp
from jax import lax
from jax.experimental import pallas as pl
from jax.experimental.pallas import tpu as pltpu
from jax.sharding import PartitionSpec as P

SWEEPS = 3
CP_DEV = 384
LANES = 128
COLS = 5
DEEP = 3
NEAR = 8
MIB = 1 << 20
ANY = pl.BlockSpec(memory_space=pl.ANY)
VMEM = pl.BlockSpec(memory_space=pltpu.VMEM)


def lane_iota(shape):
    return lax.broadcasted_iota(jnp.int32, shape, len(shape) - 1)


def lane_base(row):
    return COLS * row


def pack_kernel(depth, src, inv, low, high, cpl, out):
    lane = lane_iota((1, 1, LANES))
    for f, own in enumerate((src, inv)):
        total = jnp.zeros((own.shape[0], depth, LANES), jnp.float32)
        spans = own.shape[1]
        for row in range(spans + 4):
            s = row - 2
            if s < 0:
                both = low[f, :, s + DEEP]
            elif s >= spans:
                both = high[f, :, s - spans]
            else:
                both = own[:, s]
            ends = jnp.where(lane < LANES // 2, both[..., :LANES], both[..., LANES:])
            base = lane_base(row)
            near = pltpu.roll(ends, (base + 3) % LANES, 2)
            far = pltpu.roll(ends, (LANES // 2 + base + 2) % LANES, 2)
            at = lane - base
            total = jnp.where((at >= 0) & (at < COLS), near, total)
            at = at - LANES // 2
            total = jnp.where((at >= 0) & (at < COLS), far, total)
        for v in range(own.shape[0]):
            first = (f * own.shape[0] + v) * depth
            out[first : first + depth, :] = total[v]
    rows = 2 * src.shape[0] * depth
    out[rows : rows + 8, :] = cpl[...]


def pack_ends(source, inv_diag, low, high, cpl, depth):
    nvar, spans, _, chord = source.shape
    field = pl.BlockSpec((nvar, spans, depth, chord), lambda i: (0, 0, 0, 0))
    rows = 2 * nvar * depth + 8

    def whole(a):
        return pl.BlockSpec(a.shape, lambda i: (0,) * a.ndim)

    return pl.pallas_call(
        functools.partial(pack_kernel, depth),
        grid=(1,),
        in_specs=[field, field, whole(low), whole(high), whole(cpl)],
        out_specs=pl.BlockSpec((rows, LANES), lambda i: (0, 0)),
        out_shape=jax.ShapeDtypeStruct((rows, LANES), jnp.float32),
        compiler_params=pltpu.CompilerParams(vmem_limit_bytes=48 * MIB),
        name="pack_ends",
    )(source, inv_diag, low, high, cpl)


def route_ends(packet, me, low_of, high_of):
    count = lax.axis_size("blk")
    masks = [1 << b for b in range(count.bit_length() - 1)][::-1]
    left = lane_iota((1, LANES)) < LANES // 2
    held = packet[None]
    for mask in masks[:-1]:
        other = lax.ppermute(held, "blk", [(i, i ^ mask) for i in range(count)])
        held = jnp.concatenate([held, other], 0)

    def place(block):
        apart = me ^ block
        index = 0
        for bit, mask in enumerate(masks[:-1]):
            index = index + jnp.where((apart & mask) != 0, 1 << bit, 0)
        return index, (apart & masks[-1]) == 0

    def chosen(device):
        low, _ = place(low_of[device])
        high, _ = place(high_of[device])
        return jnp.where(
            left,
            lax.dynamic_index_in_dim(held, low, 0, keepdims=False),
            lax.dynamic_index_in_dim(held, high, 0, keepdims=False),
        )

    last = masks[-1]
    given = lax.ppermute(chosen(me ^ last), "blk", [(i, i ^ last) for i in range(count)])
    _, low_here = place(low_of[me])
    _, high_here = place(high_of[me])
    return jnp.where(jnp.where(left, low_here, high_here), chosen(me), given)


def bit(condition):
    return jnp.where(condition, 1.0, 0.0)


def expand_couplings(couplings, wide):
    rows, lanes = wide.shape
    nvar = 5
    row = lax.broadcasted_iota(jnp.int32, (rows, 32), 0)
    of = lax.broadcasted_iota(jnp.int32, (rows, 32), 1)
    pick_row = bit((row >> 4) == of).astype(jnp.bfloat16)
    col = lax.broadcasted_iota(jnp.int32, (LANES, lanes), 1)
    var = lax.broadcasted_iota(jnp.int32, (LANES, lanes), 0)
    wide_var = (col >> 4) - jnp.where(col >= 80, nvar, 0) - jnp.where(col >= 160, nvar, 0)
    pick_col = bit((wide_var == var) & (col < 240)).astype(jnp.bfloat16)
    top = couplings.astype(jnp.bfloat16)
    rest = (couplings - top.astype(jnp.float32)).astype(jnp.bfloat16)

    def spread(part):
        tall = jnp.dot(pick_row, part, preferred_element_type=jnp.float32).astype(jnp.bfloat16)
        return jnp.dot(tall, pick_col, preferred_element_type=jnp.float32)

    r = lax.broadcasted_iota(jnp.int32, (rows, lanes), 0)
    c = lax.broadcasted_iota(jnp.int32, (rows, lanes), 1)
    both = jnp.where(c < 160, spread(top), spread(rest))
    wide[...] = jnp.where((r & 15) == (c & 15), both, 0.0).astype(jnp.bfloat16)


def ribbon_sweeps(depth, own, given, scalars, faces):
    nvar = 5
    lane = lane_iota((1, LANES))
    place = lane & (LANES // 2 - 1)
    column = place - COLS * ((place * 205) >> 10)
    side = lane >= LANES // 2
    used = place < 12 * COLS
    ghost = jnp.where(side, bit(column >= 2), bit(column <= 2)) > 0.5

    def field(f, v):
        first = (f * nvar + v) * depth
        at = slice(first, first + depth)
        return jnp.where(used, jnp.where(ghost, given[at, :], own[at, :]), 0.0)

    src = [field(0, v) for v in range(nvar)]
    inv = [field(1, v) for v in range(nvar)]
    rows = 2 * nvar * depth
    mine = own[rows : rows + 8, :]
    theirs = given[rows : rows + 8, :]

    def spread(tile, index, half):
        at = (index & 63) + (LANES // 2) * half
        return jnp.broadcast_to(tile[index >> 6 : (index >> 6) + 1, at : at + 1], (1, LANES))

    own_c = [spread(mine, i, 0) for i in range(150)]
    mixed = []
    for i in range(150):
        other = jnp.where(side, spread(theirs, i, 1), spread(theirs, i, 0))
        mixed.append(jnp.where(ghost, other, own_c[i]))

    k = lax.broadcasted_iota(jnp.int32, (depth, LANES), 0)
    p = [inv[v] * src[v] for v in range(nvar)]
    for n in range(SWEEPS):
        for u in range(nvar):
            face = jnp.zeros((depth, LANES), jnp.float32)
            for v in range(nvar):
                at = u * nvar + v
                face += jnp.where(side, own_c[125 + at], own_c[100 + at]) * p[v]
            faces[n, u, 0:depth, :] = face
        if n == SWEEPS - 1:
            break
        total = list(src)
        for v in range(nvar):
            near = [
                pltpu.roll(p[v], COLS, 1),
                pltpu.roll(p[v], LANES - COLS, 1),
                jnp.where(k == 0, 0.0, pltpu.roll(p[v], 1, 0)),
                jnp.where(k == depth - 1, 0.0, pltpu.roll(p[v], depth - 1, 0)),
                pltpu.roll(p[v], 1, 1),
                pltpu.roll(p[v], LANES - 1, 1),
            ]
            for d in range(6):
                for u in range(nvar):
                    total[u] = total[u] + mixed[(d * nvar + u) * nvar + v] * near[d]
        p = [inv[v] * total[v] for v in range(nvar)]


def sweep_kernel(depth, couplings, own, given, src_in, inv_in, low, high, out, *scratch):
    src, inv, pa, pb, wide, before, coming, faces, scalars, sems, out_sem = scratch
    nvar, layers, rows, chord = pa.shape
    spans = layers - 2 * DEEP
    loads = []
    for f, (whole, to) in enumerate(((src_in, src), (inv_in, inv))):
        parts = (
            (low.at[f], to.at[:, 0:DEEP, 0:depth]),
            (whole.at[:, :, 0:depth], to.at[:, DEEP : DEEP + spans, 0:depth]),
            (high.at[f], to.at[:, DEEP + spans : layers, 0:depth]),
        )
        for j, (a, b) in enumerate(parts):
            loads.append(pltpu.make_async_copy(a, b, sems.at[3 * f + j]))
    if rows != depth:
        src[:, :, depth:rows, :] = jnp.zeros((nvar, layers, rows - depth, chord), jnp.float32)
        inv[:, :, depth:rows, :] = jnp.zeros((nvar, layers, rows - depth, chord), jnp.float32)
        faces[...] = jnp.zeros(faces.shape, jnp.float32)
    for copy in loads:
        copy.start()
    expand_couplings(couplings[...], wide)
    ribbon_sweeps(depth, own, given, scalars, faces)
    for copy in loads:
        copy.wait()

    def first(s, _):
        pa[:, s] = inv[:, s] * src[:, s]
        return 0

    lax.fori_loop(0, layers, first, 0)
    groups = rows // 16
    lane = lane_iota((1, 1, LANES))
    k = lax.broadcasted_iota(jnp.int32, (1, rows, 1), 1)

    def products(p, s, first_row, last_row):
        pieces = []
        for g in range(groups):
            x = p[:, s, 16 * g : 16 * g + 16, :].reshape(nvar * 16, chord)
            top = x.astype(jnp.bfloat16)
            rest = (x - top.astype(jnp.float32)).astype(jnp.bfloat16)
            none = jnp.zeros((16, chord), jnp.bfloat16)
            parts = jnp.concatenate([top, rest, top, none], 0)
            y = jnp.dot(wide[first_row:last_row, :], parts, preferred_element_type=jnp.float32)
            pieces.append(y.reshape((last_row - first_row) // 16, 16, chord))
        return jnp.concatenate(pieces, 1) if groups > 1 else pieces[0]

    step = 16 * nvar
    for n in range(SWEEPS):
        p, after = (pa, pb) if n % 2 == 0 else (pb, pa)
        coming[...] = products(p, n, 0, step)

        def layer(s, _):
            every = products(p, s, 0, 6 * step)
            after[:, s - 1] = inv[:, s - 1] * (before[...] + every[nvar : 2 * nvar])
            total = src[:, s] + coming[...]
            total += jnp.where(k == 0, 0.0, pltpu.roll(every[2 * nvar : 3 * nvar], 1, 1))
            total += jnp.where(k == rows - 1, 0.0, pltpu.roll(every[3 * nvar : 4 * nvar], rows - 1, 1))
            face = faces[n]
            base = COLS * (s - 1)
            at_low = pltpu.roll(face, LANES - 2 - base, 2)
            at_high = pltpu.roll(face, lax.rem(2 * LANES - 1 - LANES // 2 - 2 - base, LANES), 2)
            a = pltpu.roll(every[4 * nvar : 5 * nvar, :, :LANES], 1, 2)
            b = pltpu.roll(every[4 * nvar : 5 * nvar, :, LANES:], 1, 2)
            c = pltpu.roll(every[5 * nvar :, :, :LANES], LANES - 1, 2)
            d = pltpu.roll(every[5 * nvar :, :, LANES:], LANES - 1, 2)
            left = jnp.where(lane == 0, at_low, a) + jnp.where(lane == LANES - 1, d, c)
            right = jnp.where(lane == 0, a, b) + jnp.where(lane == LANES - 1, at_high, d)
            before[:, :, :LANES] = total[..., :LANES] + left
            before[:, :, LANES:] = total[..., LANES:] + right
            coming[...] = every[:nvar]
            return 0

        lax.fori_loop(n + 1, layers - 1 - n, layer, 0)
        last = layers - 1 - n
        after[:, last - 1] = inv[:, last - 1] * (before[...] + products(p, last, step, 2 * step))
    result = pb if SWEEPS % 2 else pa
    copy = pltpu.make_async_copy(
        result.at[:, DEEP : DEEP + spans, 0:depth], out, out_sem
    )
    copy.start()
    copy.wait()


def sweep_slab(couplings, own, given, source, inv_diag, low, high, depth):
    nvar, spans, _, chord = source.shape
    layers = spans + 2 * DEEP
    rows = max(depth, 16)
    f32 = jnp.float32
    field = pltpu.VMEM((nvar, layers, rows, chord), f32)
    layer = pltpu.VMEM((nvar, rows, chord), f32)
    return pl.pallas_call(
        functools.partial(sweep_kernel, depth),
        in_specs=[VMEM, VMEM, VMEM, ANY, ANY, ANY, ANY],
        out_specs=ANY,
        out_shape=jax.ShapeDtypeStruct((nvar, spans, depth, chord), f32),
        scratch_shapes=[
            field,
            field,
            field,
            field,
            pltpu.VMEM((6 * nvar * 16, 256), jnp.bfloat16),
            layer,
            layer,
            pltpu.VMEM((SWEEPS, nvar, rows, LANES), f32),
            pltpu.VMEM((8, LANES), f32),
            pltpu.SemaphoreType.DMA((6,)),
            pltpu.SemaphoreType.DMA,
        ],
        compiler_params=pltpu.CompilerParams(vmem_limit_bytes=56 * MIB),
        cost_estimate=pl.CostEstimate(
            flops=2 * 40 * 480 * 256 * 256 * (rows // 16), bytes_accessed=16 * MIB, transcendentals=0
        ),
        name=f"sweeps_{depth}",
    )(couplings, own, given, source, inv_diag, low, high)


def wall_kernel(bits, adjoint, jac, weight, ids, out, sens, hi_index, lo_index):
    nvar, spans, _, chord = adjoint.shape
    slots = ids.shape[0]
    dims = jac.shape[0]
    tall = out.shape[1]
    layer = []
    for v in range(nvar):
        for k in range(2):
            layer.append(jnp.concatenate([adjoint[v, s, k : k + 1, :] for s in range(spans)], 0))
    for c in range(dims):
        total = jnp.zeros((spans, chord), jnp.float32)
        for v in range(nvar):
            for k in range(2):
                total += jac[c, v, k] * layer[2 * v + k]
        sens[c] = total
    point = ids[...]
    line = point >> 7
    device = (line * 171) >> 9
    third = line - 3 * device
    pair = device >> 1
    turned = jnp.zeros_like(pair)
    for b in range(bits):
        turned = turned | (((pair >> b) & 1) << (bits - 1 - b))
    hi_index[...] = jnp.where(point < 0, -1, 3 * turned + third)
    lo_index[...] = ((device & 1) << 7) + (point & 127)
    out[...] = jnp.zeros(out.shape, jnp.float32)
    rows = lax.broadcasted_iota(jnp.int32, (tall, chord), 0)
    cols = lax.broadcasted_iota(jnp.int32, (2 * LANES, chord), 0)

    def one(m, _):
        his = hi_index[m]
        los = lo_index[m]
        w = weight[m]
        values = [w * sens[c] for c in range(dims)]
        tops = [x.astype(jnp.bfloat16).astype(jnp.float32) for x in values]
        rests = [x - t for x, t in zip(values, tops)]
        total = jnp.zeros((2 * dims * tall, 2 * LANES), jnp.float32)
        for s in range(spans):
            hit = rows == his[s : s + 1, :]
            left = [
                jnp.where(hit, x[s : s + 1, :], 0.0).astype(jnp.bfloat16) for x in tops + rests
            ]
            right = bit(cols == los[s : s + 1, :]).astype(jnp.bfloat16)
            total += lax.dot_general(
                jnp.concatenate(left, 0),
                right,
                (((1,), (1,)), ((), ())),
                preferred_element_type=jnp.float32,
            )
        for c in range(dims):
            out[c] += total[c * tall : (c + 1) * tall] + total[(dims + c) * tall : (dims + c + 1) * tall]
        return 0

    lax.fori_loop(0, slots, one, 0)


def wall_points(adjoint, wall_jac, weight, ids, n_dev):
    tall = -(-(n_dev // 2 * 3) // 16) * 16
    spans, chord = ids.shape[1:]
    bits = (n_dev // 2).bit_length() - 1
    return pl.pallas_call(
        functools.partial(wall_kernel, bits),
        in_specs=[VMEM] * 4,
        out_specs=VMEM,
        out_shape=jax.ShapeDtypeStruct((wall_jac.shape[0], tall, 2 * LANES), jnp.float32),
        scratch_shapes=[
            pltpu.VMEM((wall_jac.shape[0], spans, chord), jnp.float32),
            pltpu.VMEM(ids.shape, jnp.int32),
            pltpu.VMEM(ids.shape, jnp.int32),
        ],
        compiler_params=pltpu.CompilerParams(vmem_limit_bytes=48 * MIB),
        name="wall_points",
    )(adjoint, wall_jac, weight, ids)


def reduce_points(partial, n_dev):
    n_blk, n_sub = lax.axis_size("blk"), lax.axis_size("sub")
    blk, sub = lax.axis_index("blk"), lax.axis_index("sub")
    partial = partial[:, : n_dev // 2 * 3]
    steps = [("sub", sub, n_sub, 1 << b) for b in range(n_sub.bit_length() - 1)]
    steps += [("blk", blk, n_blk, 1 << b) for b in range(n_blk.bit_length() - 1)]
    for number, (axis, me, count, mask) in enumerate(steps):
        dim = 2 if number == 0 else 1
        half = partial.shape[dim] // 2
        mine = jnp.where((me & mask) != 0, half, 0)
        keep = lax.dynamic_slice_in_dim(partial, mine, half, dim)
        send = lax.dynamic_slice_in_dim(partial, half - mine, half, dim)
        partial = keep + lax.ppermute(send, axis, [(i, i ^ mask) for i in range(count)])
    return partial.reshape(partial.shape[0], -1)


def span_halo(source, inv_diag, depth):
    count = lax.axis_size("sub")
    up = [(i, i + 1) for i in range(count - 1)]
    down = [(b, a) for a, b in up]
    spans = source.shape[1]
    first = jnp.stack([source[:, :DEEP, :depth], inv_diag[:, :DEEP, :depth]])
    last = jnp.stack([source[:, spans - DEEP :, :depth], inv_diag[:, spans - DEEP :, :depth]])
    return lax.ppermute(last, "sub", up), lax.ppermute(first, "sub", down)


def body(source, inv_diag, coupling, face_map, wall_jac, ffd_weight, cp_ids):
    nvar = source.shape[0]
    me = lax.axis_index("blk")
    n_dev = lax.axis_size("blk") * lax.axis_size("sub")
    couplings = jnp.pad(coupling[0].reshape(6 * nvar, nvar), ((0, 2), (0, LANES - nvar)))
    flat = jnp.pad(coupling[0].reshape(-1), (0, 8 * 64 - 6 * nvar * nvar)).reshape(8, 64)
    cpl = jnp.concatenate([flat, flat], 1)

    def sweep(depth):
        low, high = span_halo(source, inv_diag, depth)
        packet = pack_ends(source, inv_diag, low, high, cpl, depth)
        given = route_ends(packet, me, face_map[:, 0], face_map[:, 1])
        return sweep_slab(couplings, packet, given, source, inv_diag, low, high, depth)

    wall = sweep(NEAR)
    partial = wall_points(wall, wall_jac, ffd_weight, cp_ids, n_dev)
    adjoint = sweep(source.shape[2])
    return adjoint, reduce_points(partial, n_dev)


def solution(mesh):
    field = P(None, "sub", None, "blk")
    in_specs = (
        field,
        field,
        P("blk", None, None, None),
        P(),
        P(None, None, None, "sub", "blk"),
        P(None, "sub", "blk"),
        P(None, "sub", "blk"),
    )
    out_specs = (field, P(None, ("blk", "sub")))
    return jax.shard_map(body, mesh=mesh, in_specs=in_specs, out_specs=out_specs, check_vma=False)
```

time: 549 us -> 133 us (0.24)
  matrix products: 143 us -> 0 us
  blocking collectives: 94.3 us -> 0 us
  other arithmetic: 93.5 us -> 5.44 us
  waiting for transfers between devices: 119 us -> 37.2 us
  local copies, waits for them, and re-layouts: 65.8 us -> 8.87 us
  Pallas kernels: 0 us -> 48.2 us
  starting transfers between devices: 11.4 us -> 29 us
  between operations: 18.4 us -> 3.41 us
    dot_general x18 -> x0, matrix products: 143 us -> none  [couple(): jnp.einsum('uv,vsni->usni', matrix, field, precision=lax.Precision.HIGHEST)]
    reduce_scatter x1 -> x0, waiting for transfers between devices: 119 us -> none  [body(): lax.psum_scatter(partial_sums, ('blk', 'sub'), scatter_dimension=1, tiled...]
    all_gather x3 -> x0, blocking collectives: 94.3 us -> none  [relax_piece(): all_ends = lax.all_gather(chord_ends, 'blk', axis=0, tiled=True)]
    scatter-add x1 -> x0, other arithmetic: 83 us -> none  [one_row(): jax.ops.segment_sum(values, slots, num_segments=points_all + 1)[:points_all]]
    pallas_call x0 -> x5, Pallas kernels: none -> 48.2 us  [the longest x2 37.6 us: sweep_slab(): pl.pallas_call(functools.partial(sweep_kernel, depth), in_specs=[VMEM, VM...]
    slice x17 -> x1, local copies, waits for them, and re-layouts: 42.9 us -> 0.01 us  [sweep(): given = route_ends(packet, me, face_map[:, 0], face_map[:, 1])]
    ppermute x6 -> x15, waiting for transfers between devices: 0.02 us -> 37.2 us  [the longest x5 18.4 us: reduce_points(): lax.ppermute(send, axis, [(i, i ^ mask) for i in range(count)])]
    ppermute x6 -> x15, starting transfers between devices: 11.3 us -> 29 us  [the longest x4 11.5 us: span_halo(): return (lax.ppermute(last, 'sub', up), lax.ppermute(first, 'sub', down))]
  transfers between devices with their start and end apart: 7 -> 15, of which waited for: 1 -> 9; matrix products, arithmetic and copies ran while one was open for 22% -> 7% of each run, Pallas kernels for 0% -> 13%
where the time goes in v1:
time: 133 us; the launch traced here: 132 us
  Pallas kernels  48.2 us (36%)
  waiting for transfers between devices  37.2 us (28%)
  starting transfers between devices  29 us (22%)
  local copies, waits for them, and re-layouts  8.87 us (7%)
  other arithmetic  5.44 us (4%)
  between operations  3.41 us (3%)
    pallas_call x2, Pallas kernels, sweep_slab(): pl.pallas_call(functools.partial(sweep_kernel, depth), in_specs=[VMEM, VM...  37.6 us
    ppermute x5, waiting for transfers between devices, reduce_points(): lax.ppermute(send, axis, [(i, i ^ mask) for i in range(count)])  18.4 us
    ppermute x4, waiting for transfers between devices, route_ends(): other = lax.ppermute(held, 'blk', [(i, i ^ mask) for i in range(count)])  15.5 us
    ppermute x4, starting transfers between devices, span_halo(): return (lax.ppermute(last, 'sub', up), lax.ppermute(first, 'sub', down))  11.5 us
    ppermute x5, starting transfers between devices, reduce_points(): lax.ppermute(send, axis, [(i, i ^ mask) for i in range(count)])  7.46 us
    ppermute x4, starting transfers between devices, route_ends(): other = lax.ppermute(held, 'blk', [(i, i ^ mask) for i in range(count)])  6.91 us
    pallas_call x2, Pallas kernels, pack_ends(): pl.pallas_call(functools.partial(pack_kernel, depth), grid=(1,), in_specs...  6.32 us
    pallas_call x1, Pallas kernels, wall_points(): pl.pallas_call(functools.partial(wall_kernel, bits), in_specs=[VMEM] * 4,...  4.26 us
  transfers between devices with their start and end apart: 15, of which 9 were waited for; matrix products, arithmetic and copies ran while one was open for 7% of the time, Pallas kernels for 13%

profile of v1, /device:TPU:0, one launch (start us, length us, event | category | flops | bytes accessed | tf_op | source)
XLA Modules:
  0.0 132.1 jit_solution(6007557364399537851)
XLA Ops:
  0.6 1.1 slice_bitcast_fusion.4
  1.8 2.4 %collective-permute-start.5 = (f32[2,5,3,8,256]{4,3,2,1,0:T(8,128)S(1)}, f32[2,5,3,8,256]{4,3,2,1,0:T(8,128)S(1)}, u32[]{:S(2)}, u32[]{:S(2)}) collective-permute-start(f32[2,5,3,8,256]{4,3,2,1,0:T(8,128)S(1)} %pad_maximum_fusion.4), channel_id=1, source_target_pairs={{0,1},{1,2},{2,3},{4,5},{5,6},{6,7},{8,9},{9,10},{10,11},{12,13},{... | collective-permute-start | bytes 737288 | tf_op jit(solution)/shard_map/ppermute | solution.py:405
  4.2 0.7 pad_maximum_fusion.5
  4.9 1.3 collective-permute-start.6
  6.2 2.4 %slice_bitcast_fusion = (f32[1,5,3,64,256]{4,3,2,1,0:T(8,128)S(1)}, f32[1,5,3,64,256]{4,3,2,1,0:T(8,128)S(1)}, f32[1,5,3,64,256]{4,3,2,1,0:T(8,128)S(1)}, f32[1,5,3,64,256]{4,3,2,1,0:T(8,128)S(1)}) fusion(f32[5,8,64,256]{3,2,1,0:T(8,128)} %inv_in.3, f32[5,8,64,256]{3,2,1,0:T(8,128)} %src_in.3), kind=kLoop, calls=%fused_computation.3 | loop fusion | bytes 7864320 | tf_op jit(solution)/shard_map/stack | solution.py:403
  8.5 1.4 %pad_maximum_fusion = f32[2,5,3,64,256]{4,3,2,1,0:T(8,128)} fusion(f32[1,5,3,64,256]{4,3,2,1,0:T(8,128)S(1)} %get-tuple-element.9, f32[1,5,3,64,256]{4,3,2,1,0:T(8,128)S(1)} %get-tuple-element.16), kind=kLoop, calls=%fused_computation | loop fusion | flops 491520 | bytes 3932160 | tf_op jit(solution)/shard_map/stack | solution.py:404
  9.9 6.4 %collective-permute-start = (f32[2,5,3,64,256]{4,3,2,1,0:T(8,128)}, f32[2,5,3,64,256]{4,3,2,1,0:T(8,128)}, u32[]{:S(2)}, u32[]{:S(2)}) collective-permute-start(f32[2,5,3,64,256]{4,3,2,1,0:T(8,128)} %pad_maximum_fusion), channel_id=1, source_target_pairs={{0,1},{1,2},{2,3},{4,5},{5,6},{6,7},{8,9},{9,10},{10,11},{12,13},{... | collective-permute-start | bytes 5898248 | tf_op jit(solution)/shard_map/ppermute | solution.py:405
  16.4 1.4 %pad_maximum_fusion.1 = f32[2,5,3,64,256]{4,3,2,1,0:T(8,128)} fusion(f32[1,5,3,64,256]{4,3,2,1,0:T(8,128)S(1)} %get-tuple-element.8, f32[1,5,3,64,256]{4,3,2,1,0:T(8,128)S(1)} %get-tuple-element.17), kind=kLoop, calls=%fused_computation.1 | loop fusion | flops 491520 | bytes 3932160 | tf_op jit(solution)/shard_map/stack | solution.py:403
  17.8 1.4 %collective-permute-start.1 = (f32[2,5,3,64,256]{4,3,2,1,0:T(8,128)}, f32[2,5,3,64,256]{4,3,2,1,0:T(8,128)}, u32[]{:S(2)}, u32[]{:S(2)}) collective-permute-start(f32[2,5,3,64,256]{4,3,2,1,0:T(8,128)} %pad_maximum_fusion.1), channel_id=1, source_target_pairs={{1,0},{2,1},{3,2},{5,4},{6,5},{7,6},{9,8},{10,9},{11,10},{13,12},{... | collective-permute-start | bytes 5898248 | tf_op jit(solution)/shard_map/ppermute | solution.py:405
  19.2 0.1 copy.13
  19.3 0.1 reshape_squeeze.7
  19.5 0.1 reshape.26
  19.5 0.1 pad_maximum_fusion.8.cpl
  19.7 1.8 %copy-done.1 = f32[5,8,64,256]{3,2,1,0:T(8,128)S(1)} copy-done((f32[5,8,64,256]{3,2,1,0:T(8,128)S(1)}, f32[5,8,64,256]{3,2,1,0:T(8,128)}, u32[]{:S(2)}) %copy-start.1) | copy-done | bytes 2621464
  21.5 0.3 pack_ends.3.own
  21.8 0.4 copy-done.6
  22.2 2.6 %collective-permute-start.7 = (f32[1,88,128]{2,1,0:T(8,128)S(1)}, f32[1,88,128]{2,1,0:T(8,128)S(1)}, u32[]{:S(2)}, u32[]{:S(2)}) collective-permute-start(f32[1,88,128]{2,1,0:T(8,128)S(1)} %bitcast.50), channel_id=1, source_target_pairs={{0,16},{4,20},{8,24},{12,28},{16,0},{20,4},{24,8},{28,12},{1,17},{... | collective-permute-start | bytes 135176 | tf_op jit(solution)/shard_map/ppermute | solution.py:82
  24.8 0.6 constant_dynamic-slice_fusion.7
  27.9 1.6 %collective-permute-start.8 = (f32[2,88,128]{2,1,0:T(8,128)S(1)}, f32[2,88,128]{2,1,0:T(8,128)S(1)}, u32[]{:S(2)}, u32[]{:S(2)}) collective-permute-start(f32[2,88,128]{2,1,0:T(8,128)S(1)} %pad_maximum_fusion.7), channel_id=1, source_target_pairs={{0,8},{4,12},{8,0},{12,4},{16,24},{20,28},{24,16},{28,20},{1,9},{5... | collective-permute-start | bytes 270344 | tf_op jit(solution)/shard_map/ppermute | solution.py:82
  29.6 3.8 %collective-permute-done.8 = f32[2,88,128]{2,1,0:T(8,128)S(1)} collective-permute-done((f32[2,88,128]{2,1,0:T(8,128)S(1)}, f32[2,88,128]{2,1,0:T(8,128)S(1)}, u32[]{:S(2)}, u32[]{:S(2)}) %collective-permute-start.8) | collective-permute-done | bytes 90144 | tf_op jit(solution)/shard_map/ppermute | solution.py:82
  33.4 1.6 %collective-permute-start.9 = (f32[88,128]{1,0:T(8,128)S(1)}, f32[88,128]{1,0:T(8,128)S(1)}, u32[]{:S(2)}, u32[]{:S(2)}) collective-permute-start(f32[88,128]{1,0:T(8,128)S(1)} %bitcast_select_fusion.2), channel_id=1, source_target_pairs={{0,4},{4,0},{8,12},{12,8},{16,20},{20,16},{24,28},{28,24},{1,5},{5... | collective-permute-start | bytes 135176 | tf_op jit(solution)/shard_map/ppermute | solution.py:102
  35.0 0.6 pad.8.couplings
  35.6 1.9 %collective-permute-done.9 = f32[88,128]{1,0:T(8,128)S(1)} collective-permute-done((f32[88,128]{1,0:T(8,128)S(1)}, f32[88,128]{1,0:T(8,128)S(1)}, u32[]{:S(2)}, u32[]{:S(2)}) %collective-permute-start.9) | collective-permute-done | bytes 45088 | tf_op jit(solution)/shard_map/ppermute | solution.py:102
  37.5 0.6 fusion.1.given
  38.1 12.6 %sweeps_8.1.adjoint = f32[5,8,8,256]{3,2,1,0:T(8,128)} custom-call(f32[32,128]{1,0:T(8,128)} %pad.8.couplings, f32[88,128]{1,0:T(8,128)} %copy-done.3, f32[88,128]{1,0:T(8,128)} %fusion.1.given, f32[5,8,64,256]{3,2,1,0:T(8,128)} %src_in.3, f32[5,8,64,256]{3,2,1,0:T(8,128)} %inv_in.3, f32[2,5,3,8,256]{4,3,2,1,0:T(8,128)} %copy-done.5, ...), custom_call_target="tpu_custom_call" | custom-call | flops 2516582400 | bytes 16777216 | tf_op jit(solution)/shard_map/sweeps_8/pallas_call | solution.py:281
  50.8 1.0 copy-done.4
  51.8 4.3 %wall_points.1 = f32[3,48,256]{2,1,0:T(8,128)S(1)} custom-call(f32[5,8,8,256]{3,2,1,0:T(8,128)S(1)} %copy-done.4, f32[3,5,2,8,256]{4,3,2,1,0:T(8,128)S(1)} %copy-done.7, f32[8,8,256]{2,1,0:T(8,128)S(1)} %copy-done.8, s32[8,8,256]{2,1,0:T(8,128)S(1)} %copy-done.9), custom_call_target="tpu_custom_call" | custom-call | tf_op jit(solution)/shard_map/wall_points/pallas_call | solution.py:367
  56.1 0.1 collective-permute-start.10
  56.2 1.2 collective-permute-done.10
  57.5 6.0 %pack_ends.2.own = f32[648,128]{1,0:T(8,128)S(1)} custom-call(f32[5,8,64,256]{3,2,1,0:T(8,128)} %src_in.3, f32[5,8,64,256]{3,2,1,0:T(8,128)} %inv_in.3, f32[2,5,3,64,256]{4,3,2,1,0:T(8,128)} %collective-permute-done.low, f32[2,5,3,64,256]{4,3,2,1,0:T(8,128)} %collective-permute-done.1.high, f32[8,128]{1,0:T(8,128)S(1)} %pad_maximum_fusion.8.cpl), custom_call_target="tpu_custom_call" | custom-call | tf_op jit(solution)/shard_map/pack_ends/pallas_call | solution.py:65
  63.5 2.3 %collective-permute-start.2 = (f32[1,648,128]{2,1,0:T(8,128)S(1)}, f32[1,648,128]{2,1,0:T(8,128)S(1)}, u32[]{:S(2)}, u32[]{:S(2)}) collective-permute-start(f32[1,648,128]{2,1,0:T(8,128)S(1)} %bitcast.47), channel_id=1, source_target_pairs={{0,16},{4,20},{8,24},{12,28},{16,0},{20,4},{24,8},{28,12},{1,17},{... | collective-permute-start | bytes 995336 | tf_op jit(solution)/shard_map/ppermute | solution.py:82
  65.8 1.5 %collective-permute-start.11 = (f32[3,24,128]{2,1,0:T(8,128)S(1)}, f32[3,24,128]{2,1,0:T(8,128)S(1)}, u32[]{:S(2)}, u32[]{:S(2)}) collective-permute-start(f32[3,24,128]{2,1,0:T(8,128)S(1)} %constant_dynamic-slice_fusion.2), channel_id=1, source_target_pairs={{0,2},{1,3},{2,0},{3,1},{4,6},{5,7},{6,4},{7,5},{8,10},{9,11},{10,... | collective-permute-start | bytes 110600 | tf_op jit(solution)/shard_map/ppermute | solution.py:394
  67.2 2.5 %collective-permute-done.11 = f32[3,24,128]{2,1,0:T(8,128)S(1)} collective-permute-done((f32[3,24,128]{2,1,0:T(8,128)S(1)}, f32[3,24,128]{2,1,0:T(8,128)S(1)}, u32[]{:S(2)}, u32[]{:S(2)}) %collective-permute-start.11) | collective-permute-done | bytes 36896 | tf_op jit(solution)/shard_map/ppermute | solution.py:394
  69.7 11.7 %collective-permute-done.2 = f32[1,648,128]{2,1,0:T(8,128)S(1)} collective-permute-done((f32[1,648,128]{2,1,0:T(8,128)S(1)}, f32[1,648,128]{2,1,0:T(8,128)S(1)}, u32[]{:S(2)}, u32[]{:S(2)}) %collective-permute-start.2) | collective-permute-done | bytes 331808 | tf_op jit(solution)/shard_map/ppermute | solution.py:82
  81.4 0.1 pad_maximum_fusion.3
  81.5 0.4 collective-permute-start.3
  81.9 1.5 %collective-permute-start.12 = (f32[3,12,128]{2,1,0:T(8,128)S(1)}, f32[3,12,128]{2,1,0:T(8,128)S(1)}, u32[]{:S(2)}, u32[]{:S(2)}) collective-permute-start(f32[3,12,128]{2,1,0:T(8,128)S(1)} %constant_dynamic-slice_fusion.1), channel_id=1, source_target_pairs={{0,4},{4,0},{8,12},{12,8},{16,20},{20,16},{24,28},{28,24},{1,5},{5... | collective-permute-start | bytes 55304 | tf_op jit(solution)/shard_map/ppermute | solution.py:394
  83.4 2.3 %collective-permute-done.12 = f32[3,12,128]{2,1,0:T(8,128)S(1)} collective-permute-done((f32[3,12,128]{2,1,0:T(8,128)S(1)}, f32[3,12,128]{2,1,0:T(8,128)S(1)}, u32[]{:S(2)}, u32[]{:S(2)}) %collective-permute-start.12) | collective-permute-done | bytes 18464 | tf_op jit(solution)/shard_map/ppermute | solution.py:394
  85.8 1.8 %collective-permute-start.13 = (f32[3,6,128]{2,1,0:T(8,128)S(1)}, f32[3,6,128]{2,1,0:T(8,128)S(1)}, u32[]{:S(2)}, u32[]{:S(2)}) collective-permute-start(f32[3,6,128]{2,1,0:T(8,128)S(1)} %constant_dynamic-slice_fusion), channel_id=1, source_target_pairs={{0,8},{4,12},{8,0},{12,4},{16,24},{20,28},{24,16},{28,20},{1,9},{5... | collective-permute-start | bytes 27656 | tf_op jit(solution)/shard_map/ppermute | solution.py:394
  87.5 10.4 %collective-permute-done.13 = f32[3,6,128]{2,1,0:T(8,128)S(1)} collective-permute-done((f32[3,6,128]{2,1,0:T(8,128)S(1)}, f32[3,6,128]{2,1,0:T(8,128)S(1)}, u32[]{:S(2)}, u32[]{:S(2)}) %collective-permute-start.13) | collective-permute-done | bytes 9248 | tf_op jit(solution)/shard_map/ppermute | solution.py:394
  98.0 0.1 pad_maximum_fusion.2
  98.2 1.6 %collective-permute-start.4 = (f32[648,128]{1,0:T(8,128)S(1)}, f32[648,128]{1,0:T(8,128)S(1)}, u32[]{:S(2)}, u32[]{:S(2)}) collective-permute-start(f32[648,128]{1,0:T(8,128)S(1)} %bitcast_select_fusion), channel_id=1, source_target_pairs={{0,4},{4,0},{8,12},{12,8},{16,20},{20,16},{24,28},{28,24},{1,5},{5... | collective-permute-start | bytes 995336 | tf_op jit(solution)/shard_map/ppermute | solution.py:102
  99.7 2.7 %collective-permute-start.14 = (f32[3,3,128]{2,1,0:T(4,128)S(1)}, f32[3,3,128]{2,1,0:T(4,128)S(1)}, u32[]{:S(2)}, u32[]{:S(2)}) collective-permute-start(f32[3,3,128]{2,1,0:T(4,128)S(1)} %constant_dynamic-slice_fusion.5), channel_id=1, source_target_pairs={{0,16},{4,20},{8,24},{12,28},{16,0},{20,4},{24,8},{28,12},{1,17},{... | collective-permute-start | bytes 13832 | tf_op jit(solution)/shard_map/ppermute | solution.py:394
  102.4 1.9 %collective-permute-done.14 = f32[3,3,128]{2,1,0:T(4,128)S(1)} collective-permute-done((f32[3,3,128]{2,1,0:T(4,128)S(1)}, f32[3,3,128]{2,1,0:T(4,128)S(1)}, u32[]{:S(2)}, u32[]{:S(2)}) %collective-permute-start.14) | collective-permute-done | bytes 4640 | tf_op jit(solution)/shard_map/ppermute | solution.py:394
  104.3 0.6 copy.17
  104.9 1.5 %collective-permute-done.4 = f32[648,128]{1,0:T(8,128)S(1)} collective-permute-done((f32[648,128]{1,0:T(8,128)S(1)}, f32[648,128]{1,0:T(8,128)S(1)}, u32[]{:S(2)}, u32[]{:S(2)}) %collective-permute-start.4) | collective-permute-done | bytes 331808 | tf_op jit(solution)/shard_map/ppermute | solution.py:102
  106.3 0.8 fusion.given
  107.2 25.0 %sweeps_64.1 = f32[5,8,64,256]{3,2,1,0:T(8,128)} custom-call(f32[32,128]{1,0:T(8,128)} %pad.8.couplings, f32[648,128]{1,0:T(8,128)} %copy-done.2, f32[648,128]{1,0:T(8,128)} %fusion.given, f32[5,8,64,256]{3,2,1,0:T(8,128)} %src_in.3, f32[5,8,64,256]{3,2,1,0:T(8,128)} %inv_in.3, f32[2,5,3,64,256]{4,3,2,1,0:T(8,128)} %collective-permute-done.low, ...), custom_call_target="tpu_custom_call" | custom-call | flops 10066329600 | bytes 16777216 | tf_op jit(solution)/shard_map/sweeps_64/pallas_call | solution.py:281
  (47 shorter events, 0.3 us)
Async XLA Ops:
  1.8 17.8 %collective-permute-start.5 = (f32[2,5,3,8,256]{4,3,2,1,0:T(8,128)S(1)}, f32[2,5,3,8,256]{4,3,2,1,0:T(8,128)S(1)}, u32[]{:S(2)}, u32[]{:S(2)}) collective-permute-start(f32[2,5,3,8,256]{4,3,2,1,0:T(8,128)S(1)} %pad_maximum_fusion.4), channel_id=1, source_target_pairs={{0,1},{1,2},{2,3},{4,5},{5,6},{6,7},{8,9},{9,10},{10,11},{12,13},{... | collective-permute-start | bytes 737288 | tf_op jit(solution)/shard_map/ppermute | solution.py:405
  4.9 14.7 %collective-permute-start.6 = (f32[2,5,3,8,256]{4,3,2,1,0:T(8,128)}, f32[2,5,3,8,256]{4,3,2,1,0:T(8,128)S(1)}, u32[]{:S(2)}, u32[]{:S(2)}) collective-permute-start(f32[2,5,3,8,256]{4,3,2,1,0:T(8,128)} %pad_maximum_fusion.5), channel_id=1, source_target_pairs={{1,0},{2,1},{3,2},{5,4},{6,5},{7,6},{9,8},{10,9},{11,10},{13,12},{... | collective-permute-start | bytes 737288 | tf_op jit(solution)/shard_map/ppermute | solution.py:405
  9.9 47.5 %collective-permute-start = (f32[2,5,3,64,256]{4,3,2,1,0:T(8,128)}, f32[2,5,3,64,256]{4,3,2,1,0:T(8,128)}, u32[]{:S(2)}, u32[]{:S(2)}) collective-permute-start(f32[2,5,3,64,256]{4,3,2,1,0:T(8,128)} %pad_maximum_fusion), channel_id=1, source_target_pairs={{0,1},{1,2},{2,3},{4,5},{5,6},{6,7},{8,9},{9,10},{10,11},{12,13},{... | collective-permute-start | bytes 5898248 | tf_op jit(solution)/shard_map/ppermute | solution.py:405
  16.4 2.8 %copy-start.10 = (f32[1,6,5,5]{1,0,3,2:T(1,128)S(1)}, f32[1,6,5,5]{1,0,3,2:T(1,128)}, u32[]{:S(2)}) copy-start(f32[1,6,5,5]{1,0,3,2:T(1,128)} %param.9) | copy-start | bytes 1804
  16.4 3.3 %copy-start = (f32[5,8,64,256]{3,2,1,0:T(8,128)S(1)}, f32[5,8,64,256]{3,2,1,0:T(8,128)}, u32[]{:S(2)}) copy-start(f32[5,8,64,256]{3,2,1,0:T(8,128)} %src_in.3) | copy-start | bytes 7864324
  17.8 39.7 %collective-permute-start.1 = (f32[2,5,3,64,256]{4,3,2,1,0:T(8,128)}, f32[2,5,3,64,256]{4,3,2,1,0:T(8,128)}, u32[]{:S(2)}, u32[]{:S(2)}) collective-permute-start(f32[2,5,3,64,256]{4,3,2,1,0:T(8,128)} %pad_maximum_fusion.1), channel_id=1, source_target_pairs={{1,0},{2,1},{3,2},{5,4},{6,5},{7,6},{9,8},{10,9},{11,10},{13,12},{... | collective-permute-start | bytes 5898248 | tf_op jit(solution)/shard_map/ppermute | solution.py:405
  19.5 5.2 %copy-start.11 = (s32[8,2]{0,1:T(2,128)S(1)}, s32[8,2]{0,1:T(2,128)}, u32[]{:S(2)}) copy-start(s32[8,2]{0,1:T(2,128)} %param.10) | copy-start | bytes 196
  19.6 2.2 %copy-start.5 = (f32[2,5,3,8,256]{4,3,2,1,0:T(8,128)}, f32[2,5,3,8,256]{4,3,2,1,0:T(8,128)S(1)}, u32[]{:S(2)}) copy-start(f32[2,5,3,8,256]{4,3,2,1,0:T(8,128)S(1)} %collective-permute-done.5.low) | copy-start | bytes 737284
  19.6 1.8 %copy-start.1 = (f32[5,8,64,256]{3,2,1,0:T(8,128)S(1)}, f32[5,8,64,256]{3,2,1,0:T(8,128)}, u32[]{:S(2)}) copy-start(f32[5,8,64,256]{3,2,1,0:T(8,128)} %inv_in.3) | copy-start | bytes 7864324
  21.5 0.7 copy-start.6
  22.2 16.0 %copy-start.3 = (f32[88,128]{1,0:T(8,128)}, f32[88,128]{1,0:T(8,128)S(1)}, u32[]{:S(2)}) copy-start(f32[88,128]{1,0:T(8,128)S(1)} %pack_ends.3.own) | copy-start | bytes 135172
  22.2 5.7 %collective-permute-start.7 = (f32[1,88,128]{2,1,0:T(8,128)S(1)}, f32[1,88,128]{2,1,0:T(8,128)S(1)}, u32[]{:S(2)}, u32[]{:S(2)}) collective-permute-start(f32[1,88,128]{2,1,0:T(8,128)S(1)} %bitcast.50), channel_id=1, source_target_pairs={{0,16},{4,20},{8,24},{12,28},{16,0},{20,4},{24,8},{28,12},{1,17},{... | collective-permute-start | bytes 135176 | tf_op jit(solution)/shard_map/ppermute | solution.py:82
  27.9 5.4 %collective-permute-start.8 = (f32[2,88,128]{2,1,0:T(8,128)S(1)}, f32[2,88,128]{2,1,0:T(8,128)S(1)}, u32[]{:S(2)}, u32[]{:S(2)}) collective-permute-start(f32[2,88,128]{2,1,0:T(8,128)S(1)} %pad_maximum_fusion.7), channel_id=1, source_target_pairs={{0,8},{4,12},{8,0},{12,4},{16,24},{20,28},{24,16},{28,20},{1,9},{5... | collective-permute-start | bytes 270344 | tf_op jit(solution)/shard_map/ppermute | solution.py:82
  33.4 4.1 %collective-permute-start.9 = (f32[88,128]{1,0:T(8,128)S(1)}, f32[88,128]{1,0:T(8,128)S(1)}, u32[]{:S(2)}, u32[]{:S(2)}) collective-permute-start(f32[88,128]{1,0:T(8,128)S(1)} %bitcast_select_fusion.2), channel_id=1, source_target_pairs={{0,4},{4,0},{8,12},{12,8},{16,20},{20,16},{24,28},{28,24},{1,5},{5... | collective-permute-start | bytes 135176 | tf_op jit(solution)/shard_map/ppermute | solution.py:102
  38.1 12.7 %copy-start.7 = (f32[3,5,2,8,256]{4,3,2,1,0:T(8,128)S(1)}, f32[3,5,2,8,256]{4,3,2,1,0:T(8,128)}, u32[]{:S(2)}) copy-start(f32[3,5,2,8,256]{4,3,2,1,0:T(8,128)} %jac.1) | copy-start | bytes 737284
  38.1 12.7 %copy-start.8 = (f32[8,8,256]{2,1,0:T(8,128)S(1)}, f32[8,8,256]{2,1,0:T(8,128)}, u32[]{:S(2)}) copy-start(f32[8,8,256]{2,1,0:T(8,128)} %weight.1) | copy-start | bytes 196612
  38.1 12.7 %copy-start.9 = (s32[8,8,256]{2,1,0:T(8,128)S(1)}, s32[8,8,256]{2,1,0:T(8,128)}, u32[]{:S(2)}) copy-start(s32[8,8,256]{2,1,0:T(8,128)} %ids.1) | copy-start | bytes 196612
  50.8 1.0 copy-start.4
  56.1 1.3 %collective-permute-start.10 = (f32[3,48,128]{2,1,0:T(8,128)S(1)}, f32[3,48,128]{2,1,0:T(8,128)S(1)}, u32[]{:S(2)}, u32[]{:S(2)}) collective-permute-start(f32[3,48,128]{2,1,0:T(8,128)S(1)} %constant_dynamic-slice_fusion.3), channel_id=1, source_target_pairs={{0,1},{1,0},{2,3},{3,2},{4,5},{5,4},{6,7},{7,6},{8,9},{9,8},{10,11... | collective-permute-start | bytes 221192 | tf_op jit(solution)/shard_map/ppermute | solution.py:394
  63.5 34.6 %copy-start.2 = (f32[648,128]{1,0:T(8,128)}, f32[648,128]{1,0:T(8,128)S(1)}, u32[]{:S(2)}) copy-start(f32[648,128]{1,0:T(8,128)S(1)} %pack_ends.2.own) | copy-start | bytes 995332
  63.5 17.9 %collective-permute-start.2 = (f32[1,648,128]{2,1,0:T(8,128)S(1)}, f32[1,648,128]{2,1,0:T(8,128)S(1)}, u32[]{:S(2)}, u32[]{:S(2)}) collective-permute-start(f32[1,648,128]{2,1,0:T(8,128)S(1)} %bitcast.47), channel_id=1, source_target_pairs={{0,16},{4,20},{8,24},{12,28},{16,0},{20,4},{24,8},{28,12},{1,17},{... | collective-permute-start | bytes 995336 | tf_op jit(solution)/shard_map/ppermute | solution.py:82
  65.8 4.0 %collective-permute-start.11 = (f32[3,24,128]{2,1,0:T(8,128)S(1)}, f32[3,24,128]{2,1,0:T(8,128)S(1)}, u32[]{:S(2)}, u32[]{:S(2)}) collective-permute-start(f32[3,24,128]{2,1,0:T(8,128)S(1)} %constant_dynamic-slice_fusion.2), channel_id=1, source_target_pairs={{0,2},{1,3},{2,0},{3,1},{4,6},{5,7},{6,4},{7,5},{8,10},{9,11},{10,... | collective-permute-start | bytes 110600 | tf_op jit(solution)/shard_map/ppermute | solution.py:394
  81.5 16.5 %collective-permute-start.3 = (f32[2,648,128]{2,1,0:T(8,128)S(1)}, f32[2,648,128]{2,1,0:T(8,128)S(1)}, u32[]{:S(2)}, u32[]{:S(2)}) collective-permute-start(f32[2,648,128]{2,1,0:T(8,128)S(1)} %pad_maximum_fusion.3), channel_id=1, source_target_pairs={{0,8},{4,12},{8,0},{12,4},{16,24},{20,28},{24,16},{28,20},{1,9},{5... | collective-permute-start | bytes 1990664 | tf_op jit(solution)/shard_map/ppermute | solution.py:82
  81.9 3.8 %collective-permute-start.12 = (f32[3,12,128]{2,1,0:T(8,128)S(1)}, f32[3,12,128]{2,1,0:T(8,128)S(1)}, u32[]{:S(2)}, u32[]{:S(2)}) collective-permute-start(f32[3,12,128]{2,1,0:T(8,128)S(1)} %constant_dynamic-slice_fusion.1), channel_id=1, source_target_pairs={{0,4},{4,0},{8,12},{12,8},{16,20},{20,16},{24,28},{28,24},{1,5},{5... | collective-permute-start | bytes 55304 | tf_op jit(solution)/shard_map/ppermute | solution.py:394
  85.8 12.2 %collective-permute-start.13 = (f32[3,6,128]{2,1,0:T(8,128)S(1)}, f32[3,6,128]{2,1,0:T(8,128)S(1)}, u32[]{:S(2)}, u32[]{:S(2)}) collective-permute-start(f32[3,6,128]{2,1,0:T(8,128)S(1)} %constant_dynamic-slice_fusion), channel_id=1, source_target_pairs={{0,8},{4,12},{8,0},{12,4},{16,24},{20,28},{24,16},{28,20},{1,9},{5... | collective-permute-start | bytes 27656 | tf_op jit(solution)/shard_map/ppermute | solution.py:394
  98.2 8.2 %collective-permute-start.4 = (f32[648,128]{1,0:T(8,128)S(1)}, f32[648,128]{1,0:T(8,128)S(1)}, u32[]{:S(2)}, u32[]{:S(2)}) collective-permute-start(f32[648,128]{1,0:T(8,128)S(1)} %bitcast_select_fusion), channel_id=1, source_target_pairs={{0,4},{4,0},{8,12},{12,8},{16,20},{20,16},{24,28},{28,24},{1,5},{5... | collective-permute-start | bytes 995336 | tf_op jit(solution)/shard_map/ppermute | solution.py:102
  99.7 4.5 %collective-permute-start.14 = (f32[3,3,128]{2,1,0:T(4,128)S(1)}, f32[3,3,128]{2,1,0:T(4,128)S(1)}, u32[]{:S(2)}, u32[]{:S(2)}) collective-permute-start(f32[3,3,128]{2,1,0:T(4,128)S(1)} %constant_dynamic-slice_fusion.5), channel_id=1, source_target_pairs={{0,16},{4,20},{8,24},{12,28},{16,0},{20,4},{24,8},{28,12},{1,17},{... | collective-permute-start | bytes 13832 | tf_op jit(solution)/shard_map/ppermute | solution.py:394

commit v2 on v1

--- a/solution.py
+++ b/solution.py
@@ -152,16 +152,22 @@
     mine = own[rows : rows + 8, :]
     theirs = given[rows : rows + 8, :]
 
-    def spread(tile, index, half):
-        at = (index & 63) + (LANES // 2) * half
-        return jnp.broadcast_to(tile[index >> 6 : (index >> 6) + 1, at : at + 1], (1, LANES))
-
-    own_c = [spread(mine, i, 0) for i in range(150)]
-    mixed = []
-    for i in range(150):
-        other = jnp.where(side, spread(theirs, i, 1), spread(theirs, i, 0))
-        mixed.append(jnp.where(ghost, other, own_c[i]))
-
+    one = lax.broadcasted_iota(jnp.int32, (152, 8), 0)
+    pick = bit((one >> 6) == lax.broadcasted_iota(jnp.int32, (152, 8), 1))
+    index = lax.broadcasted_iota(jnp.int32, (152, LANES), 0)
+    keep = (index & 63) == (lane_iota((152, LANES)) & 63)
+    half = lax.broadcasted_iota(jnp.int32, (LANES, LANES), 0) >> 6
+    fill = bit(half == (lane_iota((LANES, LANES)) >> 6))
+
+    def spread(tile):
+        tall = jnp.dot(pick, tile, precision=lax.Precision.HIGHEST)
+        return jnp.dot(jnp.where(keep, tall, 0.0), fill, precision=lax.Precision.HIGHEST)
+
+    own_rows = spread(mine)
+    scalars[0] = own_rows
+    scalars[1] = jnp.where(ghost, spread(theirs), own_rows)
+    mixed = [scalars[1, i : i + 1, :] for i in range(150)]
+    own_c = {i: scalars[0, i : i + 1, :] for i in range(100, 150)}
     k = lax.broadcasted_iota(jnp.int32, (depth, LANES), 0)
     p = [inv[v] * src[v] for v in range(nvar)]
     for n in range(SWEEPS):
@@ -234,33 +240,42 @@
             pieces.append(y.reshape((last_row - first_row) // 16, 16, chord))
         return jnp.concatenate(pieces, 1) if groups > 1 else pieces[0]
 
+    def along(every, n, s):
+        total = jnp.where(k == 0, 0.0, pltpu.roll(every[2 * nvar : 3 * nvar], 1, 1))
+        total += jnp.where(k == rows - 1, 0.0, pltpu.roll(every[3 * nvar : 4 * nvar], rows - 1, 1))
+        face = faces[n]
+        base = COLS * (s - 1)
+        at_low = pltpu.roll(face, LANES - 2 - base, 2)
+        at_high = pltpu.roll(face, lax.rem(2 * LANES - 1 - LANES // 2 - 2 - base, LANES), 2)
+        a = pltpu.roll(every[4 * nvar : 5 * nvar, :, :LANES], 1, 2)
+        b = pltpu.roll(every[4 * nvar : 5 * nvar, :, LANES:], 1, 2)
+        c = pltpu.roll(every[5 * nvar :, :, :LANES], LANES - 1, 2)
+        d = pltpu.roll(every[5 * nvar :, :, LANES:], LANES - 1, 2)
+        left = jnp.where(lane == 0, at_low, a) + jnp.where(lane == LANES - 1, d, c)
+        right = jnp.where(lane == 0, a, b) + jnp.where(lane == LANES - 1, at_high, d)
+        return total + jnp.concatenate([left, right], 2)
+
     step = 16 * nvar
     for n in range(SWEEPS):
         p, after = (pa, pb) if n % 2 == 0 else (pb, pa)
         coming[...] = products(p, n, 0, step)
-
-        def layer(s, _):
-            every = products(p, s, 0, 6 * step)
-            after[:, s - 1] = inv[:, s - 1] * (before[...] + every[nvar : 2 * nvar])
-            total = src[:, s] + coming[...]
-            total += jnp.where(k == 0, 0.0, pltpu.roll(every[2 * nvar : 3 * nvar], 1, 1))
-            total += jnp.where(k == rows - 1, 0.0, pltpu.roll(every[3 * nvar : 4 * nvar], rows - 1, 1))
-            face = faces[n]
-            base = COLS * (s - 1)
-            at_low = pltpu.roll(face, LANES - 2 - base, 2)
-            at_high = pltpu.roll(face, lax.rem(2 * LANES - 1 - LANES // 2 - 2 - base, LANES), 2)
-            a = pltpu.roll(every[4 * nvar : 5 * nvar, :, :LANES], 1, 2)
-            b = pltpu.roll(every[4 * nvar : 5 * nvar, :, LANES:], 1, 2)
-            c = pltpu.roll(every[5 * nvar :, :, :LANES], LANES - 1, 2)
-            d = pltpu.roll(every[5 * nvar :, :, LANES:], LANES - 1, 2)
-            left = jnp.where(lane == 0, at_low, a) + jnp.where(lane == LANES - 1, d, c)
-            right = jnp.where(lane == 0, a, b) + jnp.where(lane == LANES - 1, at_high, d)
-            before[:, :, :LANES] = total[..., :LANES] + left
-            before[:, :, LANES:] = total[..., LANES:] + right
-            coming[...] = every[:nvar]
+        full = layers - 2 - 2 * n
+        turn = 2 if groups > 1 else full
+
+        def several(i, _):
+            s0 = n + 1 + i * turn
+            every = [products(p, s0 + j, 0, 6 * step) for j in range(turn)]
+            arriving, waiting = coming[...], before[...]
+            for j in range(turn):
+                s, now = s0 + j, every[j]
+                after[:, s - 1] = inv[:, s - 1] * (waiting + now[nvar : 2 * nvar])
+                waiting = src[:, s] + arriving + along(now, n, s)
+                arriving = now[:nvar]
+            before[...] = waiting
+            coming[...] = arriving
             return 0
 
-        lax.fori_loop(n + 1, layers - 1 - n, layer, 0)
+        lax.fori_loop(0, full // turn, several, 0)
         last = layers - 1 - n
         after[:, last - 1] = inv[:, last - 1] * (before[...] + products(p, last, step, 2 * step))
     result = pb if SWEEPS % 2 else pa
@@ -292,7 +307,7 @@
             layer,
             layer,
             pltpu.VMEM((SWEEPS, nvar, rows, LANES), f32),
-            pltpu.VMEM((8, LANES), f32),
+            pltpu.VMEM((2, 152, LANES), f32),
             pltpu.SemaphoreType.DMA((6,)),
             pltpu.SemaphoreType.DMA,
         ],

time: 133 us -> 123 us (0.925)
  Pallas kernels: 48.2 us -> 38.6 us
    pallas_call x2, Pallas kernels: 37.6 us -> 28 us  [sweep_slab(): pl.pallas_call(functools.partial(sweep_kernel, depth), in_specs=[VMEM, VM...]
  transfers between devices with their start and end apart: 15 -> 15, of which waited for: 9 -> 9; matrix products, arithmetic and copies ran while one was open for 7% -> 7% of each run, Pallas kernels for 13% -> 9%
where the time goes in v2:
time: 123 us
  Pallas kernels  38.6 us (31%)
  waiting for transfers between devices  37.2 us (30%)
  starting transfers between devices  29 us (24%)
  local copies, waits for them, and re-layouts  8.87 us (7%)
  other arithmetic  5.41 us (4%)
  between operations  3.57 us (3%)
    pallas_call x2, Pallas kernels, sweep_slab(): pl.pallas_call(functools.partial(sweep_kernel, depth), in_specs=[VMEM, VM...  28 us
    ppermute x5, waiting for transfers between devices, reduce_points(): lax.ppermute(send, axis, [(i, i ^ mask) for i in range(count)])  18.4 us
    ppermute x4, waiting for transfers between devices, route_ends(): other = lax.ppermute(held, 'blk', [(i, i ^ mask) for i in range(count)])  15.5 us
    ppermute x4, starting transfers between devices, span_halo(): return (lax.ppermute(last, 'sub', up), lax.ppermute(first, 'sub', down))  11.5 us
    ppermute x5, starting transfers between devices, reduce_points(): lax.ppermute(send, axis, [(i, i ^ mask) for i in range(count)])  7.45 us
    ppermute x4, starting transfers between devices, route_ends(): other = lax.ppermute(held, 'blk', [(i, i ^ mask) for i in range(count)])  6.92 us
    pallas_call x2, Pallas kernels, pack_ends(): pl.pallas_call(functools.partial(pack_kernel, depth), grid=(1,), in_specs...  6.32 us
    pallas_call x1, Pallas kernels, wall_points(): pl.pallas_call(functools.partial(wall_kernel, bits), in_specs=[VMEM] * 4,...  4.25 us
  transfers between devices with their start and end apart: 15, of which 9 were waited for; matrix products, arithmetic and copies ran while one was open for 7% of the time, Pallas kernels for 9%

profile of v2, /device:TPU:0, one launch (start us, length us, event | category | flops | bytes accessed | tf_op | source)
XLA Modules:
  0.0 122.7 jit_solution(11444689374087143381)
XLA Ops:
  0.6 1.1 slice_bitcast_fusion.4
  1.8 2.4 %collective-permute-start.5 = (f32[2,5,3,8,256]{4,3,2,1,0:T(8,128)S(1)}, f32[2,5,3,8,256]{4,3,2,1,0:T(8,128)S(1)}, u32[]{:S(2)}, u32[]{:S(2)}) collective-permute-start(f32[2,5,3,8,256]{4,3,2,1,0:T(8,128)S(1)} %pad_maximum_fusion.4), channel_id=1, source_target_pairs={{0,1},{1,2},{2,3},{4,5},{5,6},{6,7},{8,9},{9,10},{10,11},{12,13},{... | collective-permute-start | bytes 737288 | tf_op jit(solution)/shard_map/ppermute | solution.py:420
  4.2 0.7 pad_maximum_fusion.5
  4.9 1.3 %collective-permute-start.6 = (f32[2,5,3,8,256]{4,3,2,1,0:T(8,128)}, f32[2,5,3,8,256]{4,3,2,1,0:T(8,128)S(1)}, u32[]{:S(2)}, u32[]{:S(2)}) collective-permute-start(f32[2,5,3,8,256]{4,3,2,1,0:T(8,128)} %pad_maximum_fusion.5), channel_id=1, source_target_pairs={{1,0},{2,1},{3,2},{5,4},{6,5},{7,6},{9,8},{10,9},{11,10},{13,12},{... | collective-permute-start | bytes 737288 | tf_op jit(solution)/shard_map/ppermute | solution.py:420
  6.2 2.4 %slice_bitcast_fusion = (f32[1,5,3,64,256]{4,3,2,1,0:T(8,128)S(1)}, f32[1,5,3,64,256]{4,3,2,1,0:T(8,128)S(1)}, f32[1,5,3,64,256]{4,3,2,1,0:T(8,128)S(1)}, f32[1,5,3,64,256]{4,3,2,1,0:T(8,128)S(1)}) fusion(f32[5,8,64,256]{3,2,1,0:T(8,128)} %inv_in.3, f32[5,8,64,256]{3,2,1,0:T(8,128)} %src_in.3), kind=kLoop, calls=%fused_computation.3 | loop fusion | bytes 7864320 | tf_op jit(solution)/shard_map/stack | solution.py:418
  8.5 1.4 %pad_maximum_fusion = f32[2,5,3,64,256]{4,3,2,1,0:T(8,128)} fusion(f32[1,5,3,64,256]{4,3,2,1,0:T(8,128)S(1)} %get-tuple-element.9, f32[1,5,3,64,256]{4,3,2,1,0:T(8,128)S(1)} %get-tuple-element.16), kind=kLoop, calls=%fused_computation | loop fusion | flops 491520 | bytes 3932160 | tf_op jit(solution)/shard_map/stack | solution.py:419
  9.9 6.4 %collective-permute-start = (f32[2,5,3,64,256]{4,3,2,1,0:T(8,128)}, f32[2,5,3,64,256]{4,3,2,1,0:T(8,128)}, u32[]{:S(2)}, u32[]{:S(2)}) collective-permute-start(f32[2,5,3,64,256]{4,3,2,1,0:T(8,128)} %pad_maximum_fusion), channel_id=1, source_target_pairs={{0,1},{1,2},{2,3},{4,5},{5,6},{6,7},{8,9},{9,10},{10,11},{12,13},{... | collective-permute-start | bytes 5898248 | tf_op jit(solution)/shard_map/ppermute | solution.py:420
  16.4 1.4 %pad_maximum_fusion.1 = f32[2,5,3,64,256]{4,3,2,1,0:T(8,128)} fusion(f32[1,5,3,64,256]{4,3,2,1,0:T(8,128)S(1)} %get-tuple-element.8, f32[1,5,3,64,256]{4,3,2,1,0:T(8,128)S(1)} %get-tuple-element.17), kind=kLoop, calls=%fused_computation.1 | loop fusion | flops 491520 | bytes 3932160 | tf_op jit(solution)/shard_map/stack | solution.py:418
  17.8 1.4 %collective-permute-start.1 = (f32[2,5,3,64,256]{4,3,2,1,0:T(8,128)}, f32[2,5,3,64,256]{4,3,2,1,0:T(8,128)}, u32[]{:S(2)}, u32[]{:S(2)}) collective-permute-start(f32[2,5,3,64,256]{4,3,2,1,0:T(8,128)} %pad_maximum_fusion.1), channel_id=1, source_target_pairs={{1,0},{2,1},{3,2},{5,4},{6,5},{7,6},{9,8},{10,9},{11,10},{13,12},{... | collective-permute-start | bytes 5898248 | tf_op jit(solution)/shard_map/ppermute | solution.py:420
  19.2 0.1 copy.13
  19.3 0.1 reshape_squeeze.7
  19.5 0.1 reshape.26
  19.5 0.1 pad_maximum_fusion.8.cpl
  19.7 1.8 %copy-done.1 = f32[5,8,64,256]{3,2,1,0:T(8,128)S(1)} copy-done((f32[5,8,64,256]{3,2,1,0:T(8,128)S(1)}, f32[5,8,64,256]{3,2,1,0:T(8,128)}, u32[]{:S(2)}) %copy-start.1) | copy-done | bytes 2621464
  21.5 0.3 pack_ends.3.own
  21.8 0.4 copy-done.6
  22.2 2.6 %collective-permute-start.7 = (f32[1,88,128]{2,1,0:T(8,128)S(1)}, f32[1,88,128]{2,1,0:T(8,128)S(1)}, u32[]{:S(2)}, u32[]{:S(2)}) collective-permute-start(f32[1,88,128]{2,1,0:T(8,128)S(1)} %bitcast.50), channel_id=1, source_target_pairs={{0,16},{4,20},{8,24},{12,28},{16,0},{20,4},{24,8},{28,12},{1,17},{... | collective-permute-start | bytes 135176 | tf_op jit(solution)/shard_map/ppermute | solution.py:82
  24.8 0.6 constant_dynamic-slice_fusion.7
  27.9 1.6 %collective-permute-start.8 = (f32[2,88,128]{2,1,0:T(8,128)S(1)}, f32[2,88,128]{2,1,0:T(8,128)S(1)}, u32[]{:S(2)}, u32[]{:S(2)}) collective-permute-start(f32[2,88,128]{2,1,0:T(8,128)S(1)} %pad_maximum_fusion.7), channel_id=1, source_target_pairs={{0,8},{4,12},{8,0},{12,4},{16,24},{20,28},{24,16},{28,20},{1,9},{5... | collective-permute-start | bytes 270344 | tf_op jit(solution)/shard_map/ppermute | solution.py:82
  29.6 3.8 %collective-permute-done.8 = f32[2,88,128]{2,1,0:T(8,128)S(1)} collective-permute-done((f32[2,88,128]{2,1,0:T(8,128)S(1)}, f32[2,88,128]{2,1,0:T(8,128)S(1)}, u32[]{:S(2)}, u32[]{:S(2)}) %collective-permute-start.8) | collective-permute-done | bytes 90144 | tf_op jit(solution)/shard_map/ppermute | solution.py:82
  33.4 1.6 %collective-permute-start.9 = (f32[88,128]{1,0:T(8,128)S(1)}, f32[88,128]{1,0:T(8,128)S(1)}, u32[]{:S(2)}, u32[]{:S(2)}) collective-permute-start(f32[88,128]{1,0:T(8,128)S(1)} %bitcast_select_fusion.2), channel_id=1, source_target_pairs={{0,4},{4,0},{8,12},{12,8},{16,20},{20,16},{24,28},{28,24},{1,5},{5... | collective-permute-start | bytes 135176 | tf_op jit(solution)/shard_map/ppermute | solution.py:102
  35.0 0.6 pad.8.couplings
  35.6 1.9 %collective-permute-done.9 = f32[88,128]{1,0:T(8,128)S(1)} collective-permute-done((f32[88,128]{1,0:T(8,128)S(1)}, f32[88,128]{1,0:T(8,128)S(1)}, u32[]{:S(2)}, u32[]{:S(2)}) %collective-permute-start.9) | collective-permute-done | bytes 45088 | tf_op jit(solution)/shard_map/ppermute | solution.py:102
  37.5 0.6 fusion.1.given
  38.1 6.9 %sweeps_8.1.adjoint = f32[5,8,8,256]{3,2,1,0:T(8,128)} custom-call(f32[32,128]{1,0:T(8,128)} %pad.8.couplings, f32[88,128]{1,0:T(8,128)} %copy-done.3, f32[88,128]{1,0:T(8,128)} %fusion.1.given, f32[5,8,64,256]{3,2,1,0:T(8,128)} %src_in.3, f32[5,8,64,256]{3,2,1,0:T(8,128)} %inv_in.3, f32[2,5,3,8,256]{4,3,2,1,0:T(8,128)} %copy-done.5, ...), custom_call_target="tpu_custom_call" | custom-call | flops 2516582400 | bytes 16777216 | tf_op jit(solution)/shard_map/sweeps_8/pallas_call | solution.py:296
  45.1 1.0 copy-done.4
  46.1 4.3 %wall_points.1 = f32[3,48,256]{2,1,0:T(8,128)S(1)} custom-call(f32[5,8,8,256]{3,2,1,0:T(8,128)S(1)} %copy-done.4, f32[3,5,2,8,256]{4,3,2,1,0:T(8,128)S(1)} %copy-done.7, f32[8,8,256]{2,1,0:T(8,128)S(1)} %copy-done.8, s32[8,8,256]{2,1,0:T(8,128)S(1)} %copy-done.9), custom_call_target="tpu_custom_call" | custom-call | tf_op jit(solution)/shard_map/wall_points/pallas_call | solution.py:382
  50.4 0.1 collective-permute-start.10
  50.5 1.2 %collective-permute-done.10 = f32[3,48,128]{2,1,0:T(8,128)S(1)} collective-permute-done((f32[3,48,128]{2,1,0:T(8,128)S(1)}, f32[3,48,128]{2,1,0:T(8,128)S(1)}, u32[]{:S(2)}, u32[]{:S(2)}) %collective-permute-start.10) | collective-permute-done | bytes 73760 | tf_op jit(solution)/shard_map/ppermute | solution.py:409
  51.8 6.0 %pack_ends.2.own = f32[648,128]{1,0:T(8,128)S(1)} custom-call(f32[5,8,64,256]{3,2,1,0:T(8,128)} %src_in.3, f32[5,8,64,256]{3,2,1,0:T(8,128)} %inv_in.3, f32[2,5,3,64,256]{4,3,2,1,0:T(8,128)} %collective-permute-done.low, f32[2,5,3,64,256]{4,3,2,1,0:T(8,128)} %collective-permute-done.1.high, f32[8,128]{1,0:T(8,128)S(1)} %pad_maximum_fusion.8.cpl), custom_call_target="tpu_custom_call" | custom-call | tf_op jit(solution)/shard_map/pack_ends/pallas_call | solution.py:65
  57.8 2.3 %collective-permute-start.2 = (f32[1,648,128]{2,1,0:T(8,128)S(1)}, f32[1,648,128]{2,1,0:T(8,128)S(1)}, u32[]{:S(2)}, u32[]{:S(2)}) collective-permute-start(f32[1,648,128]{2,1,0:T(8,128)S(1)} %bitcast.47), channel_id=1, source_target_pairs={{0,16},{4,20},{8,24},{12,28},{16,0},{20,4},{24,8},{28,12},{1,17},{... | collective-permute-start | bytes 995336 | tf_op jit(solution)/shard_map/ppermute | solution.py:82
  60.1 1.5 %collective-permute-start.11 = (f32[3,24,128]{2,1,0:T(8,128)S(1)}, f32[3,24,128]{2,1,0:T(8,128)S(1)}, u32[]{:S(2)}, u32[]{:S(2)}) collective-permute-start(f32[3,24,128]{2,1,0:T(8,128)S(1)} %constant_dynamic-slice_fusion.2), channel_id=1, source_target_pairs={{0,2},{1,3},{2,0},{3,1},{4,6},{5,7},{6,4},{7,5},{8,10},{9,11},{10,... | collective-permute-start | bytes 110600 | tf_op jit(solution)/shard_map/ppermute | solution.py:409
  61.5 2.5 %collective-permute-done.11 = f32[3,24,128]{2,1,0:T(8,128)S(1)} collective-permute-done((f32[3,24,128]{2,1,0:T(8,128)S(1)}, f32[3,24,128]{2,1,0:T(8,128)S(1)}, u32[]{:S(2)}, u32[]{:S(2)}) %collective-permute-start.11) | collective-permute-done | bytes 36896 | tf_op jit(solution)/shard_map/ppermute | solution.py:409
  64.0 11.7 %collective-permute-done.2 = f32[1,648,128]{2,1,0:T(8,128)S(1)} collective-permute-done((f32[1,648,128]{2,1,0:T(8,128)S(1)}, f32[1,648,128]{2,1,0:T(8,128)S(1)}, u32[]{:S(2)}, u32[]{:S(2)}) %collective-permute-start.2) | collective-permute-done | bytes 331808 | tf_op jit(solution)/shard_map/ppermute | solution.py:82
  75.7 0.1 pad_maximum_fusion.3
  75.8 0.4 collective-permute-start.3
  76.2 1.5 %collective-permute-start.12 = (f32[3,12,128]{2,1,0:T(8,128)S(1)}, f32[3,12,128]{2,1,0:T(8,128)S(1)}, u32[]{:S(2)}, u32[]{:S(2)}) collective-permute-start(f32[3,12,128]{2,1,0:T(8,128)S(1)} %constant_dynamic-slice_fusion.1), channel_id=1, source_target_pairs={{0,4},{4,0},{8,12},{12,8},{16,20},{20,16},{24,28},{28,24},{1,5},{5... | collective-permute-start | bytes 55304 | tf_op jit(solution)/shard_map/ppermute | solution.py:409
  77.7 2.3 %collective-permute-done.12 = f32[3,12,128]{2,1,0:T(8,128)S(1)} collective-permute-done((f32[3,12,128]{2,1,0:T(8,128)S(1)}, f32[3,12,128]{2,1,0:T(8,128)S(1)}, u32[]{:S(2)}, u32[]{:S(2)}) %collective-permute-start.12) | collective-permute-done | bytes 18464 | tf_op jit(solution)/shard_map/ppermute | solution.py:409
  80.1 1.8 %collective-permute-start.13 = (f32[3,6,128]{2,1,0:T(8,128)S(1)}, f32[3,6,128]{2,1,0:T(8,128)S(1)}, u32[]{:S(2)}, u32[]{:S(2)}) collective-permute-start(f32[3,6,128]{2,1,0:T(8,128)S(1)} %constant_dynamic-slice_fusion), channel_id=1, source_target_pairs={{0,8},{4,12},{8,0},{12,4},{16,24},{20,28},{24,16},{28,20},{1,9},{5... | collective-permute-start | bytes 27656 | tf_op jit(solution)/shard_map/ppermute | solution.py:409
  81.8 10.4 %collective-permute-done.13 = f32[3,6,128]{2,1,0:T(8,128)S(1)} collective-permute-done((f32[3,6,128]{2,1,0:T(8,128)S(1)}, f32[3,6,128]{2,1,0:T(8,128)S(1)}, u32[]{:S(2)}, u32[]{:S(2)}) %collective-permute-start.13) | collective-permute-done | bytes 9248 | tf_op jit(solution)/shard_map/ppermute | solution.py:409
  92.3 0.1 pad_maximum_fusion.2
  92.5 1.6 %collective-permute-start.4 = (f32[648,128]{1,0:T(8,128)S(1)}, f32[648,128]{1,0:T(8,128)S(1)}, u32[]{:S(2)}, u32[]{:S(2)}) collective-permute-start(f32[648,128]{1,0:T(8,128)S(1)} %bitcast_select_fusion), channel_id=1, source_target_pairs={{0,4},{4,0},{8,12},{12,8},{16,20},{20,16},{24,28},{28,24},{1,5},{5... | collective-permute-start | bytes 995336 | tf_op jit(solution)/shard_map/ppermute | solution.py:102
  94.0 2.7 %collective-permute-start.14 = (f32[3,3,128]{2,1,0:T(4,128)S(1)}, f32[3,3,128]{2,1,0:T(4,128)S(1)}, u32[]{:S(2)}, u32[]{:S(2)}) collective-permute-start(f32[3,3,128]{2,1,0:T(4,128)S(1)} %constant_dynamic-slice_fusion.5), channel_id=1, source_target_pairs={{0,16},{4,20},{8,24},{12,28},{16,0},{20,4},{24,8},{28,12},{1,17},{... | collective-permute-start | bytes 13832 | tf_op jit(solution)/shard_map/ppermute | solution.py:409
  96.7 1.9 %collective-permute-done.14 = f32[3,3,128]{2,1,0:T(4,128)S(1)} collective-permute-done((f32[3,3,128]{2,1,0:T(4,128)S(1)}, f32[3,3,128]{2,1,0:T(4,128)S(1)}, u32[]{:S(2)}, u32[]{:S(2)}) %collective-permute-start.14) | collective-permute-done | bytes 4640 | tf_op jit(solution)/shard_map/ppermute | solution.py:409
  98.6 0.6 copy.17
  99.2 1.5 %collective-permute-done.4 = f32[648,128]{1,0:T(8,128)S(1)} collective-permute-done((f32[648,128]{1,0:T(8,128)S(1)}, f32[648,128]{1,0:T(8,128)S(1)}, u32[]{:S(2)}, u32[]{:S(2)}) %collective-permute-start.4) | collective-permute-done | bytes 331808 | tf_op jit(solution)/shard_map/ppermute | solution.py:102
  100.6 0.8 fusion.given
  101.4 21.1 %sweeps_64.1 = f32[5,8,64,256]{3,2,1,0:T(8,128)} custom-call(f32[32,128]{1,0:T(8,128)} %pad.8.couplings, f32[648,128]{1,0:T(8,128)} %copy-done.2, f32[648,128]{1,0:T(8,128)} %fusion.given, f32[5,8,64,256]{3,2,1,0:T(8,128)} %src_in.3, f32[5,8,64,256]{3,2,1,0:T(8,128)} %inv_in.3, f32[2,5,3,64,256]{4,3,2,1,0:T(8,128)} %collective-permute-done.low, ...), custom_call_target="tpu_custom_call" | custom-call | flops 10066329600 | bytes 16777216 | tf_op jit(solution)/shard_map/sweeps_64/pallas_call | solution.py:296
  (47 shorter events, 0.3 us)
Async XLA Ops:
  1.8 17.8 %collective-permute-start.5 = (f32[2,5,3,8,256]{4,3,2,1,0:T(8,128)S(1)}, f32[2,5,3,8,256]{4,3,2,1,0:T(8,128)S(1)}, u32[]{:S(2)}, u32[]{:S(2)}) collective-permute-start(f32[2,5,3,8,256]{4,3,2,1,0:T(8,128)S(1)} %pad_maximum_fusion.4), channel_id=1, source_target_pairs={{0,1},{1,2},{2,3},{4,5},{5,6},{6,7},{8,9},{9,10},{10,11},{12,13},{... | collective-permute-start | bytes 737288 | tf_op jit(solution)/shard_map/ppermute | solution.py:420
  4.9 14.7 %collective-permute-start.6 = (f32[2,5,3,8,256]{4,3,2,1,0:T(8,128)}, f32[2,5,3,8,256]{4,3,2,1,0:T(8,128)S(1)}, u32[]{:S(2)}, u32[]{:S(2)}) collective-permute-start(f32[2,5,3,8,256]{4,3,2,1,0:T(8,128)} %pad_maximum_fusion.5), channel_id=1, source_target_pairs={{1,0},{2,1},{3,2},{5,4},{6,5},{7,6},{9,8},{10,9},{11,10},{13,12},{... | collective-permute-start | bytes 737288 | tf_op jit(solution)/shard_map/ppermute | solution.py:420
  9.9 41.8 %collective-permute-start = (f32[2,5,3,64,256]{4,3,2,1,0:T(8,128)}, f32[2,5,3,64,256]{4,3,2,1,0:T(8,128)}, u32[]{:S(2)}, u32[]{:S(2)}) collective-permute-start(f32[2,5,3,64,256]{4,3,2,1,0:T(8,128)} %pad_maximum_fusion), channel_id=1, source_target_pairs={{0,1},{1,2},{2,3},{4,5},{5,6},{6,7},{8,9},{9,10},{10,11},{12,13},{... | collective-permute-start | bytes 5898248 | tf_op jit(solution)/shard_map/ppermute | solution.py:420
  16.4 2.8 %copy-start.10 = (f32[1,6,5,5]{1,0,3,2:T(1,128)S(1)}, f32[1,6,5,5]{1,0,3,2:T(1,128)}, u32[]{:S(2)}) copy-start(f32[1,6,5,5]{1,0,3,2:T(1,128)} %param.9) | copy-start | bytes 1804
  16.4 3.3 %copy-start = (f32[5,8,64,256]{3,2,1,0:T(8,128)S(1)}, f32[5,8,64,256]{3,2,1,0:T(8,128)}, u32[]{:S(2)}) copy-start(f32[5,8,64,256]{3,2,1,0:T(8,128)} %src_in.3) | copy-start | bytes 7864324
  17.8 34.0 %collective-permute-start.1 = (f32[2,5,3,64,256]{4,3,2,1,0:T(8,128)}, f32[2,5,3,64,256]{4,3,2,1,0:T(8,128)}, u32[]{:S(2)}, u32[]{:S(2)}) collective-permute-start(f32[2,5,3,64,256]{4,3,2,1,0:T(8,128)} %pad_maximum_fusion.1), channel_id=1, source_target_pairs={{1,0},{2,1},{3,2},{5,4},{6,5},{7,6},{9,8},{10,9},{11,10},{13,12},{... | collective-permute-start | bytes 5898248 | tf_op jit(solution)/shard_map/ppermute | solution.py:420
  19.5 5.2 %copy-start.11 = (s32[8,2]{0,1:T(2,128)S(1)}, s32[8,2]{0,1:T(2,128)}, u32[]{:S(2)}) copy-start(s32[8,2]{0,1:T(2,128)} %param.10) | copy-start | bytes 196
  19.6 2.2 %copy-start.5 = (f32[2,5,3,8,256]{4,3,2,1,0:T(8,128)}, f32[2,5,3,8,256]{4,3,2,1,0:T(8,128)S(1)}, u32[]{:S(2)}) copy-start(f32[2,5,3,8,256]{4,3,2,1,0:T(8,128)S(1)} %collective-permute-done.5.low) | copy-start | bytes 737284
  19.6 1.8 %copy-start.1 = (f32[5,8,64,256]{3,2,1,0:T(8,128)S(1)}, f32[5,8,64,256]{3,2,1,0:T(8,128)}, u32[]{:S(2)}) copy-start(f32[5,8,64,256]{3,2,1,0:T(8,128)} %inv_in.3) | copy-start | bytes 7864324
  21.5 0.7 copy-start.6
  22.2 16.0 %copy-start.3 = (f32[88,128]{1,0:T(8,128)}, f32[88,128]{1,0:T(8,128)S(1)}, u32[]{:S(2)}) copy-start(f32[88,128]{1,0:T(8,128)S(1)} %pack_ends.3.own) | copy-start | bytes 135172
  22.2 5.7 %collective-permute-start.7 = (f32[1,88,128]{2,1,0:T(8,128)S(1)}, f32[1,88,128]{2,1,0:T(8,128)S(1)}, u32[]{:S(2)}, u32[]{:S(2)}) collective-permute-start(f32[1,88,128]{2,1,0:T(8,128)S(1)} %bitcast.50), channel_id=1, source_target_pairs={{0,16},{4,20},{8,24},{12,28},{16,0},{20,4},{24,8},{28,12},{1,17},{... | collective-permute-start | bytes 135176 | tf_op jit(solution)/shard_map/ppermute | solution.py:82
  27.9 5.4 %collective-permute-start.8 = (f32[2,88,128]{2,1,0:T(8,128)S(1)}, f32[2,88,128]{2,1,0:T(8,128)S(1)}, u32[]{:S(2)}, u32[]{:S(2)}) collective-permute-start(f32[2,88,128]{2,1,0:T(8,128)S(1)} %pad_maximum_fusion.7), channel_id=1, source_target_pairs={{0,8},{4,12},{8,0},{12,4},{16,24},{20,28},{24,16},{28,20},{1,9},{5... | collective-permute-start | bytes 270344 | tf_op jit(solution)/shard_map/ppermute | solution.py:82
  33.4 4.1 %collective-permute-start.9 = (f32[88,128]{1,0:T(8,128)S(1)}, f32[88,128]{1,0:T(8,128)S(1)}, u32[]{:S(2)}, u32[]{:S(2)}) collective-permute-start(f32[88,128]{1,0:T(8,128)S(1)} %bitcast_select_fusion.2), channel_id=1, source_target_pairs={{0,4},{4,0},{8,12},{12,8},{16,20},{20,16},{24,28},{28,24},{1,5},{5... | collective-permute-start | bytes 135176 | tf_op jit(solution)/shard_map/ppermute | solution.py:102
  38.1 7.0 %copy-start.7 = (f32[3,5,2,8,256]{4,3,2,1,0:T(8,128)S(1)}, f32[3,5,2,8,256]{4,3,2,1,0:T(8,128)}, u32[]{:S(2)}) copy-start(f32[3,5,2,8,256]{4,3,2,1,0:T(8,128)} %jac.1) | copy-start | bytes 737284
  38.1 7.0 %copy-start.8 = (f32[8,8,256]{2,1,0:T(8,128)S(1)}, f32[8,8,256]{2,1,0:T(8,128)}, u32[]{:S(2)}) copy-start(f32[8,8,256]{2,1,0:T(8,128)} %weight.1) | copy-start | bytes 196612
  38.1 7.0 %copy-start.9 = (s32[8,8,256]{2,1,0:T(8,128)S(1)}, s32[8,8,256]{2,1,0:T(8,128)}, u32[]{:S(2)}) copy-start(s32[8,8,256]{2,1,0:T(8,128)} %ids.1) | copy-start | bytes 196612
  45.1 1.0 copy-start.4
  50.4 1.3 %collective-permute-start.10 = (f32[3,48,128]{2,1,0:T(8,128)S(1)}, f32[3,48,128]{2,1,0:T(8,128)S(1)}, u32[]{:S(2)}, u32[]{:S(2)}) collective-permute-start(f32[3,48,128]{2,1,0:T(8,128)S(1)} %constant_dynamic-slice_fusion.3), channel_id=1, source_target_pairs={{0,1},{1,0},{2,3},{3,2},{4,5},{5,4},{6,7},{7,6},{8,9},{9,8},{10,11... | collective-permute-start | bytes 221192 | tf_op jit(solution)/shard_map/ppermute | solution.py:409
  57.8 34.6 %copy-start.2 = (f32[648,128]{1,0:T(8,128)}, f32[648,128]{1,0:T(8,128)S(1)}, u32[]{:S(2)}) copy-start(f32[648,128]{1,0:T(8,128)S(1)} %pack_ends.2.own) | copy-start | bytes 995332
  57.8 17.9 %collective-permute-start.2 = (f32[1,648,128]{2,1,0:T(8,128)S(1)}, f32[1,648,128]{2,1,0:T(8,128)S(1)}, u32[]{:S(2)}, u32[]{:S(2)}) collective-permute-start(f32[1,648,128]{2,1,0:T(8,128)S(1)} %bitcast.47), channel_id=1, source_target_pairs={{0,16},{4,20},{8,24},{12,28},{16,0},{20,4},{24,8},{28,12},{1,17},{... | collective-permute-start | bytes 995336 | tf_op jit(solution)/shard_map/ppermute | solution.py:82
  60.1 4.0 %collective-permute-start.11 = (f32[3,24,128]{2,1,0:T(8,128)S(1)}, f32[3,24,128]{2,1,0:T(8,128)S(1)}, u32[]{:S(2)}, u32[]{:S(2)}) collective-permute-start(f32[3,24,128]{2,1,0:T(8,128)S(1)} %constant_dynamic-slice_fusion.2), channel_id=1, source_target_pairs={{0,2},{1,3},{2,0},{3,1},{4,6},{5,7},{6,4},{7,5},{8,10},{9,11},{10,... | collective-permute-start | bytes 110600 | tf_op jit(solution)/shard_map/ppermute | solution.py:409
  75.8 16.5 %collective-permute-start.3 = (f32[2,648,128]{2,1,0:T(8,128)S(1)}, f32[2,648,128]{2,1,0:T(8,128)S(1)}, u32[]{:S(2)}, u32[]{:S(2)}) collective-permute-start(f32[2,648,128]{2,1,0:T(8,128)S(1)} %pad_maximum_fusion.3), channel_id=1, source_target_pairs={{0,8},{4,12},{8,0},{12,4},{16,24},{20,28},{24,16},{28,20},{1,9},{5... | collective-permute-start | bytes 1990664 | tf_op jit(solution)/shard_map/ppermute | solution.py:82
  76.2 3.8 %collective-permute-start.12 = (f32[3,12,128]{2,1,0:T(8,128)S(1)}, f32[3,12,128]{2,1,0:T(8,128)S(1)}, u32[]{:S(2)}, u32[]{:S(2)}) collective-permute-start(f32[3,12,128]{2,1,0:T(8,128)S(1)} %constant_dynamic-slice_fusion.1), channel_id=1, source_target_pairs={{0,4},{4,0},{8,12},{12,8},{16,20},{20,16},{24,28},{28,24},{1,5},{5... | collective-permute-start | bytes 55304 | tf_op jit(solution)/shard_map/ppermute | solution.py:409
  80.1 12.2 %collective-permute-start.13 = (f32[3,6,128]{2,1,0:T(8,128)S(1)}, f32[3,6,128]{2,1,0:T(8,128)S(1)}, u32[]{:S(2)}, u32[]{:S(2)}) collective-permute-start(f32[3,6,128]{2,1,0:T(8,128)S(1)} %constant_dynamic-slice_fusion), channel_id=1, source_target_pairs={{0,8},{4,12},{8,0},{12,4},{16,24},{20,28},{24,16},{28,20},{1,9},{5... | collective-permute-start | bytes 27656 | tf_op jit(solution)/shard_map/ppermute | solution.py:409
  92.5 8.2 %collective-permute-start.4 = (f32[648,128]{1,0:T(8,128)S(1)}, f32[648,128]{1,0:T(8,128)S(1)}, u32[]{:S(2)}, u32[]{:S(2)}) collective-permute-start(f32[648,128]{1,0:T(8,128)S(1)} %bitcast_select_fusion), channel_id=1, source_target_pairs={{0,4},{4,0},{8,12},{12,8},{16,20},{20,16},{24,28},{28,24},{1,5},{5... | collective-permute-start | bytes 995336 | tf_op jit(solution)/shard_map/ppermute | solution.py:102
  94.0 4.5 %collective-permute-start.14 = (f32[3,3,128]{2,1,0:T(4,128)S(1)}, f32[3,3,128]{2,1,0:T(4,128)S(1)}, u32[]{:S(2)}, u32[]{:S(2)}) collective-permute-start(f32[3,3,128]{2,1,0:T(4,128)S(1)} %constant_dynamic-slice_fusion.5), channel_id=1, source_target_pairs={{0,16},{4,20},{8,24},{12,28},{16,0},{20,4},{24,8},{28,12},{1,17},{... | collective-permute-start | bytes 13832 | tf_op jit(solution)/shard_map/ppermute | solution.py:409

commit v3 on v2

v3 whole, which is shorter than its diff:
```python
import functools

import jax
import jax.numpy as jnp
from jax import lax
from jax.experimental import pallas as pl
from jax.experimental.pallas import tpu as pltpu
from jax.sharding import PartitionSpec as P

SWEEPS = 3
LANES = 128
HALF = LANES // 2
COLS = 6
DEEP = 3
NEAR = 8
MIB = 1 << 20
ANY = pl.BlockSpec(memory_space=pl.ANY)
VMEM = pl.BlockSpec(memory_space=pltpu.VMEM)
SMEM = pl.BlockSpec(memory_space=pltpu.SMEM)


def lane_iota(shape):
    return lax.broadcasted_iota(jnp.int32, shape, len(shape) - 1)


def bit(condition):
    return jnp.where(condition, 1.0, 0.0)


def lane_base(s):
    return COLS * (s + 1)


def chord_tile(layers):
    lane = lane_iota((1, 1, LANES))
    total = None
    for s, both in layers:
        ends = jnp.where(lane < HALF, both[..., :LANES], both[..., LANES:])
        base = lane_base(s)
        near = pltpu.roll(ends, (base + 3) % LANES, 2)
        far = pltpu.roll(ends, (HALF + base + 2) % LANES, 2)
        at = lane - base
        total = jnp.where((at >= 0) & (at < 5), near, 0.0 if total is None else total)
        at = at - HALF
        total = jnp.where((at >= 0) & (at < 5), far, total)
    return total


def send_kernel(even, after, src, inv, tile, inner, outer):
    spans = src.shape[1]
    for f, field in enumerate((src, inv)):
        tile[f] = chord_tile([(s, field[:, s]) for s in range(spans)])
    for out, up in ((inner, even[0]), (outer, 1 - even[0])):
        for j in range(DEEP):
            s = jnp.where(up == 1, spans - 1 - j, j)
            if j < DEEP - 1:
                out[j] = src[:, s]
                out[DEEP - 1 + j] = inv[:, s]
            else:
                out[2 * (DEEP - 1)] = src[:, s] * inv[:, s]


def make_sends(even, after, source, inv_diag, depth, step):
    nvar, spans, _, chord = source.shape
    field = pl.BlockSpec((step, spans, depth, chord), lambda v: (v, 0, 0, 0))
    halo = pl.BlockSpec((5, step, depth, chord), lambda v: (0, v, 0, 0))
    f32 = jnp.float32
    return pl.pallas_call(
        send_kernel,
        grid=(nvar // step,),
        in_specs=[SMEM, ANY, field, field],
        out_specs=[pl.BlockSpec((2, step, depth, LANES), lambda v: (0, v, 0, 0)), halo, halo],
        out_shape=[
            jax.ShapeDtypeStruct((2, nvar, depth, LANES), f32),
            jax.ShapeDtypeStruct((5, nvar, depth, chord), f32),
            jax.ShapeDtypeStruct((5, nvar, depth, chord), f32),
        ],
        compiler_params=pltpu.CompilerParams(vmem_limit_bytes=48 * MIB),
        cost_estimate=pl.CostEstimate(
            flops=0, bytes_accessed=16 * nvar * spans * depth * chord, transcendentals=0
        ),
        name=f"sends_{depth}",
    )(even, after, source, inv_diag)


def merge(low, high, own, packet, full, depth):
    nvar = own.shape[1]
    lane = lane_iota((1, 1, LANES))
    place = lane & (HALF - 1)
    first, last = place < COLS, (place >= lane_base(8)) & (place < lane_base(9))
    src, inv = [
        jnp.where(first, pltpu.roll(low[f], LANES - 8 * COLS, 2), jnp.where(last, pltpu.roll(high[f], 8 * COLS, 2), own[f]))
        for f in range(2)
    ]
    full[0] = src
    full[1] = inv
    slot = place - COLS * ((place * 43) >> 8)
    is_src = slot < 3
    side = lane >= HALF
    tile = jnp.where(
        side,
        jnp.where(is_src, pltpu.roll(src, LANES - 2, 2), pltpu.roll(inv, 1, 2)),
        jnp.where(is_src, src, pltpu.roll(inv, 3, 2)),
    )
    far = ((low[0], 60 - 44), (low[1], 61 - 44), (high[0], 62 - 14), (high[1], 63 - 14))
    for at, (part, shift) in enumerate(far):
        tile = jnp.where(place == 60 + at, pltpu.roll(part, shift, 2), tile)
    for v in range(nvar):
        packet[v * depth : (v + 1) * depth, :] = tile[v]


def near_merge_kernel(even, own, inner, outer, cpl, packet, full):
    depth = own.shape[2]
    up = jnp.full((1, 1, 1), even[0], jnp.int32) == 1

    def layer(j, low):
        return jnp.where(up, outer[j], inner[j]) if low else jnp.where(up, inner[j], outer[j])

    low = [chord_tile([(7, layer(2 * f, True)), (6, layer(2 * f + 1, True))]) for f in range(2)]
    high = [chord_tile([(0, layer(2 * f, False)), (1, layer(2 * f + 1, False))]) for f in range(2)]
    merge(low, high, own, packet, full, depth)
    rows = own.shape[1] * depth
    packet[rows : rows + 8, :] = cpl[...]


def bulk_merge_kernel(even, own, inner, outer, after, a, b, packet, full, a_same, b_same):
    depth = own.shape[2]
    up = jnp.full((1, 1, 1), even[0], jnp.int32) == 1
    low = [jnp.where(up, outer[f], inner[f]) for f in range(2)]
    high = [jnp.where(up, inner[f], outer[f]) for f in range(2)]
    merge(low, high, own, packet, full, depth)


def near_merge(even, own, inner, outer, cpl):
    _, nvar, depth, _ = own.shape
    return pl.pallas_call(
        near_merge_kernel,
        in_specs=[SMEM, VMEM, VMEM, VMEM, VMEM],
        out_specs=[VMEM, VMEM],
        out_shape=[
            jax.ShapeDtypeStruct((nvar * depth + 8, LANES), jnp.float32),
            jax.ShapeDtypeStruct(own.shape, jnp.float32),
        ],
        compiler_params=pltpu.CompilerParams(vmem_limit_bytes=32 * MIB),
        name="near_merge",
    )(even, own, inner, outer, cpl)


def bulk_merge(even, own, inner, outer, after, a, b):
    _, nvar, depth, _ = own.shape
    return pl.pallas_call(
        bulk_merge_kernel,
        in_specs=[SMEM, VMEM, VMEM, VMEM, ANY, ANY, ANY],
        out_specs=[VMEM, VMEM, ANY, ANY],
        out_shape=[
            jax.ShapeDtypeStruct((nvar * depth, LANES), jnp.float32),
            jax.ShapeDtypeStruct(own.shape, jnp.float32),
            jax.ShapeDtypeStruct(a.shape, a.dtype),
            jax.ShapeDtypeStruct(b.shape, b.dtype),
        ],
        input_output_aliases={5: 2, 6: 3},
        compiler_params=pltpu.CompilerParams(vmem_limit_bytes=48 * MIB),
        name="bulk_merge",
    )(even, own, inner, outer, after, a, b)


def route_ends(packet, me, low_of, high_of):
    count = lax.axis_size("blk")
    masks = [1 << b for b in range(count.bit_length() - 1)][::-1]
    left = lane_iota((1, LANES)) < HALF
    held = packet[None]
    first = None
    for mask in masks[:-1]:
        other = lax.ppermute(held, "blk", [(i, i ^ mask) for i in range(count)])
        first = other if first is None else first
        held = jnp.concatenate([held, other], 0)

    def place(block):
        apart = me ^ block
        index = 0
        for bit, mask in enumerate(masks[:-1]):
            index = index + jnp.where((apart & mask) != 0, 1 << bit, 0)
        return index, (apart & masks[-1]) == 0

    def chosen(device):
        low, _ = place(low_of[device])
        high, _ = place(high_of[device])
        return jnp.where(
            left,
            lax.dynamic_index_in_dim(held, low, 0, keepdims=False),
            lax.dynamic_index_in_dim(held, high, 0, keepdims=False),
        )

    last = masks[-1]
    given = lax.ppermute(chosen(me ^ last), "blk", [(i, i ^ last) for i in range(count)])
    _, low_here = place(low_of[me])
    _, high_here = place(high_of[me])
    return jnp.where(jnp.where(left, low_here, high_here), chosen(me), given), first, held


def expand_couplings(couplings, wide):
    rows, lanes = wide.shape
    nvar = 5
    row = lax.broadcasted_iota(jnp.int32, (rows, 32), 0)
    of = lax.broadcasted_iota(jnp.int32, (rows, 32), 1)
    pick_row = bit((row >> 4) == of).astype(jnp.bfloat16)
    col = lax.broadcasted_iota(jnp.int32, (LANES, lanes), 1)
    var = lax.broadcasted_iota(jnp.int32, (LANES, lanes), 0)
    wide_var = (col >> 4) - jnp.where(col >= 80, nvar, 0) - jnp.where(col >= 160, nvar, 0)
    pick_col = bit((wide_var == var) & (col < 240)).astype(jnp.bfloat16)
    top = couplings.astype(jnp.bfloat16)
    rest = (couplings - top.astype(jnp.float32)).astype(jnp.bfloat16)

    def spread(part):
        tall = jnp.dot(pick_row, part, preferred_element_type=jnp.float32).astype(jnp.bfloat16)
        return jnp.dot(tall, pick_col, preferred_element_type=jnp.float32)

    r = lax.broadcasted_iota(jnp.int32, (rows, lanes), 0)
    c = lax.broadcasted_iota(jnp.int32, (rows, lanes), 1)
    both = jnp.where(c < 160, spread(top), spread(rest))
    wide[...] = jnp.where((r & 15) == (c & 15), both, 0.0).astype(jnp.bfloat16)


def ribbon_sweeps(depth, full, given, mine, theirs, scalars, faces):
    nvar = 5
    lane = lane_iota((1, LANES))
    place = lane & (HALF - 1)
    slot = place - COLS * ((place * 43) >> 8)
    side = lane >= HALF
    inside = (place < lane_base(9)) & (slot < 5)
    ghost = (jnp.where(side, bit(slot >= 2), bit(slot <= 2)) > 0.5) & inside
    own = inside & jnp.logical_not(ghost)
    before, beyond = place == 60, place == 62

    def field(f, v):
        got = given[v * depth : (v + 1) * depth, :]
        turns = ((0, 2, 64, 0), (LANES - 3, LANES - 1, 63, LANES - 1))[f]
        moved = [pltpu.roll(got, t, 1) if t else got for t in turns]
        x = jnp.where(ghost, jnp.where(side, moved[1], moved[0]), 0.0)
        x = jnp.where(before, moved[2], jnp.where(beyond, moved[3], x))
        return jnp.where(own, full[f, v], x)

    src = [field(0, v) for v in range(nvar)]
    inv = [field(1, v) for v in range(nvar)]
    one = lax.broadcasted_iota(jnp.int32, (152, 8), 0)
    pick = bit((one >> 6) == lax.broadcasted_iota(jnp.int32, (152, 8), 1))
    index = lax.broadcasted_iota(jnp.int32, (152, LANES), 0)
    keep = (index & 63) == (lane_iota((152, LANES)) & 63)
    half = lax.broadcasted_iota(jnp.int32, (LANES, LANES), 0) >> 6
    fill = bit(half == (lane_iota((LANES, LANES)) >> 6))

    def spread(tile):
        tall = jnp.dot(pick, tile, precision=lax.Precision.HIGHEST)
        return jnp.dot(jnp.where(keep, tall, 0.0), fill, precision=lax.Precision.HIGHEST)

    own_rows = spread(mine[...])
    scalars[0] = own_rows
    scalars[1] = jnp.where(ghost, spread(theirs[...]), own_rows)
    mixed = [scalars[1, i : i + 1, :] for i in range(150)]
    own_c = {i: scalars[0, i : i + 1, :] for i in range(100, 150)}
    high_face = (side & jnp.logical_not(lane == HALF + 60)) | (lane == 60)
    k = lax.broadcasted_iota(jnp.int32, (depth, LANES), 0)
    p = [inv[v] * src[v] for v in range(nvar)]
    for n in range(SWEEPS):
        for u in range(nvar):
            face = jnp.zeros((depth, LANES), jnp.float32)
            for v in range(nvar):
                at = u * nvar + v
                face += jnp.where(high_face, own_c[125 + at], own_c[100 + at]) * p[v]
            faces[n, u, 0:depth, :] = face
        if n == SWEEPS - 1:
            break
        total = list(src)
        for v in range(nvar):
            near = [
                pltpu.roll(p[v], COLS, 1),
                pltpu.roll(p[v], LANES - COLS, 1),
                jnp.where(k == 0, 0.0, pltpu.roll(p[v], 1, 0)),
                jnp.where(k == depth - 1, 0.0, pltpu.roll(p[v], depth - 1, 0)),
                pltpu.roll(p[v], 1, 1),
                pltpu.roll(p[v], LANES - 1, 1),
            ]
            for d in range(6):
                for u in range(nvar):
                    total[u] = total[u] + mixed[(d * nvar + u) * nvar + v] * near[d]
        p = [inv[v] * total[v] for v in range(nvar)]


def run_sweeps(depth, even, couplings, full, given, mine, theirs, src_in, inv_in, inner, outer, scratch):
    src, inv, pa, pb, wide, before, coming, faces, scalars, sems = scratch
    nvar, layers, rows, chord = pa.shape
    spans = layers - 2 * DEEP
    moves = [
        (src_in.at[:, :, 0:depth], src.at[:, DEEP : DEEP + spans, 0:depth]),
        (inv_in.at[:, :, 0:depth], inv.at[:, DEEP : DEEP + spans, 0:depth]),
    ]
    for halo, up in ((inner, even[0]), (outer, 1 - even[0])):
        for j in range(DEEP):
            s = jnp.where(up == 1, DEEP + spans + j, DEEP - 1 - j)
            if j < DEEP - 1:
                moves.append((halo.at[j], src.at[:, s, 0:depth]))
                moves.append((halo.at[DEEP - 1 + j], inv.at[:, s, 0:depth]))
            else:
                moves.append((halo.at[2 * (DEEP - 1)], src.at[:, s, 0:depth]))
    loads = [pltpu.make_async_copy(x, y, sems.at[j]) for j, (x, y) in enumerate(moves)]
    if rows != depth:
        none = jnp.zeros((nvar, layers, rows - depth, chord), jnp.float32)
        src[:, :, depth:rows, :] = none
        inv[:, :, depth:rows, :] = none
        faces[...] = jnp.zeros(faces.shape, jnp.float32)
    for copy in loads:
        copy.start()
    ones = jnp.ones((nvar, rows, chord), jnp.float32)
    inv[:, 0] = ones
    inv[:, layers - 1] = ones
    expand_couplings(couplings[...], wide)
    ribbon_sweeps(depth, full, given, mine, theirs, scalars, faces)
    for copy in loads:
        copy.wait()

    def first(s, _):
        pa[:, s] = inv[:, s] * src[:, s]
        return 0

    lax.fori_loop(0, layers, first, 0)
    groups = rows // 16
    lane = lane_iota((1, 1, LANES))
    k = lax.broadcasted_iota(jnp.int32, (1, rows, 1), 1)

    def products(p, s, first_row, last_row):
        pieces = []
        for g in range(groups):
            x = p[:, s, 16 * g : 16 * g + 16, :].reshape(nvar * 16, chord)
            top = x.astype(jnp.bfloat16)
            rest = (x - top.astype(jnp.float32)).astype(jnp.bfloat16)
            none = jnp.zeros((16, chord), jnp.bfloat16)
            parts = jnp.concatenate([top, rest, top, none], 0)
            y = jnp.dot(wide[first_row:last_row, :], parts, preferred_element_type=jnp.float32)
            pieces.append(y.reshape((last_row - first_row) // 16, 16, chord))
        return jnp.concatenate(pieces, 1) if groups > 1 else pieces[0]

    def along(every, n, s):
        total = jnp.where(k == 0, 0.0, pltpu.roll(every[2 * nvar : 3 * nvar], 1, 1))
        total += jnp.where(k == rows - 1, 0.0, pltpu.roll(every[3 * nvar : 4 * nvar], rows - 1, 1))
        face = faces[n]
        at_low = pltpu.roll(face, lax.rem(LANES + 10 - COLS * s, LANES), 2)
        at_high = pltpu.roll(face, lax.rem(LANES + 73 - COLS * s, LANES), 2)
        a = pltpu.roll(every[4 * nvar : 5 * nvar, :, :LANES], 1, 2)
        b = pltpu.roll(every[4 * nvar : 5 * nvar, :, LANES:], 1, 2)
        c = pltpu.roll(every[5 * nvar :, :, :LANES], LANES - 1, 2)
        d = pltpu.roll(every[5 * nvar :, :, LANES:], LANES - 1, 2)
        left = jnp.where(lane == 0, at_low, a) + jnp.where(lane == LANES - 1, d, c)
        right = jnp.where(lane == 0, a, b) + jnp.where(lane == LANES - 1, at_high, d)
        return total + jnp.concatenate([left, right], 2)

    step = 16 * nvar
    for n in range(SWEEPS):
        p, after = (pa, pb) if n % 2 == 0 else (pb, pa)
        coming[...] = products(p, n, 0, step)
        full = layers - 2 - 2 * n
        turn = 2 if groups > 1 else full

        def several(i, _):
            s0 = n + 1 + i * turn
            every = [products(p, s0 + j, 0, 6 * step) for j in range(turn)]
            arriving, waiting = coming[...], before[...]
            for j in range(turn):
                s, now = s0 + j, every[j]
                after[:, s - 1] = inv[:, s - 1] * (waiting + now[nvar : 2 * nvar])
                waiting = src[:, s] + arriving + along(now, n, s)
                arriving = now[:nvar]
            before[...] = waiting
            coming[...] = arriving
            return 0

        lax.fori_loop(0, full // turn, several, 0)
        last = layers - 1 - n
        after[:, last - 1] = inv[:, last - 1] * (before[...] + products(p, last, step, 2 * step))
    result = pb if SWEEPS % 2 else pa
    return result


def sweep_scratch(nvar, spans, chord, depth):
    rows = max(depth, 16)
    f32 = jnp.float32
    field = pltpu.VMEM((nvar, spans + 2 * DEEP, rows, chord), f32)
    layer = pltpu.VMEM((nvar, rows, chord), f32)
    return [
        field,
        field,
        field,
        field,
        pltpu.VMEM((6 * nvar * 16, 256), jnp.bfloat16),
        layer,
        layer,
        pltpu.VMEM((SWEEPS, nvar, rows, LANES), f32),
        pltpu.VMEM((2, 152, LANES), f32),
        pltpu.SemaphoreType.DMA((12,)),
    ]


def bulk_kernel(
    depth, even, couplings, full, given, mine, theirs, src_in, inv_in, inner, outer, after, out, *scratch
):
    *scratch, out_sem = scratch
    result = run_sweeps(
        depth, even, couplings, full, given, mine, theirs, src_in, inv_in, inner, outer, scratch
    )
    spans = out.shape[1]
    copy = pltpu.make_async_copy(result.at[:, DEEP : DEEP + spans, 0:depth], out, out_sem)
    copy.start()
    copy.wait()


def coupling_rows(shape):
    rows = shape[0] - 8
    return pl.BlockSpec((8, LANES), lambda i: (rows // 8, 0))


def whole(a):
    return pl.BlockSpec(a.shape, lambda i: (0,) * a.ndim)


def bulk_sweeps(even, couplings, full, given, mine, theirs, source, inv_diag, inner, outer, after):
    nvar, spans, depth, chord = source.shape
    return pl.pallas_call(
        functools.partial(bulk_kernel, depth),
        grid=(1,),
        in_specs=[SMEM, whole(couplings), whole(full), whole(given), coupling_rows(mine.shape)]
        + [coupling_rows(theirs.shape), ANY, ANY, ANY, ANY, ANY],
        out_specs=ANY,
        out_shape=jax.ShapeDtypeStruct(source.shape, jnp.float32),
        scratch_shapes=sweep_scratch(nvar, spans, chord, depth) + [pltpu.SemaphoreType.DMA],
        compiler_params=pltpu.CompilerParams(vmem_limit_bytes=56 * MIB),
        cost_estimate=pl.CostEstimate(
            flops=2 * 40 * 480 * 256 * 256 * (depth // 16), bytes_accessed=16 * MIB, transcendentals=0
        ),
        name="bulk_sweeps",
    )(even, couplings, full, given, mine, theirs, source, inv_diag, inner, outer, after)


def near_kernel(even, couplings, full, given, mine, theirs, src_in, inv_in, inner, outer, jac, after, sens, *scratch):
    adjoint = run_sweeps(
        NEAR, even, couplings, full, given, mine, theirs, src_in, inv_in, inner, outer, scratch
    )
    dims, nvar = jac.shape[:2]
    spans, chord = sens.shape[1:]
    layer = []
    for v in range(nvar):
        for k in range(2):
            layer.append(
                jnp.concatenate([adjoint[v, DEEP + s, k : k + 1, :] for s in range(spans)], 0)
            )
    for c in range(dims):
        total = jnp.zeros((spans, chord), jnp.float32)
        for v in range(nvar):
            for k in range(2):
                total += jac[c, v, k] * layer[2 * v + k]
        sens[c] = total


def near_sweeps(even, couplings, full, given, packet, source, inv_diag, inner, outer, jac, after):
    nvar, spans, _, chord = source.shape
    shape = (jac.shape[0], spans, chord)
    return pl.pallas_call(
        near_kernel,
        grid=(1,),
        in_specs=[SMEM, whole(couplings), whole(full), whole(given), coupling_rows(packet.shape)]
        + [coupling_rows(given.shape), ANY, ANY, ANY, ANY, whole(jac), ANY],
        out_specs=pl.BlockSpec(shape, lambda i: (0, 0, 0)),
        out_shape=jax.ShapeDtypeStruct(shape, jnp.float32),
        scratch_shapes=sweep_scratch(nvar, spans, chord, NEAR),
        compiler_params=pltpu.CompilerParams(vmem_limit_bytes=48 * MIB),
        cost_estimate=pl.CostEstimate(flops=5 * 10**9, bytes_accessed=4 * MIB, transcendentals=0),
        name="near_sweeps",
    )(even, couplings, full, given, packet, given, source, inv_diag, inner, outer, jac, after)


def point_indices(bits, ids, hi_index, lo_index):
    point = ids[...]
    line = point >> 7
    device = (line * 171) >> 9
    third = line - 3 * device
    pair = device >> 1
    turned = jnp.zeros_like(pair)
    for b in range(bits):
        turned = turned | (((pair >> b) & 1) << (bits - 1 - b))
    hi_index[...] = jnp.where(point < 0, -1, 3 * turned + third)
    lo_index[...] = ((device & 1) << 7) + (point & 127)


def scatter_kernel(bits, sens, weight, ids, after, out, hi_index, lo_index):
    point_indices(bits, ids, hi_index, lo_index)
    dims, spans, chord = sens.shape
    slots = weight.shape[0]
    tall = out.shape[1]
    out[...] = jnp.zeros(out.shape, jnp.float32)
    rows = lax.broadcasted_iota(jnp.int32, (tall, chord), 0)
    cols = lax.broadcasted_iota(jnp.int32, (2 * LANES, chord), 0)

    def one(m, _):
        his = hi_index[m]
        los = lo_index[m]
        w = weight[m]
        values = [w * sens[c] for c in range(dims)]
        tops = [x.astype(jnp.bfloat16).astype(jnp.float32) for x in values]
        rests = [x - t for x, t in zip(values, tops)]
        total = jnp.zeros((2 * dims * tall, 2 * LANES), jnp.float32)
        for s in range(spans):
            hit = rows == his[s : s + 1, :]
            left = [
                jnp.where(hit, x[s : s + 1, :], 0.0).astype(jnp.bfloat16) for x in tops + rests
            ]
            right = bit(cols == los[s : s + 1, :]).astype(jnp.bfloat16)
            total += lax.dot_general(
                jnp.concatenate(left, 0),
                right,
                (((1,), (1,)), ((), ())),
                preferred_element_type=jnp.float32,
            )
        for c in range(dims):
            out[c] += total[c * tall : (c + 1) * tall] + total[(dims + c) * tall : (dims + c + 1) * tall]
        return 0

    lax.fori_loop(0, slots, one, 0)


def scatter_points(sens, weight, ids, after, n_dev):
    tall = -(-(n_dev // 2 * 3) // 16) * 16
    bits = (n_dev // 2).bit_length() - 1
    shape = (sens.shape[0], tall, 2 * LANES)
    return pl.pallas_call(
        functools.partial(scatter_kernel, bits),
        in_specs=[VMEM, VMEM, VMEM, ANY],
        out_specs=VMEM,
        out_shape=jax.ShapeDtypeStruct(shape, jnp.float32),
        scratch_shapes=[pltpu.VMEM(ids.shape, jnp.int32), pltpu.VMEM(ids.shape, jnp.int32)],
        compiler_params=pltpu.CompilerParams(vmem_limit_bytes=48 * MIB),
        cost_estimate=pl.CostEstimate(flops=4 * 10**9, bytes_accessed=MIB, transcendentals=0),
        name="scatter_points",
    )(sens, weight, ids, after)


def add_kernel(a, b, c, d, after, out):
    total = (a[...] + b[...]) + (c[...] + d[...])
    for j in range(total.shape[1]):
        out[:, LANES * j : LANES * (j + 1)] = total[:, j]


def add_points(parts, after):
    dims, rows, lanes = parts[0].shape
    return pl.pallas_call(
        add_kernel,
        in_specs=[VMEM] * 4 + [ANY],
        out_specs=VMEM,
        out_shape=jax.ShapeDtypeStruct((dims, rows * lanes), jnp.float32),
        name="add_points",
    )(*parts, after)


def halve_points(partial, after, n_dev):
    n_blk, n_sub = lax.axis_size("blk"), lax.axis_size("sub")
    blk, sub = lax.axis_index("blk"), lax.axis_index("sub")
    partial = partial[:, : n_dev // 2 * 3]
    steps = [("sub", sub, n_sub, 1 << b) for b in range(n_sub.bit_length() - 1)]
    steps += [("blk", blk, n_blk, 1 << b) for b in range(n_blk.bit_length() - 3)]
    for number, (axis, me, count, mask) in enumerate(steps):
        dim = 2 if number == 0 else 1
        half = partial.shape[dim] // 2
        mine = jnp.where((me & mask) != 0, half, 0)
        keep = lax.dynamic_slice_in_dim(partial, mine, half, dim)
        send = lax.dynamic_slice_in_dim(partial, half - mine, half, dim)
        partial = keep + lax.ppermute(send, axis, [(i, i ^ mask) for i in range(count)])
        if number == 1:
            partial, after = lax.optimization_barrier((partial, after))
    return partial, after


def quarter_points(partial):
    count, me = lax.axis_size("blk"), lax.axis_index("blk")
    late, last = count // 4, count // 2
    rows = partial.shape[1] // 4

    def quarter(device):
        place = jnp.where((device & late) != 0, 2, 0) + jnp.where((device & last) != 0, 1, 0)
        return lax.dynamic_slice_in_dim(partial, place * rows, rows, 1)

    parts = [quarter(me)]
    for mask in (last, late, late | last):
        parts.append(lax.ppermute(quarter(me ^ mask), "blk", [(i, i ^ mask) for i in range(count)]))
    return parts


def swap_spans(inner, outer):
    count = lax.axis_size("sub")
    pairs = [(i, i ^ 1) for i in range(count)]
    others = [(i, i + 1) for i in range(1, count - 1, 2)] + [(i, i - 1) for i in range(2, count, 2)]
    return lax.ppermute(inner, "sub", pairs), lax.ppermute(outer, "sub", others)


def body(source, inv_diag, coupling, face_map, wall_jac, ffd_weight, cp_ids):
    nvar = source.shape[0]
    me = lax.axis_index("blk")
    n_dev = lax.axis_size("blk") * lax.axis_size("sub")
    even = (1 - (lax.axis_index("sub") & 1)).astype(jnp.int32).reshape(1)
    couplings = jnp.pad(coupling[0].reshape(6 * nvar, nvar), ((0, 2), (0, LANES - nvar)))
    flat = jnp.pad(coupling[0].reshape(-1), (0, 8 * HALF - 6 * nvar * nvar)).reshape(8, HALF)
    cpl = jnp.concatenate([flat, flat], 1)
    low_of, high_of = face_map[:, 0], face_map[:, 1]

    own, inner, outer = make_sends(even, even, source, inv_diag, NEAR, nvar)
    inner, outer = swap_spans(inner, outer)
    packet, full = near_merge(even, own, inner, outer, cpl)
    given, _, held = route_ends(packet, me, low_of, high_of)

    bulk_own, bulk_inner, bulk_outer = make_sends(even, packet, source, inv_diag, source.shape[2], 1)
    tiles = swap_spans(bulk_own, bulk_own)
    bulk_packet, bulk_full, bulk_inner, bulk_outer = bulk_merge(
        even, bulk_own, *tiles, held, bulk_inner, bulk_outer
    )
    bulk_inner, bulk_outer = swap_spans(bulk_inner, bulk_outer)
    bulk_given, bulk_first, _ = route_ends(bulk_packet, me, low_of, high_of)

    sens = near_sweeps(
        even, couplings, full, given, packet, source, inv_diag, inner, outer, wall_jac, bulk_packet
    )
    partial = scatter_points(sens, ffd_weight, cp_ids, bulk_first, n_dev)
    partial, bulk_outer = halve_points(partial, bulk_outer, n_dev)
    adjoint = bulk_sweeps(
        even, couplings, bulk_full, bulk_given, packet, given, source, inv_diag, bulk_inner, bulk_outer, partial
    )
    return adjoint, add_points(quarter_points(partial), adjoint)


def solution(mesh):
    field = P(None, "sub", None, "blk")
    in_specs = (
        field,
        field,
        P("blk", None, None, None),
        P(),
        P(None, None, None, "sub", "blk"),
        P(None, "sub", "blk"),
        P(None, "sub", "blk"),
    )
    out_specs = (field, P(None, ("blk", "sub")))
    return jax.shard_map(body, mesh=mesh, in_specs=in_specs, out_specs=out_specs, check_vma=False)
```

time: 123 us -> 104 us (0.85)
  waiting for transfers between devices: 37.2 us -> 16.4 us
  other arithmetic: 5.41 us -> 1.6 us
  starting transfers between devices: 29 us -> 32 us
  Pallas kernels: 38.6 us -> 40 us
    ppermute x9 -> x12, waiting for transfers between devices: 18.4 us -> 0.54 us  [the longest x3 0.52 us: halve_points(): lax.ppermute(send, axis, [(i, i ^ mask) for i in range(count)])]
    ppermute x4, waiting for transfers between devices: 15.5 us -> 10.3 us  [route_ends(): other = lax.ppermute(held, 'blk', [(i, i ^ mask) for i in range(count)])]
    unnamed x25 -> x54, local copies, waits for them, and re-layouts: 3.79 us -> 7.9 us
    another operation x4 -> x0, other arithmetic: 3.56 us -> none  [the longest x2 2.13 us: span_halo(): first = jnp.stack([source[:, :DEEP, :depth], inv_diag[:, :DEEP, :depth]])]
    another operation x2 -> x0, local copies, waits for them, and re-layouts: 3.48 us -> none  [span_halo(): first = jnp.stack([source[:, :DEEP, :depth], inv_diag[:, :DEEP, :depth]])]
    ppermute x2, waiting for transfers between devices: 3.4 us -> 5.59 us  [route_ends(): lax.ppermute(chosen(me ^ last), 'blk', [(i, i ^ last) for i in range(coun...]
    ppermute x4, starting transfers between devices: 6.92 us -> 8.85 us  [route_ends(): other = lax.ppermute(held, 'blk', [(i, i ^ mask) for i in range(count)])]
    pallas_call x5 -> x8, Pallas kernels: 38.6 us -> 40 us  [the longest x1 20.9 us: bulk_sweeps(): pl.pallas_call(functools.partial(bulk_kernel, depth), grid=(1,), in_specs...]
  transfers between devices with their start and end apart: 15 -> 18, of which waited for: 9 -> 5; matrix products, arithmetic and copies ran while one was open for 7% -> 3% of each run, Pallas kernels for 9% -> 35%
where the time goes in v3:
time: 104 us; the launch traced here: 103 us
  Pallas kernels  40 us (38%)
  starting transfers between devices  32 us (31%)
  waiting for transfers between devices  16.4 us (16%)
  local copies, waits for them, and re-layouts  9.57 us (9%)
  between operations  3.84 us (4%)
  other arithmetic  1.6 us (2%)
    pallas_call x1, Pallas kernels, bulk_sweeps(): pl.pallas_call(functools.partial(bulk_kernel, depth), grid=(1,), in_specs...  20.9 us
    ppermute x4, waiting for transfers between devices, route_ends(): other = lax.ppermute(held, 'blk', [(i, i ^ mask) for i in range(count)])  10.3 us
    ppermute x4, starting transfers between devices, route_ends(): other = lax.ppermute(held, 'blk', [(i, i ^ mask) for i in range(count)])  8.85 us
    ppermute x3, starting transfers between devices, swap_spans(): lax.ppermute(inner, 'sub', pairs)  8.48 us
    unnamed x54, local copies, waits for them, and re-layouts  7.9 us
    pallas_call x2, Pallas kernels, make_sends(): pl.pallas_call(send_kernel, grid=(nvar // step,), in_specs=[SMEM, ANY, fi...  6.26 us
    ppermute x2, waiting for transfers between devices, route_ends(): lax.ppermute(chosen(me ^ last), 'blk', [(i, i ^ last) for i in range(coun...  5.59 us
    pallas_call x1, Pallas kernels, near_sweeps(): pl.pallas_call(near_kernel, grid=(1,), in_specs=[SMEM, whole(couplings),...  5.4 us
  transfers between devices with their start and end apart: 18, of which 5 were waited for; matrix products, arithmetic and copies ran while one was open for 3% of the time, Pallas kernels for 35%

profile of v3, /device:TPU:0, one launch (start us, length us, event | category | flops | bytes accessed | tf_op | source)
XLA Modules:
  0.0 103.4 jit_solution(8011385655690700400)
XLA Ops:
  0.6 1.7 %copy-done = f32[5,8,64,256]{3,2,1,0:T(8,128)S(1)} copy-done((f32[5,8,64,256]{3,2,1,0:T(8,128)S(1)}, f32[5,8,64,256]{3,2,1,0:T(8,128)}, u32[]{:S(2)}) %copy-start) | copy-done | bytes 2621464
  2.4 1.7 %copy-done.2 = f32[5,8,64,256]{3,2,1,0:T(8,128)S(1)} copy-done((f32[5,8,64,256]{3,2,1,0:T(8,128)S(1)}, f32[5,8,64,256]{3,2,1,0:T(8,128)}, u32[]{:S(2)}) %copy-start.2) | copy-done | bytes 2621464
  4.1 0.3 sends_8.1
  4.4 0.5 collective-permute-start
  4.9 0.7 collective-permute-start.1
  5.6 0.1 copy.15
  5.7 0.1 reshape_squeeze.7
  5.9 0.1 reshape.27
  5.9 0.1 pad_maximum_fusion.4.cpl
  6.0 0.3 near_merge.1
  6.4 4.0 %collective-permute-start.4 = (f32[1,48,128]{2,1,0:T(8,128)S(1)}, f32[1,48,128]{2,1,0:T(8,128)S(1)}, u32[]{:S(2)}, u32[]{:S(2)}) collective-permute-start(f32[1,48,128]{2,1,0:T(8,128)S(1)} %bitcast.30), channel_id=1, source_target_pairs={{0,16},{4,20},{8,24},{12,28},{16,0},{20,4},{24,8},{28,12},{1,17},{... | collective-permute-start | bytes 73736 | tf_op jit(solution)/shard_map/ppermute | solution.py:174
  10.4 1.8 %collective-permute-done.4 = f32[1,48,128]{2,1,0:T(8,128)S(1)} collective-permute-done((f32[1,48,128]{2,1,0:T(8,128)S(1)}, f32[1,48,128]{2,1,0:T(8,128)S(1)}, u32[]{:S(2)}, u32[]{:S(2)}) %collective-permute-start.4) | collective-permute-done | bytes 24608 | tf_op jit(solution)/shard_map/ppermute | solution.py:174
  12.2 1.9 %collective-permute-start.5 = (f32[2,48,128]{2,1,0:T(8,128)S(1)}, f32[2,48,128]{2,1,0:T(8,128)S(1)}, u32[]{:S(2)}, u32[]{:S(2)}) collective-permute-start(f32[2,48,128]{2,1,0:T(8,128)S(1)} %pad_maximum_fusion.3), channel_id=1, source_target_pairs={{0,8},{4,12},{8,0},{12,4},{16,24},{20,28},{24,16},{28,20},{1,9},{5... | collective-permute-start | bytes 147464 | tf_op jit(solution)/shard_map/ppermute | solution.py:174
  14.1 0.7 constant_dynamic-slice_fusion.9
  17.4 0.0 copy-start.3
  17.4 6.0 %sends_64.1 = (f32[2,5,64,128]{3,2,1,0:T(8,128)S(1)}, f32[5,5,64,256]{3,2,1,0:T(8,128)}, f32[5,5,64,256]{3,2,1,0:T(8,128)S(1)}) custom-call(s32[1]{0:T(128)} %bitcast.even.after, f32[48,128]{1,0:T(8,128)S(1)} %get-tuple-element.19.after.mine, f32[5,8,64,256]{3,2,1,0:T(8,128)} %src_in.3, f32[5,8,64,256]{3,2,1,0:T(8,128)} %inv_in.3), custom_call_target="tpu_custom_call" | custom-call | bytes 10485760 | tf_op jit(solution)/shard_map/sends_64/pallas_call | solution.py:68
  23.4 1.2 %copy-done.4 = f32[5,5,64,256]{3,2,1,0:T(8,128)} copy-done((f32[5,5,64,256]{3,2,1,0:T(8,128)}, f32[5,5,64,256]{3,2,1,0:T(8,128)S(1)}, u32[]{:S(2)}) %copy-start.4) | copy-done | bytes 1638424
  24.6 4.9 %collective-permute-start.2 = (f32[2,5,64,128]{3,2,1,0:T(8,128)S(1)}, f32[2,5,64,128]{3,2,1,0:T(8,128)S(1)}, u32[]{:S(2)}, u32[]{:S(2)}) collective-permute-start(f32[2,5,64,128]{3,2,1,0:T(8,128)S(1)} %get-tuple-element.20.own), channel_id=1, source_target_pairs={{0,1},{1,0},{2,3},{3,2},{4,5},{5,4},{6,7},{7,6},{8,9},{9,8},{10,11... | collective-permute-start | bytes 983048 | tf_op jit(solution)/shard_map/ppermute | solution.py:598
  29.5 1.4 %collective-permute-start.3 = (f32[2,5,64,128]{3,2,1,0:T(8,128)S(1)}, f32[2,5,64,128]{3,2,1,0:T(8,128)}, u32[]{:S(2)}, u32[]{:S(2)}) collective-permute-start(f32[2,5,64,128]{3,2,1,0:T(8,128)S(1)} %get-tuple-element.20.own), channel_id=1, source_target_pairs={{1,2},{2,1},{5,6},{6,5},{9,10},{10,9},{13,14},{14,13},{17,18},{18,... | collective-permute-start | bytes 983048 | tf_op jit(solution)/shard_map/ppermute | solution.py:598
  30.9 1.6 %collective-permute-start.9 = (f32[48,128]{1,0:T(8,128)S(1)}, f32[48,128]{1,0:T(8,128)S(1)}, u32[]{:S(2)}, u32[]{:S(2)}) collective-permute-start(f32[48,128]{1,0:T(8,128)S(1)} %bitcast_select_fusion.2), channel_id=1, source_target_pairs={{0,4},{4,0},{8,12},{12,8},{16,20},{20,16},{24,28},{28,24},{1,5},{5... | collective-permute-start | bytes 73736 | tf_op jit(solution)/shard_map/ppermute | solution.py:195
  32.6 2.2 %collective-permute-done.9 = f32[48,128]{1,0:T(8,128)S(1)} collective-permute-done((f32[48,128]{1,0:T(8,128)S(1)}, f32[48,128]{1,0:T(8,128)S(1)}, u32[]{:S(2)}, u32[]{:S(2)}) %collective-permute-start.9) | collective-permute-done | bytes 24608 | tf_op jit(solution)/shard_map/ppermute | solution.py:195
  34.8 0.7 fusion.1.given.theirs
  35.5 1.4 %copy-done.5 = f32[5,5,64,256]{3,2,1,0:T(8,128)S(1)} copy-done((f32[5,5,64,256]{3,2,1,0:T(8,128)S(1)}, f32[5,5,64,256]{3,2,1,0:T(8,128)}, u32[]{:S(2)}) %copy-start.5) | copy-done | bytes 1638424
  37.0 1.6 %bulk_merge.1 = (f32[320,128]{1,0:T(8,128)S(1)}, f32[2,5,64,128]{3,2,1,0:T(8,128)S(1)}, f32[5,5,64,256]{3,2,1,0:T(8,128)}, f32[5,5,64,256]{3,2,1,0:T(8,128)S(1)}) custom-call(s32[1]{0:T(128)} %bitcast.even.after, f32[2,5,64,128]{3,2,1,0:T(8,128)S(1)} %get-tuple-element.20.own, ...), custom_call_target="tpu_custom_call", output_to_operand_aliasing={{2}: (5, {}), {3}: (6, {})} | custom-call | tf_op jit(solution)/shard_map/bulk_merge/pallas_call | solution.py:151
  38.6 2.6 %collective-permute-start.6 = (f32[1,320,128]{2,1,0:T(8,128)S(1)}, f32[1,320,128]{2,1,0:T(8,128)S(1)}, u32[]{:S(2)}, u32[]{:S(2)}) collective-permute-start(f32[1,320,128]{2,1,0:T(8,128)S(1)} %bitcast.27), channel_id=1, source_target_pairs={{0,16},{4,20},{8,24},{12,28},{16,0},{20,4},{24,8},{28,12},{1,17},{... | collective-permute-start | bytes 491528 | tf_op jit(solution)/shard_map/ppermute | solution.py:174
  41.2 3.0 %collective-permute-start.10 = (f32[5,5,64,256]{3,2,1,0:T(8,128)}, f32[5,5,64,256]{3,2,1,0:T(8,128)S(1)}, u32[]{:S(2)}, u32[]{:S(2)}) collective-permute-start(f32[5,5,64,256]{3,2,1,0:T(8,128)} %get-tuple-element.25), channel_id=1, source_target_pairs={{0,1},{1,0},{2,3},{3,2},{4,5},{5,4},{6,7},{7,6},{8,9},{9,8},{10,11... | collective-permute-start | bytes 4915208 | tf_op jit(solution)/shard_map/ppermute | solution.py:598
  44.2 0.9 collective-permute-start.13
  45.3 5.4 %near_sweeps.1.sens = f32[3,8,256]{2,1,0:T(8,128)S(1)} custom-call(s32[1]{0:T(128)} %bitcast.even.after, f32[32,128]{1,0:T(8,128)S(1)} %pad.8.couplings, f32[2,5,8,128]{3,2,1,0:T(8,128)S(1)} %get-tuple-element.26.full, f32[48,128]{1,0:T(8,128)S(1)} %fusion.1.given.theirs, f32[48,128]{1,0:T(8,128)S(1)} %get-tuple-element.19.after.mine, ...), custom_call_target="tpu_custom_call" | custom-call | flops 5000000000 | bytes 4194304 | tf_op jit(solution)/shard_map/near_sweeps/pallas_call | solution.py:465
  50.7 4.2 %scatter_points.1 = f32[3,48,256]{2,1,0:T(8,128)S(1)} custom-call(f32[3,8,256]{2,1,0:T(8,128)S(1)} %near_sweeps.1.sens, f32[8,8,256]{2,1,0:T(8,128)S(1)} %copy-done.15, s32[8,8,256]{2,1,0:T(8,128)S(1)} %copy-done.16, f32[1,320,128]{2,1,0:T(8,128)S(1)} %collective-permute-done.6.after), custom_call_target="tpu_custom_call" | custom-call | flops 4000000000 | bytes 1048576 | tf_op jit(solution)/shard_map/scatter_points/pallas_call | solution.py:532
  54.9 3.2 %collective-permute-start.11 = (f32[3,48,128]{2,1,0:T(8,128)S(1)}, f32[3,48,128]{2,1,0:T(8,128)S(1)}, u32[]{:S(2)}, u32[]{:S(2)}) collective-permute-start(f32[3,48,128]{2,1,0:T(8,128)S(1)} %constant_dynamic-slice_fusion.5), channel_id=1, source_target_pairs={{0,1},{1,0},{2,3},{3,2},{4,5},{5,4},{6,7},{7,6},{8,9},{9,8},{10,11... | collective-permute-start | bytes 221192 | tf_op jit(solution)/shard_map/ppermute | solution.py:573
  58.2 0.4 collective-permute-start.7
  58.6 0.5 collective-permute-done.11
  59.1 0.3 collective-permute-start.12
  59.4 8.5 %collective-permute-done.7 = f32[2,320,128]{2,1,0:T(8,128)S(1)} collective-permute-done((f32[2,320,128]{2,1,0:T(8,128)S(1)}, f32[2,320,128]{2,1,0:T(8,128)S(1)}, u32[]{:S(2)}, u32[]{:S(2)}) %collective-permute-start.7) | collective-permute-done | bytes 327712 | tf_op jit(solution)/shard_map/ppermute | solution.py:174
  68.0 1.6 %collective-permute-start.8 = (f32[320,128]{1,0:T(8,128)S(1)}, f32[320,128]{1,0:T(8,128)S(1)}, u32[]{:S(2)}, u32[]{:S(2)}) collective-permute-start(f32[320,128]{1,0:T(8,128)S(1)} %bitcast_select_fusion), channel_id=1, source_target_pairs={{0,4},{4,0},{8,12},{12,8},{16,20},{20,16},{24,28},{28,24},{1,5},{5... | collective-permute-start | bytes 491528 | tf_op jit(solution)/shard_map/ppermute | solution.py:195
  69.6 0.6 collective-permute-start.14
  70.2 3.4 %collective-permute-done.8 = f32[320,128]{1,0:T(8,128)S(1)} collective-permute-done((f32[320,128]{1,0:T(8,128)S(1)}, f32[320,128]{1,0:T(8,128)S(1)}, u32[]{:S(2)}, u32[]{:S(2)}) %collective-permute-start.8) | collective-permute-done | bytes 163872 | tf_op jit(solution)/shard_map/ppermute | solution.py:195
  73.6 0.7 fusion.given
  74.3 0.6 constant_dynamic-slice_fusion.7
  74.9 0.2 collective-permute-start.15
  75.1 0.5 collective-permute-start.16
  75.6 3.8 %collective-permute-start.17 = (f32[3,3,128]{2,1,0:T(4,128)S(1)}, f32[3,3,128]{2,1,0:T(4,128)S(1)}, u32[]{:S(2)}, u32[]{:S(2)}) collective-permute-start(f32[3,3,128]{2,1,0:T(4,128)S(1)} %get-tuple-element.30), channel_id=1, source_target_pairs={{0,24},{4,28},{8,16},{12,20},{16,8},{20,12},{24,0},{28,4},{1,25},{... | collective-permute-start | bytes 13832 | tf_op jit(solution)/shard_map/ppermute | solution.py:590
  79.3 1.1 %copy-done.25 = f32[5,5,64,256]{3,2,1,0:T(8,128)} copy-done((f32[5,5,64,256]{3,2,1,0:T(8,128)}, f32[5,5,64,256]{3,2,1,0:T(8,128)S(1)}, u32[]{:S(2)}) %copy-start.25) | copy-done | bytes 1638424
  80.5 20.9 %bulk_sweeps.1.after = f32[5,8,64,256]{3,2,1,0:T(8,128)} custom-call(s32[1]{0:T(128)} %bitcast.even.after, f32[32,128]{1,0:T(8,128)} %copy-done.12, f32[2,5,64,128]{3,2,1,0:T(8,128)} %copy-done.13, f32[320,128]{1,0:T(8,128)} %fusion.given, f32[48,128]{1,0:T(8,128)} %copy-done.6, f32[48,128]{1,0:T(8,128)} %copy-done.11, f32[5,8,64,256]{3,2,1,0:T(8,128)} %src_in.3, ...), custom_call_target="tpu_custom_call" | custom-call | flops 10066329600 | bytes 16777216 | tf_op jit(solution)/shard_map/bulk_sweeps/pallas_call | solution.py:426
  101.4 0.5 copy-done.21
  102.0 0.0 copy-done.22
  102.0 0.0 copy-done.23
  102.0 1.3 %add_points.1 = f32[3,384]{1,0:T(4,128)} custom-call(f32[3,3,128]{2,1,0:T(4,128)} %get-tuple-element.33.a, f32[3,3,128]{2,1,0:T(4,128)} %copy-done.21, f32[3,3,128]{2,1,0:T(4,128)} %copy-done.22, f32[3,3,128]{2,1,0:T(4,128)} %copy-done.23, f32[5,8,64,256]{3,2,1,0:T(8,128)} %bulk_sweeps.1.after), custom_call_target="tpu_custom_call" | custom-call | tf_op jit(solution)/shard_map/add_points/pallas_call | solution.py:552
  (76 shorter events, 0.3 us)
Async XLA Ops:
  0.6 1.7 %copy-start = (f32[5,8,64,256]{3,2,1,0:T(8,128)S(1)}, f32[5,8,64,256]{3,2,1,0:T(8,128)}, u32[]{:S(2)}) copy-start(f32[5,8,64,256]{3,2,1,0:T(8,128)} %src_in.3) | copy-start | bytes 7864324
  2.4 1.7 %copy-start.2 = (f32[5,8,64,256]{3,2,1,0:T(8,128)S(1)}, f32[5,8,64,256]{3,2,1,0:T(8,128)}, u32[]{:S(2)}) copy-start(f32[5,8,64,256]{3,2,1,0:T(8,128)} %inv_in.3) | copy-start | bytes 7864324
  4.1 1.5 %copy-start.18 = (f32[1,6,5,5]{1,0,3,2:T(1,128)S(1)}, f32[1,6,5,5]{1,0,3,2:T(1,128)}, u32[]{:S(2)}) copy-start(f32[1,6,5,5]{1,0,3,2:T(1,128)} %param.9) | copy-start | bytes 1804
  4.1 6.2 %copy-start.24 = (s32[8,2]{0,1:T(2,128)S(1)}, s32[8,2]{0,1:T(2,128)}, u32[]{:S(2)}) copy-start(s32[8,2]{0,1:T(2,128)} %param.10) | copy-start | bytes 196
  4.4 1.6 %collective-permute-start = (f32[5,5,8,256]{3,2,1,0:T(8,128)S(1)}, f32[5,5,8,256]{3,2,1,0:T(8,128)S(1)}, u32[]{:S(2)}, u32[]{:S(2)}) collective-permute-start(f32[5,5,8,256]{3,2,1,0:T(8,128)S(1)} %get-tuple-element.17), channel_id=1, source_target_pairs={{0,1},{1,0},{2,3},{3,2},{4,5},{5,4},{6,7},{7,6},{8,9},{9,8},{10,11... | collective-permute-start | bytes 614408 | tf_op jit(solution)/shard_map/ppermute | solution.py:598
  4.9 1.1 %collective-permute-start.1 = (f32[5,5,8,256]{3,2,1,0:T(8,128)S(1)}, f32[5,5,8,256]{3,2,1,0:T(8,128)S(1)}, u32[]{:S(2)}, u32[]{:S(2)}) collective-permute-start(f32[5,5,8,256]{3,2,1,0:T(8,128)S(1)} %get-tuple-element.18), channel_id=1, source_target_pairs={{1,2},{2,1},{5,6},{6,5},{9,10},{10,9},{13,14},{14,13},{17,18},{18,... | collective-permute-start | bytes 614408 | tf_op jit(solution)/shard_map/ppermute | solution.py:598
  6.0 11.4 %copy-start.7 = (f32[5,5,8,256]{3,2,1,0:T(8,128)}, f32[5,5,8,256]{3,2,1,0:T(8,128)S(1)}, u32[]{:S(2)}) copy-start(f32[5,5,8,256]{3,2,1,0:T(8,128)S(1)} %collective-permute-done.inner) | copy-start | bytes 614404
  6.0 11.4 %copy-start.9 = (f32[5,5,8,256]{3,2,1,0:T(8,128)}, f32[5,5,8,256]{3,2,1,0:T(8,128)S(1)}, u32[]{:S(2)}) copy-start(f32[5,5,8,256]{3,2,1,0:T(8,128)S(1)} %collective-permute-done.1.outer) | copy-start | bytes 614404
  6.4 38.8 %copy-start.6 = (f32[48,128]{1,0:T(8,128)}, f32[48,128]{1,0:T(8,128)S(1)}, u32[]{:S(2)}) copy-start(f32[48,128]{1,0:T(8,128)S(1)} %get-tuple-element.19.after.mine) | copy-start | bytes 73732
  6.4 5.8 %collective-permute-start.4 = (f32[1,48,128]{2,1,0:T(8,128)S(1)}, f32[1,48,128]{2,1,0:T(8,128)S(1)}, u32[]{:S(2)}, u32[]{:S(2)}) collective-permute-start(f32[1,48,128]{2,1,0:T(8,128)S(1)} %bitcast.30), channel_id=1, source_target_pairs={{0,16},{4,20},{8,24},{12,28},{16,0},{20,4},{24,8},{28,12},{1,17},{... | collective-permute-start | bytes 73736 | tf_op jit(solution)/shard_map/ppermute | solution.py:174
  12.2 18.7 %collective-permute-start.5 = (f32[2,48,128]{2,1,0:T(8,128)S(1)}, f32[2,48,128]{2,1,0:T(8,128)S(1)}, u32[]{:S(2)}, u32[]{:S(2)}) collective-permute-start(f32[2,48,128]{2,1,0:T(8,128)S(1)} %pad_maximum_fusion.3), channel_id=1, source_target_pairs={{0,8},{4,12},{8,0},{12,4},{16,24},{20,28},{24,16},{28,20},{1,9},{5... | collective-permute-start | bytes 147464 | tf_op jit(solution)/shard_map/ppermute | solution.py:174
  14.1 18.5 %copy-start.19 = (pred[128]{0:T(512)(128)(4,1)}, pred[128]{0:T(512)(128)(4,1)S(1)}, u32[]{:S(2)}) copy-start(pred[128]{0:T(512)(128)(4,1)S(1)} %iota_compare_fusion) | copy-start | bytes 388
  17.4 27.8 %copy-start.3 = (f32[5,8,64,256]{3,2,1,0:T(8,128)S(1)}, f32[5,8,64,256]{3,2,1,0:T(8,128)}, u32[]{:S(2)}) copy-start(f32[5,8,64,256]{3,2,1,0:T(8,128)} %inv_in.3) | copy-start | bytes 7864324
  23.4 1.2 %copy-start.4 = (f32[5,5,64,256]{3,2,1,0:T(8,128)}, f32[5,5,64,256]{3,2,1,0:T(8,128)S(1)}, u32[]{:S(2)}) copy-start(f32[5,5,64,256]{3,2,1,0:T(8,128)S(1)} %get-tuple-element.22.b) | copy-start | bytes 4915204
  24.6 10.9 %collective-permute-start.2 = (f32[2,5,64,128]{3,2,1,0:T(8,128)S(1)}, f32[2,5,64,128]{3,2,1,0:T(8,128)S(1)}, u32[]{:S(2)}, u32[]{:S(2)}) collective-permute-start(f32[2,5,64,128]{3,2,1,0:T(8,128)S(1)} %get-tuple-element.20.own), channel_id=1, source_target_pairs={{0,1},{1,0},{2,3},{3,2},{4,5},{5,4},{6,7},{7,6},{8,9},{9,8},{10,11... | collective-permute-start | bytes 983048 | tf_op jit(solution)/shard_map/ppermute | solution.py:598
  29.5 6.0 %collective-permute-start.3 = (f32[2,5,64,128]{3,2,1,0:T(8,128)S(1)}, f32[2,5,64,128]{3,2,1,0:T(8,128)}, u32[]{:S(2)}, u32[]{:S(2)}) collective-permute-start(f32[2,5,64,128]{3,2,1,0:T(8,128)S(1)} %get-tuple-element.20.own), channel_id=1, source_target_pairs={{1,2},{2,1},{5,6},{6,5},{9,10},{10,9},{13,14},{14,13},{17,18},{18,... | collective-permute-start | bytes 983048 | tf_op jit(solution)/shard_map/ppermute | solution.py:598
  30.9 3.9 %collective-permute-start.9 = (f32[48,128]{1,0:T(8,128)S(1)}, f32[48,128]{1,0:T(8,128)S(1)}, u32[]{:S(2)}, u32[]{:S(2)}) collective-permute-start(f32[48,128]{1,0:T(8,128)S(1)} %bitcast_select_fusion.2), channel_id=1, source_target_pairs={{0,4},{4,0},{8,12},{12,8},{16,20},{20,16},{24,28},{28,24},{1,5},{5... | collective-permute-start | bytes 73736 | tf_op jit(solution)/shard_map/ppermute | solution.py:195
  32.6 12.6 %copy-start.12 = (f32[32,128]{1,0:T(8,128)}, f32[32,128]{1,0:T(8,128)S(1)}, u32[]{:S(2)}) copy-start(f32[32,128]{1,0:T(8,128)S(1)} %pad.8.couplings) | copy-start | bytes 49156
  35.5 9.7 %copy-start.11 = (f32[48,128]{1,0:T(8,128)}, f32[48,128]{1,0:T(8,128)S(1)}, u32[]{:S(2)}) copy-start(f32[48,128]{1,0:T(8,128)S(1)} %fusion.1.given.theirs) | copy-start | bytes 73732
  35.5 1.4 %copy-start.5 = (f32[5,5,64,256]{3,2,1,0:T(8,128)S(1)}, f32[5,5,64,256]{3,2,1,0:T(8,128)}, u32[]{:S(2)}) copy-start(f32[5,5,64,256]{3,2,1,0:T(8,128)} %copy-done.4) | copy-start | bytes 4915204
  36.9 8.3 %copy-start.1 = (f32[5,8,64,256]{3,2,1,0:T(8,128)S(1)}, f32[5,8,64,256]{3,2,1,0:T(8,128)}, u32[]{:S(2)}) copy-start(f32[5,8,64,256]{3,2,1,0:T(8,128)} %src_in.3) | copy-start | bytes 7864324
  36.9 8.3 %copy-start.8 = (f32[5,5,8,256]{3,2,1,0:T(8,128)S(1)}, f32[5,5,8,256]{3,2,1,0:T(8,128)}, u32[]{:S(2)}) copy-start(f32[5,5,8,256]{3,2,1,0:T(8,128)} %copy-done.7) | copy-start | bytes 614404
  37.0 8.3 %copy-start.10 = (f32[5,5,8,256]{3,2,1,0:T(8,128)S(1)}, f32[5,5,8,256]{3,2,1,0:T(8,128)}, u32[]{:S(2)}) copy-start(f32[5,5,8,256]{3,2,1,0:T(8,128)} %copy-done.9) | copy-start | bytes 614404
  37.0 8.3 %copy-start.14 = (f32[3,5,2,8,256]{4,3,2,1,0:T(8,128)S(1)}, f32[3,5,2,8,256]{4,3,2,1,0:T(8,128)}, u32[]{:S(2)}) copy-start(f32[3,5,2,8,256]{4,3,2,1,0:T(8,128)} %jac.1) | copy-start | bytes 737284
  38.6 12.1 %copy-start.13 = (f32[2,5,64,128]{3,2,1,0:T(8,128)}, f32[2,5,64,128]{3,2,1,0:T(8,128)S(1)}, u32[]{:S(2)}) copy-start(f32[2,5,64,128]{3,2,1,0:T(8,128)S(1)} %get-tuple-element.23.full) | copy-start | bytes 983044
  38.6 12.1 %collective-permute-start.6 = (f32[1,320,128]{2,1,0:T(8,128)S(1)}, f32[1,320,128]{2,1,0:T(8,128)S(1)}, u32[]{:S(2)}, u32[]{:S(2)}) collective-permute-start(f32[1,320,128]{2,1,0:T(8,128)S(1)} %bitcast.27), channel_id=1, source_target_pairs={{0,16},{4,20},{8,24},{12,28},{16,0},{20,4},{24,8},{28,12},{1,17},{... | collective-permute-start | bytes 491528 | tf_op jit(solution)/shard_map/ppermute | solution.py:174
  41.2 38.2 %collective-permute-start.10 = (f32[5,5,64,256]{3,2,1,0:T(8,128)}, f32[5,5,64,256]{3,2,1,0:T(8,128)S(1)}, u32[]{:S(2)}, u32[]{:S(2)}) collective-permute-start(f32[5,5,64,256]{3,2,1,0:T(8,128)} %get-tuple-element.25), channel_id=1, source_target_pairs={{0,1},{1,0},{2,3},{3,2},{4,5},{5,4},{6,7},{7,6},{8,9},{9,8},{10,11... | collective-permute-start | bytes 4915208 | tf_op jit(solution)/shard_map/ppermute | solution.py:598
  44.2 25.4 %collective-permute-start.13 = (f32[5,5,64,256]{3,2,1,0:T(8,128)S(1)}, f32[5,5,64,256]{3,2,1,0:T(8,128)S(1)}, u32[]{:S(2)}, u32[]{:S(2)}) collective-permute-start(f32[5,5,64,256]{3,2,1,0:T(8,128)S(1)} %get-tuple-element.27), channel_id=1, source_target_pairs={{1,2},{2,1},{5,6},{6,5},{9,10},{10,9},{13,14},{14,13},{17,18},{18,... | collective-permute-start | bytes 4915208 | tf_op jit(solution)/shard_map/ppermute | solution.py:598
  45.2 5.5 %copy-start.15 = (f32[8,8,256]{2,1,0:T(8,128)S(1)}, f32[8,8,256]{2,1,0:T(8,128)}, u32[]{:S(2)}) copy-start(f32[8,8,256]{2,1,0:T(8,128)} %weight.1) | copy-start | bytes 196612
  45.2 5.4 %copy-start.16 = (s32[8,8,256]{2,1,0:T(8,128)S(1)}, s32[8,8,256]{2,1,0:T(8,128)}, u32[]{:S(2)}) copy-start(s32[8,8,256]{2,1,0:T(8,128)} %ids.1) | copy-start | bytes 196612
  54.9 13.0 %copy-start.20 = (pred[128]{0:T(512)(128)(4,1)S(1)}, pred[128]{0:T(512)(128)(4,1)}, u32[]{:S(2)}) copy-start(pred[128]{0:T(512)(128)(4,1)} %copy-done.19) | copy-start | bytes 388
  54.9 4.1 %collective-permute-start.11 = (f32[3,48,128]{2,1,0:T(8,128)S(1)}, f32[3,48,128]{2,1,0:T(8,128)S(1)}, u32[]{:S(2)}, u32[]{:S(2)}) collective-permute-start(f32[3,48,128]{2,1,0:T(8,128)S(1)} %constant_dynamic-slice_fusion.5), channel_id=1, source_target_pairs={{0,1},{1,0},{2,3},{3,2},{4,5},{5,4},{6,7},{7,6},{8,9},{9,8},{10,11... | collective-permute-start | bytes 221192 | tf_op jit(solution)/shard_map/ppermute | solution.py:573
  58.2 9.7 %collective-permute-start.7 = (f32[2,320,128]{2,1,0:T(8,128)S(1)}, f32[2,320,128]{2,1,0:T(8,128)S(1)}, u32[]{:S(2)}, u32[]{:S(2)}) collective-permute-start(f32[2,320,128]{2,1,0:T(8,128)S(1)} %pad_maximum_fusion.1), channel_id=1, source_target_pairs={{0,8},{4,12},{8,0},{12,4},{16,24},{20,28},{24,16},{28,20},{1,9},{5... | collective-permute-start | bytes 983048 | tf_op jit(solution)/shard_map/ppermute | solution.py:174
  59.1 10.4 %collective-permute-start.12 = (f32[3,24,128]{2,1,0:T(8,128)S(1)}, f32[3,24,128]{2,1,0:T(8,128)S(1)}, u32[]{:S(2)}, u32[]{:S(2)}) collective-permute-start(f32[3,24,128]{2,1,0:T(8,128)S(1)} %constant_dynamic-slice_fusion.4), channel_id=1, source_target_pairs={{0,2},{1,3},{2,0},{3,1},{4,6},{5,7},{6,4},{7,5},{8,10},{9,11},{10,... | collective-permute-start | bytes 110600 | tf_op jit(solution)/shard_map/ppermute | solution.py:573
  68.0 5.6 %collective-permute-start.8 = (f32[320,128]{1,0:T(8,128)S(1)}, f32[320,128]{1,0:T(8,128)S(1)}, u32[]{:S(2)}, u32[]{:S(2)}) collective-permute-start(f32[320,128]{1,0:T(8,128)S(1)} %bitcast_select_fusion), channel_id=1, source_target_pairs={{0,4},{4,0},{8,12},{12,8},{16,20},{20,16},{24,28},{28,24},{1,5},{5... | collective-permute-start | bytes 491528 | tf_op jit(solution)/shard_map/ppermute | solution.py:195
  69.6 9.8 %copy-start.26 = (f32[5,5,64,256]{3,2,1,0:T(8,128)}, f32[5,5,64,256]{3,2,1,0:T(8,128)S(1)}, u32[]{:S(2)}) copy-start(f32[5,5,64,256]{3,2,1,0:T(8,128)S(1)} %collective-permute-done.13.outer) | copy-start | bytes 4915204
  69.6 4.7 %collective-permute-start.14 = (f32[3,12,128]{2,1,0:T(8,128)S(1)}, f32[3,12,128]{2,1,0:T(8,128)S(1)}, u32[]{:S(2)}, u32[]{:S(2)}) collective-permute-start(f32[3,12,128]{2,1,0:T(8,128)S(1)} %constant_dynamic-slice_fusion.3), channel_id=1, source_target_pairs={{0,4},{4,0},{8,12},{12,8},{16,20},{20,16},{24,28},{28,24},{1,5},{5... | collective-permute-start | bytes 55304 | tf_op jit(solution)/shard_map/ppermute | solution.py:573
  74.3 5.0 %copy-start.17 = (f32[3,12,128]{2,1,0:T(8,128)}, f32[3,12,128]{2,1,0:T(8,128)S(1)}, u32[]{:S(2)}) copy-start(f32[3,12,128]{2,1,0:T(8,128)S(1)} %dynamic-slice_add_fusion.2.after) | copy-start | bytes 55300
  74.9 26.4 %collective-permute-start.15 = (f32[3,3,128]{2,1,0:T(4,128)S(1)}, f32[3,3,128]{2,1,0:T(4,128)S(1)}, u32[]{:S(2)}, u32[]{:S(2)}) collective-permute-start(f32[3,3,128]{2,1,0:T(4,128)S(1)} %get-tuple-element.32), channel_id=1, source_target_pairs={{0,16},{4,20},{8,24},{12,28},{16,0},{20,4},{24,8},{28,12},{1,17},{... | collective-permute-start | bytes 13832 | tf_op jit(solution)/shard_map/ppermute | solution.py:590
  75.1 26.3 %collective-permute-start.16 = (f32[3,3,128]{2,1,0:T(4,128)S(1)}, f32[3,3,128]{2,1,0:T(4,128)S(1)}, u32[]{:S(2)}, u32[]{:S(2)}) collective-permute-start(f32[3,3,128]{2,1,0:T(4,128)S(1)} %get-tuple-element.31), channel_id=1, source_target_pairs={{0,8},{4,12},{8,0},{12,4},{16,24},{20,28},{24,16},{28,20},{1,9},{5... | collective-permute-start | bytes 13832 | tf_op jit(solution)/shard_map/ppermute | solution.py:590
  75.6 25.8 %collective-permute-start.17 = (f32[3,3,128]{2,1,0:T(4,128)S(1)}, f32[3,3,128]{2,1,0:T(4,128)S(1)}, u32[]{:S(2)}, u32[]{:S(2)}) collective-permute-start(f32[3,3,128]{2,1,0:T(4,128)S(1)} %get-tuple-element.30), channel_id=1, source_target_pairs={{0,24},{4,28},{8,16},{12,20},{16,8},{20,12},{24,0},{28,4},{1,25},{... | collective-permute-start | bytes 13832 | tf_op jit(solution)/shard_map/ppermute | solution.py:590
  79.3 1.2 %copy-start.25 = (f32[5,5,64,256]{3,2,1,0:T(8,128)}, f32[5,5,64,256]{3,2,1,0:T(8,128)S(1)}, u32[]{:S(2)}) copy-start(f32[5,5,64,256]{3,2,1,0:T(8,128)S(1)} %collective-permute-done.10.inner) | copy-start | bytes 4915204
  101.4 0.6 copy-start.21
  101.4 0.6 copy-start.22
  101.4 0.6 copy-start.23

commit v4 on v3

--- a/solution.py
+++ b/solution.py
@@ -14,6 +14,7 @@
 DEEP = 3
 NEAR = 8
 MIB = 1 << 20
+VMEM_BYTES = 60 * MIB
 ANY = pl.BlockSpec(memory_space=pl.ANY)
 VMEM = pl.BlockSpec(memory_space=pltpu.VMEM)
 SMEM = pl.BlockSpec(memory_space=pltpu.SMEM)
@@ -75,7 +76,7 @@
             jax.ShapeDtypeStruct((5, nvar, depth, chord), f32),
             jax.ShapeDtypeStruct((5, nvar, depth, chord), f32),
         ],
-        compiler_params=pltpu.CompilerParams(vmem_limit_bytes=48 * MIB),
+        compiler_params=pltpu.CompilerParams(vmem_limit_bytes=VMEM_BYTES),
         cost_estimate=pl.CostEstimate(
             flops=0, bytes_accessed=16 * nvar * spans * depth * chord, transcendentals=0
         ),
@@ -141,7 +142,7 @@
             jax.ShapeDtypeStruct((nvar * depth + 8, LANES), jnp.float32),
             jax.ShapeDtypeStruct(own.shape, jnp.float32),
         ],
-        compiler_params=pltpu.CompilerParams(vmem_limit_bytes=32 * MIB),
+        compiler_params=pltpu.CompilerParams(vmem_limit_bytes=VMEM_BYTES),
         name="near_merge",
     )(even, own, inner, outer, cpl)
 
@@ -159,7 +160,7 @@
             jax.ShapeDtypeStruct(b.shape, b.dtype),
         ],
         input_output_aliases={5: 2, 6: 3},
-        compiler_params=pltpu.CompilerParams(vmem_limit_bytes=48 * MIB),
+        compiler_params=pltpu.CompilerParams(vmem_limit_bytes=VMEM_BYTES),
         name="bulk_merge",
     )(even, own, inner, outer, after, a, b)
 
@@ -195,7 +196,7 @@
     given = lax.ppermute(chosen(me ^ last), "blk", [(i, i ^ last) for i in range(count)])
     _, low_here = place(low_of[me])
     _, high_here = place(high_of[me])
-    return jnp.where(jnp.where(left, low_here, high_here), chosen(me), given), first, held
+    return jnp.where(jnp.where(left, low_here, high_here), chosen(me), given), first
 
 
 def expand_couplings(couplings, wide):
@@ -286,43 +287,61 @@
         p = [inv[v] * total[v] for v in range(nvar)]
 
 
-def run_sweeps(depth, even, couplings, full, given, mine, theirs, src_in, inv_in, inner, outer, scratch):
-    src, inv, pa, pb, wide, before, coming, faces, scalars, sems = scratch
+def run_sweeps(depth, even, couplings, full, given, mine, theirs, src_in, inv_in, inner, outer, scratch, out=None):
+    src, inv, pa, pb, wide, before, coming, faces, scalars, sems, out_sems = scratch
     nvar, layers, rows, chord = pa.shape
     spans = layers - 2 * DEEP
-    moves = [
-        (src_in.at[:, :, 0:depth], src.at[:, DEEP : DEEP + spans, 0:depth]),
-        (inv_in.at[:, :, 0:depth], inv.at[:, DEEP : DEEP + spans, 0:depth]),
-    ]
-    for halo, up in ((inner, even[0]), (outer, 1 - even[0])):
-        for j in range(DEEP):
-            s = jnp.where(up == 1, DEEP + spans + j, DEEP - 1 - j)
-            if j < DEEP - 1:
-                moves.append((halo.at[j], src.at[:, s, 0:depth]))
-                moves.append((halo.at[DEEP - 1 + j], inv.at[:, s, 0:depth]))
-            else:
-                moves.append((halo.at[2 * (DEEP - 1)], src.at[:, s, 0:depth]))
-    loads = [pltpu.make_async_copy(x, y, sems.at[j]) for j, (x, y) in enumerate(moves)]
+
+    def move(f, at, start):
+        to, field = ((src, src_in), (inv, inv_in))[f]
+
+        def one(ref, layer):
+            copy = pltpu.make_async_copy(ref, to.at[:, layer, 0:depth], sems.at[f, layer])
+            copy.start() if start else copy.wait()
+
+        if not start or DEEP <= at < DEEP + spans:
+            one(field.at[:, at - DEEP if start else 0, 0:depth], at)
+            return
+        low = at < DEEP
+        j = DEEP - 1 - at if low else at - DEEP - spans
+        piece = f * (DEEP - 1) + j if j < DEEP - 1 else 2 * (DEEP - 1)
+        if f == 1 and j == DEEP - 1:
+            return
+
+        @pl.when(even[0] == (0 if low else 1))
+        def _():
+            one(inner.at[piece], at)
+
+        @pl.when(even[0] == (1 if low else 0))
+        def _():
+            one(outer.at[piece], at)
+
     if rows != depth:
         none = jnp.zeros((nvar, layers, rows - depth, chord), jnp.float32)
         src[:, :, depth:rows, :] = none
         inv[:, :, depth:rows, :] = none
         faces[...] = jnp.zeros(faces.shape, jnp.float32)
-    for copy in loads:
-        copy.start()
+    for at in range(layers):
+        for f in range(2):
+            move(f, at, True)
     ones = jnp.ones((nvar, rows, chord), jnp.float32)
     inv[:, 0] = ones
     inv[:, layers - 1] = ones
     expand_couplings(couplings[...], wide)
     ribbon_sweeps(depth, full, given, mine, theirs, scalars, faces)
-    for copy in loads:
-        copy.wait()
-
-    def first(s, _):
-        pa[:, s] = inv[:, s] * src[:, s]
-        return 0
-
-    lax.fori_loop(0, layers, first, 0)
+
+    def arrive(at, edge=False):
+        move(0, at, False)
+        if not edge:
+            move(1, at, False)
+        pa[:, at] = inv[:, at] * src[:, at]
+
+    def leave(at, start):
+        copy = pltpu.make_async_copy(
+            pb.at[:, at, 0:depth], out.at[:, at - DEEP], out_sems.at[at - DEEP]
+        )
+        copy.start() if start else copy.wait()
+
     groups = rows // 16
     lane = lane_iota((1, 1, LANES))
     k = lax.broadcasted_iota(jnp.int32, (1, rows, 1), 1)
@@ -356,12 +375,17 @@
     step = 16 * nvar
     for n in range(SWEEPS):
         p, after = (pa, pb) if n % 2 == 0 else (pb, pa)
+        if n == 0:
+            arrive(0, True)
         coming[...] = products(p, n, 0, step)
         full = layers - 2 - 2 * n
         turn = 2 if groups > 1 else full
 
         def several(i, _):
             s0 = n + 1 + i * turn
+            if n == 0:
+                for j in range(turn):
+                    arrive(s0 + j)
             every = [products(p, s0 + j, 0, 6 * step) for j in range(turn)]
             arriving, waiting = coming[...], before[...]
             for j in range(turn):
@@ -371,13 +395,26 @@
                 arriving = now[:nvar]
             before[...] = waiting
             coming[...] = arriving
+            if n == SWEEPS - 1 and out is not None:
+                for j in range(turn - 1):
+                    leave(s0 + j, True)
+
+                @pl.when(i > 0)
+                def _():
+                    leave(s0 - 1, True)
+
             return 0
 
         lax.fori_loop(0, full // turn, several, 0)
         last = layers - 1 - n
+        if n == 0:
+            arrive(last, True)
         after[:, last - 1] = inv[:, last - 1] * (before[...] + products(p, last, step, 2 * step))
-    result = pb if SWEEPS % 2 else pa
-    return result
+    if out is not None:
+        leave(DEEP + spans - 1, True)
+        for at in range(DEEP, DEEP + spans):
+            leave(at, False)
+    return pb
 
 
 def sweep_scratch(nvar, spans, chord, depth):
@@ -395,21 +432,17 @@
         layer,
         pltpu.VMEM((SWEEPS, nvar, rows, LANES), f32),
         pltpu.VMEM((2, 152, LANES), f32),
-        pltpu.SemaphoreType.DMA((12,)),
+        pltpu.SemaphoreType.DMA((2, spans + 2 * DEEP)),
+        pltpu.SemaphoreType.DMA((spans,)),
     ]
 
 
 def bulk_kernel(
     depth, even, couplings, full, given, mine, theirs, src_in, inv_in, inner, outer, after, out, *scratch
 ):
-    *scratch, out_sem = scratch
-    result = run_sweeps(
-        depth, even, couplings, full, given, mine, theirs, src_in, inv_in, inner, outer, scratch
+    run_sweeps(
+        depth, even, couplings, full, given, mine, theirs, src_in, inv_in, inner, outer, scratch, out
     )
-    spans = out.shape[1]
-    copy = pltpu.make_async_copy(result.at[:, DEEP : DEEP + spans, 0:depth], out, out_sem)
-    copy.start()
-    copy.wait()
 
 
 def coupling_rows(shape):
@@ -430,8 +463,8 @@
         + [coupling_rows(theirs.shape), ANY, ANY, ANY, ANY, ANY],
         out_specs=ANY,
         out_shape=jax.ShapeDtypeStruct(source.shape, jnp.float32),
-        scratch_shapes=sweep_scratch(nvar, spans, chord, depth) + [pltpu.SemaphoreType.DMA],
-        compiler_params=pltpu.CompilerParams(vmem_limit_bytes=56 * MIB),
+        scratch_shapes=sweep_scratch(nvar, spans, chord, depth),
+        compiler_params=pltpu.CompilerParams(vmem_limit_bytes=VMEM_BYTES),
         cost_estimate=pl.CostEstimate(
             flops=2 * 40 * 480 * 256 * 256 * (depth // 16), bytes_accessed=16 * MIB, transcendentals=0
         ),
@@ -470,7 +503,7 @@
         out_specs=pl.BlockSpec(shape, lambda i: (0, 0, 0)),
         out_shape=jax.ShapeDtypeStruct(shape, jnp.float32),
         scratch_shapes=sweep_scratch(nvar, spans, chord, NEAR),
-        compiler_params=pltpu.CompilerParams(vmem_limit_bytes=48 * MIB),
+        compiler_params=pltpu.CompilerParams(vmem_limit_bytes=VMEM_BYTES),
         cost_estimate=pl.CostEstimate(flops=5 * 10**9, bytes_accessed=4 * MIB, transcendentals=0),
         name="near_sweeps",
     )(even, couplings, full, given, packet, given, source, inv_diag, inner, outer, jac, after)
@@ -535,27 +568,10 @@
         out_specs=VMEM,
         out_shape=jax.ShapeDtypeStruct(shape, jnp.float32),
         scratch_shapes=[pltpu.VMEM(ids.shape, jnp.int32), pltpu.VMEM(ids.shape, jnp.int32)],
-        compiler_params=pltpu.CompilerParams(vmem_limit_bytes=48 * MIB),
+        compiler_params=pltpu.CompilerParams(vmem_limit_bytes=VMEM_BYTES),
         cost_estimate=pl.CostEstimate(flops=4 * 10**9, bytes_accessed=MIB, transcendentals=0),
         name="scatter_points",
     )(sens, weight, ids, after)
-
-
-def add_kernel(a, b, c, d, after, out):
-    total = (a[...] + b[...]) + (c[...] + d[...])
-    for j in range(total.shape[1]):
-        out[:, LANES * j : LANES * (j + 1)] = total[:, j]
-
-
-def add_points(parts, after):
-    dims, rows, lanes = parts[0].shape
-    return pl.pallas_call(
-        add_kernel,
-        in_specs=[VMEM] * 4 + [ANY],
-        out_specs=VMEM,
-        out_shape=jax.ShapeDtypeStruct((dims, rows * lanes), jnp.float32),
-        name="add_points",
-    )(*parts, after)
 
 
 def halve_points(partial, after, n_dev):
@@ -611,15 +627,15 @@
     own, inner, outer = make_sends(even, even, source, inv_diag, NEAR, nvar)
     inner, outer = swap_spans(inner, outer)
     packet, full = near_merge(even, own, inner, outer, cpl)
-    given, _, held = route_ends(packet, me, low_of, high_of)
-
-    bulk_own, bulk_inner, bulk_outer = make_sends(even, packet, source, inv_diag, source.shape[2], 1)
+    given, _ = route_ends(packet, me, low_of, high_of)
+
+    bulk_own, bulk_inner, bulk_outer = make_sends(even, own, source, inv_diag, source.shape[2], 1)
     tiles = swap_spans(bulk_own, bulk_own)
     bulk_packet, bulk_full, bulk_inner, bulk_outer = bulk_merge(
-        even, bulk_own, *tiles, held, bulk_inner, bulk_outer
+        even, bulk_own, *tiles, packet, bulk_inner, bulk_outer
     )
     bulk_inner, bulk_outer = swap_spans(bulk_inner, bulk_outer)
-    bulk_given, bulk_first, _ = route_ends(bulk_packet, me, low_of, high_of)
+    bulk_given, bulk_first = route_ends(bulk_packet, me, low_of, high_of)
 
     sens = near_sweeps(
         even, couplings, full, given, packet, source, inv_diag, inner, outer, wall_jac, bulk_packet
@@ -629,7 +645,9 @@
     adjoint = bulk_sweeps(
         even, couplings, bulk_full, bulk_given, packet, given, source, inv_diag, bulk_inner, bulk_outer, partial
     )
-    return adjoint, add_points(quarter_points(partial), adjoint)
+    parts, adjoint = lax.optimization_barrier((quarter_points(partial), adjoint))
+    total = (parts[0] + parts[1]) + (parts[2] + parts[3])
+    return adjoint, total.reshape(total.shape[0], -1)
 
 
 def solution(mesh):

time: 104 us -> 107 us (1.029)
  Pallas kernels: 40 us -> 47.1 us
  starting transfers between devices: 32 us -> 27 us
  other arithmetic: 1.6 us -> 6.31 us
  local copies, waits for them, and re-layouts: 9.57 us -> 5.98 us
    unnamed x54 -> x21, local copies, waits for them, and re-layouts: 7.9 us -> 3.44 us
    pallas_call x1, Pallas kernels: 5.4 us -> 8.85 us  [near_sweeps(): pl.pallas_call(near_kernel, grid=(1,), in_specs=[SMEM, whole(couplings),...]
    concatenate x4, other arithmetic: 0.08 us -> 3.39 us  [route_ends(): held = jnp.concatenate([held, other], 0)]
    ppermute x3, starting transfers between devices: 4.14 us -> 1.07 us  [halve_points(): lax.ppermute(send, axis, [(i, i ^ mask) for i in range(count)])]
    pallas_call x2, Pallas kernels: 6.26 us -> 8.71 us  [make_sends(): pl.pallas_call(send_kernel, grid=(nvar // step,), in_specs=[SMEM, ANY, fi...]
    pallas_call x1, Pallas kernels: 4.2 us -> 5.89 us  [scatter_points(): pl.pallas_call(functools.partial(scatter_kernel, bits), in_specs=[VMEM, V...]
    pallas_call x1, Pallas kernels: 0.31 us -> 1.96 us  [near_merge(): pl.pallas_call(near_merge_kernel, in_specs=[SMEM, VMEM, VMEM, VMEM, VMEM]...]
    pallas_call x1, Pallas kernels: 20.9 us -> 19.3 us  [bulk_sweeps(): pl.pallas_call(functools.partial(bulk_kernel, depth), grid=(1,), in_specs...]
  transfers between devices with their start and end apart: 18 -> 18, of which waited for: 5 -> 4; matrix products, arithmetic and copies ran while one was open for 3% -> 8% of each run, Pallas kernels for 35% -> 40%
where the time goes in v4:
time: 107 us; the launch traced here: 106 us
  Pallas kernels  47.1 us (44%)
  starting transfers between devices  27 us (25%)
  waiting for transfers between devices  15.9 us (15%)
  other arithmetic  6.31 us (6%)
  local copies, waits for them, and re-layouts  5.98 us (6%)
  between operations  3.54 us (3%)
    pallas_call x1, Pallas kernels, bulk_sweeps(): pl.pallas_call(functools.partial(bulk_kernel, depth), grid=(1,), in_specs...  19.3 us
    ppermute x4, waiting for transfers between devices, route_ends(): other = lax.ppermute(held, 'blk', [(i, i ^ mask) for i in range(count)])  10.3 us
    pallas_call x1, Pallas kernels, near_sweeps(): pl.pallas_call(near_kernel, grid=(1,), in_specs=[SMEM, whole(couplings),...  8.85 us
    pallas_call x2, Pallas kernels, make_sends(): pl.pallas_call(send_kernel, grid=(nvar // step,), in_specs=[SMEM, ANY, fi...  8.71 us
    ppermute x3, starting transfers between devices, swap_spans(): lax.ppermute(inner, 'sub', pairs)  8.5 us
    ppermute x4, starting transfers between devices, route_ends(): other = lax.ppermute(held, 'blk', [(i, i ^ mask) for i in range(count)])  7.78 us
    pallas_call x1, Pallas kernels, scatter_points(): pl.pallas_call(functools.partial(scatter_kernel, bits), in_specs=[VMEM, V...  5.89 us
    ppermute x2, waiting for transfers between devices, route_ends(): lax.ppermute(chosen(me ^ last), 'blk', [(i, i ^ last) for i in range(coun...  5.56 us
  transfers between devices with their start and end apart: 18, of which 4 were waited for; matrix products, arithmetic and copies ran while one was open for 8% of the time, Pallas kernels for 40%

profile of v4, /device:TPU:0, one launch (start us, length us, event | category | flops | bytes accessed | tf_op | source)
XLA Modules:
  0.0 105.8 jit_solution(14062936502247268780)
XLA Ops:
  0.6 2.0 %sends_8.1 = (f32[2,5,8,128]{3,2,1,0:T(8,128)}, f32[5,5,8,256]{3,2,1,0:T(8,128)}, f32[5,5,8,256]{3,2,1,0:T(8,128)}) custom-call(s32[1]{0:T(128)} %bitcast.even.after, s32[1]{0:T(128)} %bitcast.even.after, f32[5,8,64,256]{3,2,1,0:T(8,128)} %src_in.3, f32[5,8,64,256]{3,2,1,0:T(8,128)} %inv_in.3), custom_call_target="tpu_custom_call" | custom-call | bytes 1310720 | tf_op jit(solution)/shard_map/sends_8/pallas_call | solution.py:69
  2.7 0.5 collective-permute-start
  3.1 0.7 collective-permute-start.1
  3.8 6.7 %sends_64.1 = (f32[2,5,64,128]{3,2,1,0:T(8,128)}, f32[5,5,64,256]{3,2,1,0:T(8,128)}, f32[5,5,64,256]{3,2,1,0:T(8,128)}) custom-call(s32[1]{0:T(128)} %bitcast.even.after, f32[2,5,8,128]{3,2,1,0:T(8,128)} %get-tuple-element.21.own.after, f32[5,8,64,256]{3,2,1,0:T(8,128)} %src_in.3, f32[5,8,64,256]{3,2,1,0:T(8,128)} %inv_in.3), custom_call_target="tpu_custom_call" | custom-call | bytes 10485760 | tf_op jit(solution)/shard_map/sends_64/pallas_call | solution.py:69
  10.5 3.9 %collective-permute-start.5 = (f32[2,5,64,128]{3,2,1,0:T(8,128)}, f32[2,5,64,128]{3,2,1,0:T(8,128)S(1)}, u32[]{:S(2)}, u32[]{:S(2)}) collective-permute-start(f32[2,5,64,128]{3,2,1,0:T(8,128)} %get-tuple-element.26.own), channel_id=1, source_target_pairs={{0,1},{1,0},{2,3},{3,2},{4,5},{5,4},{6,7},{7,6},{8,9},{9,8},{10,11... | collective-permute-start | bytes 983048 | tf_op jit(solution)/shard_map/ppermute | solution.py:614
  14.4 0.7 collective-permute-start.6
  15.0 0.1 copy.15
  15.2 0.1 reshape_squeeze.7
  15.3 0.1 reshape.30
  15.4 0.7 pad_maximum_fusion.4.cpl
  16.1 0.7 copy-done.4
  16.7 0.7 copy-done.5
  17.4 2.0 %near_merge.1 = (f32[48,128]{1,0:T(8,128)}, f32[2,5,8,128]{3,2,1,0:T(8,128)}) custom-call(s32[1]{0:T(128)} %bitcast.even.after, f32[2,5,8,128]{3,2,1,0:T(8,128)} %get-tuple-element.21.own.after, f32[5,5,8,256]{3,2,1,0:T(8,128)} %copy-done.4, f32[5,5,8,256]{3,2,1,0:T(8,128)} %copy-done.5, f32[8,128]{1,0:T(8,128)} %pad_maximum_fusion.4.cpl), custom_call_target="tpu_custom_call" | custom-call | tf_op jit(solution)/shard_map/near_merge/pallas_call | solution.py:137
  19.4 2.6 %collective-permute-start.2 = (f32[1,48,128]{2,1,0:T(8,128)}, f32[1,48,128]{2,1,0:T(8,128)S(1)}, u32[]{:S(2)}, u32[]{:S(2)}) collective-permute-start(f32[1,48,128]{2,1,0:T(8,128)} %bitcast.35), channel_id=1, source_target_pairs={{0,16},{4,20},{8,24},{12,28},{16,0},{20,4},{24,8},{28,12},{1,17},{... | collective-permute-start | bytes 73736 | tf_op jit(solution)/shard_map/ppermute | solution.py:175
  22.0 2.3 %collective-permute-done.2 = f32[1,48,128]{2,1,0:T(8,128)S(1)} collective-permute-done((f32[1,48,128]{2,1,0:T(8,128)}, f32[1,48,128]{2,1,0:T(8,128)S(1)}, u32[]{:S(2)}, u32[]{:S(2)}) %collective-permute-start.2) | collective-permute-done | bytes 24608 | tf_op jit(solution)/shard_map/ppermute | solution.py:175
  24.3 0.7 pad_maximum_fusion.3
  25.0 1.7 %collective-permute-start.3 = (f32[2,48,128]{2,1,0:T(8,128)S(1)}, f32[2,48,128]{2,1,0:T(8,128)S(1)}, u32[]{:S(2)}, u32[]{:S(2)}) collective-permute-start(f32[2,48,128]{2,1,0:T(8,128)S(1)} %pad_maximum_fusion.3), channel_id=1, source_target_pairs={{0,8},{4,12},{8,0},{12,4},{16,24},{20,28},{24,16},{28,20},{1,9},{5... | collective-permute-start | bytes 147464 | tf_op jit(solution)/shard_map/ppermute | solution.py:175
  26.7 0.7 constant_dynamic-slice_fusion.9
  30.0 0.7 pad_maximum_fusion.2
  30.7 1.6 %collective-permute-start.4 = (f32[48,128]{1,0:T(8,128)S(1)}, f32[48,128]{1,0:T(8,128)S(1)}, u32[]{:S(2)}, u32[]{:S(2)}) collective-permute-start(f32[48,128]{1,0:T(8,128)S(1)} %bitcast_select_fusion.2), channel_id=1, source_target_pairs={{0,4},{4,0},{8,12},{12,8},{16,20},{20,16},{24,28},{28,24},{1,5},{5... | collective-permute-start | bytes 73736 | tf_op jit(solution)/shard_map/ppermute | solution.py:196
  32.4 0.6 pad.8.couplings
  33.0 1.6 %collective-permute-done.4 = f32[48,128]{1,0:T(8,128)S(1)} collective-permute-done((f32[48,128]{1,0:T(8,128)S(1)}, f32[48,128]{1,0:T(8,128)S(1)}, u32[]{:S(2)}, u32[]{:S(2)}) %collective-permute-start.4) | collective-permute-done | bytes 24608 | tf_op jit(solution)/shard_map/ppermute | solution.py:196
  34.6 0.6 fusion.1.given.theirs
  35.2 0.7 copy-done.2
  36.0 0.1 copy-done.3
  36.1 2.3 %bulk_merge.1 = (f32[320,128]{1,0:T(8,128)}, f32[2,5,64,128]{3,2,1,0:T(8,128)}, f32[5,5,64,256]{3,2,1,0:T(8,128)}, f32[5,5,64,256]{3,2,1,0:T(8,128)}) custom-call(s32[1]{0:T(128)} %bitcast.even.after, f32[2,5,64,128]{3,2,1,0:T(8,128)} %get-tuple-element.26.own, f32[2,5,64,128]{3,2,1,0:T(8,128)} %copy-done.2, ...), custom_call_target="tpu_custom_call", output_to_operand_aliasing={{2}: (5, {}), {3}: (6, {})} | custom-call | tf_op jit(solution)/shard_map/bulk_merge/pallas_call | solution.py:152
  38.4 2.7 %collective-permute-start.7 = (f32[1,320,128]{2,1,0:T(8,128)}, f32[1,320,128]{2,1,0:T(8,128)S(1)}, u32[]{:S(2)}, u32[]{:S(2)}) collective-permute-start(f32[1,320,128]{2,1,0:T(8,128)} %bitcast.32), channel_id=1, source_target_pairs={{0,16},{4,20},{8,24},{12,28},{16,0},{20,4},{24,8},{28,12},{1,17},{... | collective-permute-start | bytes 491528 | tf_op jit(solution)/shard_map/ppermute | solution.py:175
  41.1 0.8 collective-permute-start.10
  41.8 4.2 %collective-permute-start.17 = (f32[5,5,64,256]{3,2,1,0:T(8,128)}, f32[5,5,64,256]{3,2,1,0:T(8,128)}, u32[]{:S(2)}, u32[]{:S(2)}) collective-permute-start(f32[5,5,64,256]{3,2,1,0:T(8,128)} %get-tuple-element.33), channel_id=1, source_target_pairs={{0,1},{1,0},{2,3},{3,2},{4,5},{5,4},{6,7},{7,6},{8,9},{9,8},{10,11... | collective-permute-start | bytes 4915208 | tf_op jit(solution)/shard_map/ppermute | solution.py:614
  46.0 8.8 %near_sweeps.1.sens = f32[3,8,256]{2,1,0:T(8,128)} custom-call(s32[1]{0:T(128)} %bitcast.even.after, f32[32,128]{1,0:T(8,128)} %pad.8.couplings, f32[2,5,8,128]{3,2,1,0:T(8,128)} %get-tuple-element.24.full, f32[48,128]{1,0:T(8,128)} %fusion.1.given.theirs, f32[48,128]{1,0:T(8,128)} %get-tuple-element.25.after.mine, f32[48,128]{1,0:T(8,128)} %fusion.1.given.theirs, ...), custom_call_target="tpu_custom_call" | custom-call | flops 5000000000 | bytes 4194304 | tf_op jit(solution)/shard_map/near_sweeps/pallas_call | solution.py:498
  54.9 0.7 copy-done.1
  55.6 5.9 %scatter_points.1 = f32[3,48,256]{2,1,0:T(8,128)} custom-call(f32[3,8,256]{2,1,0:T(8,128)} %near_sweeps.1.sens, f32[8,8,256]{2,1,0:T(8,128)} %weight.1, s32[8,8,256]{2,1,0:T(8,128)} %ids.1, f32[1,320,128]{2,1,0:T(8,128)} %copy-done.1), custom_call_target="tpu_custom_call" | custom-call | flops 4000000000 | bytes 1048576 | tf_op jit(solution)/shard_map/scatter_points/pallas_call | solution.py:565
  61.4 0.9 constant_dynamic-slice_fusion.6
  62.4 0.9 pad_maximum_fusion.1
  63.3 0.9 collective-permute-start.15
  64.2 0.9 dynamic-slice_add_fusion
  65.1 0.4 collective-permute-start.9
  65.5 7.9 %collective-permute-done.15 = f32[2,320,128]{2,1,0:T(8,128)S(1)} collective-permute-done((f32[2,320,128]{2,1,0:T(8,128)S(1)}, f32[2,320,128]{2,1,0:T(8,128)S(1)}, u32[]{:S(2)}, u32[]{:S(2)}) %collective-permute-start.15) | collective-permute-done | bytes 327712 | tf_op jit(solution)/shard_map/ppermute | solution.py:175
  73.5 1.0 pad_maximum_fusion
  74.5 1.6 %collective-permute-start.16 = (f32[320,128]{1,0:T(8,128)S(1)}, f32[320,128]{1,0:T(8,128)S(1)}, u32[]{:S(2)}, u32[]{:S(2)}) collective-permute-start(f32[320,128]{1,0:T(8,128)S(1)} %bitcast_select_fusion), channel_id=1, source_target_pairs={{0,4},{4,0},{8,12},{12,8},{16,20},{20,16},{24,28},{28,24},{1,5},{5... | collective-permute-start | bytes 491528 | tf_op jit(solution)/shard_map/ppermute | solution.py:196
  76.1 0.6 collective-permute-start.11
  76.7 3.9 %collective-permute-done.16 = f32[320,128]{1,0:T(8,128)S(1)} collective-permute-done((f32[320,128]{1,0:T(8,128)S(1)}, f32[320,128]{1,0:T(8,128)S(1)}, u32[]{:S(2)}, u32[]{:S(2)}) %collective-permute-start.16) | collective-permute-done | bytes 163872 | tf_op jit(solution)/shard_map/ppermute | solution.py:196
  80.6 0.7 fusion.given
  81.4 0.2 collective-permute-start.12
  81.6 0.8 collective-permute-start.13
  82.4 3.4 %collective-permute-start.14 = (f32[3,3,128]{2,1,0:T(4,128)S(1)}, f32[3,3,128]{2,1,0:T(4,128)S(1)}, u32[]{:S(2)}, u32[]{:S(2)}) collective-permute-start(f32[3,3,128]{2,1,0:T(4,128)S(1)} %get-tuple-element.40), channel_id=1, source_target_pairs={{0,24},{4,28},{8,16},{12,20},{16,8},{20,12},{24,0},{28,4},{1,25},{... | collective-permute-start | bytes 13832 | tf_op jit(solution)/shard_map/ppermute | solution.py:606
  85.8 19.3 %bulk_sweeps.1 = f32[5,8,64,256]{3,2,1,0:T(8,128)} custom-call(s32[1]{0:T(128)} %bitcast.even.after, f32[32,128]{1,0:T(8,128)} %pad.8.couplings, f32[2,5,64,128]{3,2,1,0:T(8,128)} %get-tuple-element.32.full, f32[320,128]{1,0:T(8,128)} %fusion.given, f32[48,128]{1,0:T(8,128)} %get-tuple-element.25.after.mine, f32[48,128]{1,0:T(8,128)} %fusion.1.given.theirs, ...), custom_call_target="tpu_custom_call" | custom-call | flops 10066329600 | bytes 16777216 | tf_op jit(solution)/shard_map/bulk_sweeps/pallas_call | solution.py:459
  105.2 0.6 copy.19
  (43 shorter events, 0.2 us)
Async XLA Ops:
  2.7 13.4 %collective-permute-start = (f32[5,5,8,256]{3,2,1,0:T(8,128)}, f32[5,5,8,256]{3,2,1,0:T(8,128)S(1)}, u32[]{:S(2)}, u32[]{:S(2)}) collective-permute-start(f32[5,5,8,256]{3,2,1,0:T(8,128)} %get-tuple-element.22), channel_id=1, source_target_pairs={{0,1},{1,0},{2,3},{3,2},{4,5},{5,4},{6,7},{7,6},{8,9},{9,8},{10,11... | collective-permute-start | bytes 614408 | tf_op jit(solution)/shard_map/ppermute | solution.py:614
  3.1 12.9 %collective-permute-start.1 = (f32[5,5,8,256]{3,2,1,0:T(8,128)}, f32[5,5,8,256]{3,2,1,0:T(8,128)S(1)}, u32[]{:S(2)}, u32[]{:S(2)}) collective-permute-start(f32[5,5,8,256]{3,2,1,0:T(8,128)} %get-tuple-element.23), channel_id=1, source_target_pairs={{1,2},{2,1},{5,6},{6,5},{9,10},{10,9},{13,14},{14,13},{17,18},{18,... | collective-permute-start | bytes 614408 | tf_op jit(solution)/shard_map/ppermute | solution.py:614
  3.8 11.3 %copy-start.7 = (f32[1,6,5,5]{1,0,3,2:T(1,128)S(1)}, f32[1,6,5,5]{1,0,3,2:T(1,128)}, u32[]{:S(2)}) copy-start(f32[1,6,5,5]{1,0,3,2:T(1,128)} %param.9) | copy-start | bytes 1804
  3.8 18.2 %copy-start.8 = (s32[8,2]{0,1:T(2,128)S(1)}, s32[8,2]{0,1:T(2,128)}, u32[]{:S(2)}) copy-start(s32[8,2]{0,1:T(2,128)} %param.10) | copy-start | bytes 196
  10.5 24.7 %collective-permute-start.5 = (f32[2,5,64,128]{3,2,1,0:T(8,128)}, f32[2,5,64,128]{3,2,1,0:T(8,128)S(1)}, u32[]{:S(2)}, u32[]{:S(2)}) collective-permute-start(f32[2,5,64,128]{3,2,1,0:T(8,128)} %get-tuple-element.26.own), channel_id=1, source_target_pairs={{0,1},{1,0},{2,3},{3,2},{4,5},{5,4},{6,7},{7,6},{8,9},{9,8},{10,11... | collective-permute-start | bytes 983048 | tf_op jit(solution)/shard_map/ppermute | solution.py:614
  14.4 20.9 %collective-permute-start.6 = (f32[2,5,64,128]{3,2,1,0:T(8,128)}, f32[2,5,64,128]{3,2,1,0:T(8,128)S(1)}, u32[]{:S(2)}, u32[]{:S(2)}) collective-permute-start(f32[2,5,64,128]{3,2,1,0:T(8,128)} %get-tuple-element.26.own), channel_id=1, source_target_pairs={{1,2},{2,1},{5,6},{6,5},{9,10},{10,9},{13,14},{14,13},{17,18},{18,... | collective-permute-start | bytes 983048 | tf_op jit(solution)/shard_map/ppermute | solution.py:614
  16.0 0.7 copy-start.4
  16.7 0.7 copy-start.5
  19.4 4.9 %collective-permute-start.2 = (f32[1,48,128]{2,1,0:T(8,128)}, f32[1,48,128]{2,1,0:T(8,128)S(1)}, u32[]{:S(2)}, u32[]{:S(2)}) collective-permute-start(f32[1,48,128]{2,1,0:T(8,128)} %bitcast.35), channel_id=1, source_target_pairs={{0,16},{4,20},{8,24},{12,28},{16,0},{20,4},{24,8},{28,12},{1,17},{... | collective-permute-start | bytes 73736 | tf_op jit(solution)/shard_map/ppermute | solution.py:175
  25.0 4.9 %collective-permute-start.3 = (f32[2,48,128]{2,1,0:T(8,128)S(1)}, f32[2,48,128]{2,1,0:T(8,128)S(1)}, u32[]{:S(2)}, u32[]{:S(2)}) collective-permute-start(f32[2,48,128]{2,1,0:T(8,128)S(1)} %pad_maximum_fusion.3), channel_id=1, source_target_pairs={{0,8},{4,12},{8,0},{12,4},{16,24},{20,28},{24,16},{28,20},{1,9},{5... | collective-permute-start | bytes 147464 | tf_op jit(solution)/shard_map/ppermute | solution.py:175
  30.7 3.9 %collective-permute-start.4 = (f32[48,128]{1,0:T(8,128)S(1)}, f32[48,128]{1,0:T(8,128)S(1)}, u32[]{:S(2)}, u32[]{:S(2)}) collective-permute-start(f32[48,128]{1,0:T(8,128)S(1)} %bitcast_select_fusion.2), channel_id=1, source_target_pairs={{0,4},{4,0},{8,12},{12,8},{16,20},{20,16},{24,28},{28,24},{1,5},{5... | collective-permute-start | bytes 73736 | tf_op jit(solution)/shard_map/ppermute | solution.py:196
  35.2 0.7 copy-start.2
  35.2 0.8 copy-start.3
  38.4 16.5 %collective-permute-start.7 = (f32[1,320,128]{2,1,0:T(8,128)}, f32[1,320,128]{2,1,0:T(8,128)S(1)}, u32[]{:S(2)}, u32[]{:S(2)}) collective-permute-start(f32[1,320,128]{2,1,0:T(8,128)} %bitcast.32), channel_id=1, source_target_pairs={{0,16},{4,20},{8,24},{12,28},{16,0},{20,4},{24,8},{28,12},{1,17},{... | collective-permute-start | bytes 491528 | tf_op jit(solution)/shard_map/ppermute | solution.py:175
  41.1 35.0 %collective-permute-start.10 = (f32[5,5,64,256]{3,2,1,0:T(8,128)}, f32[5,5,64,256]{3,2,1,0:T(8,128)S(1)}, u32[]{:S(2)}, u32[]{:S(2)}) collective-permute-start(f32[5,5,64,256]{3,2,1,0:T(8,128)} %get-tuple-element.30), channel_id=1, source_target_pairs={{1,2},{2,1},{5,6},{6,5},{9,10},{10,9},{13,14},{14,13},{17,18},{18,... | collective-permute-start | bytes 4915208 | tf_op jit(solution)/shard_map/ppermute | solution.py:614
  41.8 44.0 %collective-permute-start.17 = (f32[5,5,64,256]{3,2,1,0:T(8,128)}, f32[5,5,64,256]{3,2,1,0:T(8,128)}, u32[]{:S(2)}, u32[]{:S(2)}) collective-permute-start(f32[5,5,64,256]{3,2,1,0:T(8,128)} %get-tuple-element.33), channel_id=1, source_target_pairs={{0,1},{1,0},{2,3},{3,2},{4,5},{5,4},{6,7},{7,6},{8,9},{9,8},{10,11... | collective-permute-start | bytes 4915208 | tf_op jit(solution)/shard_map/ppermute | solution.py:614
  54.9 7.5 %copy-start = (f32[320,128]{1,0:T(8,128)S(1)}, f32[320,128]{1,0:T(8,128)}, u32[]{:S(2)}) copy-start(f32[320,128]{1,0:T(8,128)} %get-tuple-element.29.after) | copy-start | bytes 491524
  54.9 0.7 copy-start.1
  62.3 1.8 %collective-permute-start.8 = (f32[3,48,128]{2,1,0:T(8,128)S(1)}, f32[3,48,128]{2,1,0:T(8,128)S(1)}, u32[]{:S(2)}, u32[]{:S(2)}) collective-permute-start(f32[3,48,128]{2,1,0:T(8,128)S(1)} %constant_dynamic-slice_fusion.6), channel_id=1, source_target_pairs={{0,1},{1,0},{2,3},{3,2},{4,5},{5,4},{6,7},{7,6},{8,9},{9,8},{10,11... | collective-permute-start | bytes 221192 | tf_op jit(solution)/shard_map/ppermute | solution.py:589
  63.3 10.2 %collective-permute-start.15 = (f32[2,320,128]{2,1,0:T(8,128)S(1)}, f32[2,320,128]{2,1,0:T(8,128)S(1)}, u32[]{:S(2)}, u32[]{:S(2)}) collective-permute-start(f32[2,320,128]{2,1,0:T(8,128)S(1)} %pad_maximum_fusion.1), channel_id=1, source_target_pairs={{0,8},{4,12},{8,0},{12,4},{16,24},{20,28},{24,16},{28,20},{1,9},{5... | collective-permute-start | bytes 983048 | tf_op jit(solution)/shard_map/ppermute | solution.py:175
  65.1 10.9 %collective-permute-start.9 = (f32[3,24,128]{2,1,0:T(8,128)S(1)}, f32[3,24,128]{2,1,0:T(8,128)S(1)}, u32[]{:S(2)}, u32[]{:S(2)}) collective-permute-start(f32[3,24,128]{2,1,0:T(8,128)S(1)} %constant_dynamic-slice_fusion.5), channel_id=1, source_target_pairs={{0,2},{1,3},{2,0},{3,1},{4,6},{5,7},{6,4},{7,5},{8,10},{9,11},{10,... | collective-permute-start | bytes 110600 | tf_op jit(solution)/shard_map/ppermute | solution.py:589
  74.5 6.1 %collective-permute-start.16 = (f32[320,128]{1,0:T(8,128)S(1)}, f32[320,128]{1,0:T(8,128)S(1)}, u32[]{:S(2)}, u32[]{:S(2)}) collective-permute-start(f32[320,128]{1,0:T(8,128)S(1)} %bitcast_select_fusion), channel_id=1, source_target_pairs={{0,4},{4,0},{8,12},{12,8},{16,20},{20,16},{24,28},{28,24},{1,5},{5... | collective-permute-start | bytes 491528 | tf_op jit(solution)/shard_map/ppermute | solution.py:196
  76.0 9.8 %copy-start.9 = (f32[5,5,64,256]{3,2,1,0:T(8,128)}, f32[5,5,64,256]{3,2,1,0:T(8,128)S(1)}, u32[]{:S(2)}) copy-start(f32[5,5,64,256]{3,2,1,0:T(8,128)S(1)} %collective-permute-done.10.outer) | copy-start | bytes 4915204
  76.1 5.2 %collective-permute-start.11 = (f32[3,12,128]{2,1,0:T(8,128)S(1)}, f32[3,12,128]{2,1,0:T(8,128)S(1)}, u32[]{:S(2)}, u32[]{:S(2)}) collective-permute-start(f32[3,12,128]{2,1,0:T(8,128)S(1)} %constant_dynamic-slice_fusion.4), channel_id=1, source_target_pairs={{0,4},{4,0},{8,12},{12,8},{16,20},{20,16},{24,28},{28,24},{1,5},{5... | collective-permute-start | bytes 55304 | tf_op jit(solution)/shard_map/ppermute | solution.py:589
  81.3 4.5 %copy-start.6 = (f32[3,12,128]{2,1,0:T(8,128)}, f32[3,12,128]{2,1,0:T(8,128)S(1)}, u32[]{:S(2)}) copy-start(f32[3,12,128]{2,1,0:T(8,128)S(1)} %dynamic-slice_add_fusion.2.after) | copy-start | bytes 55300
  81.4 23.8 %collective-permute-start.12 = (f32[3,3,128]{2,1,0:T(4,128)S(1)}, f32[3,3,128]{2,1,0:T(4,128)S(1)}, u32[]{:S(2)}, u32[]{:S(2)}) collective-permute-start(f32[3,3,128]{2,1,0:T(4,128)S(1)} %get-tuple-element.42), channel_id=1, source_target_pairs={{0,16},{4,20},{8,24},{12,28},{16,0},{20,4},{24,8},{28,12},{1,17},{... | collective-permute-start | bytes 13832 | tf_op jit(solution)/shard_map/ppermute | solution.py:606
  81.6 23.6 %collective-permute-start.13 = (f32[3,3,128]{2,1,0:T(4,128)S(1)}, f32[3,3,128]{2,1,0:T(4,128)S(1)}, u32[]{:S(2)}, u32[]{:S(2)}) collective-permute-start(f32[3,3,128]{2,1,0:T(4,128)S(1)} %get-tuple-element.41), channel_id=1, source_target_pairs={{0,8},{4,12},{8,0},{12,4},{16,24},{20,28},{24,16},{28,20},{1,9},{5... | collective-permute-start | bytes 13832 | tf_op jit(solution)/shard_map/ppermute | solution.py:606
  82.4 22.8 %collective-permute-start.14 = (f32[3,3,128]{2,1,0:T(4,128)S(1)}, f32[3,3,128]{2,1,0:T(4,128)S(1)}, u32[]{:S(2)}, u32[]{:S(2)}) collective-permute-start(f32[3,3,128]{2,1,0:T(4,128)S(1)} %get-tuple-element.40), channel_id=1, source_target_pairs={{0,24},{4,28},{8,16},{12,20},{16,8},{20,12},{24,0},{28,4},{1,25},{... | collective-permute-start | bytes 13832 | tf_op jit(solution)/shard_map/ppermute | solution.py:606

commit v5 on v4

--- a/solution.py
+++ b/solution.py
@@ -14,7 +14,6 @@
 DEEP = 3
 NEAR = 8
 MIB = 1 << 20
-VMEM_BYTES = 60 * MIB
 ANY = pl.BlockSpec(memory_space=pl.ANY)
 VMEM = pl.BlockSpec(memory_space=pltpu.VMEM)
 SMEM = pl.BlockSpec(memory_space=pltpu.SMEM)
@@ -47,7 +46,7 @@
     return total
 
 
-def send_kernel(even, after, src, inv, tile, inner, outer):
+def send_kernel(even, src, inv, tile, inner, outer):
     spans = src.shape[1]
     for f, field in enumerate((src, inv)):
         tile[f] = chord_tile([(s, field[:, s]) for s in range(spans)])
@@ -61,7 +60,7 @@
                 out[2 * (DEEP - 1)] = src[:, s] * inv[:, s]
 
 
-def make_sends(even, after, source, inv_diag, depth, step):
+def make_sends(even, source, inv_diag, depth, step):
     nvar, spans, _, chord = source.shape
     field = pl.BlockSpec((step, spans, depth, chord), lambda v: (v, 0, 0, 0))
     halo = pl.BlockSpec((5, step, depth, chord), lambda v: (0, v, 0, 0))
@@ -69,19 +68,19 @@
     return pl.pallas_call(
         send_kernel,
         grid=(nvar // step,),
-        in_specs=[SMEM, ANY, field, field],
+        in_specs=[SMEM, field, field],
         out_specs=[pl.BlockSpec((2, step, depth, LANES), lambda v: (0, v, 0, 0)), halo, halo],
         out_shape=[
             jax.ShapeDtypeStruct((2, nvar, depth, LANES), f32),
             jax.ShapeDtypeStruct((5, nvar, depth, chord), f32),
             jax.ShapeDtypeStruct((5, nvar, depth, chord), f32),
         ],
-        compiler_params=pltpu.CompilerParams(vmem_limit_bytes=VMEM_BYTES),
+        compiler_params=pltpu.CompilerParams(vmem_limit_bytes=58 * MIB),
         cost_estimate=pl.CostEstimate(
             flops=0, bytes_accessed=16 * nvar * spans * depth * chord, transcendentals=0
         ),
         name=f"sends_{depth}",
-    )(even, after, source, inv_diag)
+    )(even, source, inv_diag)
 
 
 def merge(low, high, own, packet, full, depth):
@@ -124,7 +123,7 @@
     packet[rows : rows + 8, :] = cpl[...]
 
 
-def bulk_merge_kernel(even, own, inner, outer, after, a, b, packet, full, a_same, b_same):
+def bulk_merge_kernel(even, own, inner, outer, packet, full):
     depth = own.shape[2]
     up = jnp.full((1, 1, 1), even[0], jnp.int32) == 1
     low = [jnp.where(up, outer[f], inner[f]) for f in range(2)]
@@ -142,30 +141,27 @@
             jax.ShapeDtypeStruct((nvar * depth + 8, LANES), jnp.float32),
             jax.ShapeDtypeStruct(own.shape, jnp.float32),
         ],
-        compiler_params=pltpu.CompilerParams(vmem_limit_bytes=VMEM_BYTES),
+        compiler_params=pltpu.CompilerParams(vmem_limit_bytes=8 * MIB),
         name="near_merge",
     )(even, own, inner, outer, cpl)
 
 
-def bulk_merge(even, own, inner, outer, after, a, b):
+def bulk_merge(even, own, inner, outer):
     _, nvar, depth, _ = own.shape
     return pl.pallas_call(
         bulk_merge_kernel,
-        in_specs=[SMEM, VMEM, VMEM, VMEM, ANY, ANY, ANY],
-        out_specs=[VMEM, VMEM, ANY, ANY],
+        in_specs=[SMEM, VMEM, VMEM, VMEM],
+        out_specs=[VMEM, VMEM],
         out_shape=[
             jax.ShapeDtypeStruct((nvar * depth, LANES), jnp.float32),
             jax.ShapeDtypeStruct(own.shape, jnp.float32),
-            jax.ShapeDtypeStruct(a.shape, a.dtype),
-            jax.ShapeDtypeStruct(b.shape, b.dtype),
         ],
-        input_output_aliases={5: 2, 6: 3},
-        compiler_params=pltpu.CompilerParams(vmem_limit_bytes=VMEM_BYTES),
+        compiler_params=pltpu.CompilerParams(vmem_limit_bytes=12 * MIB),
         name="bulk_merge",
-    )(even, own, inner, outer, after, a, b)
-
-
-def route_ends(packet, me, low_of, high_of):
+    )(even, own, inner, outer)
+
+
+def route_ends(packet, me, low_of, high_of, after=None):
     count = lax.axis_size("blk")
     masks = [1 << b for b in range(count.bit_length() - 1)][::-1]
     left = lane_iota((1, LANES)) < HALF
@@ -173,7 +169,10 @@
     first = None
     for mask in masks[:-1]:
         other = lax.ppermute(held, "blk", [(i, i ^ mask) for i in range(count)])
-        first = other if first is None else first
+        if first is None:
+            first = other
+            if after is not None:
+                held, _ = lax.optimization_barrier((held, after))
         held = jnp.concatenate([held, other], 0)
 
     def place(block):
@@ -344,40 +343,59 @@
 
     groups = rows // 16
     lane = lane_iota((1, 1, LANES))
-    k = lax.broadcasted_iota(jnp.int32, (1, rows, 1), 1)
-
-    def products(p, s, first_row, last_row):
-        pieces = []
+    k = lax.broadcasted_iota(jnp.int32, (1, 16, 1), 1)
+    first_row, last_row = k == 0, k == 15
+
+    def products(p, s, g, first, last):
+        x = p[:, s, 16 * g : 16 * g + 16, :].reshape(nvar * 16, chord)
+        top = x.astype(jnp.bfloat16)
+        rest = (x - top.astype(jnp.float32)).astype(jnp.bfloat16)
+        none = jnp.zeros((16, chord), jnp.bfloat16)
+        parts = jnp.concatenate([top, rest, top, none], 0)
+        y = jnp.dot(wide[first:last, :], parts, preferred_element_type=jnp.float32)
+        return y.reshape((last - first) // 16, 16, chord)
+
+    step = 16 * nvar
+
+    def one_layer(p, after, n, s):
+        below, waiting = None, None
         for g in range(groups):
-            x = p[:, s, 16 * g : 16 * g + 16, :].reshape(nvar * 16, chord)
-            top = x.astype(jnp.bfloat16)
-            rest = (x - top.astype(jnp.float32)).astype(jnp.bfloat16)
-            none = jnp.zeros((16, chord), jnp.bfloat16)
-            parts = jnp.concatenate([top, rest, top, none], 0)
-            y = jnp.dot(wide[first_row:last_row, :], parts, preferred_element_type=jnp.float32)
-            pieces.append(y.reshape((last_row - first_row) // 16, 16, chord))
-        return jnp.concatenate(pieces, 1) if groups > 1 else pieces[0]
-
-    def along(every, n, s):
-        total = jnp.where(k == 0, 0.0, pltpu.roll(every[2 * nvar : 3 * nvar], 1, 1))
-        total += jnp.where(k == rows - 1, 0.0, pltpu.roll(every[3 * nvar : 4 * nvar], rows - 1, 1))
-        face = faces[n]
-        at_low = pltpu.roll(face, lax.rem(LANES + 10 - COLS * s, LANES), 2)
-        at_high = pltpu.roll(face, lax.rem(LANES + 73 - COLS * s, LANES), 2)
-        a = pltpu.roll(every[4 * nvar : 5 * nvar, :, :LANES], 1, 2)
-        b = pltpu.roll(every[4 * nvar : 5 * nvar, :, LANES:], 1, 2)
-        c = pltpu.roll(every[5 * nvar :, :, :LANES], LANES - 1, 2)
-        d = pltpu.roll(every[5 * nvar :, :, LANES:], LANES - 1, 2)
-        left = jnp.where(lane == 0, at_low, a) + jnp.where(lane == LANES - 1, d, c)
-        right = jnp.where(lane == 0, a, b) + jnp.where(lane == LANES - 1, at_high, d)
-        return total + jnp.concatenate([left, right], 2)
-
-    step = 16 * nvar
+            at = slice(16 * g, 16 * g + 16)
+            every = products(p, s, g, 0, 6 * step)
+            span_low, span_high, normal_low, normal_high, chord_low, chord_high = [
+                every[d * nvar : (d + 1) * nvar] for d in range(6)
+            ]
+            after[:, s - 1, at] = inv[:, s - 1, at] * (before[:, at] + span_high)
+            total = src[:, s, at] + coming[:, at]
+            coming[:, at] = span_low
+            total += jnp.where(
+                first_row, 0.0 if below is None else below, pltpu.roll(normal_low, 1, 1)
+            )
+            below = normal_low[:, 15:16]
+            total += jnp.where(last_row, 0.0, pltpu.roll(normal_high, 15, 1))
+            face = faces[n, :, at]
+            at_low = pltpu.roll(face, lax.rem(LANES + 10 - COLS * s, LANES), 2)
+            at_high = pltpu.roll(face, lax.rem(LANES + 73 - COLS * s, LANES), 2)
+            a = pltpu.roll(chord_low[..., :LANES], 1, 2)
+            b = pltpu.roll(chord_low[..., LANES:], 1, 2)
+            c = pltpu.roll(chord_high[..., :LANES], LANES - 1, 2)
+            d = pltpu.roll(chord_high[..., LANES:], LANES - 1, 2)
+            left = jnp.where(lane == 0, at_low, a) + jnp.where(lane == LANES - 1, d, c)
+            right = jnp.where(lane == 0, a, b) + jnp.where(lane == LANES - 1, at_high, d)
+            total += jnp.concatenate([left, right], 2)
+            if g > 0:
+                before[:, 16 * g - 16 : 16 * g] = waiting + jnp.where(
+                    last_row, normal_high[:, 0:1], 0.0
+                )
+            waiting = total
+        before[:, rows - 16 : rows] = waiting
+
     for n in range(SWEEPS):
         p, after = (pa, pb) if n % 2 == 0 else (pb, pa)
         if n == 0:
             arrive(0, True)
-        coming[...] = products(p, n, 0, step)
+        for g in range(groups):
+            coming[:, 16 * g : 16 * g + 16] = products(p, n, g, 0, step)
         full = layers - 2 - 2 * n
         turn = 2 if groups > 1 else full
 
@@ -386,15 +404,8 @@
             if n == 0:
                 for j in range(turn):
                     arrive(s0 + j)
-            every = [products(p, s0 + j, 0, 6 * step) for j in range(turn)]
-            arriving, waiting = coming[...], before[...]
             for j in range(turn):
-                s, now = s0 + j, every[j]
-                after[:, s - 1] = inv[:, s - 1] * (waiting + now[nvar : 2 * nvar])
-                waiting = src[:, s] + arriving + along(now, n, s)
-                arriving = now[:nvar]
-            before[...] = waiting
-            coming[...] = arriving
+                one_layer(p, after, n, s0 + j)
             if n == SWEEPS - 1 and out is not None:
                 for j in range(turn - 1):
                     leave(s0 + j, True)
@@ -405,11 +416,17 @@
 
             return 0
 
-        lax.fori_loop(0, full // turn, several, 0)
+        if turn == full:
+            several(0, 0)
+        else:
+            lax.fori_loop(0, full // turn, several, 0)
         last = layers - 1 - n
         if n == 0:
             arrive(last, True)
-        after[:, last - 1] = inv[:, last - 1] * (before[...] + products(p, last, step, 2 * step))
+        for g in range(groups):
+            at = slice(16 * g, 16 * g + 16)
+            span_high = products(p, last, g, step, 2 * step)
+            after[:, last - 1, at] = inv[:, last - 1, at] * (before[:, at] + span_high)
     if out is not None:
         leave(DEEP + spans - 1, True)
         for at in range(DEEP, DEEP + spans):
@@ -438,7 +455,7 @@
 
 
 def bulk_kernel(
-    depth, even, couplings, full, given, mine, theirs, src_in, inv_in, inner, outer, after, out, *scratch
+    depth, even, couplings, full, given, mine, theirs, src_in, inv_in, inner, outer, out, *scratch
 ):
     run_sweeps(
         depth, even, couplings, full, given, mine, theirs, src_in, inv_in, inner, outer, scratch, out
@@ -454,25 +471,25 @@
     return pl.BlockSpec(a.shape, lambda i: (0,) * a.ndim)
 
 
-def bulk_sweeps(even, couplings, full, given, mine, theirs, source, inv_diag, inner, outer, after):
+def bulk_sweeps(even, couplings, full, given, mine, theirs, source, inv_diag, inner, outer):
     nvar, spans, depth, chord = source.shape
     return pl.pallas_call(
         functools.partial(bulk_kernel, depth),
         grid=(1,),
         in_specs=[SMEM, whole(couplings), whole(full), whole(given), coupling_rows(mine.shape)]
-        + [coupling_rows(theirs.shape), ANY, ANY, ANY, ANY, ANY],
+        + [coupling_rows(theirs.shape), ANY, ANY, ANY, ANY],
         out_specs=ANY,
         out_shape=jax.ShapeDtypeStruct(source.shape, jnp.float32),
         scratch_shapes=sweep_scratch(nvar, spans, chord, depth),
-        compiler_params=pltpu.CompilerParams(vmem_limit_bytes=VMEM_BYTES),
+        compiler_params=pltpu.CompilerParams(vmem_limit_bytes=28 * MIB),
         cost_estimate=pl.CostEstimate(
             flops=2 * 40 * 480 * 256 * 256 * (depth // 16), bytes_accessed=16 * MIB, transcendentals=0
         ),
         name="bulk_sweeps",
-    )(even, couplings, full, given, mine, theirs, source, inv_diag, inner, outer, after)
-
-
-def near_kernel(even, couplings, full, given, mine, theirs, src_in, inv_in, inner, outer, jac, after, sens, *scratch):
+    )(even, couplings, full, given, mine, theirs, source, inv_diag, inner, outer)
+
+
+def near_kernel(even, couplings, full, given, mine, theirs, src_in, inv_in, inner, outer, jac, sens, *scratch):
     adjoint = run_sweeps(
         NEAR, even, couplings, full, given, mine, theirs, src_in, inv_in, inner, outer, scratch
     )
@@ -492,21 +509,21 @@
         sens[c] = total
 
 
-def near_sweeps(even, couplings, full, given, packet, source, inv_diag, inner, outer, jac, after):
+def near_sweeps(even, couplings, full, given, packet, source, inv_diag, inner, outer, jac):
     nvar, spans, _, chord = source.shape
     shape = (jac.shape[0], spans, chord)
     return pl.pallas_call(
         near_kernel,
         grid=(1,),
         in_specs=[SMEM, whole(couplings), whole(full), whole(given), coupling_rows(packet.shape)]
-        + [coupling_rows(given.shape), ANY, ANY, ANY, ANY, whole(jac), ANY],
+        + [coupling_rows(given.shape), ANY, ANY, ANY, ANY, whole(jac)],
         out_specs=pl.BlockSpec(shape, lambda i: (0, 0, 0)),
         out_shape=jax.ShapeDtypeStruct(shape, jnp.float32),
         scratch_shapes=sweep_scratch(nvar, spans, chord, NEAR),
-        compiler_params=pltpu.CompilerParams(vmem_limit_bytes=VMEM_BYTES),
+        compiler_params=pltpu.CompilerParams(vmem_limit_bytes=16 * MIB),
         cost_estimate=pl.CostEstimate(flops=5 * 10**9, bytes_accessed=4 * MIB, transcendentals=0),
         name="near_sweeps",
-    )(even, couplings, full, given, packet, given, source, inv_diag, inner, outer, jac, after)
+    )(even, couplings, full, given, packet, given, source, inv_diag, inner, outer, jac)
 
 
 def point_indices(bits, ids, hi_index, lo_index):
@@ -522,7 +539,7 @@
     lo_index[...] = ((device & 1) << 7) + (point & 127)
 
 
-def scatter_kernel(bits, sens, weight, ids, after, out, hi_index, lo_index):
+def scatter_kernel(bits, sens, weight, ids, out, hi_index, lo_index):
     point_indices(bits, ids, hi_index, lo_index)
     dims, spans, chord = sens.shape
     slots = weight.shape[0]
@@ -558,20 +575,20 @@
     lax.fori_loop(0, slots, one, 0)
 
 
-def scatter_points(sens, weight, ids, after, n_dev):
+def scatter_points(sens, weight, ids, n_dev):
     tall = -(-(n_dev // 2 * 3) // 16) * 16
     bits = (n_dev // 2).bit_length() - 1
     shape = (sens.shape[0], tall, 2 * LANES)
     return pl.pallas_call(
         functools.partial(scatter_kernel, bits),
-        in_specs=[VMEM, VMEM, VMEM, ANY],
+        in_specs=[VMEM, VMEM, VMEM],
         out_specs=VMEM,
         out_shape=jax.ShapeDtypeStruct(shape, jnp.float32),
         scratch_shapes=[pltpu.VMEM(ids.shape, jnp.int32), pltpu.VMEM(ids.shape, jnp.int32)],
-        compiler_params=pltpu.CompilerParams(vmem_limit_bytes=VMEM_BYTES),
+        compiler_params=pltpu.CompilerParams(vmem_limit_bytes=12 * MIB),
         cost_estimate=pl.CostEstimate(flops=4 * 10**9, bytes_accessed=MIB, transcendentals=0),
         name="scatter_points",
-    )(sens, weight, ids, after)
+    )(sens, weight, ids)
 
 
 def halve_points(partial, after, n_dev):
@@ -607,6 +624,10 @@
     return parts
 
 
+def ordered(x, *after):
+    return lax.optimization_barrier((x, *after))[0]
+
+
 def swap_spans(inner, outer):
     count = lax.axis_size("sub")
     pairs = [(i, i ^ 1) for i in range(count)]
@@ -624,26 +645,26 @@
     cpl = jnp.concatenate([flat, flat], 1)
     low_of, high_of = face_map[:, 0], face_map[:, 1]
 
-    own, inner, outer = make_sends(even, even, source, inv_diag, NEAR, nvar)
+    own, inner, outer = make_sends(even, source, inv_diag, NEAR, nvar)
     inner, outer = swap_spans(inner, outer)
     packet, full = near_merge(even, own, inner, outer, cpl)
-    given, _ = route_ends(packet, me, low_of, high_of)
-
-    bulk_own, bulk_inner, bulk_outer = make_sends(even, own, source, inv_diag, source.shape[2], 1)
+
+    depth = source.shape[2]
+    bulk_own, bulk_inner, bulk_outer = make_sends(ordered(even, inner), source, inv_diag, depth, 1)
     tiles = swap_spans(bulk_own, bulk_own)
-    bulk_packet, bulk_full, bulk_inner, bulk_outer = bulk_merge(
-        even, bulk_own, *tiles, packet, bulk_inner, bulk_outer
+    bulk_packet, bulk_full = bulk_merge(even, bulk_own, *tiles)
+    given, _ = route_ends(packet, me, low_of, high_of, bulk_packet)
+    bulk_inner, bulk_outer = swap_spans(
+        ordered(bulk_inner, bulk_packet), ordered(bulk_outer, bulk_packet)
     )
-    bulk_inner, bulk_outer = swap_spans(bulk_inner, bulk_outer)
     bulk_given, bulk_first = route_ends(bulk_packet, me, low_of, high_of)
 
-    sens = near_sweeps(
-        even, couplings, full, given, packet, source, inv_diag, inner, outer, wall_jac, bulk_packet
-    )
-    partial = scatter_points(sens, ffd_weight, cp_ids, bulk_first, n_dev)
+    sens = near_sweeps(even, couplings, full, given, packet, source, inv_diag, inner, outer, wall_jac)
+    partial = scatter_points(ordered(sens, bulk_first), ffd_weight, cp_ids, n_dev)
     partial, bulk_outer = halve_points(partial, bulk_outer, n_dev)
     adjoint = bulk_sweeps(
-        even, couplings, bulk_full, bulk_given, packet, given, source, inv_diag, bulk_inner, bulk_outer, partial
+        ordered(even, partial), couplings, bulk_full, bulk_given, packet, given, source, inv_diag,
+        bulk_inner, bulk_outer,
     )
     parts, adjoint = lax.optimization_barrier((quarter_points(partial), adjoint))
     total = (parts[0] + parts[1]) + (parts[2] + parts[3])

time: 107 us -> 95.4 us (0.89)
  Pallas kernels: 47.1 us -> 39.8 us
  other arithmetic: 6.31 us -> 0.28 us
  local copies, waits for them, and re-layouts: 5.98 us -> 8.62 us
  waiting for transfers between devices: 15.9 us -> 14.6 us
  starting transfers between devices: 27 us -> 28.2 us
    unnamed x21 -> x33, local copies, waits for them, and re-layouts: 3.44 us -> 7.55 us
    concatenate x4 -> x3, other arithmetic: 3.39 us -> 0.09 us  [route_ends(): held = jnp.concatenate([held, other], 0)]
    pallas_call x1, Pallas kernels: 8.85 us -> 6.83 us  [near_sweeps(): pl.pallas_call(near_kernel, grid=(1,), in_specs=[SMEM, whole(couplings),...]
    pallas_call x3, Pallas kernels: 11 us -> 9.33 us  [the longest x2 8.83 us: make_sends(): pl.pallas_call(send_kernel, grid=(nvar // step,), in_specs=[SMEM, field,...]
    pallas_call x1, Pallas kernels: 5.89 us -> 4.2 us  [scatter_points(): pl.pallas_call(functools.partial(scatter_kernel, bits), in_specs=[VMEM, V...]
    ppermute x2, waiting for transfers between devices: 5.56 us -> 3.93 us  [route_ends(): lax.ppermute(chosen(me ^ last), 'blk', [(i, i ^ last) for i in range(coun...]
    ppermute x4, starting transfers between devices: 7.78 us -> 9.1 us  [route_ends(): other = lax.ppermute(held, 'blk', [(i, i ^ mask) for i in range(count)])]
    select_n x2, other arithmetic: 1.29 us -> 0.04 us  [route_ends(): jnp.where(jnp.where(left, low_here, high_here), chosen(me), given)]
  transfers between devices with their start and end apart: 18 -> 18, of which waited for: 4 -> 4; matrix products, arithmetic and copies ran while one was open for 8% -> 1% of each run, Pallas kernels for 40% -> 40%
where the time goes in v5:
time: 95.4 us; the launch traced here: 94.9 us
  Pallas kernels  39.8 us (42%)
  starting transfers between devices  28.2 us (30%)
  waiting for transfers between devices  14.6 us (15%)
  local copies, waits for them, and re-layouts  8.62 us (9%)
  between operations  3.42 us (4%)
    pallas_call x1, Pallas kernels, bulk_sweeps(): pl.pallas_call(functools.partial(bulk_kernel, depth), grid=(1,), in_specs...  18.2 us
    ppermute x4, waiting for transfers between devices, route_ends(): other = lax.ppermute(held, 'blk', [(i, i ^ mask) for i in range(count)])  10.4 us
    ppermute x4, starting transfers between devices, route_ends(): other = lax.ppermute(held, 'blk', [(i, i ^ mask) for i in range(count)])  9.1 us
    pallas_call x2, Pallas kernels, make_sends(): pl.pallas_call(send_kernel, grid=(nvar // step,), in_specs=[SMEM, field,...  8.83 us
    unnamed x33, local copies, waits for them, and re-layouts  7.55 us
    ppermute x3, starting transfers between devices, swap_spans(): lax.ppermute(inner, 'sub', pairs)  7.38 us
    pallas_call x1, Pallas kernels, near_sweeps(): pl.pallas_call(near_kernel, grid=(1,), in_specs=[SMEM, whole(couplings),...  6.83 us
    ppermute x3, starting transfers between devices, quarter_points(): lax.ppermute(quarter(me ^ mask), 'blk', [(i, i ^ mask) for i in range(cou...  4.45 us
  transfers between devices with their start and end apart: 18, of which 4 were waited for; matrix products, arithmetic and copies ran while one was open for 1% of the time, Pallas kernels for 40%

profile of v5, /device:TPU:0, one launch (start us, length us, event | category | flops | bytes accessed | tf_op | source)
XLA Modules:
  0.0 94.9 jit_solution(16253671178780022075)
XLA Ops:
  0.6 2.0 %sends_8.1 = (f32[2,5,8,128]{3,2,1,0:T(8,128)}, f32[5,5,8,256]{3,2,1,0:T(8,128)}, f32[5,5,8,256]{3,2,1,0:T(8,128)}) custom-call(s32[1]{0:T(128)} %bitcast.even, f32[5,8,64,256]{3,2,1,0:T(8,128)} %src_in.3, f32[5,8,64,256]{3,2,1,0:T(8,128)} %inv_in.3), custom_call_target="tpu_custom_call" | custom-call | bytes 1310720 | tf_op jit(solution)/shard_map/sends_8/pallas_call | solution.py:68
  2.7 0.5 collective-permute-start
  3.1 1.5 %collective-permute-start.1 = (f32[5,5,8,256]{3,2,1,0:T(8,128)}, f32[5,5,8,256]{3,2,1,0:T(8,128)}, u32[]{:S(2)}, u32[]{:S(2)}) collective-permute-start(f32[5,5,8,256]{3,2,1,0:T(8,128)} %get-tuple-element.27), channel_id=1, source_target_pairs={{1,2},{2,1},{5,6},{6,5},{9,10},{10,9},{13,14},{14,13},{17,18},{18,... | collective-permute-start | bytes 614408 | tf_op jit(solution)/shard_map/ppermute | solution.py:635
  4.6 0.7 copy-done.4
  5.3 6.8 %sends_64.1 = (f32[2,5,64,128]{3,2,1,0:T(8,128)}, f32[5,5,64,256]{3,2,1,0:T(8,128)}, f32[5,5,64,256]{3,2,1,0:T(8,128)}) custom-call(s32[1]{0:T(128)} %bitcast.even, f32[5,8,64,256]{3,2,1,0:T(8,128)} %src_in.3, f32[5,8,64,256]{3,2,1,0:T(8,128)} %inv_in.3), custom_call_target="tpu_custom_call" | custom-call | bytes 10485760 | tf_op jit(solution)/shard_map/sends_64/pallas_call | solution.py:68
  12.1 0.7 collective-permute-start.3
  12.8 4.5 %collective-permute-start.2 = (f32[2,5,64,128]{3,2,1,0:T(8,128)}, f32[2,5,64,128]{3,2,1,0:T(8,128)S(1)}, u32[]{:S(2)}, u32[]{:S(2)}) collective-permute-start(f32[2,5,64,128]{3,2,1,0:T(8,128)} %get-tuple-element.31.own), channel_id=1, source_target_pairs={{0,1},{1,0},{2,3},{3,2},{4,5},{5,4},{6,7},{7,6},{8,9},{9,8},{10,11... | collective-permute-start | bytes 983048 | tf_op jit(solution)/shard_map/ppermute | solution.py:635
  17.3 0.7 constant_dynamic-slice_fusion.9
  20.4 0.1 copy.13
  20.6 0.1 reshape_squeeze.7
  20.7 0.1 reshape.30
  20.8 0.1 pad_maximum_fusion.3.cpl
  20.9 0.0 collective-permute-done.1.outer
  20.9 0.9 copy-done.5
  21.8 1.2 %near_merge.1 = (f32[48,128]{1,0:T(8,128)S(1)}, f32[2,5,8,128]{3,2,1,0:T(8,128)S(1)}) custom-call(s32[1]{0:T(128)} %bitcast.even, f32[2,5,8,128]{3,2,1,0:T(8,128)S(1)} %copy-done.7, f32[5,5,8,256]{3,2,1,0:T(8,128)S(1)} %copy-done.5, f32[5,5,8,256]{3,2,1,0:T(8,128)} %collective-permute-done.1.outer, f32[8,128]{1,0:T(8,128)S(1)} %pad_maximum_fusion.3.cpl), custom_call_target="tpu_custom_call" | custom-call | tf_op jit(solution)/shard_map/near_merge/pallas_call | solution.py:136
  23.0 3.2 %collective-permute-start.4 = (f32[1,48,128]{2,1,0:T(8,128)S(1)}, f32[1,48,128]{2,1,0:T(8,128)S(1)}, u32[]{:S(2)}, u32[]{:S(2)}) collective-permute-start(f32[1,48,128]{2,1,0:T(8,128)S(1)} %bitcast.35), channel_id=1, source_target_pairs={{0,16},{4,20},{8,24},{12,28},{16,0},{20,4},{24,8},{28,12},{1,17},{... | collective-permute-start | bytes 73736 | tf_op jit(solution)/shard_map/ppermute | solution.py:171
  26.3 0.0 collective-permute-done.3.outer
  26.3 0.0 collective-permute-done.2.inner
  26.3 1.0 %copy-done.3 = f32[2,5,64,128]{3,2,1,0:T(8,128)S(1)} copy-done((f32[2,5,64,128]{3,2,1,0:T(8,128)S(1)}, f32[2,5,64,128]{3,2,1,0:T(8,128)}, u32[]{:S(2)}) %copy-start.3) | copy-done | bytes 327704
  27.3 0.5 bulk_merge.1
  27.8 0.7 copy-done.8
  28.5 1.6 %collective-permute-start.5 = (f32[2,48,128]{2,1,0:T(8,128)S(1)}, f32[2,48,128]{2,1,0:T(8,128)S(1)}, u32[]{:S(2)}, u32[]{:S(2)}) collective-permute-start(f32[2,48,128]{2,1,0:T(8,128)S(1)} %pad_maximum_fusion.2), channel_id=1, source_target_pairs={{0,8},{4,12},{8,0},{12,4},{16,24},{20,28},{24,16},{28,20},{1,9},{5... | collective-permute-start | bytes 147464 | tf_op jit(solution)/shard_map/ppermute | solution.py:171
  30.2 2.5 %collective-permute-done.5 = f32[2,48,128]{2,1,0:T(8,128)S(1)} collective-permute-done((f32[2,48,128]{2,1,0:T(8,128)S(1)}, f32[2,48,128]{2,1,0:T(8,128)S(1)}, u32[]{:S(2)}, u32[]{:S(2)}) %collective-permute-start.5) | collective-permute-done | bytes 49184 | tf_op jit(solution)/shard_map/ppermute | solution.py:171
  32.7 1.7 %collective-permute-start.6 = (f32[48,128]{1,0:T(8,128)S(1)}, f32[48,128]{1,0:T(8,128)S(1)}, u32[]{:S(2)}, u32[]{:S(2)}) collective-permute-start(f32[48,128]{1,0:T(8,128)S(1)} %bitcast_select_fusion.2), channel_id=1, source_target_pairs={{0,4},{4,0},{8,12},{12,8},{16,20},{20,16},{24,28},{28,24},{1,5},{5... | collective-permute-start | bytes 73736 | tf_op jit(solution)/shard_map/ppermute | solution.py:195
  34.4 2.4 %collective-permute-start.7 = (f32[1,320,128]{2,1,0:T(8,128)S(1)}, f32[1,320,128]{2,1,0:T(8,128)S(1)}, u32[]{:S(2)}, u32[]{:S(2)}) collective-permute-start(f32[1,320,128]{2,1,0:T(8,128)S(1)} %bitcast.32), channel_id=1, source_target_pairs={{0,16},{4,20},{8,24},{12,28},{16,0},{20,4},{24,8},{28,12},{1,17},{... | collective-permute-start | bytes 491528 | tf_op jit(solution)/shard_map/ppermute | solution.py:171
  36.8 0.8 collective-permute-start.10
  37.6 2.4 %collective-permute-start.17 = (f32[5,5,64,256]{3,2,1,0:T(8,128)}, f32[5,5,64,256]{3,2,1,0:T(8,128)S(1)}, u32[]{:S(2)}, u32[]{:S(2)}) collective-permute-start(f32[5,5,64,256]{3,2,1,0:T(8,128)} %get-tuple-element.41), channel_id=1, source_target_pairs={{0,1},{1,0},{2,3},{3,2},{4,5},{5,4},{6,7},{7,6},{8,9},{9,8},{10,11... | collective-permute-start | bytes 4915208 | tf_op jit(solution)/shard_map/ppermute | solution.py:635
  40.0 0.0 copy-start.1
  40.0 1.7 %copy-done.1 = f32[5,8,64,256]{3,2,1,0:T(8,128)S(1)} copy-done((f32[5,8,64,256]{3,2,1,0:T(8,128)S(1)}, f32[5,8,64,256]{3,2,1,0:T(8,128)}, u32[]{:S(2)}) %copy-start.1) | copy-done | bytes 2621464
  41.7 0.9 copy-done.6
  42.7 0.9 copy-done.10
  43.6 6.8 %near_sweeps.1.sens = f32[3,8,256]{2,1,0:T(8,128)S(1)} custom-call(s32[1]{0:T(128)} %bitcast.even, f32[32,128]{1,0:T(8,128)S(1)} %pad.8.couplings, f32[2,5,8,128]{3,2,1,0:T(8,128)S(1)} %get-tuple-element.28.full, f32[48,128]{1,0:T(8,128)S(1)} %fusion.1.given.theirs, f32[48,128]{1,0:T(8,128)S(1)} %get-tuple-element.29.mine, ...), custom_call_target="tpu_custom_call" | custom-call | flops 5000000000 | bytes 4194304 | tf_op jit(solution)/shard_map/near_sweeps/pallas_call | solution.py:515
  50.5 4.2 %scatter_points.1 = f32[3,48,256]{2,1,0:T(8,128)S(1)} custom-call(f32[3,8,256]{2,1,0:T(8,128)S(1)} %near_sweeps.1.sens, f32[8,8,256]{2,1,0:T(8,128)S(1)} %copy-done.11, s32[8,8,256]{2,1,0:T(8,128)S(1)} %copy-done.12), custom_call_target="tpu_custom_call" | custom-call | flops 4000000000 | bytes 1048576 | tf_op jit(solution)/shard_map/scatter_points/pallas_call | solution.py:582
  54.7 0.1 collective-permute-start.8
  54.8 0.0 copy-start.2
  54.8 1.8 %collective-permute-start.15 = (f32[2,320,128]{2,1,0:T(8,128)S(1)}, f32[2,320,128]{2,1,0:T(8,128)S(1)}, u32[]{:S(2)}, u32[]{:S(2)}) collective-permute-start(f32[2,320,128]{2,1,0:T(8,128)S(1)} %pad_maximum_fusion.1), channel_id=1, source_target_pairs={{0,8},{4,12},{8,0},{12,4},{16,24},{20,28},{24,16},{28,20},{1,9},{5... | collective-permute-start | bytes 983048 | tf_op jit(solution)/shard_map/ppermute | solution.py:171
  56.7 0.4 collective-permute-start.9
  57.1 7.9 %collective-permute-done.15 = f32[2,320,128]{2,1,0:T(8,128)S(1)} collective-permute-done((f32[2,320,128]{2,1,0:T(8,128)S(1)}, f32[2,320,128]{2,1,0:T(8,128)S(1)}, u32[]{:S(2)}, u32[]{:S(2)}) %collective-permute-start.15) | collective-permute-done | bytes 327712 | tf_op jit(solution)/shard_map/ppermute | solution.py:171
  65.0 0.1 pad_maximum_fusion
  65.1 0.6 collective-permute-start.16
  65.8 1.6 %collective-permute-start.11 = (f32[3,12,128]{2,1,0:T(8,128)S(1)}, f32[3,12,128]{2,1,0:T(8,128)S(1)}, u32[]{:S(2)}, u32[]{:S(2)}) collective-permute-start(f32[3,12,128]{2,1,0:T(8,128)S(1)} %constant_dynamic-slice_fusion.4), channel_id=1, source_target_pairs={{0,4},{4,0},{8,12},{12,8},{16,20},{20,16},{24,28},{28,24},{1,5},{5... | collective-permute-start | bytes 55304 | tf_op jit(solution)/shard_map/ppermute | solution.py:606
  67.3 3.9 %collective-permute-done.16 = f32[320,128]{1,0:T(8,128)S(1)} collective-permute-done((f32[320,128]{1,0:T(8,128)S(1)}, f32[320,128]{1,0:T(8,128)S(1)}, u32[]{:S(2)}, u32[]{:S(2)}) %collective-permute-start.16) | collective-permute-done | bytes 163872 | tf_op jit(solution)/shard_map/ppermute | solution.py:195
  71.3 0.2 collective-permute-done.11
  71.6 1.6 %collective-permute-start.14 = (f32[3,3,128]{2,1,0:T(4,128)S(1)}, f32[3,3,128]{2,1,0:T(4,128)S(1)}, u32[]{:S(2)}, u32[]{:S(2)}) collective-permute-start(f32[3,3,128]{2,1,0:T(4,128)S(1)} %get-tuple-element.48), channel_id=1, source_target_pairs={{0,24},{4,28},{8,16},{12,20},{16,8},{20,12},{24,0},{28,4},{1,25},{... | collective-permute-start | bytes 13832 | tf_op jit(solution)/shard_map/ppermute | solution.py:623
  73.1 0.3 collective-permute-start.13
  73.4 2.6 %collective-permute-start.12 = (f32[3,3,128]{2,1,0:T(4,128)S(1)}, f32[3,3,128]{2,1,0:T(4,128)S(1)}, u32[]{:S(2)}, u32[]{:S(2)}) collective-permute-start(f32[3,3,128]{2,1,0:T(4,128)S(1)} %get-tuple-element.50), channel_id=1, source_target_pairs={{0,16},{4,20},{8,24},{12,28},{16,0},{20,4},{24,8},{28,12},{1,17},{... | collective-permute-start | bytes 13832 | tf_op jit(solution)/shard_map/ppermute | solution.py:623
  76.0 18.2 %bulk_sweeps.1 = f32[5,8,64,256]{3,2,1,0:T(8,128)} custom-call(s32[1]{0:T(128)} %bitcast.even, f32[32,128]{1,0:T(8,128)S(1)} %pad.8.couplings, f32[2,5,64,128]{3,2,1,0:T(8,128)S(1)} %copy-done.9, f32[320,128]{1,0:T(8,128)S(1)} %fusion.given, f32[48,128]{1,0:T(8,128)S(1)} %get-tuple-element.29.mine, f32[48,128]{1,0:T(8,128)S(1)} %fusion.1.given.theirs, ...), custom_call_target="tpu_custom_call" | custom-call | flops 10066329600 | bytes 16777216 | tf_op jit(solution)/shard_map/bulk_sweeps/pallas_call | solution.py:476
  94.3 0.6 copy.17
  (55 shorter events, 0.3 us)
Async XLA Ops:
  2.7 1.9 %collective-permute-start = (f32[5,5,8,256]{3,2,1,0:T(8,128)}, f32[5,5,8,256]{3,2,1,0:T(8,128)S(1)}, u32[]{:S(2)}, u32[]{:S(2)}) collective-permute-start(f32[5,5,8,256]{3,2,1,0:T(8,128)} %get-tuple-element.26), channel_id=1, source_target_pairs={{0,1},{1,0},{2,3},{3,2},{4,5},{5,4},{6,7},{7,6},{8,9},{9,8},{10,11... | collective-permute-start | bytes 614408 | tf_op jit(solution)/shard_map/ppermute | solution.py:635
  3.1 14.2 %copy-start.14 = (s32[8,2]{0,1:T(2,128)S(1)}, s32[8,2]{0,1:T(2,128)}, u32[]{:S(2)}) copy-start(s32[8,2]{0,1:T(2,128)} %param.10) | copy-start | bytes 196
  3.1 17.3 %copy-start.13 = (f32[1,6,5,5]{1,0,3,2:T(1,128)S(1)}, f32[1,6,5,5]{1,0,3,2:T(1,128)}, u32[]{:S(2)}) copy-start(f32[1,6,5,5]{1,0,3,2:T(1,128)} %param.9) | copy-start | bytes 1804
  3.1 17.7 %copy-start.7 = (f32[2,5,8,128]{3,2,1,0:T(8,128)S(1)}, f32[2,5,8,128]{3,2,1,0:T(8,128)}, u32[]{:S(2)}) copy-start(f32[2,5,8,128]{3,2,1,0:T(8,128)} %get-tuple-element.25.own) | copy-start | bytes 122884
  3.1 17.7 %collective-permute-start.1 = (f32[5,5,8,256]{3,2,1,0:T(8,128)}, f32[5,5,8,256]{3,2,1,0:T(8,128)}, u32[]{:S(2)}, u32[]{:S(2)}) collective-permute-start(f32[5,5,8,256]{3,2,1,0:T(8,128)} %get-tuple-element.27), channel_id=1, source_target_pairs={{1,2},{2,1},{5,6},{6,5},{9,10},{10,9},{13,14},{14,13},{17,18},{18,... | collective-permute-start | bytes 614408 | tf_op jit(solution)/shard_map/ppermute | solution.py:635
  4.6 0.7 copy-start.4
  5.3 34.7 %copy-start = (f32[5,8,64,256]{3,2,1,0:T(8,128)S(1)}, f32[5,8,64,256]{3,2,1,0:T(8,128)}, u32[]{:S(2)}) copy-start(f32[5,8,64,256]{3,2,1,0:T(8,128)} %src_in.3) | copy-start | bytes 7864324
  12.1 14.2 %collective-permute-start.3 = (f32[2,5,64,128]{3,2,1,0:T(8,128)}, f32[2,5,64,128]{3,2,1,0:T(8,128)S(1)}, u32[]{:S(2)}, u32[]{:S(2)}) collective-permute-start(f32[2,5,64,128]{3,2,1,0:T(8,128)} %get-tuple-element.31.own), channel_id=1, source_target_pairs={{1,2},{2,1},{5,6},{6,5},{9,10},{10,9},{13,14},{14,13},{17,18},{18,... | collective-permute-start | bytes 983048 | tf_op jit(solution)/shard_map/ppermute | solution.py:635
  12.8 13.5 %collective-permute-start.2 = (f32[2,5,64,128]{3,2,1,0:T(8,128)}, f32[2,5,64,128]{3,2,1,0:T(8,128)S(1)}, u32[]{:S(2)}, u32[]{:S(2)}) collective-permute-start(f32[2,5,64,128]{3,2,1,0:T(8,128)} %get-tuple-element.31.own), channel_id=1, source_target_pairs={{0,1},{1,0},{2,3},{3,2},{4,5},{5,4},{6,7},{7,6},{8,9},{9,8},{10,11... | collective-permute-start | bytes 983048 | tf_op jit(solution)/shard_map/ppermute | solution.py:635
  20.9 0.9 copy-start.5
  23.0 5.5 %collective-permute-start.4 = (f32[1,48,128]{2,1,0:T(8,128)S(1)}, f32[1,48,128]{2,1,0:T(8,128)S(1)}, u32[]{:S(2)}, u32[]{:S(2)}) collective-permute-start(f32[1,48,128]{2,1,0:T(8,128)S(1)} %bitcast.35), channel_id=1, source_target_pairs={{0,16},{4,20},{8,24},{12,28},{16,0},{20,4},{24,8},{28,12},{1,17},{... | collective-permute-start | bytes 73736 | tf_op jit(solution)/shard_map/ppermute | solution.py:171
  26.3 1.0 %copy-start.3 = (f32[2,5,64,128]{3,2,1,0:T(8,128)S(1)}, f32[2,5,64,128]{3,2,1,0:T(8,128)}, u32[]{:S(2)}) copy-start(f32[2,5,64,128]{3,2,1,0:T(8,128)} %get-tuple-element.31.own) | copy-start | bytes 983044
  27.8 0.7 copy-start.8
  28.5 4.2 %collective-permute-start.5 = (f32[2,48,128]{2,1,0:T(8,128)S(1)}, f32[2,48,128]{2,1,0:T(8,128)S(1)}, u32[]{:S(2)}, u32[]{:S(2)}) collective-permute-start(f32[2,48,128]{2,1,0:T(8,128)S(1)} %pad_maximum_fusion.2), channel_id=1, source_target_pairs={{0,8},{4,12},{8,0},{12,4},{16,24},{20,28},{24,16},{28,20},{1,9},{5... | collective-permute-start | bytes 147464 | tf_op jit(solution)/shard_map/ppermute | solution.py:171
  32.7 7.3 %collective-permute-start.6 = (f32[48,128]{1,0:T(8,128)S(1)}, f32[48,128]{1,0:T(8,128)S(1)}, u32[]{:S(2)}, u32[]{:S(2)}) collective-permute-start(f32[48,128]{1,0:T(8,128)S(1)} %bitcast_select_fusion.2), channel_id=1, source_target_pairs={{0,4},{4,0},{8,12},{12,8},{16,20},{20,16},{24,28},{28,24},{1,5},{5... | collective-permute-start | bytes 73736 | tf_op jit(solution)/shard_map/ppermute | solution.py:195
  34.4 16.0 %collective-permute-start.7 = (f32[1,320,128]{2,1,0:T(8,128)S(1)}, f32[1,320,128]{2,1,0:T(8,128)S(1)}, u32[]{:S(2)}, u32[]{:S(2)}) collective-permute-start(f32[1,320,128]{2,1,0:T(8,128)S(1)} %bitcast.32), channel_id=1, source_target_pairs={{0,16},{4,20},{8,24},{12,28},{16,0},{20,4},{24,8},{28,12},{1,17},{... | collective-permute-start | bytes 491528 | tf_op jit(solution)/shard_map/ppermute | solution.py:171
  36.8 28.9 %collective-permute-start.10 = (f32[5,5,64,256]{3,2,1,0:T(8,128)}, f32[5,5,64,256]{3,2,1,0:T(8,128)S(1)}, u32[]{:S(2)}, u32[]{:S(2)}) collective-permute-start(f32[5,5,64,256]{3,2,1,0:T(8,128)} %get-tuple-element.36), channel_id=1, source_target_pairs={{1,2},{2,1},{5,6},{6,5},{9,10},{10,9},{13,14},{14,13},{17,18},{18,... | collective-permute-start | bytes 4915208 | tf_op jit(solution)/shard_map/ppermute | solution.py:635
  37.6 38.4 %collective-permute-start.17 = (f32[5,5,64,256]{3,2,1,0:T(8,128)}, f32[5,5,64,256]{3,2,1,0:T(8,128)S(1)}, u32[]{:S(2)}, u32[]{:S(2)}) collective-permute-start(f32[5,5,64,256]{3,2,1,0:T(8,128)} %get-tuple-element.41), channel_id=1, source_target_pairs={{0,1},{1,0},{2,3},{3,2},{4,5},{5,4},{6,7},{7,6},{8,9},{9,8},{10,11... | collective-permute-start | bytes 4915208 | tf_op jit(solution)/shard_map/ppermute | solution.py:635
  40.0 1.7 %copy-start.1 = (f32[5,8,64,256]{3,2,1,0:T(8,128)S(1)}, f32[5,8,64,256]{3,2,1,0:T(8,128)}, u32[]{:S(2)}) copy-start(f32[5,8,64,256]{3,2,1,0:T(8,128)} %inv_in.3) | copy-start | bytes 7864324
  41.7 0.9 copy-start.6
  42.7 0.9 copy-start.10
  43.6 6.9 %copy-start.11 = (f32[8,8,256]{2,1,0:T(8,128)S(1)}, f32[8,8,256]{2,1,0:T(8,128)}, u32[]{:S(2)}) copy-start(f32[8,8,256]{2,1,0:T(8,128)} %weight.1) | copy-start | bytes 196612
  43.6 6.9 %copy-start.12 = (s32[8,8,256]{2,1,0:T(8,128)S(1)}, s32[8,8,256]{2,1,0:T(8,128)}, u32[]{:S(2)}) copy-start(s32[8,8,256]{2,1,0:T(8,128)} %ids.1) | copy-start | bytes 196612
  54.7 2.0 %collective-permute-start.8 = (f32[3,48,128]{2,1,0:T(8,128)S(1)}, f32[3,48,128]{2,1,0:T(8,128)S(1)}, u32[]{:S(2)}, u32[]{:S(2)}) collective-permute-start(f32[3,48,128]{2,1,0:T(8,128)S(1)} %constant_dynamic-slice_fusion.6), channel_id=1, source_target_pairs={{0,1},{1,0},{2,3},{3,2},{4,5},{5,4},{6,7},{7,6},{8,9},{9,8},{10,11... | collective-permute-start | bytes 221192 | tf_op jit(solution)/shard_map/ppermute | solution.py:606
  54.8 21.2 %copy-start.2 = (f32[5,8,64,256]{3,2,1,0:T(8,128)S(1)}, f32[5,8,64,256]{3,2,1,0:T(8,128)}, u32[]{:S(2)}) copy-start(f32[5,8,64,256]{3,2,1,0:T(8,128)} %inv_in.3) | copy-start | bytes 7864324
  54.8 21.2 %copy-start.9 = (f32[2,5,64,128]{3,2,1,0:T(8,128)S(1)}, f32[2,5,64,128]{3,2,1,0:T(8,128)}, u32[]{:S(2)}) copy-start(f32[2,5,64,128]{3,2,1,0:T(8,128)} %copy-done.8) | copy-start | bytes 983044
  54.8 10.2 %collective-permute-start.15 = (f32[2,320,128]{2,1,0:T(8,128)S(1)}, f32[2,320,128]{2,1,0:T(8,128)S(1)}, u32[]{:S(2)}, u32[]{:S(2)}) collective-permute-start(f32[2,320,128]{2,1,0:T(8,128)S(1)} %pad_maximum_fusion.1), channel_id=1, source_target_pairs={{0,8},{4,12},{8,0},{12,4},{16,24},{20,28},{24,16},{28,20},{1,9},{5... | collective-permute-start | bytes 983048 | tf_op jit(solution)/shard_map/ppermute | solution.py:171
  56.7 9.0 %collective-permute-start.9 = (f32[3,24,128]{2,1,0:T(8,128)S(1)}, f32[3,24,128]{2,1,0:T(8,128)S(1)}, u32[]{:S(2)}, u32[]{:S(2)}) collective-permute-start(f32[3,24,128]{2,1,0:T(8,128)S(1)} %constant_dynamic-slice_fusion.5), channel_id=1, source_target_pairs={{0,2},{1,3},{2,0},{3,1},{4,6},{5,7},{6,4},{7,5},{8,10},{9,11},{10,... | collective-permute-start | bytes 110600 | tf_op jit(solution)/shard_map/ppermute | solution.py:606
  65.1 6.1 %collective-permute-start.16 = (f32[320,128]{1,0:T(8,128)S(1)}, f32[320,128]{1,0:T(8,128)S(1)}, u32[]{:S(2)}, u32[]{:S(2)}) collective-permute-start(f32[320,128]{1,0:T(8,128)S(1)} %bitcast_select_fusion), channel_id=1, source_target_pairs={{0,4},{4,0},{8,12},{12,8},{16,20},{20,16},{24,28},{28,24},{1,5},{5... | collective-permute-start | bytes 491528 | tf_op jit(solution)/shard_map/ppermute | solution.py:195
  65.8 5.7 %collective-permute-start.11 = (f32[3,12,128]{2,1,0:T(8,128)S(1)}, f32[3,12,128]{2,1,0:T(8,128)S(1)}, u32[]{:S(2)}, u32[]{:S(2)}) collective-permute-start(f32[3,12,128]{2,1,0:T(8,128)S(1)} %constant_dynamic-slice_fusion.4), channel_id=1, source_target_pairs={{0,4},{4,0},{8,12},{12,8},{16,20},{20,16},{24,28},{28,24},{1,5},{5... | collective-permute-start | bytes 55304 | tf_op jit(solution)/shard_map/ppermute | solution.py:606
  71.6 22.7 %collective-permute-start.14 = (f32[3,3,128]{2,1,0:T(4,128)S(1)}, f32[3,3,128]{2,1,0:T(4,128)S(1)}, u32[]{:S(2)}, u32[]{:S(2)}) collective-permute-start(f32[3,3,128]{2,1,0:T(4,128)S(1)} %get-tuple-element.48), channel_id=1, source_target_pairs={{0,24},{4,28},{8,16},{12,20},{16,8},{20,12},{24,0},{28,4},{1,25},{... | collective-permute-start | bytes 13832 | tf_op jit(solution)/shard_map/ppermute | solution.py:623
  73.1 21.2 %collective-permute-start.13 = (f32[3,3,128]{2,1,0:T(4,128)S(1)}, f32[3,3,128]{2,1,0:T(4,128)S(1)}, u32[]{:S(2)}, u32[]{:S(2)}) collective-permute-start(f32[3,3,128]{2,1,0:T(4,128)S(1)} %get-tuple-element.49), channel_id=1, source_target_pairs={{0,8},{4,12},{8,0},{12,4},{16,24},{20,28},{24,16},{28,20},{1,9},{5... | collective-permute-start | bytes 13832 | tf_op jit(solution)/shard_map/ppermute | solution.py:623
  73.4 20.8 %collective-permute-start.12 = (f32[3,3,128]{2,1,0:T(4,128)S(1)}, f32[3,3,128]{2,1,0:T(4,128)S(1)}, u32[]{:S(2)}, u32[]{:S(2)}) collective-permute-start(f32[3,3,128]{2,1,0:T(4,128)S(1)} %get-tuple-element.50), channel_id=1, source_target_pairs={{0,16},{4,20},{8,24},{12,28},{16,0},{20,4},{24,8},{28,12},{1,17},{... | collective-permute-start | bytes 13832 | tf_op jit(solution)/shard_map/ppermute | solution.py:623

commit v6 on v5

--- a/solution.py
+++ b/solution.py
@@ -12,7 +12,6 @@
 HALF = LANES // 2
 COLS = 6
 DEEP = 3
-NEAR = 8
 MIB = 1 << 20
 ANY = pl.BlockSpec(memory_space=pl.ANY)
 VMEM = pl.BlockSpec(memory_space=pltpu.VMEM)
@@ -46,40 +45,62 @@
     return total
 
 
-def send_kernel(even, src, inv, tile, inner, outer):
+def ends_kernel(src, inv, tile):
+    for f, field in enumerate((src, inv)):
+        tile[f] = chord_tile([(s, field[:, s]) for s in range(field.shape[1])])
+
+
+def chord_ends(source, inv_diag):
+    nvar, spans, depth, chord = source.shape
+    field = pl.BlockSpec((1, spans, depth, chord), lambda v: (v, 0, 0, 0))
+    return pl.pallas_call(
+        ends_kernel,
+        grid=(nvar,),
+        in_specs=[field, field],
+        out_specs=pl.BlockSpec((2, 1, depth, LANES), lambda v: (0, v, 0, 0)),
+        out_shape=jax.ShapeDtypeStruct((2, nvar, depth, LANES), jnp.float32),
+        compiler_params=pltpu.CompilerParams(vmem_limit_bytes=56 * MIB),
+        name="chord_ends",
+    )(source, inv_diag)
+
+
+def layers_kernel(even, src, inv, inner, outer, held, sems):
     spans = src.shape[1]
-    for f, field in enumerate((src, inv)):
-        tile[f] = chord_tile([(s, field[:, s]) for s in range(spans)])
-    for out, up in ((inner, even[0]), (outer, 1 - even[0])):
+    copies, last = [], []
+    for side, (out, up) in enumerate(((inner, even[0]), (outer, 1 - even[0]))):
         for j in range(DEEP):
             s = jnp.where(up == 1, spans - 1 - j, j)
-            if j < DEEP - 1:
-                out[j] = src[:, s]
-                out[DEEP - 1 + j] = inv[:, s]
-            else:
-                out[2 * (DEEP - 1)] = src[:, s] * inv[:, s]
-
-
-def make_sends(even, source, inv_diag, depth, step):
-    nvar, spans, _, chord = source.shape
-    field = pl.BlockSpec((step, spans, depth, chord), lambda v: (v, 0, 0, 0))
-    halo = pl.BlockSpec((5, step, depth, chord), lambda v: (0, v, 0, 0))
-    f32 = jnp.float32
+            for f, field in enumerate((src, inv)):
+                to = out.at[f * (DEEP - 1) + j] if j < DEEP - 1 else held.at[side, f]
+                copy = pltpu.make_async_copy(field.at[:, s], to, sems.at[side, f, j])
+                copy.start()
+                (copies if j < DEEP - 1 else last).append(copy)
+    for copy in last:
+        copy.wait()
+    for side, out in enumerate((inner, outer)):
+        held[side, 0] = held[side, 0] * held[side, 1]
+        copy = pltpu.make_async_copy(held.at[side, 0], out.at[2 * (DEEP - 1)], sems.at[side, 0, DEEP])
+        copy.start()
+        copies.append(copy)
+    for copy in copies:
+        copy.wait()
+
+
+def span_layers(even, source, inv_diag):
+    nvar, _, depth, chord = source.shape
+    shape = jax.ShapeDtypeStruct((5, nvar, depth, chord), jnp.float32)
     return pl.pallas_call(
-        send_kernel,
-        grid=(nvar // step,),
-        in_specs=[SMEM, field, field],
-        out_specs=[pl.BlockSpec((2, step, depth, LANES), lambda v: (0, v, 0, 0)), halo, halo],
-        out_shape=[
-            jax.ShapeDtypeStruct((2, nvar, depth, LANES), f32),
-            jax.ShapeDtypeStruct((5, nvar, depth, chord), f32),
-            jax.ShapeDtypeStruct((5, nvar, depth, chord), f32),
+        layers_kernel,
+        in_specs=[SMEM, ANY, ANY],
+        out_specs=[ANY, ANY],
+        out_shape=[shape, shape],
+        scratch_shapes=[
+            pltpu.VMEM((2, 2, nvar, depth, chord), jnp.float32),
+            pltpu.SemaphoreType.DMA((2, 2, DEEP + 1)),
         ],
-        compiler_params=pltpu.CompilerParams(vmem_limit_bytes=58 * MIB),
-        cost_estimate=pl.CostEstimate(
-            flops=0, bytes_accessed=16 * nvar * spans * depth * chord, transcendentals=0
-        ),
-        name=f"sends_{depth}",
+        compiler_params=pltpu.CompilerParams(vmem_limit_bytes=56 * MIB),
+        cost_estimate=pl.CostEstimate(flops=0, bytes_accessed=8 * MIB, transcendentals=0),
+        name="span_layers",
     )(even, source, inv_diag)
 
 
@@ -109,93 +130,68 @@
         packet[v * depth : (v + 1) * depth, :] = tile[v]
 
 
-def near_merge_kernel(even, own, inner, outer, cpl, packet, full):
-    depth = own.shape[2]
-    up = jnp.full((1, 1, 1), even[0], jnp.int32) == 1
-
-    def layer(j, low):
-        return jnp.where(up, outer[j], inner[j]) if low else jnp.where(up, inner[j], outer[j])
-
-    low = [chord_tile([(7, layer(2 * f, True)), (6, layer(2 * f + 1, True))]) for f in range(2)]
-    high = [chord_tile([(0, layer(2 * f, False)), (1, layer(2 * f + 1, False))]) for f in range(2)]
-    merge(low, high, own, packet, full, depth)
-    rows = own.shape[1] * depth
-    packet[rows : rows + 8, :] = cpl[...]
-
-
-def bulk_merge_kernel(even, own, inner, outer, packet, full):
+def merge_kernel(even, own, inner, outer, cpl, packet, full):
     depth = own.shape[2]
     up = jnp.full((1, 1, 1), even[0], jnp.int32) == 1
     low = [jnp.where(up, outer[f], inner[f]) for f in range(2)]
     high = [jnp.where(up, inner[f], outer[f]) for f in range(2)]
     merge(low, high, own, packet, full, depth)
-
-
-def near_merge(even, own, inner, outer, cpl):
+    rows = own.shape[1] * depth
+    packet[rows : rows + 8, :] = cpl[...]
+
+
+def merge_ends(even, own, inner, outer, cpl):
     _, nvar, depth, _ = own.shape
     return pl.pallas_call(
-        near_merge_kernel,
+        merge_kernel,
         in_specs=[SMEM, VMEM, VMEM, VMEM, VMEM],
         out_specs=[VMEM, VMEM],
         out_shape=[
             jax.ShapeDtypeStruct((nvar * depth + 8, LANES), jnp.float32),
             jax.ShapeDtypeStruct(own.shape, jnp.float32),
         ],
-        compiler_params=pltpu.CompilerParams(vmem_limit_bytes=8 * MIB),
-        name="near_merge",
+        compiler_params=pltpu.CompilerParams(vmem_limit_bytes=12 * MIB),
+        name="merge_ends",
     )(even, own, inner, outer, cpl)
 
 
-def bulk_merge(even, own, inner, outer):
-    _, nvar, depth, _ = own.shape
-    return pl.pallas_call(
-        bulk_merge_kernel,
-        in_specs=[SMEM, VMEM, VMEM, VMEM],
-        out_specs=[VMEM, VMEM],
-        out_shape=[
-            jax.ShapeDtypeStruct((nvar * depth, LANES), jnp.float32),
-            jax.ShapeDtypeStruct(own.shape, jnp.float32),
-        ],
-        compiler_params=pltpu.CompilerParams(vmem_limit_bytes=12 * MIB),
-        name="bulk_merge",
-    )(even, own, inner, outer)
-
-
-def route_ends(packet, me, low_of, high_of, after=None):
+def exchange_masks(count):
+    return [1 << b for b in range(count.bit_length() - 1)][::-1]
+
+
+def place_of(me, block, masks):
+    apart = me ^ block
+    index = 0
+    for bit_of, mask in enumerate(masks[:-1]):
+        index = index + jnp.where((apart & mask) != 0, 1 << bit_of, 0)
+    return index, jnp.where((apart & masks[-1]) == 0, 1, 0)
+
+
+def pick_kernel(masks, me, faces, held, out):
+    other = me[0] ^ masks[-1]
+    low, _ = place_of(me[0], faces[other, 0], masks)
+    high, _ = place_of(me[0], faces[other, 1], masks)
+    out[...] = jnp.where(lane_iota((1, LANES)) < HALF, held[low], held[high])
+
+
+def route_ends(packet, me, face_map):
     count = lax.axis_size("blk")
-    masks = [1 << b for b in range(count.bit_length() - 1)][::-1]
-    left = lane_iota((1, LANES)) < HALF
-    held = packet[None]
-    first = None
+    masks = exchange_masks(count)
+    held, first = packet[None], None
     for mask in masks[:-1]:
         other = lax.ppermute(held, "blk", [(i, i ^ mask) for i in range(count)])
-        if first is None:
-            first = other
-            if after is not None:
-                held, _ = lax.optimization_barrier((held, after))
+        first = other if first is None else first
         held = jnp.concatenate([held, other], 0)
-
-    def place(block):
-        apart = me ^ block
-        index = 0
-        for bit, mask in enumerate(masks[:-1]):
-            index = index + jnp.where((apart & mask) != 0, 1 << bit, 0)
-        return index, (apart & masks[-1]) == 0
-
-    def chosen(device):
-        low, _ = place(low_of[device])
-        high, _ = place(high_of[device])
-        return jnp.where(
-            left,
-            lax.dynamic_index_in_dim(held, low, 0, keepdims=False),
-            lax.dynamic_index_in_dim(held, high, 0, keepdims=False),
-        )
-
+    picked = pl.pallas_call(
+        functools.partial(pick_kernel, masks),
+        in_specs=[SMEM, SMEM, VMEM],
+        out_specs=VMEM,
+        out_shape=jax.ShapeDtypeStruct(packet.shape, packet.dtype),
+        compiler_params=pltpu.CompilerParams(vmem_limit_bytes=12 * MIB),
+        name="pick_ends",
+    )(me, face_map, held)
     last = masks[-1]
-    given = lax.ppermute(chosen(me ^ last), "blk", [(i, i ^ last) for i in range(count)])
-    _, low_here = place(low_of[me])
-    _, high_here = place(high_of[me])
-    return jnp.where(jnp.where(left, low_here, high_here), chosen(me), given), first
+    return held, lax.ppermute(picked, "blk", [(i, i ^ last) for i in range(count)]), first
 
 
 def expand_couplings(couplings, wide):
@@ -221,7 +217,7 @@
     wide[...] = jnp.where((r & 15) == (c & 15), both, 0.0).astype(jnp.bfloat16)
 
 
-def ribbon_sweeps(depth, full, given, mine, theirs, scalars, faces):
+def ribbon_sweeps(depth, full, given, mine, scalars, faces):
     nvar = 5
     lane = lane_iota((1, LANES))
     place = lane & (HALF - 1)
@@ -233,7 +229,7 @@
     before, beyond = place == 60, place == 62
 
     def field(f, v):
-        got = given[v * depth : (v + 1) * depth, :]
+        got = given(v * depth, depth)
         turns = ((0, 2, 64, 0), (LANES - 3, LANES - 1, 63, LANES - 1))[f]
         moved = [pltpu.roll(got, t, 1) if t else got for t in turns]
         x = jnp.where(ghost, jnp.where(side, moved[1], moved[0]), 0.0)
@@ -255,7 +251,7 @@
 
     own_rows = spread(mine[...])
     scalars[0] = own_rows
-    scalars[1] = jnp.where(ghost, spread(theirs[...]), own_rows)
+    scalars[1] = jnp.where(ghost, spread(given(nvar * depth, 8)), own_rows)
     mixed = [scalars[1, i : i + 1, :] for i in range(150)]
     own_c = {i: scalars[0, i : i + 1, :] for i in range(100, 150)}
     high_face = (side & jnp.logical_not(lane == HALF + 60)) | (lane == 60)
@@ -286,20 +282,22 @@
         p = [inv[v] * total[v] for v in range(nvar)]
 
 
-def run_sweeps(depth, even, couplings, full, given, mine, theirs, src_in, inv_in, inner, outer, scratch, out=None):
+def run_sweeps(sweeps, even, couplings, ribbon, src_in, inv_in, inner, outer, p_in, out, scratch):
     src, inv, pa, pb, wide, before, coming, faces, scalars, sems, out_sems = scratch
     nvar, layers, rows, chord = pa.shape
     spans = layers - 2 * DEEP
-
-    def move(f, at, start):
-        to, field = ((src, src_in), (inv, inv_in))[f]
-
-        def one(ref, layer):
-            copy = pltpu.make_async_copy(ref, to.at[:, layer, 0:depth], sems.at[f, layer])
-            copy.start() if start else copy.wait()
-
-        if not start or DEEP <= at < DEEP + spans:
-            one(field.at[:, at - DEEP if start else 0, 0:depth], at)
+    start_at, stop_at = sweeps[0], layers - 1 - sweeps[0]
+    whole_at = [at for at in range(start_at, stop_at + 1)]
+
+    def one(f, ref, at, start):
+        to = (src, inv, pb)[f]
+        copy = pltpu.make_async_copy(ref, to.at[:, at], sems.at[f, at])
+        copy.start() if start else copy.wait()
+
+    def bring(f, at):
+        field = (src_in, inv_in)[f]
+        if DEEP <= at < DEEP + spans:
+            one(f, field.at[:, at - DEEP], at, True)
             return
         low = at < DEEP
         j = DEEP - 1 - at if low else at - DEEP - spans
@@ -309,35 +307,49 @@
 
         @pl.when(even[0] == (0 if low else 1))
         def _():
-            one(inner.at[piece], at)
+            one(f, inner.at[piece], at, True)
 
         @pl.when(even[0] == (1 if low else 0))
         def _():
-            one(outer.at[piece], at)
-
-    if rows != depth:
-        none = jnp.zeros((nvar, layers, rows - depth, chord), jnp.float32)
-        src[:, :, depth:rows, :] = none
-        inv[:, :, depth:rows, :] = none
-        faces[...] = jnp.zeros(faces.shape, jnp.float32)
-    for at in range(layers):
-        for f in range(2):
-            move(f, at, True)
-    ones = jnp.ones((nvar, rows, chord), jnp.float32)
-    inv[:, 0] = ones
-    inv[:, layers - 1] = ones
+            one(f, outer.at[piece], at, True)
+
+    for at in whole_at:
+        bring(0, at)
+        bring(1, at)
+        if p_in is not None:
+            one(2, p_in.at[:, at - 1], at, True)
+    if p_in is None:
+        ones = jnp.ones((nvar, rows, chord), jnp.float32)
+        inv[:, 0] = ones
+        inv[:, layers - 1] = ones
     expand_couplings(couplings[...], wide)
-    ribbon_sweeps(depth, full, given, mine, theirs, scalars, faces)
+    if ribbon is not None:
+        ribbon_sweeps(rows, *ribbon, scalars, faces)
+
+    def face_tiles(n, s, at):
+        face = faces[n, :, at]
+        at_low = pltpu.roll(face, lax.rem(LANES + 10 - COLS * s, LANES), 2)
+        at_high = pltpu.roll(face, lax.rem(LANES + 73 - COLS * s, LANES), 2)
+        return at_low, at_high
 
     def arrive(at, edge=False):
-        move(0, at, False)
-        if not edge:
-            move(1, at, False)
-        pa[:, at] = inv[:, at] * src[:, at]
+        one(0, src_in.at[:, 0], at, False)
+        if p_in is None:
+            if not edge:
+                one(1, src_in.at[:, 0], at, False)
+            pa[:, at] = inv[:, at] * src[:, at]
+            return
+        one(1, src_in.at[:, 0], at, False)
+        one(2, src_in.at[:, 0], at, False)
+        low, high = face_tiles(0, at, slice(0, rows))
+        pb[:, at, :, :LANES] += inv[:, at, :, :LANES] * jnp.where(lane == 0, low, 0.0)
+        pb[:, at, :, LANES:] += inv[:, at, :, LANES:] * jnp.where(lane == LANES - 1, high, 0.0)
+
+    leave_from = sweeps[-1] + 1
 
     def leave(at, start):
         copy = pltpu.make_async_copy(
-            pb.at[:, at, 0:depth], out.at[:, at - DEEP], out_sems.at[at - DEEP]
+            pb.at[:, at], out.at[:, at - leave_from], out_sems.at[at - leave_from]
         )
         copy.start() if start else copy.wait()
 
@@ -373,9 +385,7 @@
             )
             below = normal_low[:, 15:16]
             total += jnp.where(last_row, 0.0, pltpu.roll(normal_high, 15, 1))
-            face = faces[n, :, at]
-            at_low = pltpu.roll(face, lax.rem(LANES + 10 - COLS * s, LANES), 2)
-            at_high = pltpu.roll(face, lax.rem(LANES + 73 - COLS * s, LANES), 2)
+            at_low, at_high = face_tiles(n, s, at) if n > 0 else (0.0, 0.0)
             a = pltpu.roll(chord_low[..., :LANES], 1, 2)
             b = pltpu.roll(chord_low[..., LANES:], 1, 2)
             c = pltpu.roll(chord_high[..., :LANES], LANES - 1, 2)
@@ -390,23 +400,23 @@
             waiting = total
         before[:, rows - 16 : rows] = waiting
 
-    for n in range(SWEEPS):
+    for n in sweeps:
         p, after = (pa, pb) if n % 2 == 0 else (pb, pa)
-        if n == 0:
-            arrive(0, True)
+        if n == sweeps[0]:
+            arrive(start_at, True)
         for g in range(groups):
             coming[:, 16 * g : 16 * g + 16] = products(p, n, g, 0, step)
         full = layers - 2 - 2 * n
-        turn = 2 if groups > 1 else full
+        turn = 2
 
         def several(i, _):
             s0 = n + 1 + i * turn
-            if n == 0:
+            if n == sweeps[0]:
                 for j in range(turn):
                     arrive(s0 + j)
             for j in range(turn):
                 one_layer(p, after, n, s0 + j)
-            if n == SWEEPS - 1 and out is not None:
+            if n == sweeps[-1]:
                 for j in range(turn - 1):
                     leave(s0 + j, True)
 
@@ -416,26 +426,19 @@
 
             return 0
 
-        if turn == full:
-            several(0, 0)
-        else:
-            lax.fori_loop(0, full // turn, several, 0)
+        lax.fori_loop(0, full // turn, several, 0)
         last = layers - 1 - n
-        if n == 0:
+        if n == sweeps[0]:
             arrive(last, True)
         for g in range(groups):
             at = slice(16 * g, 16 * g + 16)
             span_high = products(p, last, g, step, 2 * step)
             after[:, last - 1, at] = inv[:, last - 1, at] * (before[:, at] + span_high)
-    if out is not None:
-        leave(DEEP + spans - 1, True)
-        for at in range(DEEP, DEEP + spans):
-            leave(at, False)
-    return pb
-
-
-def sweep_scratch(nvar, spans, chord, depth):
-    rows = max(depth, 16)
+    leave(layers - 1 - leave_from, True)
+    return pb, lambda: [leave(at, False) for at in range(leave_from, layers - leave_from)]
+
+
+def sweep_scratch(nvar, spans, chord, rows):
     f32 = jnp.float32
     field = pltpu.VMEM((nvar, spans + 2 * DEEP, rows, chord), f32)
     layer = pltpu.VMEM((nvar, rows, chord), f32)
@@ -449,81 +452,77 @@
         layer,
         pltpu.VMEM((SWEEPS, nvar, rows, LANES), f32),
         pltpu.VMEM((2, 152, LANES), f32),
-        pltpu.SemaphoreType.DMA((2, spans + 2 * DEEP)),
-        pltpu.SemaphoreType.DMA((spans,)),
+        pltpu.SemaphoreType.DMA((3, spans + 2 * DEEP)),
+        pltpu.SemaphoreType.DMA((spans + 2 * DEEP,)),
     ]
 
 
-def bulk_kernel(
-    depth, even, couplings, full, given, mine, theirs, src_in, inv_in, inner, outer, out, *scratch
-):
-    run_sweeps(
-        depth, even, couplings, full, given, mine, theirs, src_in, inv_in, inner, outer, scratch, out
-    )
-
-
-def coupling_rows(shape):
-    rows = shape[0] - 8
-    return pl.BlockSpec((8, LANES), lambda i: (rows // 8, 0))
-
-
-def whole(a):
-    return pl.BlockSpec(a.shape, lambda i: (0,) * a.ndim)
-
-
-def bulk_sweeps(even, couplings, full, given, mine, theirs, source, inv_diag, inner, outer):
+def first_kernel(even, couplings, src_in, inv_in, inner, outer, out, *scratch):
+    _, done = run_sweeps([0], even, couplings, None, src_in, inv_in, inner, outer, None, out, scratch)
+    done()
+
+
+def first_sweep(even, couplings, source, inv_diag, inner, outer):
     nvar, spans, depth, chord = source.shape
     return pl.pallas_call(
-        functools.partial(bulk_kernel, depth),
-        grid=(1,),
-        in_specs=[SMEM, whole(couplings), whole(full), whole(given), coupling_rows(mine.shape)]
-        + [coupling_rows(theirs.shape), ANY, ANY, ANY, ANY],
+        first_kernel,
+        in_specs=[SMEM, VMEM, ANY, ANY, ANY, ANY],
         out_specs=ANY,
-        out_shape=jax.ShapeDtypeStruct(source.shape, jnp.float32),
+        out_shape=jax.ShapeDtypeStruct((nvar, spans + 4, depth, chord), jnp.float32),
         scratch_shapes=sweep_scratch(nvar, spans, chord, depth),
         compiler_params=pltpu.CompilerParams(vmem_limit_bytes=28 * MIB),
-        cost_estimate=pl.CostEstimate(
-            flops=2 * 40 * 480 * 256 * 256 * (depth // 16), bytes_accessed=16 * MIB, transcendentals=0
-        ),
-        name="bulk_sweeps",
-    )(even, couplings, full, given, mine, theirs, source, inv_diag, inner, outer)
-
-
-def near_kernel(even, couplings, full, given, mine, theirs, src_in, inv_in, inner, outer, jac, sens, *scratch):
-    adjoint = run_sweeps(
-        NEAR, even, couplings, full, given, mine, theirs, src_in, inv_in, inner, outer, scratch
+        cost_estimate=pl.CostEstimate(flops=7 * 10**9, bytes_accessed=16 * MIB, transcendentals=0),
+        name="first_sweep",
+    )(even, couplings, source, inv_diag, inner, outer)
+
+
+def last_kernel(masks, even, me, faces, *rest):
+    couplings, full, held, given, src_in, inv_in, inner, outer, p_in, jac, out, sens, *scratch = rest
+    low, low_held = place_of(me[0], faces[me[0], 0], masks)
+    high, high_held = place_of(me[0], faces[me[0], 1], masks)
+    left = lane_iota((1, LANES)) < HALF
+    keep = jnp.where(left, low_held, high_held) == 1
+
+    def ends(first, count):
+        at = pl.ds(first, count)
+        return jnp.where(keep, jnp.where(left, held[low, at], held[high, at]), given[at])
+
+    nvar, spans, depth, chord = out.shape
+    mine = held.at[0, nvar * depth : nvar * depth + 8]
+    result, done = run_sweeps(
+        [1, 2], even, couplings, (full, ends, mine), src_in, inv_in, inner, outer, p_in, out, scratch
     )
-    dims, nvar = jac.shape[:2]
-    spans, chord = sens.shape[1:]
     layer = []
     for v in range(nvar):
         for k in range(2):
             layer.append(
-                jnp.concatenate([adjoint[v, DEEP + s, k : k + 1, :] for s in range(spans)], 0)
+                jnp.concatenate([result[v, DEEP + s, k : k + 1, :] for s in range(spans)], 0)
             )
-    for c in range(dims):
+    for c in range(jac.shape[0]):
         total = jnp.zeros((spans, chord), jnp.float32)
         for v in range(nvar):
             for k in range(2):
                 total += jac[c, v, k] * layer[2 * v + k]
         sens[c] = total
-
-
-def near_sweeps(even, couplings, full, given, packet, source, inv_diag, inner, outer, jac):
-    nvar, spans, _, chord = source.shape
-    shape = (jac.shape[0], spans, chord)
+    done()
+
+
+def last_sweeps(even, me, face_map, couplings, full, held, given, source, inv_diag, inner, outer, p, jac):
+    nvar, spans, depth, chord = source.shape
+    masks = exchange_masks(lax.axis_size("blk"))
     return pl.pallas_call(
-        near_kernel,
-        grid=(1,),
-        in_specs=[SMEM, whole(couplings), whole(full), whole(given), coupling_rows(packet.shape)]
-        + [coupling_rows(given.shape), ANY, ANY, ANY, ANY, whole(jac)],
-        out_specs=pl.BlockSpec(shape, lambda i: (0, 0, 0)),
-        out_shape=jax.ShapeDtypeStruct(shape, jnp.float32),
-        scratch_shapes=sweep_scratch(nvar, spans, chord, NEAR),
-        compiler_params=pltpu.CompilerParams(vmem_limit_bytes=16 * MIB),
-        cost_estimate=pl.CostEstimate(flops=5 * 10**9, bytes_accessed=4 * MIB, transcendentals=0),
-        name="near_sweeps",
-    )(even, couplings, full, given, packet, given, source, inv_diag, inner, outer, jac)
+        functools.partial(last_kernel, masks),
+        in_specs=[SMEM, SMEM, SMEM, VMEM, VMEM, VMEM, VMEM, ANY, ANY, ANY, ANY, ANY, VMEM],
+        out_specs=[ANY, VMEM],
+        out_shape=[
+            jax.ShapeDtypeStruct(source.shape, jnp.float32),
+            jax.ShapeDtypeStruct((jac.shape[0], spans, chord), jnp.float32),
+        ],
+        scratch_shapes=sweep_scratch(nvar, spans, chord, depth),
+        compiler_params=pltpu.CompilerParams(vmem_limit_bytes=32 * MIB),
+        cost_estimate=pl.CostEstimate(flops=11 * 10**9, bytes_accessed=16 * MIB, transcendentals=0),
+        name="last_sweeps",
+    )(even, me, face_map, couplings, full, held, given, source, inv_diag, inner, outer, p, jac)
 
 
 def point_indices(bits, ids, hi_index, lo_index):
@@ -591,7 +590,7 @@
     )(sens, weight, ids)
 
 
-def halve_points(partial, after, n_dev):
+def halve_points(partial, n_dev):
     n_blk, n_sub = lax.axis_size("blk"), lax.axis_size("sub")
     blk, sub = lax.axis_index("blk"), lax.axis_index("sub")
     partial = partial[:, : n_dev // 2 * 3]
@@ -604,9 +603,7 @@
         keep = lax.dynamic_slice_in_dim(partial, mine, half, dim)
         send = lax.dynamic_slice_in_dim(partial, half - mine, half, dim)
         partial = keep + lax.ppermute(send, axis, [(i, i ^ mask) for i in range(count)])
-        if number == 1:
-            partial, after = lax.optimization_barrier((partial, after))
-    return partial, after
+    return partial
 
 
 def quarter_points(partial):
@@ -637,36 +634,25 @@
 
 def body(source, inv_diag, coupling, face_map, wall_jac, ffd_weight, cp_ids):
     nvar = source.shape[0]
-    me = lax.axis_index("blk")
     n_dev = lax.axis_size("blk") * lax.axis_size("sub")
     even = (1 - (lax.axis_index("sub") & 1)).astype(jnp.int32).reshape(1)
+    me = lax.axis_index("blk").astype(jnp.int32).reshape(1)
     couplings = jnp.pad(coupling[0].reshape(6 * nvar, nvar), ((0, 2), (0, LANES - nvar)))
     flat = jnp.pad(coupling[0].reshape(-1), (0, 8 * HALF - 6 * nvar * nvar)).reshape(8, HALF)
     cpl = jnp.concatenate([flat, flat], 1)
-    low_of, high_of = face_map[:, 0], face_map[:, 1]
-
-    own, inner, outer = make_sends(even, source, inv_diag, NEAR, nvar)
-    inner, outer = swap_spans(inner, outer)
-    packet, full = near_merge(even, own, inner, outer, cpl)
-
-    depth = source.shape[2]
-    bulk_own, bulk_inner, bulk_outer = make_sends(ordered(even, inner), source, inv_diag, depth, 1)
-    tiles = swap_spans(bulk_own, bulk_own)
-    bulk_packet, bulk_full = bulk_merge(even, bulk_own, *tiles)
-    given, _ = route_ends(packet, me, low_of, high_of, bulk_packet)
-    bulk_inner, bulk_outer = swap_spans(
-        ordered(bulk_inner, bulk_packet), ordered(bulk_outer, bulk_packet)
+
+    own = chord_ends(source, inv_diag)
+    tiles = swap_spans(own, own)
+    inner, outer = span_layers(ordered(even, own), source, inv_diag)
+    packet, full = merge_ends(even, own, *tiles, cpl)
+    held, given, first = route_ends(packet, me, face_map)
+    inner, outer = swap_spans(ordered(inner, first), ordered(outer, tiles[1]))
+    p = first_sweep(ordered(even, held), couplings, source, inv_diag, inner, outer)
+    adjoint, sens = last_sweeps(
+        even, me, face_map, couplings, full, held, given, source, inv_diag, inner, outer, p, wall_jac
     )
-    bulk_given, bulk_first = route_ends(bulk_packet, me, low_of, high_of)
-
-    sens = near_sweeps(even, couplings, full, given, packet, source, inv_diag, inner, outer, wall_jac)
-    partial = scatter_points(ordered(sens, bulk_first), ffd_weight, cp_ids, n_dev)
-    partial, bulk_outer = halve_points(partial, bulk_outer, n_dev)
-    adjoint = bulk_sweeps(
-        ordered(even, partial), couplings, bulk_full, bulk_given, packet, given, source, inv_diag,
-        bulk_inner, bulk_outer,
-    )
-    parts, adjoint = lax.optimization_barrier((quarter_points(partial), adjoint))
+    partial = halve_points(scatter_points(sens, ffd_weight, cp_ids, n_dev), n_dev)
+    parts = quarter_points(partial)
     total = (parts[0] + parts[1]) + (parts[2] + parts[3])
     return adjoint, total.reshape(total.shape[0], -1)
 

time: 95.4 us -> 169 us (1.77)
  Pallas kernels: 39.8 us -> 113 us
  local copies, waits for them, and re-layouts: 8.62 us -> 3.82 us
  waiting for transfers between devices: 14.6 us -> 17.7 us
  starting transfers between devices: 28.2 us -> 31.2 us
  between operations: 3.42 us -> 0.87 us
    pallas_call x6, Pallas kernels: 35.6 us -> 109 us  [the longest x1 80.7 us: span_layers(): pl.pallas_call(layers_kernel, in_specs=[SMEM, ANY, ANY], out_specs=[ANY,...]
    ppermute x3, starting transfers between devices: 2.09 us -> 8.54 us  [halve_points(): lax.ppermute(send, axis, [(i, i ^ mask) for i in range(count)])]
    ppermute x3, waiting for transfers between devices: 0.23 us -> 5.25 us  [halve_points(): lax.ppermute(send, axis, [(i, i ^ mask) for i in range(count)])]
    ppermute x4 -> x2, starting transfers between devices: 9.1 us -> 4.23 us  [route_ends(): other = lax.ppermute(held, 'blk', [(i, i ^ mask) for i in range(count)])]
    unnamed x33 -> x20, local copies, waits for them, and re-layouts: 7.55 us -> 3.42 us
    ppermute x2 -> x1, waiting for transfers between devices: 3.93 us -> 0.01 us  [route_ends(): lax.ppermute(picked, 'blk', [(i, i ^ last) for i in range(count)])]
    ppermute x3, waiting for transfers between devices: 0.01 us -> 2.95 us  [quarter_points(): lax.ppermute(quarter(me ^ mask), 'blk', [(i, i ^ mask) for i in range(cou...]
    ppermute x3 -> x2, starting transfers between devices: 7.38 us -> 9.82 us  [swap_spans(): lax.ppermute(inner, 'sub', pairs)]
  transfers between devices with their start and end apart: 18 -> 13, of which waited for: 4 -> 7; matrix products, arithmetic and copies ran while one was open for 1% -> 1% of each run, Pallas kernels for 40% -> 53%
where the time goes in v6:
time: 169 us
  Pallas kernels  113 us (67%)
  starting transfers between devices  31.2 us (18%)
  waiting for transfers between devices  17.7 us (10%)
  local copies, waits for them, and re-layouts  3.82 us (2%)
  other arithmetic  1.92 us (1%)
    pallas_call x1, Pallas kernels, span_layers(): pl.pallas_call(layers_kernel, in_specs=[SMEM, ANY, ANY], out_specs=[ANY,...  80.7 us
    pallas_call x1, Pallas kernels, last_sweeps(): pl.pallas_call(functools.partial(last_kernel, masks), in_specs=[SMEM, SME...  14.2 us
    ppermute x2, starting transfers between devices, swap_spans(): lax.ppermute(inner, 'sub', pairs)  9.82 us
    ppermute x3, starting transfers between devices, halve_points(): lax.ppermute(send, axis, [(i, i ^ mask) for i in range(count)])  8.54 us
    ppermute x2, waiting for transfers between devices, route_ends(): other = lax.ppermute(held, 'blk', [(i, i ^ mask) for i in range(count)])  8.44 us
    pallas_call x1, Pallas kernels, first_sweep(): pl.pallas_call(first_kernel, in_specs=[SMEM, VMEM, ANY, ANY, ANY, ANY], o...  7.84 us
    pallas_call x1, Pallas kernels, chord_ends(): pl.pallas_call(ends_kernel, grid=(nvar,), in_specs=[field, field], out_sp...  5.4 us
    ppermute x3, waiting for transfers between devices, halve_points(): lax.ppermute(send, axis, [(i, i ^ mask) for i in range(count)])  5.25 us
  transfers between devices with their start and end apart: 13, of which 7 were waited for; matrix products, arithmetic and copies ran while one was open for 1% of the time, Pallas kernels for 53%

profile of v6, /device:TPU:0, one launch (start us, length us, event | category | flops | bytes accessed | tf_op | source)
XLA Modules:
  0.0 169.0 jit_solution(15598138283085444573)
XLA Ops:
  0.6 5.4 %chord_ends.1.own = f32[2,5,64,128]{3,2,1,0:T(8,128)} custom-call(f32[5,8,64,256]{3,2,1,0:T(8,128)} %rest_4_.1, f32[5,8,64,256]{3,2,1,0:T(8,128)} %rest_5_.1), custom_call_target="tpu_custom_call" | custom-call | tf_op jit(solution)/shard_map/chord_ends/pallas_call | solution.py:56
  6.0 0.7 collective-permute-start.1
  6.7 4.4 %collective-permute-start = (f32[2,5,64,128]{3,2,1,0:T(8,128)}, f32[2,5,64,128]{3,2,1,0:T(8,128)S(1)}, u32[]{:S(2)}, u32[]{:S(2)}) collective-permute-start(f32[2,5,64,128]{3,2,1,0:T(8,128)} %chord_ends.1.own), channel_id=1, source_target_pairs={{0,1},{1,0},{2,3},{3,2},{4,5},{5,4},{6,7},{7,6},{8,9},{9,8},{10,11... | collective-permute-start | bytes 983048 | tf_op jit(solution)/shard_map/ppermute | solution.py:632
  11.1 0.1 copy.17
  11.2 0.1 reshape_squeeze.7
  11.3 0.1 reshape.18
  11.4 0.1 pad_maximum_fusion.2.cpl
  11.5 0.0 collective-permute-done.1.outer
  11.5 1.1 collective-permute-done.inner
  12.6 1.0 copy-done.3
  13.5 0.5 merge_ends.1
  14.0 0.0 copy-start.8
  14.0 2.7 %collective-permute-start.2 = (f32[1,328,128]{2,1,0:T(8,128)S(1)}, f32[1,328,128]{2,1,0:T(8,128)S(1)}, u32[]{:S(2)}, u32[]{:S(2)}) collective-permute-start(f32[1,328,128]{2,1,0:T(8,128)S(1)} %bitcast.8), channel_id=1, source_target_pairs={{0,16},{4,20},{8,24},{12,28},{16,0},{20,4},{24,8},{28,12},{1,17},{... | collective-permute-start | bytes 503816 | tf_op jit(solution)/shard_map/ppermute | solution.py:182
  16.7 80.7 %span_layers.1 = (f32[5,5,64,256]{3,2,1,0:T(8,128)}, f32[5,5,64,256]{3,2,1,0:T(8,128)}) custom-call(s32[1]{0:T(128)} %bitcast.even, f32[5,8,64,256]{3,2,1,0:T(8,128)} %rest_4_.1, f32[5,8,64,256]{3,2,1,0:T(8,128)} %rest_5_.1), custom_call_target="tpu_custom_call" | custom-call | bytes 8388608 | tf_op jit(solution)/shard_map/span_layers/pallas_call | solution.py:92
  97.4 0.0 copy-start
  97.4 2.0 %collective-permute-start.6 = (f32[5,5,64,256]{3,2,1,0:T(8,128)}, f32[5,5,64,256]{3,2,1,0:T(8,128)}, u32[]{:S(2)}, u32[]{:S(2)}) collective-permute-start(f32[5,5,64,256]{3,2,1,0:T(8,128)} %get-tuple-element.18), channel_id=1, source_target_pairs={{1,2},{2,1},{5,6},{6,5},{9,10},{10,9},{13,14},{14,13},{17,18},{18,... | collective-permute-start | bytes 4915208 | tf_op jit(solution)/shard_map/ppermute | solution.py:632
  99.3 0.0 collective-permute-done.2
  99.3 5.4 %collective-permute-start.5 = (f32[5,5,64,256]{3,2,1,0:T(8,128)}, f32[5,5,64,256]{3,2,1,0:T(8,128)}, u32[]{:S(2)}, u32[]{:S(2)}) collective-permute-start(f32[5,5,64,256]{3,2,1,0:T(8,128)} %get-tuple-element.16), channel_id=1, source_target_pairs={{0,1},{1,0},{2,3},{3,2},{4,5},{5,4},{6,7},{7,6},{8,9},{9,8},{10,11... | collective-permute-start | bytes 4915208 | tf_op jit(solution)/shard_map/ppermute | solution.py:632
  104.8 0.8 pad_maximum_fusion.1
  105.6 1.6 collective-permute-start.3
  107.2 0.1 copy.16.faces
  107.2 8.4 %collective-permute-done.3 = f32[2,328,128]{2,1,0:T(8,128)} collective-permute-done((f32[2,328,128]{2,1,0:T(8,128)}, f32[2,328,128]{2,1,0:T(8,128)}, u32[]{:S(2)}, u32[]{:S(2)}) %collective-permute-start.3) | collective-permute-done | bytes 335904 | tf_op jit(solution)/shard_map/ppermute | solution.py:182
  115.7 1.0 pad_maximum_fusion.held.rest_2_
  116.7 0.0 copy-start.4
  116.7 0.6 pick_ends.1
  117.4 1.6 collective-permute-start.4
  118.9 0.0 collective-permute-done.6.outer.rest_7_
  118.9 0.0 copy-start.1
  118.9 1.7 %copy-done.1 = f32[5,8,64,256]{3,2,1,0:T(8,128)S(1)} copy-done((f32[5,8,64,256]{3,2,1,0:T(8,128)S(1)}, f32[5,8,64,256]{3,2,1,0:T(8,128)}, u32[]{:S(2)}) %copy-start.1) | copy-done | bytes 2621464
  120.7 7.8 %first_sweep.1.rest_8_ = f32[5,12,64,256]{3,2,1,0:T(8,128)S(1)} custom-call(s32[1]{0:T(128)} %bitcast.even, f32[32,128]{1,0:T(8,128)S(1)} %pad.8.couplings.rest_0_, f32[5,8,64,256]{3,2,1,0:T(8,128)S(1)} %copy-done, f32[5,8,64,256]{3,2,1,0:T(8,128)S(1)} %copy-done.1, f32[5,5,64,256]{3,2,1,0:T(8,128)} %collective-permute-done.5.inner.rest_6_, ...), custom_call_target="tpu_custom_call" | custom-call | flops 7000000000 | bytes 16777216 | tf_op jit(solution)/shard_map/first_sweep/pallas_call | solution.py:467
  128.5 0.0 collective-permute-done.4.rest_3_
  128.6 0.0 copy-start.5
  128.6 0.0 copy-start.6
  128.6 14.2 %last_sweeps.1 = (f32[5,8,64,256]{3,2,1,0:T(8,128)}, f32[3,8,256]{2,1,0:T(8,128)S(1)}) custom-call(s32[1]{0:T(128)} %bitcast.even, s32[1]{0:T(128)} %bitcast.1.me, s32[8,2]{1,0:T(8,128)S(1)} %copy.16.faces, f32[32,128]{1,0:T(8,128)S(1)} %pad.8.couplings.rest_0_, f32[2,5,64,128]{3,2,1,0:T(8,128)S(1)} %get-tuple-element.12.rest_1_, ...), custom_call_target="tpu_custom_call" | custom-call | flops 11000000512 | bytes 16777216 | tf_op jit(solution)/shard_map/last_sweeps/pallas_call | solution.py:513
  142.8 4.2 %scatter_points.1 = f32[3,48,256]{2,1,0:T(8,128)S(1)} custom-call(f32[3,8,256]{2,1,0:T(8,128)S(1)} %get-tuple-element.21.sens, f32[8,8,256]{2,1,0:T(8,128)S(1)} %copy-done.5, s32[8,8,256]{2,1,0:T(8,128)S(1)} %copy-done.6), custom_call_target="tpu_custom_call" | custom-call | flops 4000000000 | bytes 1048576 | tf_op jit(solution)/shard_map/scatter_points/pallas_call | solution.py:581
  147.1 5.0 %collective-permute-start.7 = (f32[3,48,128]{2,1,0:T(8,128)S(1)}, f32[3,48,128]{2,1,0:T(8,128)S(1)}, u32[]{:S(2)}, u32[]{:S(2)}) collective-permute-start(f32[3,48,128]{2,1,0:T(8,128)S(1)} %constant_dynamic-slice_fusion.5), channel_id=1, source_target_pairs={{0,1},{1,0},{2,3},{3,2},{4,5},{5,4},{6,7},{7,6},{8,9},{9,8},{10,11... | collective-permute-start | bytes 221192 | tf_op jit(solution)/shard_map/ppermute | solution.py:605
  152.0 0.9 collective-permute-done.7
  153.0 2.0 %collective-permute-start.8 = (f32[3,24,128]{2,1,0:T(8,128)S(1)}, f32[3,24,128]{2,1,0:T(8,128)S(1)}, u32[]{:S(2)}, u32[]{:S(2)}) collective-permute-start(f32[3,24,128]{2,1,0:T(8,128)S(1)} %constant_dynamic-slice_fusion.4), channel_id=1, source_target_pairs={{0,2},{1,3},{2,0},{3,1},{4,6},{5,7},{6,4},{7,5},{8,10},{9,11},{10,... | collective-permute-start | bytes 110600 | tf_op jit(solution)/shard_map/ppermute | solution.py:605
  155.0 2.0 %collective-permute-done.8 = f32[3,24,128]{2,1,0:T(8,128)S(1)} collective-permute-done((f32[3,24,128]{2,1,0:T(8,128)S(1)}, f32[3,24,128]{2,1,0:T(8,128)S(1)}, u32[]{:S(2)}, u32[]{:S(2)}) %collective-permute-start.8) | collective-permute-done | bytes 36896 | tf_op jit(solution)/shard_map/ppermute | solution.py:605
  157.0 1.5 collective-permute-start.9
  158.6 2.3 %collective-permute-done.9 = f32[3,12,128]{2,1,0:T(8,128)S(1)} collective-permute-done((f32[3,12,128]{2,1,0:T(8,128)S(1)}, f32[3,12,128]{2,1,0:T(8,128)S(1)}, u32[]{:S(2)}, u32[]{:S(2)}) %collective-permute-start.9) | collective-permute-done | bytes 18464 | tf_op jit(solution)/shard_map/ppermute | solution.py:605
  160.9 0.4 collective-permute-start.10
  161.3 1.6 collective-permute-start.11
  162.9 2.5 %collective-permute-start.12 = (f32[3,3,128]{2,1,0:T(4,128)S(1)}, f32[3,3,128]{2,1,0:T(4,128)S(1)}, u32[]{:S(2)}, u32[]{:S(2)}) collective-permute-start(f32[3,3,128]{2,1,0:T(4,128)S(1)} %get-tuple-element.23), channel_id=1, source_target_pairs={{0,24},{4,28},{8,16},{12,20},{16,8},{20,12},{24,0},{28,4},{1,25},{... | collective-permute-start | bytes 13832 | tf_op jit(solution)/shard_map/ppermute | solution.py:620
  165.4 0.1 collective-permute-done.10
  165.5 0.0 collective-permute-done.11
  165.5 2.8 %collective-permute-done.12 = f32[3,3,128]{2,1,0:T(4,128)S(1)} collective-permute-done((f32[3,3,128]{2,1,0:T(4,128)S(1)}, f32[3,3,128]{2,1,0:T(4,128)S(1)}, u32[]{:S(2)}, u32[]{:S(2)}) %collective-permute-start.12) | collective-permute-done | bytes 4640 | tf_op jit(solution)/shard_map/ppermute | solution.py:620
  168.4 0.6 copy.21
  (22 shorter events, 0.1 us)
Async XLA Ops:
  0.6 10.5 %copy-start.7 = (f32[1,6,5,5]{1,0,3,2:T(1,128)S(1)}, f32[1,6,5,5]{1,0,3,2:T(1,128)}, u32[]{:S(2)}) copy-start(f32[1,6,5,5]{1,0,3,2:T(1,128)} %param.9) | copy-start | bytes 1804
  6.0 5.5 %collective-permute-start.1 = (f32[2,5,64,128]{3,2,1,0:T(8,128)}, f32[2,5,64,128]{3,2,1,0:T(8,128)S(1)}, u32[]{:S(2)}, u32[]{:S(2)}) collective-permute-start(f32[2,5,64,128]{3,2,1,0:T(8,128)} %chord_ends.1.own), channel_id=1, source_target_pairs={{1,2},{2,1},{5,6},{6,5},{9,10},{10,9},{13,14},{14,13},{17,18},{18,... | collective-permute-start | bytes 983048 | tf_op jit(solution)/shard_map/ppermute | solution.py:632
  6.7 5.8 %collective-permute-start = (f32[2,5,64,128]{3,2,1,0:T(8,128)}, f32[2,5,64,128]{3,2,1,0:T(8,128)S(1)}, u32[]{:S(2)}, u32[]{:S(2)}) collective-permute-start(f32[2,5,64,128]{3,2,1,0:T(8,128)} %chord_ends.1.own), channel_id=1, source_target_pairs={{0,1},{1,0},{2,3},{3,2},{4,5},{5,4},{6,7},{7,6},{8,9},{9,8},{10,11... | collective-permute-start | bytes 983048 | tf_op jit(solution)/shard_map/ppermute | solution.py:632
  12.6 1.0 copy-start.3
  14.0 93.1 %copy-start.8 = (s32[8,2]{0,1:T(2,128)S(1)}, s32[8,2]{0,1:T(2,128)}, u32[]{:S(2)}) copy-start(s32[8,2]{0,1:T(2,128)} %param.10) | copy-start | bytes 196
  14.0 85.3 %collective-permute-start.2 = (f32[1,328,128]{2,1,0:T(8,128)S(1)}, f32[1,328,128]{2,1,0:T(8,128)S(1)}, u32[]{:S(2)}, u32[]{:S(2)}) collective-permute-start(f32[1,328,128]{2,1,0:T(8,128)S(1)} %bitcast.8), channel_id=1, source_target_pairs={{0,16},{4,20},{8,24},{12,28},{16,0},{20,4},{24,8},{28,12},{1,17},{... | collective-permute-start | bytes 503816 | tf_op jit(solution)/shard_map/ppermute | solution.py:182
  97.4 21.6 %copy-start = (f32[5,8,64,256]{3,2,1,0:T(8,128)S(1)}, f32[5,8,64,256]{3,2,1,0:T(8,128)}, u32[]{:S(2)}) copy-start(f32[5,8,64,256]{3,2,1,0:T(8,128)} %rest_4_.1) | copy-start | bytes 7864324
  97.4 21.6 %collective-permute-start.6 = (f32[5,5,64,256]{3,2,1,0:T(8,128)}, f32[5,5,64,256]{3,2,1,0:T(8,128)}, u32[]{:S(2)}, u32[]{:S(2)}) collective-permute-start(f32[5,5,64,256]{3,2,1,0:T(8,128)} %get-tuple-element.18), channel_id=1, source_target_pairs={{1,2},{2,1},{5,6},{6,5},{9,10},{10,9},{13,14},{14,13},{17,18},{18,... | collective-permute-start | bytes 4915208 | tf_op jit(solution)/shard_map/ppermute | solution.py:632
  99.3 19.6 %collective-permute-start.5 = (f32[5,5,64,256]{3,2,1,0:T(8,128)}, f32[5,5,64,256]{3,2,1,0:T(8,128)}, u32[]{:S(2)}, u32[]{:S(2)}) collective-permute-start(f32[5,5,64,256]{3,2,1,0:T(8,128)} %get-tuple-element.16), channel_id=1, source_target_pairs={{0,1},{1,0},{2,3},{3,2},{4,5},{5,4},{6,7},{7,6},{8,9},{9,8},{10,11... | collective-permute-start | bytes 4915208 | tf_op jit(solution)/shard_map/ppermute | solution.py:632
  105.6 10.1 %collective-permute-start.3 = (f32[2,328,128]{2,1,0:T(8,128)}, f32[2,328,128]{2,1,0:T(8,128)}, u32[]{:S(2)}, u32[]{:S(2)}) collective-permute-start(f32[2,328,128]{2,1,0:T(8,128)} %pad_maximum_fusion.1), channel_id=1, source_target_pairs={{0,8},{4,12},{8,0},{12,4},{16,24},{20,28},{24,16},{28,20},{1,9},{5... | collective-permute-start | bytes 1007624 | tf_op jit(solution)/shard_map/ppermute | solution.py:182
  116.7 11.8 %copy-start.4 = (f32[3,5,2,8,256]{4,3,2,1,0:T(8,128)S(1)}, f32[3,5,2,8,256]{4,3,2,1,0:T(8,128)}, u32[]{:S(2)}) copy-start(f32[3,5,2,8,256]{4,3,2,1,0:T(8,128)} %rest_9_.1) | copy-start | bytes 737284
  117.4 11.2 %collective-permute-start.4 = (f32[328,128]{1,0:T(8,128)S(1)}, f32[328,128]{1,0:T(8,128)S(1)}, u32[]{:S(2)}, u32[]{:S(2)}) collective-permute-start(f32[328,128]{1,0:T(8,128)S(1)} %pick_ends.1), channel_id=1, source_target_pairs={{0,4},{4,0},{8,12},{12,8},{16,20},{20,16},{24,28},{28,24},{1,5},{5... | collective-permute-start | bytes 503816 | tf_op jit(solution)/shard_map/ppermute | solution.py:194
  118.9 1.7 %copy-start.1 = (f32[5,8,64,256]{3,2,1,0:T(8,128)S(1)}, f32[5,8,64,256]{3,2,1,0:T(8,128)}, u32[]{:S(2)}) copy-start(f32[5,8,64,256]{3,2,1,0:T(8,128)} %rest_5_.1) | copy-start | bytes 7864324
  120.7 7.9 %copy-start.2 = (f32[5,8,64,256]{3,2,1,0:T(8,128)S(1)}, f32[5,8,64,256]{3,2,1,0:T(8,128)}, u32[]{:S(2)}) copy-start(f32[5,8,64,256]{3,2,1,0:T(8,128)} %rest_5_.1) | copy-start | bytes 7864324
  128.6 14.2 %copy-start.5 = (f32[8,8,256]{2,1,0:T(8,128)S(1)}, f32[8,8,256]{2,1,0:T(8,128)}, u32[]{:S(2)}) copy-start(f32[8,8,256]{2,1,0:T(8,128)} %weight.1) | copy-start | bytes 196612
  128.6 14.2 %copy-start.6 = (s32[8,8,256]{2,1,0:T(8,128)S(1)}, s32[8,8,256]{2,1,0:T(8,128)}, u32[]{:S(2)}) copy-start(s32[8,8,256]{2,1,0:T(8,128)} %ids.1) | copy-start | bytes 196612
  147.1 5.9 %collective-permute-start.7 = (f32[3,48,128]{2,1,0:T(8,128)S(1)}, f32[3,48,128]{2,1,0:T(8,128)S(1)}, u32[]{:S(2)}, u32[]{:S(2)}) collective-permute-start(f32[3,48,128]{2,1,0:T(8,128)S(1)} %constant_dynamic-slice_fusion.5), channel_id=1, source_target_pairs={{0,1},{1,0},{2,3},{3,2},{4,5},{5,4},{6,7},{7,6},{8,9},{9,8},{10,11... | collective-permute-start | bytes 221192 | tf_op jit(solution)/shard_map/ppermute | solution.py:605
  153.0 4.0 %collective-permute-start.8 = (f32[3,24,128]{2,1,0:T(8,128)S(1)}, f32[3,24,128]{2,1,0:T(8,128)S(1)}, u32[]{:S(2)}, u32[]{:S(2)}) collective-permute-start(f32[3,24,128]{2,1,0:T(8,128)S(1)} %constant_dynamic-slice_fusion.4), channel_id=1, source_target_pairs={{0,2},{1,3},{2,0},{3,1},{4,6},{5,7},{6,4},{7,5},{8,10},{9,11},{10,... | collective-permute-start | bytes 110600 | tf_op jit(solution)/shard_map/ppermute | solution.py:605
  157.0 3.9 %collective-permute-start.9 = (f32[3,12,128]{2,1,0:T(8,128)S(1)}, f32[3,12,128]{2,1,0:T(8,128)S(1)}, u32[]{:S(2)}, u32[]{:S(2)}) collective-permute-start(f32[3,12,128]{2,1,0:T(8,128)S(1)} %constant_dynamic-slice_fusion.3), channel_id=1, source_target_pairs={{0,4},{4,0},{8,12},{12,8},{16,20},{20,16},{24,28},{28,24},{1,5},{5... | collective-permute-start | bytes 55304 | tf_op jit(solution)/shard_map/ppermute | solution.py:605
  160.9 4.6 %collective-permute-start.10 = (f32[3,3,128]{2,1,0:T(4,128)S(1)}, f32[3,3,128]{2,1,0:T(4,128)S(1)}, u32[]{:S(2)}, u32[]{:S(2)}) collective-permute-start(f32[3,3,128]{2,1,0:T(4,128)S(1)} %get-tuple-element.22), channel_id=1, source_target_pairs={{0,16},{4,20},{8,24},{12,28},{16,0},{20,4},{24,8},{28,12},{1,17},{... | collective-permute-start | bytes 13832 | tf_op jit(solution)/shard_map/ppermute | solution.py:620
  161.3 4.2 %collective-permute-start.11 = (f32[3,3,128]{2,1,0:T(4,128)S(1)}, f32[3,3,128]{2,1,0:T(4,128)S(1)}, u32[]{:S(2)}, u32[]{:S(2)}) collective-permute-start(f32[3,3,128]{2,1,0:T(4,128)S(1)} %get-tuple-element.24), channel_id=1, source_target_pairs={{0,8},{4,12},{8,0},{12,4},{16,24},{20,28},{24,16},{28,20},{1,9},{5... | collective-permute-start | bytes 13832 | tf_op jit(solution)/shard_map/ppermute | solution.py:620
  162.9 5.4 %collective-permute-start.12 = (f32[3,3,128]{2,1,0:T(4,128)S(1)}, f32[3,3,128]{2,1,0:T(4,128)S(1)}, u32[]{:S(2)}, u32[]{:S(2)}) collective-permute-start(f32[3,3,128]{2,1,0:T(4,128)S(1)} %get-tuple-element.23), channel_id=1, source_target_pairs={{0,24},{4,28},{8,16},{12,20},{16,8},{20,12},{24,0},{28,4},{1,25},{... | collective-permute-start | bytes 13832 | tf_op jit(solution)/shard_map/ppermute | solution.py:620

commit v7 on v6

--- a/solution.py
+++ b/solution.py
@@ -45,45 +45,76 @@
     return total
 
 
-def ends_kernel(src, inv, tile):
-    for f, field in enumerate((src, inv)):
-        tile[f] = chord_tile([(s, field[:, s]) for s in range(field.shape[1])])
-
-
-def chord_ends(source, inv_diag):
+def ends_kernel(src, inv, cpl, tile, packet):
+    depth = src.shape[2]
+    tiles = [chord_tile([(s, field[:, s]) for s in range(field.shape[1])]) for field in (src, inv)]
+    for f in range(2):
+        tile[f] = tiles[f]
+    lane = lane_iota((1, LANES))
+    place = lane & (HALF - 1)
+    is_src = place - COLS * ((place * 43) >> 8) < 3
+    x, y = tiles[0][0], tiles[1][0]
+    v = pl.program_id(0)
+    packet[pl.ds(pl.multiple_of(v * depth, depth), depth), :] = jnp.where(
+        lane >= HALF,
+        jnp.where(is_src, pltpu.roll(x, LANES - 2, 1), pltpu.roll(y, 1, 1)),
+        jnp.where(is_src, x, pltpu.roll(y, 3, 1)),
+    )
+
+    @pl.when(v == 0)
+    def _():
+        rows = packet.shape[0]
+        packet[rows - 8 : rows, :] = cpl[...]
+
+
+def chord_ends(source, inv_diag, cpl):
     nvar, spans, depth, chord = source.shape
     field = pl.BlockSpec((1, spans, depth, chord), lambda v: (v, 0, 0, 0))
+    rows = nvar * depth + 8
     return pl.pallas_call(
         ends_kernel,
         grid=(nvar,),
-        in_specs=[field, field],
-        out_specs=pl.BlockSpec((2, 1, depth, LANES), lambda v: (0, v, 0, 0)),
-        out_shape=jax.ShapeDtypeStruct((2, nvar, depth, LANES), jnp.float32),
+        in_specs=[field, field, pl.BlockSpec((8, LANES), lambda v: (0, 0))],
+        out_specs=[
+            pl.BlockSpec((2, 1, depth, LANES), lambda v: (0, v, 0, 0)),
+            pl.BlockSpec((rows, LANES), lambda v: (0, 0)),
+        ],
+        out_shape=[
+            jax.ShapeDtypeStruct((2, nvar, depth, LANES), jnp.float32),
+            jax.ShapeDtypeStruct((rows, LANES), jnp.float32),
+        ],
         compiler_params=pltpu.CompilerParams(vmem_limit_bytes=56 * MIB),
         name="chord_ends",
-    )(source, inv_diag)
+    )(source, inv_diag, cpl)
 
 
 def layers_kernel(even, src, inv, inner, outer, held, sems):
     spans = src.shape[1]
-    copies, last = [], []
+    loads, stores = [], []
     for side, (out, up) in enumerate(((inner, even[0]), (outer, 1 - even[0]))):
         for j in range(DEEP):
             s = jnp.where(up == 1, spans - 1 - j, j)
             for f, field in enumerate((src, inv)):
-                to = out.at[f * (DEEP - 1) + j] if j < DEEP - 1 else held.at[side, f]
-                copy = pltpu.make_async_copy(field.at[:, s], to, sems.at[side, f, j])
-                copy.start()
-                (copies if j < DEEP - 1 else last).append(copy)
-    for copy in last:
-        copy.wait()
-    for side, out in enumerate((inner, outer)):
-        held[side, 0] = held[side, 0] * held[side, 1]
-        copy = pltpu.make_async_copy(held.at[side, 0], out.at[2 * (DEEP - 1)], sems.at[side, 0, DEEP])
-        copy.start()
-        copies.append(copy)
-    for copy in copies:
-        copy.wait()
+                at = f * DEEP + j
+                load = pltpu.make_async_copy(field.at[:, s], held.at[side, at], sems.at[0, side, at])
+                load.start()
+                loads.append((side, at, load))
+    for side, at, load in loads:
+        load.wait()
+        f, j = at // DEEP, at % DEEP
+        if j < DEEP - 1:
+            to = f * (DEEP - 1) + j
+        elif f == 0:
+            continue
+        else:
+            held[side, at] = held[side, j] * held[side, at]
+            to = 2 * (DEEP - 1)
+        out = (inner, outer)[side]
+        store = pltpu.make_async_copy(held.at[side, at], out.at[to], sems.at[1, side, at])
+        store.start()
+        stores.append(store)
+    for store in stores:
+        store.wait()
 
 
 def span_layers(even, source, inv_diag):
@@ -95,64 +126,13 @@
         out_specs=[ANY, ANY],
         out_shape=[shape, shape],
         scratch_shapes=[
-            pltpu.VMEM((2, 2, nvar, depth, chord), jnp.float32),
-            pltpu.SemaphoreType.DMA((2, 2, DEEP + 1)),
+            pltpu.VMEM((2, 2 * DEEP, nvar, depth, chord), jnp.float32),
+            pltpu.SemaphoreType.DMA((2, 2, 2 * DEEP)),
         ],
         compiler_params=pltpu.CompilerParams(vmem_limit_bytes=56 * MIB),
         cost_estimate=pl.CostEstimate(flops=0, bytes_accessed=8 * MIB, transcendentals=0),
         name="span_layers",
     )(even, source, inv_diag)
-
-
-def merge(low, high, own, packet, full, depth):
-    nvar = own.shape[1]
-    lane = lane_iota((1, 1, LANES))
-    place = lane & (HALF - 1)
-    first, last = place < COLS, (place >= lane_base(8)) & (place < lane_base(9))
-    src, inv = [
-        jnp.where(first, pltpu.roll(low[f], LANES - 8 * COLS, 2), jnp.where(last, pltpu.roll(high[f], 8 * COLS, 2), own[f]))
-        for f in range(2)
-    ]
-    full[0] = src
-    full[1] = inv
-    slot = place - COLS * ((place * 43) >> 8)
-    is_src = slot < 3
-    side = lane >= HALF
-    tile = jnp.where(
-        side,
-        jnp.where(is_src, pltpu.roll(src, LANES - 2, 2), pltpu.roll(inv, 1, 2)),
-        jnp.where(is_src, src, pltpu.roll(inv, 3, 2)),
-    )
-    far = ((low[0], 60 - 44), (low[1], 61 - 44), (high[0], 62 - 14), (high[1], 63 - 14))
-    for at, (part, shift) in enumerate(far):
-        tile = jnp.where(place == 60 + at, pltpu.roll(part, shift, 2), tile)
-    for v in range(nvar):
-        packet[v * depth : (v + 1) * depth, :] = tile[v]
-
-
-def merge_kernel(even, own, inner, outer, cpl, packet, full):
-    depth = own.shape[2]
-    up = jnp.full((1, 1, 1), even[0], jnp.int32) == 1
-    low = [jnp.where(up, outer[f], inner[f]) for f in range(2)]
-    high = [jnp.where(up, inner[f], outer[f]) for f in range(2)]
-    merge(low, high, own, packet, full, depth)
-    rows = own.shape[1] * depth
-    packet[rows : rows + 8, :] = cpl[...]
-
-
-def merge_ends(even, own, inner, outer, cpl):
-    _, nvar, depth, _ = own.shape
-    return pl.pallas_call(
-        merge_kernel,
-        in_specs=[SMEM, VMEM, VMEM, VMEM, VMEM],
-        out_specs=[VMEM, VMEM],
-        out_shape=[
-            jax.ShapeDtypeStruct((nvar * depth + 8, LANES), jnp.float32),
-            jax.ShapeDtypeStruct(own.shape, jnp.float32),
-        ],
-        compiler_params=pltpu.CompilerParams(vmem_limit_bytes=12 * MIB),
-        name="merge_ends",
-    )(even, own, inner, outer, cpl)
 
 
 def exchange_masks(count):
@@ -172,6 +152,14 @@
     low, _ = place_of(me[0], faces[other, 0], masks)
     high, _ = place_of(me[0], faces[other, 1], masks)
     out[...] = jnp.where(lane_iota((1, LANES)) < HALF, held[low], held[high])
+
+
+def choose_kernel(masks, me, faces, held, given, out):
+    low, low_held = place_of(me[0], faces[me[0], 0], masks)
+    high, high_held = place_of(me[0], faces[me[0], 1], masks)
+    left = lane_iota((1, LANES)) < HALF
+    keep = jnp.where(left, low_held, high_held) == 1
+    out[...] = jnp.where(keep, jnp.where(left, held[low], held[high]), given[...])
 
 
 def route_ends(packet, me, face_map):
@@ -182,16 +170,21 @@
         other = lax.ppermute(held, "blk", [(i, i ^ mask) for i in range(count)])
         first = other if first is None else first
         held = jnp.concatenate([held, other], 0)
-    picked = pl.pallas_call(
-        functools.partial(pick_kernel, masks),
-        in_specs=[SMEM, SMEM, VMEM],
-        out_specs=VMEM,
-        out_shape=jax.ShapeDtypeStruct(packet.shape, packet.dtype),
-        compiler_params=pltpu.CompilerParams(vmem_limit_bytes=12 * MIB),
-        name="pick_ends",
-    )(me, face_map, held)
+
+    def call(kernel, name, *operands):
+        return pl.pallas_call(
+            functools.partial(kernel, masks),
+            in_specs=[SMEM, SMEM] + [VMEM] * len(operands),
+            out_specs=VMEM,
+            out_shape=jax.ShapeDtypeStruct(packet.shape, packet.dtype),
+            compiler_params=pltpu.CompilerParams(vmem_limit_bytes=12 * MIB),
+            name=name,
+        )(me, face_map, *operands)
+
+    picked = call(pick_kernel, "pick_ends", held)
     last = masks[-1]
-    return held, lax.ppermute(picked, "blk", [(i, i ^ last) for i in range(count)]), first
+    given = lax.ppermute(picked, "blk", [(i, i ^ last) for i in range(count)])
+    return call(choose_kernel, "choose_ends", held, given), held, first
 
 
 def expand_couplings(couplings, wide):
@@ -217,7 +210,7 @@
     wide[...] = jnp.where((r & 15) == (c & 15), both, 0.0).astype(jnp.bfloat16)
 
 
-def ribbon_sweeps(depth, full, given, mine, scalars, faces):
+def ribbon_sweeps(depth, up, own, near_in, near_out, given, given_in, given_out, mine, scalars, faces):
     nvar = 5
     lane = lane_iota((1, LANES))
     place = lane & (HALF - 1)
@@ -225,19 +218,43 @@
     side = lane >= HALF
     inside = (place < lane_base(9)) & (slot < 5)
     ghost = (jnp.where(side, bit(slot >= 2), bit(slot <= 2)) > 0.5) & inside
-    own = inside & jnp.logical_not(ghost)
+    columns = inside & jnp.logical_not(ghost)
     before, beyond = place == 60, place == 62
-
-    def field(f, v):
-        got = given(v * depth, depth)
-        turns = ((0, 2, 64, 0), (LANES - 3, LANES - 1, 63, LANES - 1))[f]
-        moved = [pltpu.roll(got, t, 1) if t else got for t in turns]
-        x = jnp.where(ghost, jnp.where(side, moved[1], moved[0]), 0.0)
-        x = jnp.where(before, moved[2], jnp.where(beyond, moved[3], x))
-        return jnp.where(own, full[f, v], x)
-
-    src = [field(0, v) for v in range(nvar)]
-    inv = [field(1, v) for v in range(nvar)]
+    first = place < COLS
+    last = (place >= lane_base(8)) & (place < lane_base(9))
+    up3 = jnp.full((1, 1, 1), up, jnp.int32) == 1
+    up2 = jnp.full((1, 1), up, jnp.int32) == 1
+
+    def moved(x, by):
+        return pltpu.roll(x, by % LANES, 1) if by % LANES else x
+
+    def packet(v):
+        at = slice(v * depth, (v + 1) * depth)
+        a, b = given_in[at, :], given_out[at, :]
+        low, high = jnp.where(up2, b, a), jnp.where(up2, a, b)
+        x = given[at, :]
+        x = jnp.where(first, moved(low, -8 * COLS), jnp.where(last, moved(high, 8 * COLS), x))
+        x = jnp.where(place == 60, jnp.where(side, moved(low, 18), moved(low, 16)), x)
+        x = jnp.where(place == 61, jnp.where(side, moved(low, 16), moved(low, 14)), x)
+        x = jnp.where(place == 62, jnp.where(side, moved(high, 50), moved(high, 48)), x)
+        return jnp.where(place == 63, jnp.where(side, moved(high, 48), moved(high, 46)), x)
+
+    edge_low, edge_high = [], []
+    for f in range(2):
+        a, b = near_in[f], near_out[f]
+        edge_low.append(chord_tile([(-1, jnp.where(up3, b, a))]))
+        edge_high.append(chord_tile([(8, jnp.where(up3, a, b))]))
+
+    def field(f, v, got):
+        turns = ((0, 2, 64, 0), (-3, -1, 63, -1))[f]
+        x = jnp.where(ghost, jnp.where(side, moved(got, turns[1]), moved(got, turns[0])), 0.0)
+        x = jnp.where(before, moved(got, turns[2]), jnp.where(beyond, moved(got, turns[3]), x))
+        mid = jnp.where(first, edge_low[f][v], jnp.where(last, edge_high[f][v], own[f, v]))
+        return jnp.where(columns, mid, x)
+
+    packets = [packet(v) for v in range(nvar)]
+    src = [field(0, v, packets[v]) for v in range(nvar)]
+    inv = [field(1, v, packets[v]) for v in range(nvar)]
     one = lax.broadcasted_iota(jnp.int32, (152, 8), 0)
     pick = bit((one >> 6) == lax.broadcasted_iota(jnp.int32, (152, 8), 1))
     index = lax.broadcasted_iota(jnp.int32, (152, LANES), 0)
@@ -251,7 +268,7 @@
 
     own_rows = spread(mine[...])
     scalars[0] = own_rows
-    scalars[1] = jnp.where(ghost, spread(given(nvar * depth, 8)), own_rows)
+    scalars[1] = jnp.where(ghost, spread(given[nvar * depth : nvar * depth + 8, :]), own_rows)
     mixed = [scalars[1, i : i + 1, :] for i in range(150)]
     own_c = {i: scalars[0, i : i + 1, :] for i in range(100, 150)}
     high_face = (side & jnp.logical_not(lane == HALF + 60)) | (lane == 60)
@@ -324,7 +341,7 @@
         inv[:, layers - 1] = ones
     expand_couplings(couplings[...], wide)
     if ribbon is not None:
-        ribbon_sweeps(rows, *ribbon, scalars, faces)
+        ribbon_sweeps(rows, even[0], *ribbon, scalars, faces)
 
     def face_tiles(n, s, at):
         face = faces[n, :, at]
@@ -476,21 +493,16 @@
     )(even, couplings, source, inv_diag, inner, outer)
 
 
-def last_kernel(masks, even, me, faces, *rest):
-    couplings, full, held, given, src_in, inv_in, inner, outer, p_in, jac, out, sens, *scratch = rest
-    low, low_held = place_of(me[0], faces[me[0], 0], masks)
-    high, high_held = place_of(me[0], faces[me[0], 1], masks)
-    left = lane_iota((1, LANES)) < HALF
-    keep = jnp.where(left, low_held, high_held) == 1
-
-    def ends(first, count):
-        at = pl.ds(first, count)
-        return jnp.where(keep, jnp.where(left, held[low, at], held[high, at]), given[at])
-
-    nvar, spans, depth, chord = out.shape
-    mine = held.at[0, nvar * depth : nvar * depth + 8]
+def last_kernel(even, *rest):
+    couplings, cpl, own, in_src, in_inv, out_src, out_inv, given, given_in, given_out, *rest = rest
+    src_in, inv_in, inner, outer, p_in, jac, out, sens, *scratch = rest
+    nvar, spans, _, chord = out.shape
+    near_in, near_out = (in_src.at[0], in_inv.at[0]), (out_src.at[0], out_inv.at[0])
+    ribbon = (
+        own, [r[...] for r in near_in], [r[...] for r in near_out], given, given_in, given_out, cpl,
+    )
     result, done = run_sweeps(
-        [1, 2], even, couplings, (full, ends, mine), src_in, inv_in, inner, outer, p_in, out, scratch
+        [1, 2], even, couplings, ribbon, src_in, inv_in, inner, outer, p_in, out, scratch
     )
     layer = []
     for v in range(nvar):
@@ -507,39 +519,47 @@
     done()
 
 
-def last_sweeps(even, me, face_map, couplings, full, held, given, source, inv_diag, inner, outer, p, jac):
+def last_sweeps(even, couplings, cpl, own, givens, source, inv_diag, inner, outer, p, jac):
     nvar, spans, depth, chord = source.shape
-    masks = exchange_masks(lax.axis_size("blk"))
+
+    def whole(a):
+        return pl.BlockSpec(a.shape, lambda i: (0,) * a.ndim)
+
+    def piece(j):
+        return pl.BlockSpec((1, nvar, depth, chord), lambda i: (j, 0, 0, 0))
+
+    sens = (jac.shape[0], spans, chord)
     return pl.pallas_call(
-        functools.partial(last_kernel, masks),
-        in_specs=[SMEM, SMEM, SMEM, VMEM, VMEM, VMEM, VMEM, ANY, ANY, ANY, ANY, ANY, VMEM],
-        out_specs=[ANY, VMEM],
+        last_kernel,
+        grid=(1,),
+        in_specs=[SMEM, whole(couplings), whole(cpl), whole(own)]
+        + [piece(0), piece(DEEP - 1)] * 2
+        + [whole(a) for a in givens]
+        + [ANY] * 5
+        + [whole(jac)],
+        out_specs=[ANY, pl.BlockSpec(sens, lambda i: (0, 0, 0))],
         out_shape=[
             jax.ShapeDtypeStruct(source.shape, jnp.float32),
-            jax.ShapeDtypeStruct((jac.shape[0], spans, chord), jnp.float32),
+            jax.ShapeDtypeStruct(sens, jnp.float32),
         ],
         scratch_shapes=sweep_scratch(nvar, spans, chord, depth),
-        compiler_params=pltpu.CompilerParams(vmem_limit_bytes=32 * MIB),
+        compiler_params=pltpu.CompilerParams(vmem_limit_bytes=40 * MIB),
         cost_estimate=pl.CostEstimate(flops=11 * 10**9, bytes_accessed=16 * MIB, transcendentals=0),
         name="last_sweeps",
-    )(even, me, face_map, couplings, full, held, given, source, inv_diag, inner, outer, p, jac)
-
-
-def point_indices(bits, ids, hi_index, lo_index):
+    )(even, couplings, cpl, own, inner, inner, outer, outer, *givens, source, inv_diag, inner, outer, p, jac)
+
+
+def point_indices(ids, hi_index, lo_index):
     point = ids[...]
     line = point >> 7
     device = (line * 171) >> 9
     third = line - 3 * device
-    pair = device >> 1
-    turned = jnp.zeros_like(pair)
-    for b in range(bits):
-        turned = turned | (((pair >> b) & 1) << (bits - 1 - b))
-    hi_index[...] = jnp.where(point < 0, -1, 3 * turned + third)
+    hi_index[...] = jnp.where(point < 0, -1, 3 * (device >> 1) + third)
     lo_index[...] = ((device & 1) << 7) + (point & 127)
 
 
-def scatter_kernel(bits, sens, weight, ids, out, hi_index, lo_index):
-    point_indices(bits, ids, hi_index, lo_index)
+def scatter_kernel(sens, weight, ids, out, hi_index, lo_index):
+    point_indices(ids, hi_index, lo_index)
     dims, spans, chord = sens.shape
     slots = weight.shape[0]
     tall = out.shape[1]
@@ -576,10 +596,9 @@
 
 def scatter_points(sens, weight, ids, n_dev):
     tall = -(-(n_dev // 2 * 3) // 16) * 16
-    bits = (n_dev // 2).bit_length() - 1
     shape = (sens.shape[0], tall, 2 * LANES)
     return pl.pallas_call(
-        functools.partial(scatter_kernel, bits),
+        scatter_kernel,
         in_specs=[VMEM, VMEM, VMEM],
         out_specs=VMEM,
         out_shape=jax.ShapeDtypeStruct(shape, jnp.float32),
@@ -590,35 +609,11 @@
     )(sens, weight, ids)
 
 
-def halve_points(partial, n_dev):
-    n_blk, n_sub = lax.axis_size("blk"), lax.axis_size("sub")
-    blk, sub = lax.axis_index("blk"), lax.axis_index("sub")
-    partial = partial[:, : n_dev // 2 * 3]
-    steps = [("sub", sub, n_sub, 1 << b) for b in range(n_sub.bit_length() - 1)]
-    steps += [("blk", blk, n_blk, 1 << b) for b in range(n_blk.bit_length() - 3)]
-    for number, (axis, me, count, mask) in enumerate(steps):
-        dim = 2 if number == 0 else 1
-        half = partial.shape[dim] // 2
-        mine = jnp.where((me & mask) != 0, half, 0)
-        keep = lax.dynamic_slice_in_dim(partial, mine, half, dim)
-        send = lax.dynamic_slice_in_dim(partial, half - mine, half, dim)
-        partial = keep + lax.ppermute(send, axis, [(i, i ^ mask) for i in range(count)])
-    return partial
-
-
-def quarter_points(partial):
-    count, me = lax.axis_size("blk"), lax.axis_index("blk")
-    late, last = count // 4, count // 2
-    rows = partial.shape[1] // 4
-
-    def quarter(device):
-        place = jnp.where((device & late) != 0, 2, 0) + jnp.where((device & last) != 0, 1, 0)
-        return lax.dynamic_slice_in_dim(partial, place * rows, rows, 1)
-
-    parts = [quarter(me)]
-    for mask in (last, late, late | last):
-        parts.append(lax.ppermute(quarter(me ^ mask), "blk", [(i, i ^ mask) for i in range(count)]))
-    return parts
+def reduce_points(partial, n_dev):
+    dims = partial.shape[0]
+    parts = partial[:, : n_dev // 2 * 3].reshape(dims, n_dev // 2, 3, 2, LANES)
+    parts = parts.transpose(1, 3, 0, 2, 4).reshape(n_dev, dims, 3 * LANES)
+    return lax.all_to_all(parts, ("blk", "sub"), 0, 0, tiled=True).sum(0)
 
 
 def ordered(x, *after):
@@ -641,20 +636,17 @@
     flat = jnp.pad(coupling[0].reshape(-1), (0, 8 * HALF - 6 * nvar * nvar)).reshape(8, HALF)
     cpl = jnp.concatenate([flat, flat], 1)
 
-    own = chord_ends(source, inv_diag)
-    tiles = swap_spans(own, own)
-    inner, outer = span_layers(ordered(even, own), source, inv_diag)
-    packet, full = merge_ends(even, own, *tiles, cpl)
-    held, given, first = route_ends(packet, me, face_map)
-    inner, outer = swap_spans(ordered(inner, first), ordered(outer, tiles[1]))
+    own, packet = chord_ends(source, inv_diag, cpl)
+    inner, outer = span_layers(ordered(even, packet), source, inv_diag)
+    given, held, first = route_ends(packet, me, face_map)
+    inner, outer = swap_spans(ordered(inner, first), ordered(outer, first))
     p = first_sweep(ordered(even, held), couplings, source, inv_diag, inner, outer)
+    givens = (given, *swap_spans(given, given))
     adjoint, sens = last_sweeps(
-        even, me, face_map, couplings, full, held, given, source, inv_diag, inner, outer, p, wall_jac
+        even, couplings, cpl, own, givens, source, inv_diag, inner, outer, p, wall_jac
     )
-    partial = halve_points(scatter_points(sens, ffd_weight, cp_ids, n_dev), n_dev)
-    parts = quarter_points(partial)
-    total = (parts[0] + parts[1]) + (parts[2] + parts[3])
-    return adjoint, total.reshape(total.shape[0], -1)
+    partial = scatter_points(sens, ffd_weight, cp_ids, n_dev)
+    return adjoint, reduce_points(partial, n_dev)
 
 
 def solution(mesh):

time: 169 us -> 89.6 us (0.53)
  Pallas kernels: 113 us -> 38.4 us
  starting transfers between devices: 31.2 us -> 13 us
  blocking collectives: 0 us -> 13.6 us
    pallas_call x1, Pallas kernels: 80.7 us -> 3.57 us  [span_layers(): pl.pallas_call(layers_kernel, in_specs=[SMEM, ANY, ANY], out_specs=[ANY,...]
    all_to_all x0 -> x1, blocking collectives: none -> 13.6 us  [reduce_points(): return lax.all_to_all(parts, ('blk', 'sub'), 0, 0, tiled=True).sum(0)]
    ppermute x7 -> x1, starting transfers between devices: 14.6 us -> 1.49 us  [route_ends(): given = lax.ppermute(picked, 'blk', [(i, i ^ last) for i in range(count)])]
    ppermute x2, starting transfers between devices: 9.82 us -> 4.15 us  [swap_spans(): lax.ppermute(inner, 'sub', pairs)]
    ppermute x2, waiting for transfers between devices: 8.44 us -> 13.6 us  [route_ends(): other = lax.ppermute(held, 'blk', [(i, i ^ mask) for i in range(count)])]
    ppermute x7 -> x1, waiting for transfers between devices: 8.2 us -> 4.08 us  [route_ends(): given = lax.ppermute(picked, 'blk', [(i, i ^ last) for i in range(count)])]
    pallas_call x5, Pallas kernels: 24.9 us -> 26.9 us  [the longest x1 15.2 us: last_sweeps(): pl.pallas_call(last_kernel, grid=(1,), in_specs=[SMEM, whole(couplings),...]
    unnamed x20 -> x23, local copies, waits for them, and re-layouts: 3.42 us -> 1.86 us
  transfers between devices with their start and end apart: 13 -> 7, of which waited for: 7 -> 3; matrix products, arithmetic and copies ran while one was open for 1% -> 1% of each run, Pallas kernels for 53% -> 15%
where the time goes in v7:
time: 89.6 us; the launch traced here: 89.1 us
  Pallas kernels  38.4 us (43%)
  waiting for transfers between devices  17.7 us (20%)
  blocking collectives  13.6 us (15%)
  starting transfers between devices  13 us (15%)
  local copies, waits for them, and re-layouts  3.21 us (4%)
  other arithmetic  2.4 us (3%)
    pallas_call x1, Pallas kernels, last_sweeps(): pl.pallas_call(last_kernel, grid=(1,), in_specs=[SMEM, whole(couplings),...  15.2 us
    all_to_all x1, blocking collectives, reduce_points(): return lax.all_to_all(parts, ('blk', 'sub'), 0, 0, tiled=True).sum(0)  13.6 us
    ppermute x2, waiting for transfers between devices, route_ends(): other = lax.ppermute(held, 'blk', [(i, i ^ mask) for i in range(count)])  13.6 us
    pallas_call x1, Pallas kernels, first_sweep(): pl.pallas_call(first_kernel, in_specs=[SMEM, VMEM, ANY, ANY, ANY, ANY], o...  7.84 us
    pallas_call x1, Pallas kernels, chord_ends(): pl.pallas_call(ends_kernel, grid=(nvar,), in_specs=[field, field, pl.Bloc...  5.68 us
    ppermute x2, starting transfers between devices, route_ends(): other = lax.ppermute(held, 'blk', [(i, i ^ mask) for i in range(count)])  4.88 us
    pallas_call x1, Pallas kernels, scatter_points(): pl.pallas_call(scatter_kernel, in_specs=[VMEM, VMEM, VMEM], out_specs=VME...  4.17 us
    ppermute x2, starting transfers between devices, swap_spans(): lax.ppermute(inner, 'sub', pairs)  4.15 us
  transfers between devices with their start and end apart: 7, of which 3 were waited for; matrix products, arithmetic and copies ran while one was open for 1% of the time, Pallas kernels for 15%

profile of v7, /device:TPU:0, one launch (start us, length us, event | category | flops | bytes accessed | tf_op | source)
XLA Modules:
  0.0 89.1 jit_solution(7397675176002718223)
XLA Ops:
  0.6 0.8 copy.25
  1.5 0.1 reshape_squeeze.7
  1.6 0.1 reshape.20
  1.7 0.7 pad_maximum_fusion.2.cpl.rest_1_
  2.3 5.7 %chord_ends.1 = (f32[2,5,64,128]{3,2,1,0:T(8,128)}, f32[328,128]{1,0:T(8,128)}) custom-call(f32[5,8,64,256]{3,2,1,0:T(8,128)} %rest_10_.1, f32[5,8,64,256]{3,2,1,0:T(8,128)} %rest_11_.1, f32[8,128]{1,0:T(8,128)} %pad_maximum_fusion.2.cpl.rest_1_), custom_call_target="tpu_custom_call" | custom-call | tf_op jit(solution)/shard_map/chord_ends/pallas_call | solution.py:74
  8.0 4.0 %collective-permute-start = (f32[1,328,128]{2,1,0:T(8,128)}, f32[1,328,128]{2,1,0:T(8,128)S(1)}, u32[]{:S(2)}, u32[]{:S(2)}) collective-permute-start(f32[1,328,128]{2,1,0:T(8,128)} %bitcast.9), channel_id=1, source_target_pairs={{0,16},{4,20},{8,24},{12,28},{16,0},{20,4},{24,8},{28,12},{1,17},{... | collective-permute-start | bytes 503816 | tf_op jit(solution)/shard_map/ppermute | solution.py:170
  12.1 3.6 %span_layers.1 = (f32[5,5,64,256]{3,2,1,0:T(8,128)}, f32[5,5,64,256]{3,2,1,0:T(8,128)}) custom-call(s32[1]{0:T(128)} %bitcast.even, f32[5,8,64,256]{3,2,1,0:T(8,128)} %rest_10_.1, f32[5,8,64,256]{3,2,1,0:T(8,128)} %rest_11_.1), custom_call_target="tpu_custom_call" | custom-call | bytes 8388608 | tf_op jit(solution)/shard_map/span_layers/pallas_call | solution.py:123
  15.6 0.0 copy-start
  15.6 4.5 %collective-permute-done = f32[1,328,128]{2,1,0:T(8,128)S(1)} collective-permute-done((f32[1,328,128]{2,1,0:T(8,128)}, f32[1,328,128]{2,1,0:T(8,128)S(1)}, u32[]{:S(2)}, u32[]{:S(2)}) %collective-permute-start) | collective-permute-done | bytes 167968 | tf_op jit(solution)/shard_map/ppermute | solution.py:170
  20.1 1.8 %collective-permute-start.2 = (f32[5,5,64,256]{3,2,1,0:T(8,128)}, f32[5,5,64,256]{3,2,1,0:T(8,128)}, u32[]{:S(2)}, u32[]{:S(2)}) collective-permute-start(f32[5,5,64,256]{3,2,1,0:T(8,128)} %get-tuple-element.18), channel_id=1, source_target_pairs={{1,2},{2,1},{5,6},{6,5},{9,10},{10,9},{13,14},{14,13},{17,18},{18,... | collective-permute-start | bytes 4915208 | tf_op jit(solution)/shard_map/ppermute | solution.py:627
  22.0 1.8 %collective-permute-start.1 = (f32[5,5,64,256]{3,2,1,0:T(8,128)}, f32[5,5,64,256]{3,2,1,0:T(8,128)}, u32[]{:S(2)}, u32[]{:S(2)}) collective-permute-start(f32[5,5,64,256]{3,2,1,0:T(8,128)} %get-tuple-element.16), channel_id=1, source_target_pairs={{0,1},{1,0},{2,3},{3,2},{4,5},{5,4},{6,7},{7,6},{8,9},{9,8},{10,11... | collective-permute-start | bytes 4915208 | tf_op jit(solution)/shard_map/ppermute | solution.py:627
  23.8 0.0 copy-done.8
  23.8 0.8 collective-permute-start.3
  24.7 0.0 copy-done.10
  24.7 0.1 copy.22.faces
  24.8 0.0 copy-done.9
  24.8 9.1 %collective-permute-done.3 = f32[2,328,128]{2,1,0:T(8,128)} collective-permute-done((f32[2,328,128]{2,1,0:T(8,128)S(1)}, f32[2,328,128]{2,1,0:T(8,128)}, u32[]{:S(2)}, u32[]{:S(2)}) %collective-permute-start.3) | collective-permute-done | bytes 335904 | tf_op jit(solution)/shard_map/ppermute | solution.py:170
  33.8 1.1 %pad_maximum_fusion.held = f32[4,328,128]{2,1,0:T(8,128)S(1)} fusion(f32[2,328,128]{2,1,0:T(8,128)} %collective-permute-done.3, f32[1,328,128]{2,1,0:T(8,128)} %copy-done.9, f32[1,328,128]{2,1,0:T(8,128)S(1)} %bitcast.11), kind=kLoop, calls=%fused_computation | loop fusion | flops 335872 | bytes 1343488 | tf_op jit(solution)/shard_map/concatenate | solution.py:172
  34.9 1.3 %pick_ends.1 = f32[328,128]{1,0:T(8,128)} custom-call(s32[1]{0:T(128)} %bitcast.2.me, s32[8,2]{1,0:T(8,128)S(1)} %copy.22.faces, f32[4,328,128]{2,1,0:T(8,128)S(1)} %pad_maximum_fusion.held), custom_call_target="tpu_custom_call" | custom-call | tf_op jit(solution)/shard_map/pick_ends/pallas_call | solution.py:175
  36.2 1.5 %collective-permute-start.4 = (f32[328,128]{1,0:T(8,128)}, f32[328,128]{1,0:T(8,128)S(1)}, u32[]{:S(2)}, u32[]{:S(2)}) collective-permute-start(f32[328,128]{1,0:T(8,128)} %pick_ends.1), channel_id=1, source_target_pairs={{0,4},{4,0},{8,12},{12,8},{16,20},{20,16},{24,28},{28,24},{1,5},{5... | collective-permute-start | bytes 503816 | tf_op jit(solution)/shard_map/ppermute | solution.py:186
  37.7 4.1 %collective-permute-done.4.given = f32[328,128]{1,0:T(8,128)S(1)} collective-permute-done((f32[328,128]{1,0:T(8,128)}, f32[328,128]{1,0:T(8,128)S(1)}, u32[]{:S(2)}, u32[]{:S(2)}) %collective-permute-start.4) | collective-permute-done | bytes 167968 | tf_op jit(solution)/shard_map/ppermute | solution.py:186
  41.8 0.6 choose_ends.1.rest_7_
  42.4 0.7 collective-permute-start.6
  43.1 2.3 %collective-permute-start.5 = (f32[328,128]{1,0:T(8,128)S(1)}, f32[328,128]{1,0:T(8,128)S(1)}, u32[]{:S(2)}, u32[]{:S(2)}) collective-permute-start(f32[328,128]{1,0:T(8,128)S(1)} %choose_ends.1.rest_7_), channel_id=1, source_target_pairs={{0,1},{1,0},{2,3},{3,2},{4,5},{5,4},{6,7},{7,6},{8,9},{9,8},{10,11... | collective-permute-start | bytes 503816 | tf_op jit(solution)/shard_map/ppermute | solution.py:627
  45.4 0.0 collective-permute-done.2.outer.rest_5_.rest_6_.rest_13_
  45.4 0.0 collective-permute-done.1.inner.rest_3_.rest_4_.rest_12_
  45.4 0.0 copy-done
  45.4 0.0 copy-start.1
  45.4 1.7 %copy-done.1 = f32[5,8,64,256]{3,2,1,0:T(8,128)S(1)} copy-done((f32[5,8,64,256]{3,2,1,0:T(8,128)S(1)}, f32[5,8,64,256]{3,2,1,0:T(8,128)}, u32[]{:S(2)}) %copy-start.1) | copy-done | bytes 2621464
  47.2 7.8 %first_sweep.1.rest_14_ = f32[5,12,64,256]{3,2,1,0:T(8,128)S(1)} custom-call(s32[1]{0:T(128)} %bitcast.even, f32[32,128]{1,0:T(8,128)S(1)} %pad.8.couplings.rest_0_, f32[5,8,64,256]{3,2,1,0:T(8,128)S(1)} %copy-done, f32[5,8,64,256]{3,2,1,0:T(8,128)S(1)} %copy-done.1, f32[5,5,64,256]{3,2,1,0:T(8,128)} %collective-permute-done.1.inner.rest_3_.rest_4_.rest_12_, ...), custom_call_target="tpu_custom_call" | custom-call | flops 7000000000 | bytes 16777216 | tf_op jit(solution)/shard_map/first_sweep/pallas_call | solution.py:484
  55.0 0.0 collective-permute-done.6.rest_9_
  55.0 0.0 collective-permute-done.5.rest_8_
  55.0 0.0 copy-done.3
  55.0 0.0 copy-done.4
  55.1 0.0 copy-done.5
  55.1 0.0 copy-done.2
  55.1 0.0 copy-start.6
  55.1 0.0 copy-start.7
  55.1 15.2 %last_sweeps.1 = (f32[5,8,64,256]{3,2,1,0:T(8,128)}, f32[3,8,256]{2,1,0:T(8,128)S(1)}) custom-call(s32[1]{0:T(128)} %bitcast.even, f32[32,128]{1,0:T(8,128)S(1)} %pad.8.couplings.rest_0_, f32[8,128]{1,0:T(8,128)S(1)} %copy-done.3, f32[2,5,64,128]{3,2,1,0:T(8,128)S(1)} %copy-done.4, f32[5,5,64,256]{3,2,1,0:T(8,128)} %collective-permute-done.1.inner.rest_3_.rest_4_.rest_12_, ...), custom_call_target="tpu_custom_call" | custom-call | flops 11000000512 | bytes 16777216 | tf_op jit(solution)/shard_map/last_sweeps/pallas_call | solution.py:532
  70.3 0.0 copy-done.6
  70.3 0.0 copy-done.7
  70.3 4.2 %scatter_points.1 = f32[3,48,256]{2,1,0:T(8,128)S(1)} custom-call(f32[3,8,256]{2,1,0:T(8,128)S(1)} %get-tuple-element.21.sens, f32[8,8,256]{2,1,0:T(8,128)S(1)} %copy-done.6, s32[8,8,256]{2,1,0:T(8,128)S(1)} %copy-done.7), custom_call_target="tpu_custom_call" | custom-call | flops 4000000000 | bytes 1048576 | tf_op jit(solution)/shard_map/scatter_points/pallas_call | solution.py:600
  74.5 0.1 reshape.22
  74.6 0.1 copy.28
  74.6 0.1 reshape.23
  74.7 0.1 copy.24
  74.8 13.6 %all_to_all.5 = f32[32,3,384]{2,1,0:T(4,128)S(1)} all-to-all(f32[32,3,384]{2,1,0:T(4,128)S(1)} %copy.24), channel_id=1, replica_groups=mesh['blk'=8,'sub'=4] {'blk','sub'}, dimensions={0} | all-to-all | bytes 294912 | tf_op jit(solution)/shard_map/all_to_all | solution.py:616
  88.4 0.6 reduce_sum.9
  (11 shorter events, 0.1 us)
Async XLA Ops:
  8.0 12.1 %collective-permute-start = (f32[1,328,128]{2,1,0:T(8,128)}, f32[1,328,128]{2,1,0:T(8,128)S(1)}, u32[]{:S(2)}, u32[]{:S(2)}) collective-permute-start(f32[1,328,128]{2,1,0:T(8,128)} %bitcast.9), channel_id=1, source_target_pairs={{0,16},{4,20},{8,24},{12,28},{16,0},{20,4},{24,8},{28,12},{1,17},{... | collective-permute-start | bytes 503816 | tf_op jit(solution)/shard_map/ppermute | solution.py:170
  12.1 11.8 %copy-start.8 = (f32[328,128]{1,0:T(8,128)S(1)}, f32[328,128]{1,0:T(8,128)}, u32[]{:S(2)}) copy-start(f32[328,128]{1,0:T(8,128)} %get-tuple-element.13) | copy-start | bytes 503812
  12.1 12.6 %copy-start.10 = (s32[8,2]{0,1:T(2,128)S(1)}, s32[8,2]{0,1:T(2,128)}, u32[]{:S(2)}) copy-start(s32[8,2]{0,1:T(2,128)} %param.10) | copy-start | bytes 196
  15.6 29.8 %copy-start = (f32[5,8,64,256]{3,2,1,0:T(8,128)S(1)}, f32[5,8,64,256]{3,2,1,0:T(8,128)}, u32[]{:S(2)}) copy-start(f32[5,8,64,256]{3,2,1,0:T(8,128)} %rest_10_.1) | copy-start | bytes 7864324
  20.1 4.6 %copy-start.9 = (f32[1,328,128]{2,1,0:T(8,128)}, f32[1,328,128]{2,1,0:T(8,128)S(1)}, u32[]{:S(2)}) copy-start(f32[1,328,128]{2,1,0:T(8,128)S(1)} %collective-permute-done) | copy-start | bytes 503812
  20.1 25.3 %collective-permute-start.2 = (f32[5,5,64,256]{3,2,1,0:T(8,128)}, f32[5,5,64,256]{3,2,1,0:T(8,128)}, u32[]{:S(2)}, u32[]{:S(2)}) collective-permute-start(f32[5,5,64,256]{3,2,1,0:T(8,128)} %get-tuple-element.18), channel_id=1, source_target_pairs={{1,2},{2,1},{5,6},{6,5},{9,10},{10,9},{13,14},{14,13},{17,18},{18,... | collective-permute-start | bytes 4915208 | tf_op jit(solution)/shard_map/ppermute | solution.py:627
  22.0 23.5 %collective-permute-start.1 = (f32[5,5,64,256]{3,2,1,0:T(8,128)}, f32[5,5,64,256]{3,2,1,0:T(8,128)}, u32[]{:S(2)}, u32[]{:S(2)}) collective-permute-start(f32[5,5,64,256]{3,2,1,0:T(8,128)} %get-tuple-element.16), channel_id=1, source_target_pairs={{0,1},{1,0},{2,3},{3,2},{4,5},{5,4},{6,7},{7,6},{8,9},{9,8},{10,11... | collective-permute-start | bytes 4915208 | tf_op jit(solution)/shard_map/ppermute | solution.py:627
  23.8 10.0 %collective-permute-start.3 = (f32[2,328,128]{2,1,0:T(8,128)S(1)}, f32[2,328,128]{2,1,0:T(8,128)}, u32[]{:S(2)}, u32[]{:S(2)}) collective-permute-start(f32[2,328,128]{2,1,0:T(8,128)S(1)} %pad_maximum_fusion.1), channel_id=1, source_target_pairs={{0,8},{4,12},{8,0},{12,4},{16,24},{20,28},{24,16},{28,20},{1,9},{5... | collective-permute-start | bytes 1007624 | tf_op jit(solution)/shard_map/ppermute | solution.py:170
  36.2 5.6 %collective-permute-start.4 = (f32[328,128]{1,0:T(8,128)}, f32[328,128]{1,0:T(8,128)S(1)}, u32[]{:S(2)}, u32[]{:S(2)}) collective-permute-start(f32[328,128]{1,0:T(8,128)} %pick_ends.1), channel_id=1, source_target_pairs={{0,4},{4,0},{8,12},{12,8},{16,20},{20,16},{24,28},{28,24},{1,5},{5... | collective-permute-start | bytes 503816 | tf_op jit(solution)/shard_map/ppermute | solution.py:186
  41.8 13.3 %copy-start.3 = (f32[8,128]{1,0:T(8,128)S(1)}, f32[8,128]{1,0:T(8,128)}, u32[]{:S(2)}) copy-start(f32[8,128]{1,0:T(8,128)} %pad_maximum_fusion.2.cpl.rest_1_) | copy-start | bytes 12292
  41.8 13.3 %copy-start.4 = (f32[2,5,64,128]{3,2,1,0:T(8,128)S(1)}, f32[2,5,64,128]{3,2,1,0:T(8,128)}, u32[]{:S(2)}) copy-start(f32[2,5,64,128]{3,2,1,0:T(8,128)} %get-tuple-element.12.rest_2_) | copy-start | bytes 983044
  41.8 13.3 %copy-start.5 = (f32[3,5,2,8,256]{4,3,2,1,0:T(8,128)S(1)}, f32[3,5,2,8,256]{4,3,2,1,0:T(8,128)}, u32[]{:S(2)}) copy-start(f32[3,5,2,8,256]{4,3,2,1,0:T(8,128)} %rest_15_.1) | copy-start | bytes 737284
  42.4 12.6 %collective-permute-start.6 = (f32[328,128]{1,0:T(8,128)S(1)}, f32[328,128]{1,0:T(8,128)S(1)}, u32[]{:S(2)}, u32[]{:S(2)}) collective-permute-start(f32[328,128]{1,0:T(8,128)S(1)} %choose_ends.1.rest_7_), channel_id=1, source_target_pairs={{1,2},{2,1},{5,6},{6,5},{9,10},{10,9},{13,14},{14,13},{17,18},{18,... | collective-permute-start | bytes 503816 | tf_op jit(solution)/shard_map/ppermute | solution.py:627
  43.1 11.9 %collective-permute-start.5 = (f32[328,128]{1,0:T(8,128)S(1)}, f32[328,128]{1,0:T(8,128)S(1)}, u32[]{:S(2)}, u32[]{:S(2)}) collective-permute-start(f32[328,128]{1,0:T(8,128)S(1)} %choose_ends.1.rest_7_), channel_id=1, source_target_pairs={{0,1},{1,0},{2,3},{3,2},{4,5},{5,4},{6,7},{7,6},{8,9},{9,8},{10,11... | collective-permute-start | bytes 503816 | tf_op jit(solution)/shard_map/ppermute | solution.py:627
  45.4 1.7 %copy-start.1 = (f32[5,8,64,256]{3,2,1,0:T(8,128)S(1)}, f32[5,8,64,256]{3,2,1,0:T(8,128)}, u32[]{:S(2)}) copy-start(f32[5,8,64,256]{3,2,1,0:T(8,128)} %rest_11_.1) | copy-start | bytes 7864324
  47.2 7.9 %copy-start.2 = (f32[5,8,64,256]{3,2,1,0:T(8,128)S(1)}, f32[5,8,64,256]{3,2,1,0:T(8,128)}, u32[]{:S(2)}) copy-start(f32[5,8,64,256]{3,2,1,0:T(8,128)} %rest_11_.1) | copy-start | bytes 7864324
  55.1 15.2 %copy-start.6 = (f32[8,8,256]{2,1,0:T(8,128)S(1)}, f32[8,8,256]{2,1,0:T(8,128)}, u32[]{:S(2)}) copy-start(f32[8,8,256]{2,1,0:T(8,128)} %weight.1) | copy-start | bytes 196612
  55.1 15.2 %copy-start.7 = (s32[8,8,256]{2,1,0:T(8,128)S(1)}, s32[8,8,256]{2,1,0:T(8,128)}, u32[]{:S(2)}) copy-start(s32[8,8,256]{2,1,0:T(8,128)} %ids.1) | copy-start | bytes 196612

commit v8 on v7

--- a/solution.py
+++ b/solution.py
@@ -45,8 +45,12 @@
     return total
 
 
-def ends_kernel(src, inv, cpl, tile, packet):
-    depth = src.shape[2]
+FREE = 16
+
+
+def ends_kernel(src, inv, coupling, tile, packet, cpl):
+    depth = tile.shape[2]
+    nvar = packet.shape[0] // depth + 1
     tiles = [chord_tile([(s, field[:, s]) for s in range(field.shape[1])]) for field in (src, inv)]
     for f in range(2):
         tile[f] = tiles[f]
@@ -54,38 +58,63 @@
     place = lane & (HALF - 1)
     is_src = place - COLS * ((place * 43) >> 8) < 3
     x, y = tiles[0][0], tiles[1][0]
-    v = pl.program_id(0)
-    packet[pl.ds(pl.multiple_of(v * depth, depth), depth), :] = jnp.where(
+    both = jnp.where(
         lane >= HALF,
         jnp.where(is_src, pltpu.roll(x, LANES - 2, 1), pltpu.roll(y, 1, 1)),
         jnp.where(is_src, x, pltpu.roll(y, 3, 1)),
     )
-
-    @pl.when(v == 0)
+    both = pltpu.roll(both, LANES - COLS, 1)
+    step = pl.program_id(0)
+    free = place >= HALF - FREE
+
+    @pl.when(step == 0)
     def _():
-        rows = packet.shape[0]
-        packet[rows - 8 : rows, :] = cpl[...]
-
-
-def chord_ends(source, inv_diag, cpl):
+        for j in range(nvar - 1):
+            shift = (HALF - FREE - FREE * j) % LANES
+            packet[j * depth : (j + 1) * depth, :] = pltpu.roll(both, shift, 1) if shift else both
+        m = jnp.concatenate([coupling[u, v] for u in range(nvar) for v in range(nvar)], 0)
+        pair = lax.broadcasted_iota(jnp.int32, (nvar * nvar, LANES), 0)
+        own = bit(pair == (lane_iota((nvar * nvar, LANES)) & (HALF - 1)))
+        rows = lax.dot_general(
+            m, own, (((0,), (0,)), ((), ())), precision=lax.Precision.HIGHEST,
+            preferred_element_type=jnp.float32,
+        )
+        rows = jnp.concatenate([rows, jnp.zeros((8 - rows.shape[0], LANES), jnp.float32)], 0)
+        cpl[...] = rows
+        packet[(nvar - 1) * depth : (nvar - 1) * depth + 8, :] = rows
+
+    @pl.when(step > 0)
+    def _():
+        at = pl.ds(pl.multiple_of((step - 1) * depth, depth), depth)
+        packet[at, :] = jnp.where(free, packet[at, :], both)
+
+
+def chord_ends(source, inv_diag, coupling):
     nvar, spans, depth, chord = source.shape
-    field = pl.BlockSpec((1, spans, depth, chord), lambda v: (v, 0, 0, 0))
-    rows = nvar * depth + 8
+
+    def var(step):
+        return jnp.where(step == 0, nvar - 1, step - 1)
+
+    field = pl.BlockSpec((1, spans, depth, chord), lambda i: (var(i), 0, 0, 0))
+    rows = (nvar - 1) * depth + 8
+    small = coupling.transpose(2, 3, 0, 1)
     return pl.pallas_call(
         ends_kernel,
         grid=(nvar,),
-        in_specs=[field, field, pl.BlockSpec((8, LANES), lambda v: (0, 0))],
+        in_specs=[field, field, pl.BlockSpec(small.shape, lambda i: (0, 0, 0, 0))],
         out_specs=[
-            pl.BlockSpec((2, 1, depth, LANES), lambda v: (0, v, 0, 0)),
-            pl.BlockSpec((rows, LANES), lambda v: (0, 0)),
+            pl.BlockSpec((2, 1, depth, LANES), lambda i: (0, var(i), 0, 0)),
+            pl.BlockSpec((rows, LANES), lambda i: (0, 0)),
+            pl.BlockSpec((8, LANES), lambda i: (0, 0)),
         ],
         out_shape=[
             jax.ShapeDtypeStruct((2, nvar, depth, LANES), jnp.float32),
             jax.ShapeDtypeStruct((rows, LANES), jnp.float32),
+            jax.ShapeDtypeStruct((8, LANES), jnp.float32),
         ],
         compiler_params=pltpu.CompilerParams(vmem_limit_bytes=56 * MIB),
         name="chord_ends",
-    )(source, inv_diag, cpl)
+    )(source, inv_diag, small)
 
 
 def layers_kernel(even, src, inv, inner, outer, held, sems):
@@ -147,29 +176,37 @@
     return index, jnp.where((apart & masks[-1]) == 0, 1, 0)
 
 
-def pick_kernel(masks, me, faces, held, out):
+def held_at(index, held, more):
+    count = held.shape[0]
+    at = lax.rem(index, count)
+    return jnp.where(jnp.full((1, 1), index, jnp.int32) < count, held[at], more[at])
+
+
+def pick_kernel(masks, me, faces, held, more, out):
     other = me[0] ^ masks[-1]
     low, _ = place_of(me[0], faces[other, 0], masks)
     high, _ = place_of(me[0], faces[other, 1], masks)
-    out[...] = jnp.where(lane_iota((1, LANES)) < HALF, held[low], held[high])
-
-
-def choose_kernel(masks, me, faces, held, given, out):
+    left = lane_iota((1, LANES)) < HALF
+    out[...] = jnp.where(left, held_at(low, held, more), held_at(high, held, more))
+
+
+def choose_kernel(masks, me, faces, held, more, given, out):
     low, low_held = place_of(me[0], faces[me[0], 0], masks)
     high, high_held = place_of(me[0], faces[me[0], 1], masks)
     left = lane_iota((1, LANES)) < HALF
     keep = jnp.where(left, low_held, high_held) == 1
-    out[...] = jnp.where(keep, jnp.where(left, held[low], held[high]), given[...])
+    mine = jnp.where(left, held_at(low, held, more), held_at(high, held, more))
+    out[...] = jnp.where(keep, mine, given[...])
 
 
 def route_ends(packet, me, face_map):
     count = lax.axis_size("blk")
     masks = exchange_masks(count)
-    held, first = packet[None], None
+    held, received = packet[None], []
     for mask in masks[:-1]:
-        other = lax.ppermute(held, "blk", [(i, i ^ mask) for i in range(count)])
-        first = other if first is None else first
-        held = jnp.concatenate([held, other], 0)
+        if received:
+            held = jnp.concatenate([held, received[-1]], 0)
+        received.append(lax.ppermute(held, "blk", [(i, i ^ mask) for i in range(count)]))
 
     def call(kernel, name, *operands):
         return pl.pallas_call(
@@ -181,27 +218,34 @@
             name=name,
         )(me, face_map, *operands)
 
-    picked = call(pick_kernel, "pick_ends", held)
+    picked = call(pick_kernel, "pick_ends", held, received[-1])
     last = masks[-1]
     given = lax.ppermute(picked, "blk", [(i, i ^ last) for i in range(count)])
-    return call(choose_kernel, "choose_ends", held, given), held, first
+    return call(choose_kernel, "choose_ends", held, received[-1], given), received
 
 
 def expand_couplings(couplings, wide):
     rows, lanes = wide.shape
     nvar = 5
-    row = lax.broadcasted_iota(jnp.int32, (rows, 32), 0)
-    of = lax.broadcasted_iota(jnp.int32, (rows, 32), 1)
-    pick_row = bit((row >> 4) == of).astype(jnp.bfloat16)
+    row = lax.broadcasted_iota(jnp.int32, (rows, 8), 0)
+    of = lax.broadcasted_iota(jnp.int32, (rows, 8), 1)
+    group = row >> 4
+    pick_row = bit(((group * 205) >> 10) == of).astype(jnp.bfloat16)
+    group = lax.broadcasted_iota(jnp.int32, (rows, LANES), 0) >> 4
+    u = group - nvar * ((group * 205) >> 10)
+    pair = lane_iota((rows, LANES))
+    own = (((pair * 205) >> 10) == u) & (pair < nvar * nvar)
     col = lax.broadcasted_iota(jnp.int32, (LANES, lanes), 1)
-    var = lax.broadcasted_iota(jnp.int32, (LANES, lanes), 0)
+    lane = lax.broadcasted_iota(jnp.int32, (LANES, lanes), 0)
     wide_var = (col >> 4) - jnp.where(col >= 80, nvar, 0) - jnp.where(col >= 160, nvar, 0)
+    var = lane - nvar * ((lane * 205) >> 10)
     pick_col = bit((wide_var == var) & (col < 240)).astype(jnp.bfloat16)
     top = couplings.astype(jnp.bfloat16)
     rest = (couplings - top.astype(jnp.float32)).astype(jnp.bfloat16)
 
     def spread(part):
-        tall = jnp.dot(pick_row, part, preferred_element_type=jnp.float32).astype(jnp.bfloat16)
+        tall = jnp.dot(pick_row, part, preferred_element_type=jnp.float32)
+        tall = jnp.where(own, tall, 0.0).astype(jnp.bfloat16)
         return jnp.dot(tall, pick_col, preferred_element_type=jnp.float32)
 
     r = lax.broadcasted_iota(jnp.int32, (rows, lanes), 0)
@@ -228,11 +272,19 @@
     def moved(x, by):
         return pltpu.roll(x, by % LANES, 1) if by % LANES else x
 
+    def unpack(ref, v):
+        if v < nvar - 1:
+            return moved(ref[v * depth : (v + 1) * depth, :], COLS)
+        x = None
+        for j in range(3):
+            part = moved(ref[j * depth : (j + 1) * depth, :], COLS + FREE * (j + 1) - HALF)
+            x = part if x is None else jnp.where(place < COLS + FREE * j, x, part)
+        return x
+
     def packet(v):
-        at = slice(v * depth, (v + 1) * depth)
-        a, b = given_in[at, :], given_out[at, :]
+        a, b = unpack(given_in, v), unpack(given_out, v)
         low, high = jnp.where(up2, b, a), jnp.where(up2, a, b)
-        x = given[at, :]
+        x = unpack(given, v)
         x = jnp.where(first, moved(low, -8 * COLS), jnp.where(last, moved(high, 8 * COLS), x))
         x = jnp.where(place == 60, jnp.where(side, moved(low, 18), moved(low, 16)), x)
         x = jnp.where(place == 61, jnp.where(side, moved(low, 16), moved(low, 14)), x)
@@ -256,9 +308,10 @@
     src = [field(0, v, packets[v]) for v in range(nvar)]
     inv = [field(1, v, packets[v]) for v in range(nvar)]
     one = lax.broadcasted_iota(jnp.int32, (152, 8), 0)
-    pick = bit((one >> 6) == lax.broadcasted_iota(jnp.int32, (152, 8), 1))
+    pick = bit(((one * 41) >> 10) == lax.broadcasted_iota(jnp.int32, (152, 8), 1))
     index = lax.broadcasted_iota(jnp.int32, (152, LANES), 0)
-    keep = (index & 63) == (lane_iota((152, LANES)) & 63)
+    index = index - 25 * ((index * 41) >> 10)
+    keep = index == (lane_iota((152, LANES)) & (HALF - 1))
     half = lax.broadcasted_iota(jnp.int32, (LANES, LANES), 0) >> 6
     fill = bit(half == (lane_iota((LANES, LANES)) >> 6))
 
@@ -268,7 +321,7 @@
 
     own_rows = spread(mine[...])
     scalars[0] = own_rows
-    scalars[1] = jnp.where(ghost, spread(given[nvar * depth : nvar * depth + 8, :]), own_rows)
+    scalars[1] = jnp.where(ghost, spread(given[(nvar - 1) * depth : (nvar - 1) * depth + 8, :]), own_rows)
     mixed = [scalars[1, i : i + 1, :] for i in range(150)]
     own_c = {i: scalars[0, i : i + 1, :] for i in range(100, 150)}
     high_face = (side & jnp.logical_not(lane == HALF + 60)) | (lane == 60)
@@ -299,12 +352,12 @@
         p = [inv[v] * total[v] for v in range(nvar)]
 
 
-def run_sweeps(sweeps, even, couplings, ribbon, src_in, inv_in, inner, outer, p_in, out, scratch):
+def run_sweeps(stages, even, couplings, ribbon, src_in, inv_in, inner, outer, p_in, leaves, scratch):
     src, inv, pa, pb, wide, before, coming, faces, scalars, sems, out_sems = scratch
     nvar, layers, rows, chord = pa.shape
     spans = layers - 2 * DEEP
-    start_at, stop_at = sweeps[0], layers - 1 - sweeps[0]
-    whole_at = [at for at in range(start_at, stop_at + 1)]
+    sweeps = [stage[0] for stage in stages]
+    whole_at = sorted({at for n, a, b, _ in stages if n == sweeps[0] for at in range(a, b + 1)})
 
     def one(f, ref, at, start):
         to = (src, inv, pb)[f]
@@ -334,11 +387,11 @@
         bring(0, at)
         bring(1, at)
         if p_in is not None:
-            one(2, p_in.at[:, at - 1], at, True)
-    if p_in is None:
-        ones = jnp.ones((nvar, rows, chord), jnp.float32)
-        inv[:, 0] = ones
-        inv[:, layers - 1] = ones
+            one(2, p_in(at), at, True)
+    ones = jnp.ones((nvar, rows, chord), jnp.float32)
+    for at in (0, layers - 1):
+        if at in whole_at:
+            inv[:, at] = ones
     expand_couplings(couplings[...], wide)
     if ribbon is not None:
         ribbon_sweeps(rows, even[0], *ribbon, scalars, faces)
@@ -362,12 +415,8 @@
         pb[:, at, :, :LANES] += inv[:, at, :, :LANES] * jnp.where(lane == 0, low, 0.0)
         pb[:, at, :, LANES:] += inv[:, at, :, LANES:] * jnp.where(lane == LANES - 1, high, 0.0)
 
-    leave_from = sweeps[-1] + 1
-
     def leave(at, start):
-        copy = pltpu.make_async_copy(
-            pb.at[:, at], out.at[:, at - leave_from], out_sems.at[at - leave_from]
-        )
+        copy = pltpu.make_async_copy(pb.at[:, at], leaves(at), out_sems.at[at])
         copy.start() if start else copy.wait()
 
     groups = rows // 16
@@ -417,42 +466,56 @@
             waiting = total
         before[:, rows - 16 : rows] = waiting
 
-    for n in sweeps:
+    def stage(n, begin, last, turn):
         p, after = (pa, pb) if n % 2 == 0 else (pb, pa)
-        if n == sweeps[0]:
-            arrive(start_at, True)
+        fresh, final = n == sweeps[0], n == sweeps[-1]
+        if fresh:
+            arrive(begin, begin == 0)
         for g in range(groups):
-            coming[:, 16 * g : 16 * g + 16] = products(p, n, g, 0, step)
-        full = layers - 2 - 2 * n
-        turn = 2
+            coming[:, 16 * g : 16 * g + 16] = products(p, begin, g, 0, step)
+        turns = (last - begin - 1) // turn
 
         def several(i, _):
-            s0 = n + 1 + i * turn
-            if n == sweeps[0]:
+            s0 = begin + 1 + i * turn
+            if fresh:
                 for j in range(turn):
                     arrive(s0 + j)
             for j in range(turn):
                 one_layer(p, after, n, s0 + j)
-            if n == sweeps[-1]:
+            if final:
                 for j in range(turn - 1):
                     leave(s0 + j, True)
-
-                @pl.when(i > 0)
-                def _():
-                    leave(s0 - 1, True)
+                if turns > 1:
+
+                    @pl.when(i > 0)
+                    def _():
+                        leave(s0 - 1, True)
 
             return 0
 
-        lax.fori_loop(0, full // turn, several, 0)
-        last = layers - 1 - n
-        if n == sweeps[0]:
-            arrive(last, True)
+        if turns > 1:
+            lax.fori_loop(0, turns, several, 0)
+        else:
+            several(0, 0)
+        if fresh:
+            arrive(last, last == layers - 1)
         for g in range(groups):
             at = slice(16 * g, 16 * g + 16)
             span_high = products(p, last, g, step, 2 * step)
             after[:, last - 1, at] = inv[:, last - 1, at] * (before[:, at] + span_high)
-    leave(layers - 1 - leave_from, True)
-    return pb, lambda: [leave(at, False) for at in range(leave_from, layers - leave_from)]
+        if final:
+            leave(last - 1, True)
+            left.extend(range(begin + 1, last))
+
+    left = []
+    for n, begin, last, turn in stages:
+        stage(n, begin, last, turn)
+
+    def done():
+        for at in left:
+            leave(at, False)
+
+    return pb, done
 
 
 def sweep_scratch(nvar, spans, chord, rows):
@@ -474,35 +537,53 @@
     ]
 
 
-def first_kernel(even, couplings, src_in, inv_in, inner, outer, out, *scratch):
-    _, done = run_sweeps([0], even, couplings, None, src_in, inv_in, inner, outer, None, out, scratch)
+def inner_kernel(even, couplings, src_in, inv_in, out, *scratch):
+    _, done = run_sweeps(
+        [(0, 3, 10, 2)], even, couplings, None, src_in, inv_in, None, None, None,
+        lambda at: out.at[:, at - 4], scratch,
+    )
     done()
 
 
-def first_sweep(even, couplings, source, inv_diag, inner, outer):
+def outer_kernel(even, couplings, src_in, inv_in, inner, outer, out, *scratch):
+    _, done = run_sweeps(
+        [(0, 0, 4, 3), (0, 9, 13, 3)], even, couplings, None, src_in, inv_in, inner, outer, None,
+        lambda at: out.at[:, at - 1 if at < 4 else at - 7], scratch,
+    )
+    done()
+
+
+def first_sweep(kernel, name, flops, even, couplings, source, inv_diag, *halos):
     nvar, spans, depth, chord = source.shape
     return pl.pallas_call(
-        first_kernel,
-        in_specs=[SMEM, VMEM, ANY, ANY, ANY, ANY],
+        kernel,
+        in_specs=[SMEM, VMEM] + [ANY] * (2 + len(halos)),
         out_specs=ANY,
-        out_shape=jax.ShapeDtypeStruct((nvar, spans + 4, depth, chord), jnp.float32),
+        out_shape=jax.ShapeDtypeStruct((nvar, 6, depth, chord), jnp.float32),
         scratch_shapes=sweep_scratch(nvar, spans, chord, depth),
         compiler_params=pltpu.CompilerParams(vmem_limit_bytes=28 * MIB),
-        cost_estimate=pl.CostEstimate(flops=7 * 10**9, bytes_accessed=16 * MIB, transcendentals=0),
-        name="first_sweep",
-    )(even, couplings, source, inv_diag, inner, outer)
+        cost_estimate=pl.CostEstimate(flops=flops, bytes_accessed=4 * MIB, transcendentals=0),
+        name=name,
+    )(even, couplings, source, inv_diag, *halos)
 
 
 def last_kernel(even, *rest):
-    couplings, cpl, own, in_src, in_inv, out_src, out_inv, given, given_in, given_out, *rest = rest
-    src_in, inv_in, inner, outer, p_in, jac, out, sens, *scratch = rest
+    cpl, own, in_src, in_inv, out_src, out_inv, given, given_in, given_out, *rest = rest
+    src_in, inv_in, inner, outer, p_inner, p_outer, jac, out, sens, *scratch = rest
     nvar, spans, _, chord = out.shape
     near_in, near_out = (in_src.at[0], in_inv.at[0]), (out_src.at[0], out_inv.at[0])
     ribbon = (
         own, [r[...] for r in near_in], [r[...] for r in near_out], given, given_in, given_out, cpl,
     )
+
+    def p_in(at):
+        if 4 <= at < 10:
+            return p_inner.at[:, at - 4]
+        return p_outer.at[:, at - 1 if at < 4 else at - 7]
+
     result, done = run_sweeps(
-        [1, 2], even, couplings, ribbon, src_in, inv_in, inner, outer, p_in, out, scratch
+        [(1, 1, 12, 2), (2, 2, 11, 2)], even, cpl, ribbon, src_in, inv_in, inner, outer, p_in,
+        lambda at: out.at[:, at - DEEP], scratch,
     )
     layer = []
     for v in range(nvar):
@@ -519,7 +600,7 @@
     done()
 
 
-def last_sweeps(even, couplings, cpl, own, givens, source, inv_diag, inner, outer, p, jac):
+def last_sweeps(even, cpl, own, givens, source, inv_diag, inner, outer, p_inner, p_outer, jac):
     nvar, spans, depth, chord = source.shape
 
     def whole(a):
@@ -532,10 +613,10 @@
     return pl.pallas_call(
         last_kernel,
         grid=(1,),
-        in_specs=[SMEM, whole(couplings), whole(cpl), whole(own)]
+        in_specs=[SMEM, whole(cpl), whole(own)]
         + [piece(0), piece(DEEP - 1)] * 2
         + [whole(a) for a in givens]
-        + [ANY] * 5
+        + [ANY] * 6
         + [whole(jac)],
         out_specs=[ANY, pl.BlockSpec(sens, lambda i: (0, 0, 0))],
         out_shape=[
@@ -546,7 +627,10 @@
         compiler_params=pltpu.CompilerParams(vmem_limit_bytes=40 * MIB),
         cost_estimate=pl.CostEstimate(flops=11 * 10**9, bytes_accessed=16 * MIB, transcendentals=0),
         name="last_sweeps",
-    )(even, couplings, cpl, own, inner, inner, outer, outer, *givens, source, inv_diag, inner, outer, p, jac)
+    )(
+        even, cpl, own, inner, inner, outer, outer, *givens, source, inv_diag, inner, outer,
+        p_inner, p_outer, jac,
+    )
 
 
 def point_indices(ids, hi_index, lo_index):
@@ -610,10 +694,18 @@
 
 
 def reduce_points(partial, n_dev):
-    dims = partial.shape[0]
-    parts = partial[:, : n_dev // 2 * 3].reshape(dims, n_dev // 2, 3, 2, LANES)
-    parts = parts.transpose(1, 3, 0, 2, 4).reshape(n_dev, dims, 3 * LANES)
-    return lax.all_to_all(parts, ("blk", "sub"), 0, 0, tiled=True).sum(0)
+    count = lax.axis_size("sub")
+    odd = lax.axis_index("sub") & 1
+    partial = partial[:, : n_dev // 2 * 3]
+    keep = lax.dynamic_slice_in_dim(partial, odd * LANES, LANES, 2)
+    send = lax.dynamic_slice_in_dim(partial, (1 - odd) * LANES, LANES, 2)
+    parts = keep + lax.ppermute(send, "sub", [(i, i ^ 1) for i in range(count)])
+    dims = parts.shape[0]
+    parts = parts.reshape(dims, n_dev // 2, 3 * LANES).transpose(1, 0, 2)
+    groups = [list(range(core, n_dev, 2)) for core in range(2)]
+    return lax.all_to_all(
+        parts, ("blk", "sub"), 0, 0, tiled=True, axis_index_groups=groups
+    ).sum(0)
 
 
 def ordered(x, *after):
@@ -628,22 +720,24 @@
 
 
 def body(source, inv_diag, coupling, face_map, wall_jac, ffd_weight, cp_ids):
-    nvar = source.shape[0]
     n_dev = lax.axis_size("blk") * lax.axis_size("sub")
     even = (1 - (lax.axis_index("sub") & 1)).astype(jnp.int32).reshape(1)
     me = lax.axis_index("blk").astype(jnp.int32).reshape(1)
-    couplings = jnp.pad(coupling[0].reshape(6 * nvar, nvar), ((0, 2), (0, LANES - nvar)))
-    flat = jnp.pad(coupling[0].reshape(-1), (0, 8 * HALF - 6 * nvar * nvar)).reshape(8, HALF)
-    cpl = jnp.concatenate([flat, flat], 1)
-
-    own, packet = chord_ends(source, inv_diag, cpl)
+    own, packet, cpl = chord_ends(source, inv_diag, coupling)
     inner, outer = span_layers(ordered(even, packet), source, inv_diag)
-    given, held, first = route_ends(packet, me, face_map)
-    inner, outer = swap_spans(ordered(inner, first), ordered(outer, first))
-    p = first_sweep(ordered(even, held), couplings, source, inv_diag, inner, outer)
+    p_inner = first_sweep(
+        inner_kernel, "inner_layers", 10**8, ordered(even, packet), cpl, source, inv_diag
+    )
+    given, received = route_ends(packet, me, face_map)
+    inner, outer = swap_spans(
+        ordered(inner, received[0], p_inner), ordered(outer, received[0], p_inner)
+    )
+    p_outer = first_sweep(
+        outer_kernel, "outer_layers", 10**8, ordered(even, given), cpl, source, inv_diag, inner, outer
+    )
     givens = (given, *swap_spans(given, given))
     adjoint, sens = last_sweeps(
-        even, couplings, cpl, own, givens, source, inv_diag, inner, outer, p, wall_jac
+        even, cpl, own, givens, source, inv_diag, inner, outer, p_inner, p_outer, wall_jac
     )
     partial = scatter_points(sens, ffd_weight, cp_ids, n_dev)
     return adjoint, reduce_points(partial, n_dev)

time: 89.6 us -> 86.3 us (0.963)
  waiting for transfers between devices: 17.7 us -> 11.2 us
  starting transfers between devices: 13 us -> 15.1 us
  local copies, waits for them, and re-layouts: 3.21 us -> 5.09 us
  Pallas kernels: 38.4 us -> 40.2 us
  other arithmetic: 2.4 us -> 0.67 us
    ppermute x2 -> x3, waiting for transfers between devices: 13.6 us -> 7.67 us  [the longest x2 6.76 us: route_ends(): lax.ppermute(held, 'blk', [(i, i ^ mask) for i in range(count)])]
    ppermute x2 -> x3, starting transfers between devices: 4.88 us -> 8.92 us  [the longest x2 5.67 us: route_ends(): lax.ppermute(held, 'blk', [(i, i ^ mask) for i in range(count)])]
    unnamed x23 -> x29, local copies, waits for them, and re-layouts: 1.86 us -> 5.02 us
    ppermute x2, starting transfers between devices: 4.15 us -> 1.87 us  [swap_spans(): lax.ppermute(inner, 'sub', pairs)]
    pallas_call x2 -> x3, Pallas kernels: 23 us -> 25 us  [the longest x1 15.1 us: last_sweeps(): pl.pallas_call(last_kernel, grid=(1,), in_specs=[SMEM, whole(cpl), whole(...]
    concatenate x3 -> x1, other arithmetic: 1.76 us -> 0.03 us  [route_ends(): held = jnp.concatenate([held, received[-1]], 0)]
    another operation x3 -> x0, local copies, waits for them, and re-layouts: 0.94 us -> none  [the longest x2 0.84 us: body(): coupling[0].reshape(6 * nvar, nvar)]
  transfers between devices with their start and end apart: 7 -> 8, of which waited for: 3 -> 3; matrix products, arithmetic and copies ran while one was open for 1% -> 0% of each run, Pallas kernels for 15% -> 17%
where the time goes in v8:
time: 86.3 us; the launch traced here: 85.9 us
  Pallas kernels  40.2 us (47%)
  starting transfers between devices  15.1 us (17%)
  blocking collectives  12.8 us (15%)
  waiting for transfers between devices  11.2 us (13%)
  local copies, waits for them, and re-layouts  5.09 us (6%)
    pallas_call x1, Pallas kernels, last_sweeps(): pl.pallas_call(last_kernel, grid=(1,), in_specs=[SMEM, whole(cpl), whole(...  15.1 us
    all_to_all x1, blocking collectives, reduce_points(): lax.all_to_all(parts, ('blk', 'sub'), 0, 0, tiled=True, axis_index_groups...  12.8 us
    pallas_call x2, Pallas kernels, first_sweep(): pl.pallas_call(kernel, in_specs=[SMEM, VMEM] + [ANY] * (2 + len(halos)),...  9.85 us
    ppermute x2, waiting for transfers between devices, route_ends(): lax.ppermute(held, 'blk', [(i, i ^ mask) for i in range(count)])  6.76 us
    pallas_call x1, Pallas kernels, chord_ends(): pl.pallas_call(ends_kernel, grid=(nvar,), in_specs=[field, field, pl.Bloc...  6.04 us
    ppermute x2, starting transfers between devices, route_ends(): lax.ppermute(held, 'blk', [(i, i ^ mask) for i in range(count)])  5.67 us
    unnamed x29, local copies, waits for them, and re-layouts  5.02 us
    pallas_call x1, Pallas kernels, scatter_points(): pl.pallas_call(scatter_kernel, in_specs=[VMEM, VMEM, VMEM], out_specs=VME...  4.18 us
  transfers between devices with their start and end apart: 8, of which 3 were waited for; matrix products, arithmetic and copies ran while one was open for 0% of the time, Pallas kernels for 17%

profile of v8, /device:TPU:0, one launch (start us, length us, event | category | flops | bytes accessed | tf_op | source)
XLA Modules:
  0.0 85.9 jit_solution(18204629560158515476)
XLA Ops:
  0.6 6.0 %chord_ends.1 = (f32[2,5,64,128]{3,2,1,0:T(8,128)}, f32[264,128]{1,0:T(8,128)}, f32[8,128]{1,0:T(8,128)}) custom-call(f32[5,8,64,256]{3,2,1,0:T(8,128)} %rest_9_.1, f32[5,8,64,256]{3,2,1,0:T(8,128)} %rest_10_.1, f32[5,5,1,6]{3,2,1,0:T(1,128)} %bitcast.10), custom_call_target="tpu_custom_call" | custom-call | tf_op jit(solution)/shard_map/chord_ends/pallas_call | solution.py:101
  6.7 4.0 %collective-permute-start = (f32[1,264,128]{2,1,0:T(8,128)}, f32[1,264,128]{2,1,0:T(8,128)S(1)}, u32[]{:S(2)}, u32[]{:S(2)}) collective-permute-start(f32[1,264,128]{2,1,0:T(8,128)} %bitcast.8), channel_id=1, source_target_pairs={{0,16},{4,20},{8,24},{12,28},{16,0},{20,4},{24,8},{28,12},{1,17},{... | collective-permute-start | bytes 405512 | tf_op jit(solution)/shard_map/ppermute | solution.py:209
  10.7 0.0 copy-start
  10.7 0.0 copy-start.1
  10.7 3.7 %span_layers.1 = (f32[5,5,64,256]{3,2,1,0:T(8,128)}, f32[5,5,64,256]{3,2,1,0:T(8,128)}) custom-call(s32[1]{0:T(128)} %bitcast.even, f32[5,8,64,256]{3,2,1,0:T(8,128)} %rest_9_.1, f32[5,8,64,256]{3,2,1,0:T(8,128)} %rest_10_.1), custom_call_target="tpu_custom_call" | custom-call | bytes 8388608 | tf_op jit(solution)/shard_map/span_layers/pallas_call | solution.py:152
  14.4 0.4 copy-done
  14.8 0.8 copy-done.1
  15.6 0.0 copy-start.6
  15.6 0.7 copy-done.6
  16.3 4.6 %inner_layers.1.rest_13_ = f32[5,6,64,256]{3,2,1,0:T(8,128)S(1)} custom-call(s32[1]{0:T(128)} %bitcast.even, f32[8,128]{1,0:T(8,128)S(1)} %copy-done.6, f32[5,8,64,256]{3,2,1,0:T(8,128)S(1)} %copy-done, f32[5,8,64,256]{3,2,1,0:T(8,128)S(1)} %copy-done.1), custom_call_target="tpu_custom_call" | custom-call | flops 100000000 | bytes 4194304 | tf_op jit(solution)/shard_map/inner_layers/pallas_call | solution.py:558
  20.9 0.0 copy-start.4
  20.9 1.3 %copy-done.4 = f32[5,6,64,256]{3,2,1,0:T(8,128)} copy-done((f32[5,6,64,256]{3,2,1,0:T(8,128)}, f32[5,6,64,256]{3,2,1,0:T(8,128)S(1)}, u32[]{:S(2)}) %copy-start.4) | copy-done | bytes 1966104
  22.2 0.0 collective-permute-done
  22.2 1.9 %collective-permute-start.2 = (f32[5,5,64,256]{3,2,1,0:T(8,128)}, f32[5,5,64,256]{3,2,1,0:T(8,128)}, u32[]{:S(2)}, u32[]{:S(2)}) collective-permute-start(f32[5,5,64,256]{3,2,1,0:T(8,128)} %get-tuple-element.20), channel_id=1, source_target_pairs={{1,2},{2,1},{5,6},{6,5},{9,10},{10,9},{13,14},{14,13},{17,18},{18,... | collective-permute-start | bytes 4915208 | tf_op jit(solution)/shard_map/ppermute | solution.py:719
  24.1 1.8 %collective-permute-start.1 = (f32[5,5,64,256]{3,2,1,0:T(8,128)}, f32[5,5,64,256]{3,2,1,0:T(8,128)}, u32[]{:S(2)}, u32[]{:S(2)}) collective-permute-start(f32[5,5,64,256]{3,2,1,0:T(8,128)} %get-tuple-element.18), channel_id=1, source_target_pairs={{0,1},{1,0},{2,3},{3,2},{4,5},{5,4},{6,7},{7,6},{8,9},{9,8},{10,11... | collective-permute-start | bytes 4915208 | tf_op jit(solution)/shard_map/ppermute | solution.py:719
  25.9 0.0 copy-done.12
  26.0 1.6 %collective-permute-start.3 = (f32[2,264,128]{2,1,0:T(8,128)S(1)}, f32[2,264,128]{2,1,0:T(8,128)S(1)}, u32[]{:S(2)}, u32[]{:S(2)}) collective-permute-start(f32[2,264,128]{2,1,0:T(8,128)S(1)} %pad_maximum_fusion.held), channel_id=1, source_target_pairs={{0,8},{4,12},{8,0},{12,4},{16,24},{20,28},{24,16},{28,20},{1,9},{5... | collective-permute-start | bytes 811016 | tf_op jit(solution)/shard_map/ppermute | solution.py:209
  27.6 0.0 copy-done.13
  27.6 0.1 copy.12.faces
  27.7 6.8 %collective-permute-done.3.more = f32[2,264,128]{2,1,0:T(8,128)S(1)} collective-permute-done((f32[2,264,128]{2,1,0:T(8,128)S(1)}, f32[2,264,128]{2,1,0:T(8,128)S(1)}, u32[]{:S(2)}, u32[]{:S(2)}) %collective-permute-start.3) | collective-permute-done | bytes 270368 | tf_op jit(solution)/shard_map/ppermute | solution.py:209
  34.4 0.6 pick_ends.1
  35.1 1.6 %collective-permute-start.4 = (f32[264,128]{1,0:T(8,128)S(1)}, f32[264,128]{1,0:T(8,128)S(1)}, u32[]{:S(2)}, u32[]{:S(2)}) collective-permute-start(f32[264,128]{1,0:T(8,128)S(1)} %pick_ends.1), channel_id=1, source_target_pairs={{0,4},{4,0},{8,12},{12,8},{16,20},{20,16},{24,28},{28,24},{1,5},{5... | collective-permute-start | bytes 405512 | tf_op jit(solution)/shard_map/ppermute | solution.py:223
  36.6 3.5 %collective-permute-done.4.given = f32[264,128]{1,0:T(8,128)S(1)} collective-permute-done((f32[264,128]{1,0:T(8,128)S(1)}, f32[264,128]{1,0:T(8,128)S(1)}, u32[]{:S(2)}, u32[]{:S(2)}) %collective-permute-start.4) | collective-permute-done | bytes 135200 | tf_op jit(solution)/shard_map/ppermute | solution.py:223
  40.2 0.7 choose_ends.1.rest_6_
  40.8 0.1 collective-permute-start.5
  40.9 0.8 collective-permute-start.6
  41.8 0.0 collective-permute-done.2.outer.rest_4_.rest_5_.rest_12_
  41.8 0.0 collective-permute-done.1.inner.rest_2_.rest_3_.rest_11_
  41.8 0.0 copy-done.7
  41.8 0.0 copy-start.2
  41.8 1.7 %copy-done.2 = f32[5,8,64,256]{3,2,1,0:T(8,128)S(1)} copy-done((f32[5,8,64,256]{3,2,1,0:T(8,128)S(1)}, f32[5,8,64,256]{3,2,1,0:T(8,128)}, u32[]{:S(2)}) %copy-start.2) | copy-done | bytes 2621464
  43.5 5.2 %outer_layers.1.rest_14_ = f32[5,6,64,256]{3,2,1,0:T(8,128)S(1)} custom-call(s32[1]{0:T(128)} %bitcast.even, f32[8,128]{1,0:T(8,128)S(1)} %copy-done.7, f32[5,8,64,256]{3,2,1,0:T(8,128)S(1)} %copy-done, f32[5,8,64,256]{3,2,1,0:T(8,128)S(1)} %copy-done.2, f32[5,5,64,256]{3,2,1,0:T(8,128)} %collective-permute-done.1.inner.rest_2_.rest_3_.rest_11_, ...), custom_call_target="tpu_custom_call" | custom-call | flops 100000000 | bytes 4194304 | tf_op jit(solution)/shard_map/outer_layers/pallas_call | solution.py:558
  48.8 0.0 collective-permute-done.5.rest_7_
  48.8 0.0 collective-permute-done.6.rest_8_
  48.8 0.0 copy-done.3
  48.8 0.0 copy-done.5
  48.8 0.0 copy-done.8
  48.8 0.0 copy-done.9
  48.9 0.0 copy-start.10
  48.9 0.0 copy-start.11
  48.9 15.1 %last_sweeps.1 = (f32[5,8,64,256]{3,2,1,0:T(8,128)}, f32[3,8,256]{2,1,0:T(8,128)S(1)}) custom-call(s32[1]{0:T(128)} %bitcast.even, f32[8,128]{1,0:T(8,128)S(1)} %copy-done.7, f32[2,5,64,128]{3,2,1,0:T(8,128)S(1)} %copy-done.8, f32[5,5,64,256]{3,2,1,0:T(8,128)} %collective-permute-done.1.inner.rest_2_.rest_3_.rest_11_, ...), custom_call_target="tpu_custom_call" | custom-call | flops 11000000512 | bytes 16777216 | tf_op jit(solution)/shard_map/last_sweeps/pallas_call | solution.py:613
  64.0 0.0 copy-done.10
  64.0 0.0 copy-done.11
  64.0 4.2 %scatter_points.1 = f32[3,48,256]{2,1,0:T(8,128)S(1)} custom-call(f32[3,8,256]{2,1,0:T(8,128)S(1)} %get-tuple-element.23.sens, f32[8,8,256]{2,1,0:T(8,128)S(1)} %copy-done.10, s32[8,8,256]{2,1,0:T(8,128)S(1)} %copy-done.11), custom_call_target="tpu_custom_call" | custom-call | flops 4000000000 | bytes 1048576 | tf_op jit(solution)/shard_map/scatter_points/pallas_call | solution.py:684
  68.2 3.3 %collective-permute-start.7 = (f32[3,48,128]{2,1,0:T(8,128)S(1)}, f32[3,48,128]{2,1,0:T(8,128)S(1)}, u32[]{:S(2)}, u32[]{:S(2)}) collective-permute-start(f32[3,48,128]{2,1,0:T(8,128)S(1)} %constant_dynamic-slice_fusion), channel_id=1, source_target_pairs={{0,1},{1,0},{2,3},{3,2},{4,5},{5,4},{6,7},{7,6},{8,9},{9,8},{10,11... | collective-permute-start | bytes 221192 | tf_op jit(solution)/shard_map/ppermute | solution.py:702
  71.5 0.9 %collective-permute-done.7 = f32[3,48,128]{2,1,0:T(8,128)S(1)} collective-permute-done((f32[3,48,128]{2,1,0:T(8,128)S(1)}, f32[3,48,128]{2,1,0:T(8,128)S(1)}, u32[]{:S(2)}, u32[]{:S(2)}) %collective-permute-start.7) | collective-permute-done | bytes 73760 | tf_op jit(solution)/shard_map/ppermute | solution.py:702
  72.5 12.8 %all_to_all.5 = f32[16,3,384]{2,1,0:T(4,128)S(1)} all-to-all(f32[16,3,384]{2,1,0:T(4,128)S(1)} %bitcast.7), channel_id=1, replica_groups={{0,2,4,6,8,10,12,14,16,18,20,22,24,26,28,30},{1,3,5,7,9,11,13,15,17,19,..., dimensions={0} | all-to-all | bytes 147456 | tf_op jit(solution)/shard_map/all_to_all | solution.py:706
  85.2 0.6 reduce_sum.9
  (12 shorter events, 0.1 us)
Async XLA Ops:
  6.7 15.5 %collective-permute-start = (f32[1,264,128]{2,1,0:T(8,128)}, f32[1,264,128]{2,1,0:T(8,128)S(1)}, u32[]{:S(2)}, u32[]{:S(2)}) collective-permute-start(f32[1,264,128]{2,1,0:T(8,128)} %bitcast.8), channel_id=1, source_target_pairs={{0,16},{4,20},{8,24},{12,28},{16,0},{20,4},{24,8},{28,12},{1,17},{... | collective-permute-start | bytes 405512 | tf_op jit(solution)/shard_map/ppermute | solution.py:209
  10.7 4.1 %copy-start = (f32[5,8,64,256]{3,2,1,0:T(8,128)S(1)}, f32[5,8,64,256]{3,2,1,0:T(8,128)}, u32[]{:S(2)}) copy-start(f32[5,8,64,256]{3,2,1,0:T(8,128)} %rest_9_.1) | copy-start | bytes 7864324
  10.7 4.9 %copy-start.1 = (f32[5,8,64,256]{3,2,1,0:T(8,128)S(1)}, f32[5,8,64,256]{3,2,1,0:T(8,128)}, u32[]{:S(2)}) copy-start(f32[5,8,64,256]{3,2,1,0:T(8,128)} %rest_10_.1) | copy-start | bytes 7864324
  15.6 0.7 copy-start.6
  16.3 9.7 %copy-start.12 = (f32[264,128]{1,0:T(8,128)S(1)}, f32[264,128]{1,0:T(8,128)}, u32[]{:S(2)}) copy-start(f32[264,128]{1,0:T(8,128)} %get-tuple-element.15) | copy-start | bytes 405508
  16.3 11.3 %copy-start.13 = (s32[8,2]{0,1:T(2,128)S(1)}, s32[8,2]{0,1:T(2,128)}, u32[]{:S(2)}) copy-start(s32[8,2]{0,1:T(2,128)} %param.10) | copy-start | bytes 196
  20.9 1.3 %copy-start.4 = (f32[5,6,64,256]{3,2,1,0:T(8,128)}, f32[5,6,64,256]{3,2,1,0:T(8,128)S(1)}, u32[]{:S(2)}) copy-start(f32[5,6,64,256]{3,2,1,0:T(8,128)S(1)} %inner_layers.1.rest_13_) | copy-start | bytes 5898244
  22.2 19.6 %copy-start.7 = (f32[8,128]{1,0:T(8,128)S(1)}, f32[8,128]{1,0:T(8,128)}, u32[]{:S(2)}) copy-start(f32[8,128]{1,0:T(8,128)} %get-tuple-element.13.couplings.rest_0_) | copy-start | bytes 12292
  22.2 19.6 %collective-permute-start.2 = (f32[5,5,64,256]{3,2,1,0:T(8,128)}, f32[5,5,64,256]{3,2,1,0:T(8,128)}, u32[]{:S(2)}, u32[]{:S(2)}) collective-permute-start(f32[5,5,64,256]{3,2,1,0:T(8,128)} %get-tuple-element.20), channel_id=1, source_target_pairs={{1,2},{2,1},{5,6},{6,5},{9,10},{10,9},{13,14},{14,13},{17,18},{18,... | collective-permute-start | bytes 4915208 | tf_op jit(solution)/shard_map/ppermute | solution.py:719
  24.1 17.6 %collective-permute-start.1 = (f32[5,5,64,256]{3,2,1,0:T(8,128)}, f32[5,5,64,256]{3,2,1,0:T(8,128)}, u32[]{:S(2)}, u32[]{:S(2)}) collective-permute-start(f32[5,5,64,256]{3,2,1,0:T(8,128)} %get-tuple-element.18), channel_id=1, source_target_pairs={{0,1},{1,0},{2,3},{3,2},{4,5},{5,4},{6,7},{7,6},{8,9},{9,8},{10,11... | collective-permute-start | bytes 4915208 | tf_op jit(solution)/shard_map/ppermute | solution.py:719
  26.0 8.5 %collective-permute-start.3 = (f32[2,264,128]{2,1,0:T(8,128)S(1)}, f32[2,264,128]{2,1,0:T(8,128)S(1)}, u32[]{:S(2)}, u32[]{:S(2)}) collective-permute-start(f32[2,264,128]{2,1,0:T(8,128)S(1)} %pad_maximum_fusion.held), channel_id=1, source_target_pairs={{0,8},{4,12},{8,0},{12,4},{16,24},{20,28},{24,16},{28,20},{1,9},{5... | collective-permute-start | bytes 811016 | tf_op jit(solution)/shard_map/ppermute | solution.py:209
  35.1 5.1 %collective-permute-start.4 = (f32[264,128]{1,0:T(8,128)S(1)}, f32[264,128]{1,0:T(8,128)S(1)}, u32[]{:S(2)}, u32[]{:S(2)}) collective-permute-start(f32[264,128]{1,0:T(8,128)S(1)} %pick_ends.1), channel_id=1, source_target_pairs={{0,4},{4,0},{8,12},{12,8},{16,20},{20,16},{24,28},{28,24},{1,5},{5... | collective-permute-start | bytes 405512 | tf_op jit(solution)/shard_map/ppermute | solution.py:223
  40.8 8.0 %collective-permute-start.5 = (f32[264,128]{1,0:T(8,128)S(1)}, f32[264,128]{1,0:T(8,128)S(1)}, u32[]{:S(2)}, u32[]{:S(2)}) collective-permute-start(f32[264,128]{1,0:T(8,128)S(1)} %choose_ends.1.rest_6_), channel_id=1, source_target_pairs={{0,1},{1,0},{2,3},{3,2},{4,5},{5,4},{6,7},{7,6},{8,9},{9,8},{10,11... | collective-permute-start | bytes 405512 | tf_op jit(solution)/shard_map/ppermute | solution.py:719
  40.9 7.9 %collective-permute-start.6 = (f32[264,128]{1,0:T(8,128)S(1)}, f32[264,128]{1,0:T(8,128)S(1)}, u32[]{:S(2)}, u32[]{:S(2)}) collective-permute-start(f32[264,128]{1,0:T(8,128)S(1)} %choose_ends.1.rest_6_), channel_id=1, source_target_pairs={{1,2},{2,1},{5,6},{6,5},{9,10},{10,9},{13,14},{14,13},{17,18},{18,... | collective-permute-start | bytes 405512 | tf_op jit(solution)/shard_map/ppermute | solution.py:719
  41.8 1.7 %copy-start.2 = (f32[5,8,64,256]{3,2,1,0:T(8,128)S(1)}, f32[5,8,64,256]{3,2,1,0:T(8,128)}, u32[]{:S(2)}) copy-start(f32[5,8,64,256]{3,2,1,0:T(8,128)} %rest_10_.1) | copy-start | bytes 7864324
  43.5 5.3 %copy-start.3 = (f32[5,8,64,256]{3,2,1,0:T(8,128)S(1)}, f32[5,8,64,256]{3,2,1,0:T(8,128)}, u32[]{:S(2)}) copy-start(f32[5,8,64,256]{3,2,1,0:T(8,128)} %rest_10_.1) | copy-start | bytes 7864324
  43.5 5.3 %copy-start.5 = (f32[5,6,64,256]{3,2,1,0:T(8,128)S(1)}, f32[5,6,64,256]{3,2,1,0:T(8,128)}, u32[]{:S(2)}) copy-start(f32[5,6,64,256]{3,2,1,0:T(8,128)} %copy-done.4) | copy-start | bytes 5898244
  43.5 5.3 %copy-start.8 = (f32[2,5,64,128]{3,2,1,0:T(8,128)S(1)}, f32[2,5,64,128]{3,2,1,0:T(8,128)}, u32[]{:S(2)}) copy-start(f32[2,5,64,128]{3,2,1,0:T(8,128)} %get-tuple-element.14.rest_1_) | copy-start | bytes 983044
  43.5 5.3 %copy-start.9 = (f32[3,5,2,8,256]{4,3,2,1,0:T(8,128)S(1)}, f32[3,5,2,8,256]{4,3,2,1,0:T(8,128)}, u32[]{:S(2)}) copy-start(f32[3,5,2,8,256]{4,3,2,1,0:T(8,128)} %rest_15_.1) | copy-start | bytes 737284
  48.9 15.2 %copy-start.10 = (f32[8,8,256]{2,1,0:T(8,128)S(1)}, f32[8,8,256]{2,1,0:T(8,128)}, u32[]{:S(2)}) copy-start(f32[8,8,256]{2,1,0:T(8,128)} %weight.1) | copy-start | bytes 196612
  48.9 15.1 %copy-start.11 = (s32[8,8,256]{2,1,0:T(8,128)S(1)}, s32[8,8,256]{2,1,0:T(8,128)}, u32[]{:S(2)}) copy-start(s32[8,8,256]{2,1,0:T(8,128)} %ids.1) | copy-start | bytes 196612
  68.2 4.2 %collective-permute-start.7 = (f32[3,48,128]{2,1,0:T(8,128)S(1)}, f32[3,48,128]{2,1,0:T(8,128)S(1)}, u32[]{:S(2)}, u32[]{:S(2)}) collective-permute-start(f32[3,48,128]{2,1,0:T(8,128)S(1)} %constant_dynamic-slice_fusion), channel_id=1, source_target_pairs={{0,1},{1,0},{2,3},{3,2},{4,5},{5,4},{6,7},{7,6},{8,9},{9,8},{10,11... | collective-permute-start | bytes 221192 | tf_op jit(solution)/shard_map/ppermute | solution.py:702

commit v9 on v8

--- a/solution.py
+++ b/solution.py
@@ -31,17 +31,15 @@
 
 
 def chord_tile(layers):
-    lane = lane_iota((1, 1, LANES))
+    lane = lane_iota((1, layers[0][1].shape[1], LANES))
+    low, near, far = lane < HALF, (lane < 2) | (lane >= 125), (lane < 3) | (lane >= 126)
     total = None
     for s, both in layers:
-        ends = jnp.where(lane < HALF, both[..., :LANES], both[..., LANES:])
+        ends = jnp.where(low, both[..., :LANES], both[..., LANES:])
         base = lane_base(s)
-        near = pltpu.roll(ends, (base + 3) % LANES, 2)
-        far = pltpu.roll(ends, (HALF + base + 2) % LANES, 2)
-        at = lane - base
-        total = jnp.where((at >= 0) & (at < 5), near, 0.0 if total is None else total)
-        at = at - HALF
-        total = jnp.where((at >= 0) & (at < 5), far, total)
+        a = pltpu.roll(jnp.where(near, ends, 0.0), (base + 3) % LANES, 2)
+        b = pltpu.roll(jnp.where(far, ends, 0.0), (HALF + base + 2) % LANES, 2)
+        total = a + b if total is None else total + (a + b)
     return total
 
 
@@ -54,7 +52,7 @@
     tiles = [chord_tile([(s, field[:, s]) for s in range(field.shape[1])]) for field in (src, inv)]
     for f in range(2):
         tile[f] = tiles[f]
-    lane = lane_iota((1, LANES))
+    lane = lane_iota((depth, LANES))
     place = lane & (HALF - 1)
     is_src = place - COLS * ((place * 43) >> 8) < 3
     x, y = tiles[0][0], tiles[1][0]
@@ -158,10 +156,14 @@
             pltpu.VMEM((2, 2 * DEEP, nvar, depth, chord), jnp.float32),
             pltpu.SemaphoreType.DMA((2, 2, 2 * DEEP)),
         ],
-        compiler_params=pltpu.CompilerParams(vmem_limit_bytes=56 * MIB),
+        compiler_params=pltpu.CompilerParams(vmem_limit_bytes=8 * MIB),
         cost_estimate=pl.CostEstimate(flops=0, bytes_accessed=8 * MIB, transcendentals=0),
         name="span_layers",
     )(even, source, inv_diag)
+
+
+def ordered(x, *after):
+    return lax.optimization_barrier((x, *after))[0]
 
 
 def exchange_masks(count):
@@ -199,7 +201,7 @@
     out[...] = jnp.where(keep, mine, given[...])
 
 
-def route_ends(packet, me, face_map):
+def route_ends(packet, me, face_map, meanwhile):
     count = lax.axis_size("blk")
     masks = exchange_masks(count)
     held, received = packet[None], []
@@ -207,6 +209,8 @@
         if received:
             held = jnp.concatenate([held, received[-1]], 0)
         received.append(lax.ppermute(held, "blk", [(i, i ^ mask) for i in range(count)]))
+    other = meanwhile(received[0])
+    me = ordered(me, other[0])
 
     def call(kernel, name, *operands):
         return pl.pallas_call(
@@ -221,7 +225,7 @@
     picked = call(pick_kernel, "pick_ends", held, received[-1])
     last = masks[-1]
     given = lax.ppermute(picked, "blk", [(i, i ^ last) for i in range(count)])
-    return call(choose_kernel, "choose_ends", held, received[-1], given), received
+    return call(choose_kernel, "choose_ends", held, received[-1], given), other
 
 
 def expand_couplings(couplings, wide):
@@ -256,7 +260,7 @@
 
 def ribbon_sweeps(depth, up, own, near_in, near_out, given, given_in, given_out, mine, scalars, faces):
     nvar = 5
-    lane = lane_iota((1, LANES))
+    lane = lane_iota((depth, LANES))
     place = lane & (HALF - 1)
     slot = place - COLS * ((place * 43) >> 8)
     side = lane >= HALF
@@ -321,18 +325,18 @@
 
     own_rows = spread(mine[...])
     scalars[0] = own_rows
-    scalars[1] = jnp.where(ghost, spread(given[(nvar - 1) * depth : (nvar - 1) * depth + 8, :]), own_rows)
+    scalars[1] = jnp.where(ghost[:1], spread(given[(nvar - 1) * depth : (nvar - 1) * depth + 8, :]), own_rows)
     mixed = [scalars[1, i : i + 1, :] for i in range(150)]
     own_c = {i: scalars[0, i : i + 1, :] for i in range(100, 150)}
     high_face = (side & jnp.logical_not(lane == HALF + 60)) | (lane == 60)
+    face_c = [jnp.where(high_face[:1], own_c[125 + at], own_c[100 + at]) for at in range(25)]
     k = lax.broadcasted_iota(jnp.int32, (depth, LANES), 0)
     p = [inv[v] * src[v] for v in range(nvar)]
     for n in range(SWEEPS):
         for u in range(nvar):
             face = jnp.zeros((depth, LANES), jnp.float32)
             for v in range(nvar):
-                at = u * nvar + v
-                face += jnp.where(high_face, own_c[125 + at], own_c[100 + at]) * p[v]
+                face += face_c[u * nvar + v] * p[v]
             faces[n, u, 0:depth, :] = face
         if n == SWEEPS - 1:
             break
@@ -412,16 +416,18 @@
         one(1, src_in.at[:, 0], at, False)
         one(2, src_in.at[:, 0], at, False)
         low, high = face_tiles(0, at, slice(0, rows))
-        pb[:, at, :, :LANES] += inv[:, at, :, :LANES] * jnp.where(lane == 0, low, 0.0)
-        pb[:, at, :, LANES:] += inv[:, at, :, LANES:] * jnp.where(lane == LANES - 1, high, 0.0)
+        every = lane_iota((1, rows, LANES))
+        pb[:, at, :, :LANES] += inv[:, at, :, :LANES] * jnp.where(every == 0, low, 0.0)
+        pb[:, at, :, LANES:] += inv[:, at, :, LANES:] * jnp.where(every == LANES - 1, high, 0.0)
 
     def leave(at, start):
         copy = pltpu.make_async_copy(pb.at[:, at], leaves(at), out_sems.at[at])
         copy.start() if start else copy.wait()
 
     groups = rows // 16
-    lane = lane_iota((1, 1, LANES))
-    k = lax.broadcasted_iota(jnp.int32, (1, 16, 1), 1)
+    lane = lane_iota((1, 16, LANES))
+    first_lane, last_lane = lane == 0, lane == LANES - 1
+    k = lax.broadcasted_iota(jnp.int32, (1, 16, chord), 1)
     first_row, last_row = k == 0, k == 15
 
     def products(p, s, g, first, last):
@@ -456,8 +462,8 @@
             b = pltpu.roll(chord_low[..., LANES:], 1, 2)
             c = pltpu.roll(chord_high[..., :LANES], LANES - 1, 2)
             d = pltpu.roll(chord_high[..., LANES:], LANES - 1, 2)
-            left = jnp.where(lane == 0, at_low, a) + jnp.where(lane == LANES - 1, d, c)
-            right = jnp.where(lane == 0, a, b) + jnp.where(lane == LANES - 1, at_high, d)
+            left = jnp.where(first_lane, at_low, a) + jnp.where(last_lane, d, c)
+            right = jnp.where(first_lane, a, b) + jnp.where(last_lane, at_high, d)
             total += jnp.concatenate([left, right], 2)
             if g > 0:
                 before[:, 16 * g - 16 : 16 * g] = waiting + jnp.where(
@@ -561,7 +567,7 @@
         out_specs=ANY,
         out_shape=jax.ShapeDtypeStruct((nvar, 6, depth, chord), jnp.float32),
         scratch_shapes=sweep_scratch(nvar, spans, chord, depth),
-        compiler_params=pltpu.CompilerParams(vmem_limit_bytes=28 * MIB),
+        compiler_params=pltpu.CompilerParams(vmem_limit_bytes=24 * MIB),
         cost_estimate=pl.CostEstimate(flops=flops, bytes_accessed=4 * MIB, transcendentals=0),
         name=name,
     )(even, couplings, source, inv_diag, *halos)
@@ -624,7 +630,7 @@
             jax.ShapeDtypeStruct(sens, jnp.float32),
         ],
         scratch_shapes=sweep_scratch(nvar, spans, chord, depth),
-        compiler_params=pltpu.CompilerParams(vmem_limit_bytes=40 * MIB),
+        compiler_params=pltpu.CompilerParams(vmem_limit_bytes=30 * MIB),
         cost_estimate=pl.CostEstimate(flops=11 * 10**9, bytes_accessed=16 * MIB, transcendentals=0),
         name="last_sweeps",
     )(
@@ -708,10 +714,6 @@
     ).sum(0)
 
 
-def ordered(x, *after):
-    return lax.optimization_barrier((x, *after))[0]
-
-
 def swap_spans(inner, outer):
     count = lax.axis_size("sub")
     pairs = [(i, i ^ 1) for i in range(count)]
@@ -725,13 +727,13 @@
     me = lax.axis_index("blk").astype(jnp.int32).reshape(1)
     own, packet, cpl = chord_ends(source, inv_diag, coupling)
     inner, outer = span_layers(ordered(even, packet), source, inv_diag)
-    p_inner = first_sweep(
-        inner_kernel, "inner_layers", 10**8, ordered(even, packet), cpl, source, inv_diag
-    )
-    given, received = route_ends(packet, me, face_map)
-    inner, outer = swap_spans(
-        ordered(inner, received[0], p_inner), ordered(outer, received[0], p_inner)
-    )
+    def meanwhile(first):
+        p = first_sweep(
+            inner_kernel, "inner_layers", 10**8, ordered(even, first), cpl, source, inv_diag
+        )
+        return p, *swap_spans(ordered(inner, first), ordered(outer, first))
+
+    given, (p_inner, inner, outer) = route_ends(packet, me, face_map, meanwhile)
     p_outer = first_sweep(
         outer_kernel, "outer_layers", 10**8, ordered(even, given), cpl, source, inv_diag, inner, outer
     )

time: 86.3 us -> 83.4 us (0.966)
  waiting for transfers between devices: 11.2 us -> 7.37 us
  blocking collectives: 12.8 us -> 14.7 us
  local copies, waits for them, and re-layouts: 5.09 us -> 6.68 us
  Pallas kernels: 40.2 us -> 38.9 us
  starting transfers between devices: 15.1 us -> 14 us
    ppermute x2, waiting for transfers between devices: 6.76 us -> 2.7 us  [route_ends(): lax.ppermute(held, 'blk', [(i, i ^ mask) for i in range(count)])]
    all_to_all x1, blocking collectives: 12.8 us -> 14.7 us  [reduce_points(): lax.all_to_all(parts, ('blk', 'sub'), 0, 0, tiled=True, axis_index_groups...]
    unnamed x29, local copies, waits for them, and re-layouts: 5.02 us -> 6.61 us
    pallas_call x1, Pallas kernels: 3.67 us -> 2.23 us  [span_layers(): pl.pallas_call(layers_kernel, in_specs=[SMEM, ANY, ANY], out_specs=[ANY,...]
  transfers between devices with their start and end apart: 8 -> 8, of which waited for: 3 -> 3; matrix products, arithmetic and copies ran while one was open for 0% -> 0% of each run, Pallas kernels for 17% -> 16%
where the time goes in v9:
time: 83.4 us; the launch traced here: 83.1 us
  Pallas kernels  38.9 us (47%)
  blocking collectives  14.7 us (18%)
  starting transfers between devices  14 us (17%)
  waiting for transfers between devices  7.37 us (9%)
  local copies, waits for them, and re-layouts  6.68 us (8%)
  between operations  0.85 us (1%)
    pallas_call x1, Pallas kernels, last_sweeps(): pl.pallas_call(last_kernel, grid=(1,), in_specs=[SMEM, whole(cpl), whole(...  15.2 us
    all_to_all x1, blocking collectives, reduce_points(): lax.all_to_all(parts, ('blk', 'sub'), 0, 0, tiled=True, axis_index_groups...  14.7 us
    pallas_call x2, Pallas kernels, first_sweep(): pl.pallas_call(kernel, in_specs=[SMEM, VMEM] + [ANY] * (2 + len(halos)),...  9.84 us
    unnamed x29, local copies, waits for them, and re-layouts  6.61 us
    pallas_call x1, Pallas kernels, chord_ends(): pl.pallas_call(ends_kernel, grid=(nvar,), in_specs=[field, field, pl.Bloc...  6.16 us
    ppermute x2, starting transfers between devices, route_ends(): lax.ppermute(held, 'blk', [(i, i ^ mask) for i in range(count)])  4.87 us
    pallas_call x1, Pallas kernels, scatter_points(): pl.pallas_call(scatter_kernel, in_specs=[VMEM, VMEM, VMEM], out_specs=VME...  4.18 us
    ppermute x1, waiting for transfers between devices, route_ends(): given = lax.ppermute(picked, 'blk', [(i, i ^ last) for i in range(count)])  3.74 us
  transfers between devices with their start and end apart: 8, of which 3 were waited for; matrix products, arithmetic and copies ran while one was open for 0% of the time, Pallas kernels for 16%

profile of v9, /device:TPU:0, one launch (start us, length us, event | category | flops | bytes accessed | tf_op | source)
XLA Modules:
  0.0 83.1 jit_solution(19285434363598652)
XLA Ops:
  0.6 0.0 copy-start
  0.6 6.2 %chord_ends.1 = (f32[2,5,64,128]{3,2,1,0:T(8,128)}, f32[264,128]{1,0:T(8,128)}, f32[8,128]{1,0:T(8,128)}) custom-call(f32[5,8,64,256]{3,2,1,0:T(8,128)} %rest_9_.1, f32[5,8,64,256]{3,2,1,0:T(8,128)} %rest_10_.1, f32[5,5,1,6]{3,2,1,0:T(1,128)} %bitcast.10), custom_call_target="tpu_custom_call" | custom-call | tf_op jit(solution)/shard_map/chord_ends/pallas_call | solution.py:99
  6.8 4.0 %collective-permute-start = (f32[1,264,128]{2,1,0:T(8,128)}, f32[1,264,128]{2,1,0:T(8,128)S(1)}, u32[]{:S(2)}, u32[]{:S(2)}) collective-permute-start(f32[1,264,128]{2,1,0:T(8,128)} %bitcast.8), channel_id=1, source_target_pairs={{0,16},{4,20},{8,24},{12,28},{16,0},{20,4},{24,8},{28,12},{1,17},{... | collective-permute-start | bytes 405512 | tf_op jit(solution)/shard_map/ppermute | solution.py:211
  10.8 0.0 copy-done
  10.8 0.0 copy-start.1
  10.8 1.7 %copy-done.1 = f32[5,8,64,256]{3,2,1,0:T(8,128)S(1)} copy-done((f32[5,8,64,256]{3,2,1,0:T(8,128)S(1)}, f32[5,8,64,256]{3,2,1,0:T(8,128)}, u32[]{:S(2)}) %copy-start.1) | copy-done | bytes 2621464
  12.6 0.0 copy-start.12
  12.6 2.2 %span_layers.1 = (f32[5,5,64,256]{3,2,1,0:T(8,128)}, f32[5,5,64,256]{3,2,1,0:T(8,128)}) custom-call(s32[1]{0:T(128)} %bitcast.even, f32[5,8,64,256]{3,2,1,0:T(8,128)S(1)} %copy-done, f32[5,8,64,256]{3,2,1,0:T(8,128)S(1)} %copy-done.1), custom_call_target="tpu_custom_call" | custom-call | bytes 8388608 | tf_op jit(solution)/shard_map/span_layers/pallas_call | solution.py:150
  14.8 2.7 %collective-permute-done = f32[1,264,128]{2,1,0:T(8,128)S(1)} collective-permute-done((f32[1,264,128]{2,1,0:T(8,128)}, f32[1,264,128]{2,1,0:T(8,128)S(1)}, u32[]{:S(2)}, u32[]{:S(2)}) %collective-permute-start) | collective-permute-done | bytes 135200 | tf_op jit(solution)/shard_map/ppermute | solution.py:211
  17.5 1.8 %collective-permute-start.2 = (f32[5,5,64,256]{3,2,1,0:T(8,128)}, f32[5,5,64,256]{3,2,1,0:T(8,128)}, u32[]{:S(2)}, u32[]{:S(2)}) collective-permute-start(f32[5,5,64,256]{3,2,1,0:T(8,128)} %get-tuple-element.22), channel_id=1, source_target_pairs={{1,2},{2,1},{5,6},{6,5},{9,10},{10,9},{13,14},{14,13},{17,18},{18,... | collective-permute-start | bytes 4915208 | tf_op jit(solution)/shard_map/ppermute | solution.py:721
  19.3 1.8 %collective-permute-start.1 = (f32[5,5,64,256]{3,2,1,0:T(8,128)}, f32[5,5,64,256]{3,2,1,0:T(8,128)}, u32[]{:S(2)}, u32[]{:S(2)}) collective-permute-start(f32[5,5,64,256]{3,2,1,0:T(8,128)} %get-tuple-element.20), channel_id=1, source_target_pairs={{0,1},{1,0},{2,3},{3,2},{4,5},{5,4},{6,7},{7,6},{8,9},{9,8},{10,11... | collective-permute-start | bytes 4915208 | tf_op jit(solution)/shard_map/ppermute | solution.py:721
  21.2 0.0 copy-done.12
  21.2 0.8 %collective-permute-start.3 = (f32[2,264,128]{2,1,0:T(8,128)S(1)}, f32[2,264,128]{2,1,0:T(8,128)S(1)}, u32[]{:S(2)}, u32[]{:S(2)}) collective-permute-start(f32[2,264,128]{2,1,0:T(8,128)S(1)} %pad_maximum_fusion.held), channel_id=1, source_target_pairs={{0,8},{4,12},{8,0},{12,4},{16,24},{20,28},{24,16},{28,20},{1,9},{5... | collective-permute-start | bytes 811016 | tf_op jit(solution)/shard_map/ppermute | solution.py:211
  22.1 0.0 copy-done.13
  22.1 0.1 copy.12.faces
  22.1 0.0 copy-done.7
  22.1 1.7 %copy-done.2 = f32[5,8,64,256]{3,2,1,0:T(8,128)S(1)} copy-done((f32[5,8,64,256]{3,2,1,0:T(8,128)S(1)}, f32[5,8,64,256]{3,2,1,0:T(8,128)}, u32[]{:S(2)}) %copy-start.2) | copy-done | bytes 2621464
  23.9 4.6 %inner_layers.1.rest_13_ = f32[5,6,64,256]{3,2,1,0:T(8,128)S(1)} custom-call(s32[1]{0:T(128)} %bitcast.even, f32[8,128]{1,0:T(8,128)S(1)} %copy-done.7, f32[5,8,64,256]{3,2,1,0:T(8,128)S(1)} %copy-done, f32[5,8,64,256]{3,2,1,0:T(8,128)S(1)} %copy-done.2), custom_call_target="tpu_custom_call" | custom-call | flops 100000000 | bytes 4194304 | tf_op jit(solution)/shard_map/inner_layers/pallas_call | solution.py:564
  28.5 0.0 copy-start.5
  28.5 1.3 %copy-done.5 = f32[5,6,64,256]{3,2,1,0:T(8,128)} copy-done((f32[5,6,64,256]{3,2,1,0:T(8,128)}, f32[5,6,64,256]{3,2,1,0:T(8,128)S(1)}, u32[]{:S(2)}) %copy-start.5) | copy-done | bytes 1966104
  29.8 0.0 collective-permute-done.3.more
  29.8 0.6 pick_ends.1
  30.4 1.6 %collective-permute-start.4 = (f32[264,128]{1,0:T(8,128)S(1)}, f32[264,128]{1,0:T(8,128)S(1)}, u32[]{:S(2)}, u32[]{:S(2)}) collective-permute-start(f32[264,128]{1,0:T(8,128)S(1)} %pick_ends.1), channel_id=1, source_target_pairs={{0,4},{4,0},{8,12},{12,8},{16,20},{20,16},{24,28},{28,24},{1,5},{5... | collective-permute-start | bytes 405512 | tf_op jit(solution)/shard_map/ppermute | solution.py:227
  32.0 3.7 %collective-permute-done.4.given = f32[264,128]{1,0:T(8,128)S(1)} collective-permute-done((f32[264,128]{1,0:T(8,128)S(1)}, f32[264,128]{1,0:T(8,128)S(1)}, u32[]{:S(2)}, u32[]{:S(2)}) %collective-permute-start.4) | collective-permute-done | bytes 135200 | tf_op jit(solution)/shard_map/ppermute | solution.py:227
  35.7 0.7 choose_ends.1.rest_6_
  36.4 0.1 collective-permute-start.5
  36.5 0.8 %collective-permute-start.6 = (f32[264,128]{1,0:T(8,128)S(1)}, f32[264,128]{1,0:T(8,128)S(1)}, u32[]{:S(2)}, u32[]{:S(2)}) collective-permute-start(f32[264,128]{1,0:T(8,128)S(1)} %choose_ends.1.rest_6_), channel_id=1, source_target_pairs={{1,2},{2,1},{5,6},{6,5},{9,10},{10,9},{13,14},{14,13},{17,18},{18,... | collective-permute-start | bytes 405512 | tf_op jit(solution)/shard_map/ppermute | solution.py:721
  37.3 0.0 collective-permute-done.2.outer.rest_4_.rest_5_.rest_12_
  37.3 0.0 collective-permute-done.1.inner.rest_2_.rest_3_.rest_11_
  37.3 0.0 copy-start.3
  37.4 1.7 %copy-done.3 = f32[5,8,64,256]{3,2,1,0:T(8,128)S(1)} copy-done((f32[5,8,64,256]{3,2,1,0:T(8,128)S(1)}, f32[5,8,64,256]{3,2,1,0:T(8,128)}, u32[]{:S(2)}) %copy-start.3) | copy-done | bytes 2621464
  39.1 5.2 %outer_layers.1.rest_14_ = f32[5,6,64,256]{3,2,1,0:T(8,128)S(1)} custom-call(s32[1]{0:T(128)} %bitcast.even, f32[8,128]{1,0:T(8,128)S(1)} %copy-done.7, f32[5,8,64,256]{3,2,1,0:T(8,128)S(1)} %copy-done, f32[5,8,64,256]{3,2,1,0:T(8,128)S(1)} %copy-done.3, f32[5,5,64,256]{3,2,1,0:T(8,128)} %collective-permute-done.1.inner.rest_2_.rest_3_.rest_11_, ...), custom_call_target="tpu_custom_call" | custom-call | flops 100000000 | bytes 4194304 | tf_op jit(solution)/shard_map/outer_layers/pallas_call | solution.py:564
  44.3 0.0 collective-permute-done.5.rest_7_
  44.3 0.0 collective-permute-done.6.rest_8_
  44.4 0.0 copy-done.4
  44.4 0.0 copy-done.6
  44.4 0.0 copy-done.8
  44.4 0.0 copy-done.9
  44.4 0.0 copy-start.10
  44.4 0.0 copy-start.11
  44.4 15.2 %last_sweeps.1 = (f32[5,8,64,256]{3,2,1,0:T(8,128)}, f32[3,8,256]{2,1,0:T(8,128)S(1)}) custom-call(s32[1]{0:T(128)} %bitcast.even, f32[8,128]{1,0:T(8,128)S(1)} %copy-done.7, f32[2,5,64,128]{3,2,1,0:T(8,128)S(1)} %copy-done.8, f32[5,5,64,256]{3,2,1,0:T(8,128)} %collective-permute-done.1.inner.rest_2_.rest_3_.rest_11_, ...), custom_call_target="tpu_custom_call" | custom-call | flops 11000000512 | bytes 16777216 | tf_op jit(solution)/shard_map/last_sweeps/pallas_call | solution.py:619
  59.6 0.0 copy-done.10
  59.6 0.0 copy-done.11
  59.6 4.2 %scatter_points.1 = f32[3,48,256]{2,1,0:T(8,128)S(1)} custom-call(f32[3,8,256]{2,1,0:T(8,128)S(1)} %get-tuple-element.27.sens, f32[8,8,256]{2,1,0:T(8,128)S(1)} %copy-done.10, s32[8,8,256]{2,1,0:T(8,128)S(1)} %copy-done.11), custom_call_target="tpu_custom_call" | custom-call | flops 4000000000 | bytes 1048576 | tf_op jit(solution)/shard_map/scatter_points/pallas_call | solution.py:690
  63.8 3.0 %collective-permute-start.7 = (f32[3,48,128]{2,1,0:T(8,128)S(1)}, f32[3,48,128]{2,1,0:T(8,128)S(1)}, u32[]{:S(2)}, u32[]{:S(2)}) collective-permute-start(f32[3,48,128]{2,1,0:T(8,128)S(1)} %constant_dynamic-slice_fusion), channel_id=1, source_target_pairs={{0,1},{1,0},{2,3},{3,2},{4,5},{5,4},{6,7},{7,6},{8,9},{9,8},{10,11... | collective-permute-start | bytes 221192 | tf_op jit(solution)/shard_map/ppermute | solution.py:708
  66.8 0.9 %collective-permute-done.7 = f32[3,48,128]{2,1,0:T(8,128)S(1)} collective-permute-done((f32[3,48,128]{2,1,0:T(8,128)S(1)}, f32[3,48,128]{2,1,0:T(8,128)S(1)}, u32[]{:S(2)}, u32[]{:S(2)}) %collective-permute-start.7) | collective-permute-done | bytes 73760 | tf_op jit(solution)/shard_map/ppermute | solution.py:708
  67.8 14.7 %all_to_all.5 = f32[16,3,384]{2,1,0:T(4,128)S(1)} all-to-all(f32[16,3,384]{2,1,0:T(4,128)S(1)} %bitcast.7), channel_id=1, replica_groups={{0,2,4,6,8,10,12,14,16,18,20,22,24,26,28,30},{1,3,5,7,9,11,13,15,17,19,..., dimensions={0} | all-to-all | bytes 147456 | tf_op jit(solution)/shard_map/all_to_all | solution.py:712
  82.4 0.6 reduce_sum.9
  (12 shorter events, 0.1 us)
Async XLA Ops:
  0.6 10.2 %copy-start = (f32[5,8,64,256]{3,2,1,0:T(8,128)S(1)}, f32[5,8,64,256]{3,2,1,0:T(8,128)}, u32[]{:S(2)}) copy-start(f32[5,8,64,256]{3,2,1,0:T(8,128)} %rest_9_.1) | copy-start | bytes 7864324
  6.8 10.7 %collective-permute-start = (f32[1,264,128]{2,1,0:T(8,128)}, f32[1,264,128]{2,1,0:T(8,128)S(1)}, u32[]{:S(2)}, u32[]{:S(2)}) collective-permute-start(f32[1,264,128]{2,1,0:T(8,128)} %bitcast.8), channel_id=1, source_target_pairs={{0,16},{4,20},{8,24},{12,28},{16,0},{20,4},{24,8},{28,12},{1,17},{... | collective-permute-start | bytes 405512 | tf_op jit(solution)/shard_map/ppermute | solution.py:211
  10.8 1.7 %copy-start.1 = (f32[5,8,64,256]{3,2,1,0:T(8,128)S(1)}, f32[5,8,64,256]{3,2,1,0:T(8,128)}, u32[]{:S(2)}) copy-start(f32[5,8,64,256]{3,2,1,0:T(8,128)} %rest_10_.1) | copy-start | bytes 7864324
  12.6 8.6 %copy-start.12 = (f32[264,128]{1,0:T(8,128)S(1)}, f32[264,128]{1,0:T(8,128)}, u32[]{:S(2)}) copy-start(f32[264,128]{1,0:T(8,128)} %get-tuple-element.17) | copy-start | bytes 405508
  12.6 9.5 %copy-start.13 = (s32[8,2]{0,1:T(2,128)S(1)}, s32[8,2]{0,1:T(2,128)}, u32[]{:S(2)}) copy-start(s32[8,2]{0,1:T(2,128)} %param.10) | copy-start | bytes 196
  12.6 9.6 %copy-start.7 = (f32[8,128]{1,0:T(8,128)S(1)}, f32[8,128]{1,0:T(8,128)}, u32[]{:S(2)}) copy-start(f32[8,128]{1,0:T(8,128)} %get-tuple-element.15.couplings.rest_0_) | copy-start | bytes 12292
  17.5 19.8 %collective-permute-start.2 = (f32[5,5,64,256]{3,2,1,0:T(8,128)}, f32[5,5,64,256]{3,2,1,0:T(8,128)}, u32[]{:S(2)}, u32[]{:S(2)}) collective-permute-start(f32[5,5,64,256]{3,2,1,0:T(8,128)} %get-tuple-element.22), channel_id=1, source_target_pairs={{1,2},{2,1},{5,6},{6,5},{9,10},{10,9},{13,14},{14,13},{17,18},{18,... | collective-permute-start | bytes 4915208 | tf_op jit(solution)/shard_map/ppermute | solution.py:721
  19.3 18.0 %collective-permute-start.1 = (f32[5,5,64,256]{3,2,1,0:T(8,128)}, f32[5,5,64,256]{3,2,1,0:T(8,128)}, u32[]{:S(2)}, u32[]{:S(2)}) collective-permute-start(f32[5,5,64,256]{3,2,1,0:T(8,128)} %get-tuple-element.20), channel_id=1, source_target_pairs={{0,1},{1,0},{2,3},{3,2},{4,5},{5,4},{6,7},{7,6},{8,9},{9,8},{10,11... | collective-permute-start | bytes 4915208 | tf_op jit(solution)/shard_map/ppermute | solution.py:721
  21.2 8.6 %collective-permute-start.3 = (f32[2,264,128]{2,1,0:T(8,128)S(1)}, f32[2,264,128]{2,1,0:T(8,128)S(1)}, u32[]{:S(2)}, u32[]{:S(2)}) collective-permute-start(f32[2,264,128]{2,1,0:T(8,128)S(1)} %pad_maximum_fusion.held), channel_id=1, source_target_pairs={{0,8},{4,12},{8,0},{12,4},{16,24},{20,28},{24,16},{28,20},{1,9},{5... | collective-permute-start | bytes 811016 | tf_op jit(solution)/shard_map/ppermute | solution.py:211
  22.1 1.7 %copy-start.2 = (f32[5,8,64,256]{3,2,1,0:T(8,128)S(1)}, f32[5,8,64,256]{3,2,1,0:T(8,128)}, u32[]{:S(2)}) copy-start(f32[5,8,64,256]{3,2,1,0:T(8,128)} %rest_10_.1) | copy-start | bytes 7864324
  28.5 1.3 %copy-start.5 = (f32[5,6,64,256]{3,2,1,0:T(8,128)}, f32[5,6,64,256]{3,2,1,0:T(8,128)S(1)}, u32[]{:S(2)}) copy-start(f32[5,6,64,256]{3,2,1,0:T(8,128)S(1)} %inner_layers.1.rest_13_) | copy-start | bytes 5898244
  30.4 5.3 %collective-permute-start.4 = (f32[264,128]{1,0:T(8,128)S(1)}, f32[264,128]{1,0:T(8,128)S(1)}, u32[]{:S(2)}, u32[]{:S(2)}) collective-permute-start(f32[264,128]{1,0:T(8,128)S(1)} %pick_ends.1), channel_id=1, source_target_pairs={{0,4},{4,0},{8,12},{12,8},{16,20},{20,16},{24,28},{28,24},{1,5},{5... | collective-permute-start | bytes 405512 | tf_op jit(solution)/shard_map/ppermute | solution.py:227
  36.4 8.0 %collective-permute-start.5 = (f32[264,128]{1,0:T(8,128)S(1)}, f32[264,128]{1,0:T(8,128)S(1)}, u32[]{:S(2)}, u32[]{:S(2)}) collective-permute-start(f32[264,128]{1,0:T(8,128)S(1)} %choose_ends.1.rest_6_), channel_id=1, source_target_pairs={{0,1},{1,0},{2,3},{3,2},{4,5},{5,4},{6,7},{7,6},{8,9},{9,8},{10,11... | collective-permute-start | bytes 405512 | tf_op jit(solution)/shard_map/ppermute | solution.py:721
  36.5 7.9 %collective-permute-start.6 = (f32[264,128]{1,0:T(8,128)S(1)}, f32[264,128]{1,0:T(8,128)S(1)}, u32[]{:S(2)}, u32[]{:S(2)}) collective-permute-start(f32[264,128]{1,0:T(8,128)S(1)} %choose_ends.1.rest_6_), channel_id=1, source_target_pairs={{1,2},{2,1},{5,6},{6,5},{9,10},{10,9},{13,14},{14,13},{17,18},{18,... | collective-permute-start | bytes 405512 | tf_op jit(solution)/shard_map/ppermute | solution.py:721
  37.3 1.7 %copy-start.3 = (f32[5,8,64,256]{3,2,1,0:T(8,128)S(1)}, f32[5,8,64,256]{3,2,1,0:T(8,128)}, u32[]{:S(2)}) copy-start(f32[5,8,64,256]{3,2,1,0:T(8,128)} %rest_10_.1) | copy-start | bytes 7864324
  39.1 5.3 %copy-start.4 = (f32[5,8,64,256]{3,2,1,0:T(8,128)S(1)}, f32[5,8,64,256]{3,2,1,0:T(8,128)}, u32[]{:S(2)}) copy-start(f32[5,8,64,256]{3,2,1,0:T(8,128)} %rest_10_.1) | copy-start | bytes 7864324
  39.1 5.3 %copy-start.6 = (f32[5,6,64,256]{3,2,1,0:T(8,128)S(1)}, f32[5,6,64,256]{3,2,1,0:T(8,128)}, u32[]{:S(2)}) copy-start(f32[5,6,64,256]{3,2,1,0:T(8,128)} %copy-done.5) | copy-start | bytes 5898244
  39.1 5.3 %copy-start.8 = (f32[2,5,64,128]{3,2,1,0:T(8,128)S(1)}, f32[2,5,64,128]{3,2,1,0:T(8,128)}, u32[]{:S(2)}) copy-start(f32[2,5,64,128]{3,2,1,0:T(8,128)} %get-tuple-element.16.rest_1_) | copy-start | bytes 983044
  39.1 5.3 %copy-start.9 = (f32[3,5,2,8,256]{4,3,2,1,0:T(8,128)S(1)}, f32[3,5,2,8,256]{4,3,2,1,0:T(8,128)}, u32[]{:S(2)}) copy-start(f32[3,5,2,8,256]{4,3,2,1,0:T(8,128)} %rest_15_.1) | copy-start | bytes 737284
  44.4 15.2 %copy-start.10 = (f32[8,8,256]{2,1,0:T(8,128)S(1)}, f32[8,8,256]{2,1,0:T(8,128)}, u32[]{:S(2)}) copy-start(f32[8,8,256]{2,1,0:T(8,128)} %weight.1) | copy-start | bytes 196612
  44.4 15.2 %copy-start.11 = (s32[8,8,256]{2,1,0:T(8,128)S(1)}, s32[8,8,256]{2,1,0:T(8,128)}, u32[]{:S(2)}) copy-start(s32[8,8,256]{2,1,0:T(8,128)} %ids.1) | copy-start | bytes 196612
  63.8 3.9 %collective-permute-start.7 = (f32[3,48,128]{2,1,0:T(8,128)S(1)}, f32[3,48,128]{2,1,0:T(8,128)S(1)}, u32[]{:S(2)}, u32[]{:S(2)}) collective-permute-start(f32[3,48,128]{2,1,0:T(8,128)S(1)} %constant_dynamic-slice_fusion), channel_id=1, source_target_pairs={{0,1},{1,0},{2,3},{3,2},{4,5},{5,4},{6,7},{7,6},{8,9},{9,8},{10,11... | collective-permute-start | bytes 221192 | tf_op jit(solution)/shard_map/ppermute | solution.py:708

commit v10 on v9

--- a/solution.py
+++ b/solution.py
@@ -46,73 +46,70 @@
 FREE = 16
 
 
-def ends_kernel(src, inv, coupling, tile, packet, cpl):
-    depth = tile.shape[2]
-    nvar = packet.shape[0] // depth + 1
-    tiles = [chord_tile([(s, field[:, s]) for s in range(field.shape[1])]) for field in (src, inv)]
-    for f in range(2):
-        tile[f] = tiles[f]
+def ends_kernel(src, inv, coupling, tile, packet, cpl, held, sems):
+    nvar, _, depth, _ = src.shape
+    order = [nvar - 1, *range(nvar - 1)]
+    loads = {}
+    for v in order:
+        for f, field in enumerate((src, inv)):
+            loads[f, v] = pltpu.make_async_copy(field.at[v], held.at[f, v], sems.at[f, v])
+            loads[f, v].start()
     lane = lane_iota((depth, LANES))
     place = lane & (HALF - 1)
     is_src = place - COLS * ((place * 43) >> 8) < 3
-    x, y = tiles[0][0], tiles[1][0]
-    both = jnp.where(
-        lane >= HALF,
-        jnp.where(is_src, pltpu.roll(x, LANES - 2, 1), pltpu.roll(y, 1, 1)),
-        jnp.where(is_src, x, pltpu.roll(y, 3, 1)),
-    )
-    both = pltpu.roll(both, LANES - COLS, 1)
-    step = pl.program_id(0)
     free = place >= HALF - FREE
-
-    @pl.when(step == 0)
-    def _():
-        for j in range(nvar - 1):
-            shift = (HALF - FREE - FREE * j) % LANES
-            packet[j * depth : (j + 1) * depth, :] = pltpu.roll(both, shift, 1) if shift else both
-        m = jnp.concatenate([coupling[u, v] for u in range(nvar) for v in range(nvar)], 0)
-        pair = lax.broadcasted_iota(jnp.int32, (nvar * nvar, LANES), 0)
-        own = bit(pair == (lane_iota((nvar * nvar, LANES)) & (HALF - 1)))
-        rows = lax.dot_general(
-            m, own, (((0,), (0,)), ((), ())), precision=lax.Precision.HIGHEST,
-            preferred_element_type=jnp.float32,
+    m = jnp.concatenate([coupling[u, v] for u in range(nvar) for v in range(nvar)], 0)
+    pair = lax.broadcasted_iota(jnp.int32, (nvar * nvar, LANES), 0)
+    own = bit(pair == (lane_iota((nvar * nvar, LANES)) & (HALF - 1)))
+    rows = lax.dot_general(
+        m, own, (((0,), (0,)), ((), ())), precision=lax.Precision.HIGHEST,
+        preferred_element_type=jnp.float32,
+    )
+    rows = jnp.concatenate([rows, jnp.zeros((8 - rows.shape[0], LANES), jnp.float32)], 0)
+    cpl[...] = rows
+    packet[(nvar - 1) * depth : (nvar - 1) * depth + 8, :] = rows
+    spread = None
+    for v in order:
+        pair = []
+        for f in range(2):
+            loads[f, v].wait()
+            field = held.at[f, v]
+            one = chord_tile([(s, field[s][None]) for s in range(field.shape[0])])[0]
+            tile[f, v] = one
+            pair.append(one)
+        x, y = pair
+        both = jnp.where(
+            lane >= HALF,
+            jnp.where(is_src, pltpu.roll(x, LANES - 2, 1), pltpu.roll(y, 1, 1)),
+            jnp.where(is_src, x, pltpu.roll(y, 3, 1)),
         )
-        rows = jnp.concatenate([rows, jnp.zeros((8 - rows.shape[0], LANES), jnp.float32)], 0)
-        cpl[...] = rows
-        packet[(nvar - 1) * depth : (nvar - 1) * depth + 8, :] = rows
-
-    @pl.when(step > 0)
-    def _():
-        at = pl.ds(pl.multiple_of((step - 1) * depth, depth), depth)
-        packet[at, :] = jnp.where(free, packet[at, :], both)
+        both = pltpu.roll(both, LANES - COLS, 1)
+        if spread is None:
+            spread = both
+            continue
+        shift = (HALF - FREE - FREE * v) % LANES
+        moved = pltpu.roll(spread, shift, 1) if shift else spread
+        packet[v * depth : (v + 1) * depth, :] = jnp.where(free, moved, both)
 
 
 def chord_ends(source, inv_diag, coupling):
     nvar, spans, depth, chord = source.shape
-
-    def var(step):
-        return jnp.where(step == 0, nvar - 1, step - 1)
-
-    field = pl.BlockSpec((1, spans, depth, chord), lambda i: (var(i), 0, 0, 0))
-    rows = (nvar - 1) * depth + 8
-    small = coupling.transpose(2, 3, 0, 1)
     return pl.pallas_call(
         ends_kernel,
-        grid=(nvar,),
-        in_specs=[field, field, pl.BlockSpec(small.shape, lambda i: (0, 0, 0, 0))],
-        out_specs=[
-            pl.BlockSpec((2, 1, depth, LANES), lambda i: (0, var(i), 0, 0)),
-            pl.BlockSpec((rows, LANES), lambda i: (0, 0)),
-            pl.BlockSpec((8, LANES), lambda i: (0, 0)),
-        ],
+        in_specs=[ANY, ANY, VMEM],
+        out_specs=[VMEM] * 3,
         out_shape=[
             jax.ShapeDtypeStruct((2, nvar, depth, LANES), jnp.float32),
-            jax.ShapeDtypeStruct((rows, LANES), jnp.float32),
+            jax.ShapeDtypeStruct(((nvar - 1) * depth + 8, LANES), jnp.float32),
             jax.ShapeDtypeStruct((8, LANES), jnp.float32),
         ],
-        compiler_params=pltpu.CompilerParams(vmem_limit_bytes=56 * MIB),
+        scratch_shapes=[
+            pltpu.VMEM((2, nvar, spans, depth, chord), jnp.float32),
+            pltpu.SemaphoreType.DMA((2, nvar)),
+        ],
+        compiler_params=pltpu.CompilerParams(vmem_limit_bytes=58 * MIB),
         name="chord_ends",
-    )(source, inv_diag, small)
+    )(source, inv_diag, coupling.transpose(2, 3, 0, 1))
 
 
 def layers_kernel(even, src, inv, inner, outer, held, sems):
@@ -234,7 +231,7 @@
     row = lax.broadcasted_iota(jnp.int32, (rows, 8), 0)
     of = lax.broadcasted_iota(jnp.int32, (rows, 8), 1)
     group = row >> 4
-    pick_row = bit(((group * 205) >> 10) == of).astype(jnp.bfloat16)
+    pick_row = bit(((group * 205) >> 10) + 2 == of).astype(jnp.bfloat16)
     group = lax.broadcasted_iota(jnp.int32, (rows, LANES), 0) >> 4
     u = group - nvar * ((group * 205) >> 10)
     pair = lane_iota((rows, LANES))
@@ -356,8 +353,8 @@
         p = [inv[v] * total[v] for v in range(nvar)]
 
 
-def run_sweeps(stages, even, couplings, ribbon, src_in, inv_in, inner, outer, p_in, leaves, scratch):
-    src, inv, pa, pb, wide, before, coming, faces, scalars, sems, out_sems = scratch
+def run_sweeps(stages, even, scalar, couplings, ribbon, src_in, inv_in, inner, outer, p_in, leaves, scratch):
+    src, inv, pa, pb, wide, faces, scalars, sems, out_sems = scratch
     nvar, layers, rows, chord = pa.shape
     spans = layers - 2 * DEEP
     sweeps = [stage[0] for stage in stages]
@@ -400,117 +397,116 @@
     if ribbon is not None:
         ribbon_sweeps(rows, even[0], *ribbon, scalars, faces)
 
-    def face_tiles(n, s, at):
-        face = faces[n, :, at]
-        at_low = pltpu.roll(face, lax.rem(LANES + 10 - COLS * s, LANES), 2)
-        at_high = pltpu.roll(face, lax.rem(LANES + 73 - COLS * s, LANES), 2)
+    def face_tiles(n, s, at, u):
+        face = faces[n, u, at]
+        at_low = pltpu.roll(face, lax.rem(LANES + 10 - COLS * s, LANES), 1)
+        at_high = pltpu.roll(face, lax.rem(LANES + 73 - COLS * s, LANES), 1)
         return at_low, at_high
 
-    def arrive(at, edge=False):
+    def arrive(at):
         one(0, src_in.at[:, 0], at, False)
         if p_in is None:
-            if not edge:
+            if not isinstance(at, int) or 0 < at < layers - 1:
                 one(1, src_in.at[:, 0], at, False)
             pa[:, at] = inv[:, at] * src[:, at]
             return
         one(1, src_in.at[:, 0], at, False)
         one(2, src_in.at[:, 0], at, False)
-        low, high = face_tiles(0, at, slice(0, rows))
-        every = lane_iota((1, rows, LANES))
-        pb[:, at, :, :LANES] += inv[:, at, :, :LANES] * jnp.where(every == 0, low, 0.0)
-        pb[:, at, :, LANES:] += inv[:, at, :, LANES:] * jnp.where(every == LANES - 1, high, 0.0)
+        every = lane_iota((rows, LANES))
+        for u in range(nvar):
+            low, high = face_tiles(0, at, slice(0, rows), u)
+            pb[u, at, :, :LANES] += inv[u, at, :, :LANES] * jnp.where(every == 0, low, 0.0)
+            pb[u, at, :, LANES:] += inv[u, at, :, LANES:] * jnp.where(every == LANES - 1, high, 0.0)
 
     def leave(at, start):
         copy = pltpu.make_async_copy(pb.at[:, at], leaves(at), out_sems.at[at])
         copy.start() if start else copy.wait()
 
     groups = rows // 16
-    lane = lane_iota((1, 16, LANES))
+    lane = lane_iota((16, LANES))
     first_lane, last_lane = lane == 0, lane == LANES - 1
-    k = lax.broadcasted_iota(jnp.int32, (1, 16, chord), 1)
+    k = lax.broadcasted_iota(jnp.int32, (16, chord), 0)
     first_row, last_row = k == 0, k == 15
 
-    def products(p, s, g, first, last):
+    def products(p, s, g):
         x = p[:, s, 16 * g : 16 * g + 16, :].reshape(nvar * 16, chord)
         top = x.astype(jnp.bfloat16)
         rest = (x - top.astype(jnp.float32)).astype(jnp.bfloat16)
         none = jnp.zeros((16, chord), jnp.bfloat16)
         parts = jnp.concatenate([top, rest, top, none], 0)
-        y = jnp.dot(wide[first:last, :], parts, preferred_element_type=jnp.float32)
-        return y.reshape((last - first) // 16, 16, chord)
-
-    step = 16 * nvar
+        y = jnp.dot(wide[...], parts, preferred_element_type=jnp.float32)
+        return y.reshape(4 * nvar, 16, chord)
+
+    def span_terms(p, s, at, u):
+        total = src[u, s, at]
+        for v in range(nvar):
+            total += scalar[0, u * nvar + v] * p[v, s - 1, at]
+            total += scalar[1, u * nvar + v] * p[v, s + 1, at]
+        return total
 
     def one_layer(p, after, n, s):
         below, waiting = None, None
         for g in range(groups):
             at = slice(16 * g, 16 * g + 16)
-            every = products(p, s, g, 0, 6 * step)
-            span_low, span_high, normal_low, normal_high, chord_low, chord_high = [
-                every[d * nvar : (d + 1) * nvar] for d in range(6)
-            ]
-            after[:, s - 1, at] = inv[:, s - 1, at] * (before[:, at] + span_high)
-            total = src[:, s, at] + coming[:, at]
-            coming[:, at] = span_low
-            total += jnp.where(
-                first_row, 0.0 if below is None else below, pltpu.roll(normal_low, 1, 1)
-            )
-            below = normal_low[:, 15:16]
-            total += jnp.where(last_row, 0.0, pltpu.roll(normal_high, 15, 1))
-            at_low, at_high = face_tiles(n, s, at) if n > 0 else (0.0, 0.0)
-            a = pltpu.roll(chord_low[..., :LANES], 1, 2)
-            b = pltpu.roll(chord_low[..., LANES:], 1, 2)
-            c = pltpu.roll(chord_high[..., :LANES], LANES - 1, 2)
-            d = pltpu.roll(chord_high[..., LANES:], LANES - 1, 2)
-            left = jnp.where(first_lane, at_low, a) + jnp.where(last_lane, d, c)
-            right = jnp.where(first_lane, a, b) + jnp.where(last_lane, at_high, d)
-            total += jnp.concatenate([left, right], 2)
-            if g > 0:
-                before[:, 16 * g - 16 : 16 * g] = waiting + jnp.where(
-                    last_row, normal_high[:, 0:1], 0.0
+            every = products(p, s, g)
+            totals = []
+            for u in range(nvar):
+                normal_low, normal_high, chord_low, chord_high = [
+                    every[d * nvar + u] for d in range(4)
+                ]
+                total = span_terms(p, s, at, u)
+                total += jnp.where(
+                    first_row, 0.0 if below is None else below[u], pltpu.roll(normal_low, 1, 0)
                 )
-            waiting = total
-        before[:, rows - 16 : rows] = waiting
+                total += jnp.where(last_row, 0.0, pltpu.roll(normal_high, 15, 0))
+                a = pltpu.roll(chord_low[:, :LANES], 1, 1)
+                b = pltpu.roll(chord_low[:, LANES:], 1, 1)
+                c = pltpu.roll(chord_high[:, :LANES], LANES - 1, 1)
+                d = pltpu.roll(chord_high[:, LANES:], LANES - 1, 1)
+                at_low, at_high = face_tiles(n, s, at, u) if n > 0 else (0.0, 0.0)
+                left = jnp.where(first_lane, at_low, a) + jnp.where(last_lane, d, c)
+                right = jnp.where(first_lane, a, b) + jnp.where(last_lane, at_high, d)
+                totals.append(total + jnp.concatenate([left, right], 1))
+                if g > 0:
+                    done_at = slice(16 * g - 16, 16 * g)
+                    after[u, s, done_at] = inv[u, s, done_at] * (
+                        waiting[u] + jnp.where(last_row, normal_high[0:1], 0.0)
+                    )
+            below = [every[u][15:16] for u in range(nvar)]
+            waiting = totals
+        done_at = slice(rows - 16, rows)
+        for u in range(nvar):
+            after[u, s, done_at] = inv[u, s, done_at] * waiting[u]
 
     def stage(n, begin, last, turn):
         p, after = (pa, pb) if n % 2 == 0 else (pb, pa)
         fresh, final = n == sweeps[0], n == sweeps[-1]
-        if fresh:
-            arrive(begin, begin == 0)
-        for g in range(groups):
-            coming[:, 16 * g : 16 * g + 16] = products(p, begin, g, 0, step)
+        if fresh and p_in is None:
+            for at in range(begin, last + 1):
+                arrive(at)
+            fresh = False
+        elif fresh:
+            arrive(begin)
+            arrive(begin + 1)
         turns = (last - begin - 1) // turn
 
         def several(i, _):
             s0 = begin + 1 + i * turn
             if fresh:
                 for j in range(turn):
-                    arrive(s0 + j)
+                    arrive(s0 + j + 1)
             for j in range(turn):
                 one_layer(p, after, n, s0 + j)
             if final:
-                for j in range(turn - 1):
+                for j in range(turn):
                     leave(s0 + j, True)
-                if turns > 1:
-
-                    @pl.when(i > 0)
-                    def _():
-                        leave(s0 - 1, True)
-
             return 0
 
         if turns > 1:
             lax.fori_loop(0, turns, several, 0)
         else:
             several(0, 0)
-        if fresh:
-            arrive(last, last == layers - 1)
-        for g in range(groups):
-            at = slice(16 * g, 16 * g + 16)
-            span_high = products(p, last, g, step, 2 * step)
-            after[:, last - 1, at] = inv[:, last - 1, at] * (before[:, at] + span_high)
         if final:
-            leave(last - 1, True)
             left.extend(range(begin + 1, last))
 
     left = []
@@ -527,15 +523,12 @@
 def sweep_scratch(nvar, spans, chord, rows):
     f32 = jnp.float32
     field = pltpu.VMEM((nvar, spans + 2 * DEEP, rows, chord), f32)
-    layer = pltpu.VMEM((nvar, rows, chord), f32)
     return [
         field,
         field,
         field,
         field,
-        pltpu.VMEM((6 * nvar * 16, 256), jnp.bfloat16),
-        layer,
-        layer,
+        pltpu.VMEM((4 * nvar * 16, 256), jnp.bfloat16),
         pltpu.VMEM((SWEEPS, nvar, rows, LANES), f32),
         pltpu.VMEM((2, 152, LANES), f32),
         pltpu.SemaphoreType.DMA((3, spans + 2 * DEEP)),
@@ -543,17 +536,17 @@
     ]
 
 
-def inner_kernel(even, couplings, src_in, inv_in, out, *scratch):
+def inner_kernel(even, scalar, couplings, src_in, inv_in, out, *scratch):
     _, done = run_sweeps(
-        [(0, 3, 10, 2)], even, couplings, None, src_in, inv_in, None, None, None,
+        [(0, 3, 10, 2)], even, scalar, couplings, None, src_in, inv_in, None, None, None,
         lambda at: out.at[:, at - 4], scratch,
     )
     done()
 
 
-def outer_kernel(even, couplings, src_in, inv_in, inner, outer, out, *scratch):
+def outer_kernel(even, scalar, couplings, src_in, inv_in, inner, outer, out, *scratch):
     _, done = run_sweeps(
-        [(0, 0, 4, 3), (0, 9, 13, 3)], even, couplings, None, src_in, inv_in, inner, outer, None,
+        [(0, 0, 4, 3), (0, 9, 13, 3)], even, scalar, couplings, None, src_in, inv_in, inner, outer, None,
         lambda at: out.at[:, at - 1 if at < 4 else at - 7], scratch,
     )
     done()
@@ -563,17 +556,17 @@
     nvar, spans, depth, chord = source.shape
     return pl.pallas_call(
         kernel,
-        in_specs=[SMEM, VMEM] + [ANY] * (2 + len(halos)),
+        in_specs=[SMEM, SMEM, VMEM] + [ANY] * (2 + len(halos)),
         out_specs=ANY,
         out_shape=jax.ShapeDtypeStruct((nvar, 6, depth, chord), jnp.float32),
         scratch_shapes=sweep_scratch(nvar, spans, chord, depth),
         compiler_params=pltpu.CompilerParams(vmem_limit_bytes=24 * MIB),
         cost_estimate=pl.CostEstimate(flops=flops, bytes_accessed=4 * MIB, transcendentals=0),
         name=name,
-    )(even, couplings, source, inv_diag, *halos)
-
-
-def last_kernel(even, *rest):
+    )(even, couplings, couplings, source, inv_diag, *halos)
+
+
+def last_kernel(even, scalar, *rest):
     cpl, own, in_src, in_inv, out_src, out_inv, given, given_in, given_out, *rest = rest
     src_in, inv_in, inner, outer, p_inner, p_outer, jac, out, sens, *scratch = rest
     nvar, spans, _, chord = out.shape
@@ -588,7 +581,7 @@
         return p_outer.at[:, at - 1 if at < 4 else at - 7]
 
     result, done = run_sweeps(
-        [(1, 1, 12, 2), (2, 2, 11, 2)], even, cpl, ribbon, src_in, inv_in, inner, outer, p_in,
+        [(1, 1, 12, 2), (2, 2, 11, 2)], even, scalar, cpl, ribbon, src_in, inv_in, inner, outer, p_in,
         lambda at: out.at[:, at - DEEP], scratch,
     )
     layer = []
@@ -619,7 +612,7 @@
     return pl.pallas_call(
         last_kernel,
         grid=(1,),
-        in_specs=[SMEM, whole(cpl), whole(own)]
+        in_specs=[SMEM, SMEM, whole(cpl), whole(own)]
         + [piece(0), piece(DEEP - 1)] * 2
         + [whole(a) for a in givens]
         + [ANY] * 6
@@ -631,10 +624,10 @@
         ],
         scratch_shapes=sweep_scratch(nvar, spans, chord, depth),
         compiler_params=pltpu.CompilerParams(vmem_limit_bytes=30 * MIB),
-        cost_estimate=pl.CostEstimate(flops=11 * 10**9, bytes_accessed=16 * MIB, transcendentals=0),
+        cost_estimate=pl.CostEstimate(flops=10**9, bytes_accessed=16 * MIB, transcendentals=0),
         name="last_sweeps",
     )(
-        even, cpl, own, inner, inner, outer, outer, *givens, source, inv_diag, inner, outer,
+        even, cpl, cpl, own, inner, inner, outer, outer, *givens, source, inv_diag, inner, outer,
         p_inner, p_outer, jac,
     )
 

time: 83.4 us -> 85.8 us (1.029)
  Pallas kernels: 38.9 us -> 42.1 us
  starting transfers between devices: 14 us -> 13.1 us
    pallas_call x4, Pallas kernels: 31.2 us -> 34.4 us  [the longest x1 17.1 us: last_sweeps(): pl.pallas_call(last_kernel, grid=(1,), in_specs=[SMEM, SMEM, whole(cpl),...]
    ppermute x1, starting transfers between devices: 2.95 us -> 2.07 us  [reduce_points(): parts = keep + lax.ppermute(send, 'sub', [(i, i ^ 1) for i in range(count)])]
  transfers between devices with their start and end apart: 8 -> 8, of which waited for: 3 -> 3; matrix products, arithmetic and copies ran while one was open for 0% -> 0% of each run, Pallas kernels for 16% -> 18%
where the time goes in v10:
time: 85.8 us; the launch traced here: 85.5 us
  Pallas kernels  42.1 us (49%)
  blocking collectives  14.7 us (17%)
  starting transfers between devices  13.1 us (15%)
  waiting for transfers between devices  7.37 us (9%)
  local copies, waits for them, and re-layouts  6.68 us (8%)
  between operations  0.86 us (1%)
    pallas_call x1, Pallas kernels, last_sweeps(): pl.pallas_call(last_kernel, grid=(1,), in_specs=[SMEM, SMEM, whole(cpl),...  17.1 us
    all_to_all x1, blocking collectives, reduce_points(): lax.all_to_all(parts, ('blk', 'sub'), 0, 0, tiled=True, axis_index_groups...  14.7 us
    pallas_call x2, Pallas kernels, first_sweep(): pl.pallas_call(kernel, in_specs=[SMEM, SMEM, VMEM] + [ANY] * (2 + len(hal...  11.8 us
    unnamed x29, local copies, waits for them, and re-layouts  6.61 us
    pallas_call x1, Pallas kernels, chord_ends(): pl.pallas_call(ends_kernel, in_specs=[ANY, ANY, VMEM], out_specs=[VMEM] *...  5.58 us
    ppermute x2, starting transfers between devices, route_ends(): lax.ppermute(held, 'blk', [(i, i ^ mask) for i in range(count)])  4.94 us
    pallas_call x1, Pallas kernels, scatter_points(): pl.pallas_call(scatter_kernel, in_specs=[VMEM, VMEM, VMEM], out_specs=VME...  4.18 us
    ppermute x1, waiting for transfers between devices, route_ends(): given = lax.ppermute(picked, 'blk', [(i, i ^ last) for i in range(count)])  3.74 us
  transfers between devices with their start and end apart: 8, of which 3 were waited for; matrix products, arithmetic and copies ran while one was open for 0% of the time, Pallas kernels for 18%

profile of v10, /device:TPU:0, one launch (start us, length us, event | category | flops | bytes accessed | tf_op | source)
XLA Modules:
  0.0 85.5 jit_solution(7074031708013680642)
XLA Ops:
  0.6 0.0 copy-start
  0.6 5.6 %chord_ends.1 = (f32[2,5,64,128]{3,2,1,0:T(8,128)}, f32[264,128]{1,0:T(8,128)}, f32[8,128]{1,0:T(8,128)}) custom-call(f32[5,8,64,256]{3,2,1,0:T(8,128)} %rest_9_.1, f32[5,8,64,256]{3,2,1,0:T(8,128)} %rest_10_.1, f32[5,5,1,6]{3,2,1,0:T(1,128)} %bitcast.10), custom_call_target="tpu_custom_call" | custom-call | tf_op jit(solution)/shard_map/chord_ends/pallas_call | solution.py:97
  6.2 4.1 %collective-permute-start = (f32[1,264,128]{2,1,0:T(8,128)}, f32[1,264,128]{2,1,0:T(8,128)S(1)}, u32[]{:S(2)}, u32[]{:S(2)}) collective-permute-start(f32[1,264,128]{2,1,0:T(8,128)} %bitcast.8), channel_id=1, source_target_pairs={{0,16},{4,20},{8,24},{12,28},{16,0},{20,4},{24,8},{28,12},{1,17},{... | collective-permute-start | bytes 405512 | tf_op jit(solution)/shard_map/ppermute | solution.py:208
  10.3 0.0 copy-done
  10.3 0.0 copy-start.1
  10.3 1.7 %copy-done.1 = f32[5,8,64,256]{3,2,1,0:T(8,128)S(1)} copy-done((f32[5,8,64,256]{3,2,1,0:T(8,128)S(1)}, f32[5,8,64,256]{3,2,1,0:T(8,128)}, u32[]{:S(2)}) %copy-start.1) | copy-done | bytes 2621464
  12.1 0.0 copy-start.12
  12.1 2.2 %span_layers.1 = (f32[5,5,64,256]{3,2,1,0:T(8,128)}, f32[5,5,64,256]{3,2,1,0:T(8,128)}) custom-call(s32[1]{0:T(128)} %bitcast.even, f32[5,8,64,256]{3,2,1,0:T(8,128)S(1)} %copy-done, f32[5,8,64,256]{3,2,1,0:T(8,128)S(1)} %copy-done.1), custom_call_target="tpu_custom_call" | custom-call | bytes 8388608 | tf_op jit(solution)/shard_map/span_layers/pallas_call | solution.py:147
  14.3 2.7 %collective-permute-done = f32[1,264,128]{2,1,0:T(8,128)S(1)} collective-permute-done((f32[1,264,128]{2,1,0:T(8,128)}, f32[1,264,128]{2,1,0:T(8,128)S(1)}, u32[]{:S(2)}, u32[]{:S(2)}) %collective-permute-start) | collective-permute-done | bytes 135200 | tf_op jit(solution)/shard_map/ppermute | solution.py:208
  17.0 1.8 %collective-permute-start.2 = (f32[5,5,64,256]{3,2,1,0:T(8,128)}, f32[5,5,64,256]{3,2,1,0:T(8,128)}, u32[]{:S(2)}, u32[]{:S(2)}) collective-permute-start(f32[5,5,64,256]{3,2,1,0:T(8,128)} %get-tuple-element.22), channel_id=1, source_target_pairs={{1,2},{2,1},{5,6},{6,5},{9,10},{10,9},{13,14},{14,13},{17,18},{18,... | collective-permute-start | bytes 4915208 | tf_op jit(solution)/shard_map/ppermute | solution.py:714
  18.8 1.8 %collective-permute-start.1 = (f32[5,5,64,256]{3,2,1,0:T(8,128)}, f32[5,5,64,256]{3,2,1,0:T(8,128)}, u32[]{:S(2)}, u32[]{:S(2)}) collective-permute-start(f32[5,5,64,256]{3,2,1,0:T(8,128)} %get-tuple-element.20), channel_id=1, source_target_pairs={{0,1},{1,0},{2,3},{3,2},{4,5},{5,4},{6,7},{7,6},{8,9},{9,8},{10,11... | collective-permute-start | bytes 4915208 | tf_op jit(solution)/shard_map/ppermute | solution.py:714
  20.7 0.0 copy-done.12
  20.7 0.8 collective-permute-start.3
  21.6 0.0 copy-done.13
  21.6 0.1 copy.12.faces
  21.6 0.0 copy-done.9
  21.6 1.7 %copy-done.2 = f32[5,8,64,256]{3,2,1,0:T(8,128)S(1)} copy-done((f32[5,8,64,256]{3,2,1,0:T(8,128)S(1)}, f32[5,8,64,256]{3,2,1,0:T(8,128)}, u32[]{:S(2)}) %copy-start.2) | copy-done | bytes 2621464
  23.4 5.5 %inner_layers.1.rest_13_ = f32[5,6,64,256]{3,2,1,0:T(8,128)S(1)} custom-call(s32[1]{0:T(128)} %bitcast.even, f32[8,128]{1,0:T(8,128)S(1)} %copy-done.9, f32[8,128]{1,0:T(8,128)S(1)} %copy-done.9, f32[5,8,64,256]{3,2,1,0:T(8,128)S(1)} %copy-done, f32[5,8,64,256]{3,2,1,0:T(8,128)S(1)} %copy-done.2), custom_call_target="tpu_custom_call" | custom-call | flops 100000000 | bytes 4194304 | tf_op jit(solution)/shard_map/inner_layers/pallas_call | solution.py:557
  28.9 0.0 copy-start.5
  28.9 1.3 %copy-done.5 = f32[5,6,64,256]{3,2,1,0:T(8,128)} copy-done((f32[5,6,64,256]{3,2,1,0:T(8,128)}, f32[5,6,64,256]{3,2,1,0:T(8,128)S(1)}, u32[]{:S(2)}) %copy-start.5) | copy-done | bytes 1966104
  30.2 0.0 collective-permute-done.3.more
  30.2 0.6 pick_ends.1
  30.8 1.6 %collective-permute-start.4 = (f32[264,128]{1,0:T(8,128)S(1)}, f32[264,128]{1,0:T(8,128)S(1)}, u32[]{:S(2)}, u32[]{:S(2)}) collective-permute-start(f32[264,128]{1,0:T(8,128)S(1)} %pick_ends.1), channel_id=1, source_target_pairs={{0,4},{4,0},{8,12},{12,8},{16,20},{20,16},{24,28},{28,24},{1,5},{5... | collective-permute-start | bytes 405512 | tf_op jit(solution)/shard_map/ppermute | solution.py:224
  32.4 3.7 %collective-permute-done.4.given = f32[264,128]{1,0:T(8,128)S(1)} collective-permute-done((f32[264,128]{1,0:T(8,128)S(1)}, f32[264,128]{1,0:T(8,128)S(1)}, u32[]{:S(2)}, u32[]{:S(2)}) %collective-permute-start.4) | collective-permute-done | bytes 135200 | tf_op jit(solution)/shard_map/ppermute | solution.py:224
  36.1 0.7 choose_ends.1.rest_6_
  36.8 0.1 collective-permute-start.5
  36.8 0.8 collective-permute-start.6
  37.7 0.0 collective-permute-done.2.outer.rest_4_.rest_5_.rest_12_
  37.7 0.0 collective-permute-done.1.inner.rest_2_.rest_3_.rest_11_
  37.7 0.0 copy-start.3
  37.7 1.7 %copy-done.3 = f32[5,8,64,256]{3,2,1,0:T(8,128)S(1)} copy-done((f32[5,8,64,256]{3,2,1,0:T(8,128)S(1)}, f32[5,8,64,256]{3,2,1,0:T(8,128)}, u32[]{:S(2)}) %copy-start.3) | copy-done | bytes 2621464
  39.5 6.3 %outer_layers.1.rest_14_ = f32[5,6,64,256]{3,2,1,0:T(8,128)S(1)} custom-call(s32[1]{0:T(128)} %bitcast.even, f32[8,128]{1,0:T(8,128)S(1)} %copy-done.9, f32[8,128]{1,0:T(8,128)S(1)} %copy-done.9, f32[5,8,64,256]{3,2,1,0:T(8,128)S(1)} %copy-done, f32[5,8,64,256]{3,2,1,0:T(8,128)S(1)} %copy-done.3, ...), custom_call_target="tpu_custom_call" | custom-call | flops 100000000 | bytes 4194304 | tf_op jit(solution)/shard_map/outer_layers/pallas_call | solution.py:557
  45.8 0.0 collective-permute-done.5.rest_7_
  45.8 0.0 collective-permute-done.6.rest_8_
  45.8 0.0 copy-done.4
  45.8 0.0 copy-done.6
  45.8 0.0 copy-done.7
  45.8 0.0 copy-done.8
  45.8 0.0 copy-start.10
  45.8 0.0 copy-start.11
  45.9 17.1 %last_sweeps.1 = (f32[5,8,64,256]{3,2,1,0:T(8,128)}, f32[3,8,256]{2,1,0:T(8,128)S(1)}) custom-call(s32[1]{0:T(128)} %bitcast.even, f32[8,128]{1,0:T(8,128)S(1)} %copy-done.9, f32[8,128]{1,0:T(8,128)S(1)} %copy-done.9, f32[2,5,64,128]{3,2,1,0:T(8,128)S(1)} %copy-done.7, f32[5,5,64,256]{3,2,1,0:T(8,128)} %collective-permute-done.1.inner.rest_2_.rest_3_.rest_11_, ...), custom_call_target="tpu_custom_call" | custom-call | flops 1000000000 | bytes 16777216 | tf_op jit(solution)/shard_map/last_sweeps/pallas_call | solution.py:612
  62.9 0.0 copy-done.10
  62.9 0.0 copy-done.11
  62.9 4.2 %scatter_points.1 = f32[3,48,256]{2,1,0:T(8,128)S(1)} custom-call(f32[3,8,256]{2,1,0:T(8,128)S(1)} %get-tuple-element.27.sens, f32[8,8,256]{2,1,0:T(8,128)S(1)} %copy-done.10, s32[8,8,256]{2,1,0:T(8,128)S(1)} %copy-done.11), custom_call_target="tpu_custom_call" | custom-call | flops 4000000000 | bytes 1048576 | tf_op jit(solution)/shard_map/scatter_points/pallas_call | solution.py:683
  67.1 2.1 %collective-permute-start.7 = (f32[3,48,128]{2,1,0:T(8,128)S(1)}, f32[3,48,128]{2,1,0:T(8,128)S(1)}, u32[]{:S(2)}, u32[]{:S(2)}) collective-permute-start(f32[3,48,128]{2,1,0:T(8,128)S(1)} %constant_dynamic-slice_fusion), channel_id=1, source_target_pairs={{0,1},{1,0},{2,3},{3,2},{4,5},{5,4},{6,7},{7,6},{8,9},{9,8},{10,11... | collective-permute-start | bytes 221192 | tf_op jit(solution)/shard_map/ppermute | solution.py:701
  69.2 0.9 %collective-permute-done.7 = f32[3,48,128]{2,1,0:T(8,128)S(1)} collective-permute-done((f32[3,48,128]{2,1,0:T(8,128)S(1)}, f32[3,48,128]{2,1,0:T(8,128)S(1)}, u32[]{:S(2)}, u32[]{:S(2)}) %collective-permute-start.7) | collective-permute-done | bytes 73760 | tf_op jit(solution)/shard_map/ppermute | solution.py:701
  70.2 14.7 %all_to_all.5 = f32[16,3,384]{2,1,0:T(4,128)S(1)} all-to-all(f32[16,3,384]{2,1,0:T(4,128)S(1)} %bitcast.7), channel_id=1, replica_groups={{0,2,4,6,8,10,12,14,16,18,20,22,24,26,28,30},{1,3,5,7,9,11,13,15,17,19,..., dimensions={0} | all-to-all | bytes 147456 | tf_op jit(solution)/shard_map/all_to_all | solution.py:705
  84.9 0.6 reduce_sum.9
  (12 shorter events, 0.1 us)
Async XLA Ops:
  0.6 9.7 %copy-start = (f32[5,8,64,256]{3,2,1,0:T(8,128)S(1)}, f32[5,8,64,256]{3,2,1,0:T(8,128)}, u32[]{:S(2)}) copy-start(f32[5,8,64,256]{3,2,1,0:T(8,128)} %rest_9_.1) | copy-start | bytes 7864324
  6.2 10.8 %collective-permute-start = (f32[1,264,128]{2,1,0:T(8,128)}, f32[1,264,128]{2,1,0:T(8,128)S(1)}, u32[]{:S(2)}, u32[]{:S(2)}) collective-permute-start(f32[1,264,128]{2,1,0:T(8,128)} %bitcast.8), channel_id=1, source_target_pairs={{0,16},{4,20},{8,24},{12,28},{16,0},{20,4},{24,8},{28,12},{1,17},{... | collective-permute-start | bytes 405512 | tf_op jit(solution)/shard_map/ppermute | solution.py:208
  10.3 1.7 %copy-start.1 = (f32[5,8,64,256]{3,2,1,0:T(8,128)S(1)}, f32[5,8,64,256]{3,2,1,0:T(8,128)}, u32[]{:S(2)}) copy-start(f32[5,8,64,256]{3,2,1,0:T(8,128)} %rest_10_.1) | copy-start | bytes 7864324
  12.1 8.6 %copy-start.12 = (f32[264,128]{1,0:T(8,128)S(1)}, f32[264,128]{1,0:T(8,128)}, u32[]{:S(2)}) copy-start(f32[264,128]{1,0:T(8,128)} %get-tuple-element.17) | copy-start | bytes 405508
  12.1 9.5 %copy-start.13 = (s32[8,2]{0,1:T(2,128)S(1)}, s32[8,2]{0,1:T(2,128)}, u32[]{:S(2)}) copy-start(s32[8,2]{0,1:T(2,128)} %param.10) | copy-start | bytes 196
  12.1 9.6 %copy-start.9 = (f32[8,128]{1,0:T(8,128)S(1)}, f32[8,128]{1,0:T(8,128)}, u32[]{:S(2)}) copy-start(f32[8,128]{1,0:T(8,128)} %get-tuple-element.15.scalar.couplings.rest_0_) | copy-start | bytes 12292
  17.0 20.7 %collective-permute-start.2 = (f32[5,5,64,256]{3,2,1,0:T(8,128)}, f32[5,5,64,256]{3,2,1,0:T(8,128)}, u32[]{:S(2)}, u32[]{:S(2)}) collective-permute-start(f32[5,5,64,256]{3,2,1,0:T(8,128)} %get-tuple-element.22), channel_id=1, source_target_pairs={{1,2},{2,1},{5,6},{6,5},{9,10},{10,9},{13,14},{14,13},{17,18},{18,... | collective-permute-start | bytes 4915208 | tf_op jit(solution)/shard_map/ppermute | solution.py:714
  18.8 18.9 %collective-permute-start.1 = (f32[5,5,64,256]{3,2,1,0:T(8,128)}, f32[5,5,64,256]{3,2,1,0:T(8,128)}, u32[]{:S(2)}, u32[]{:S(2)}) collective-permute-start(f32[5,5,64,256]{3,2,1,0:T(8,128)} %get-tuple-element.20), channel_id=1, source_target_pairs={{0,1},{1,0},{2,3},{3,2},{4,5},{5,4},{6,7},{7,6},{8,9},{9,8},{10,11... | collective-permute-start | bytes 4915208 | tf_op jit(solution)/shard_map/ppermute | solution.py:714
  20.7 9.4 %collective-permute-start.3 = (f32[2,264,128]{2,1,0:T(8,128)S(1)}, f32[2,264,128]{2,1,0:T(8,128)S(1)}, u32[]{:S(2)}, u32[]{:S(2)}) collective-permute-start(f32[2,264,128]{2,1,0:T(8,128)S(1)} %pad_maximum_fusion.held), channel_id=1, source_target_pairs={{0,8},{4,12},{8,0},{12,4},{16,24},{20,28},{24,16},{28,20},{1,9},{5... | collective-permute-start | bytes 811016 | tf_op jit(solution)/shard_map/ppermute | solution.py:208
  21.6 1.7 %copy-start.2 = (f32[5,8,64,256]{3,2,1,0:T(8,128)S(1)}, f32[5,8,64,256]{3,2,1,0:T(8,128)}, u32[]{:S(2)}) copy-start(f32[5,8,64,256]{3,2,1,0:T(8,128)} %rest_10_.1) | copy-start | bytes 7864324
  28.9 1.3 %copy-start.5 = (f32[5,6,64,256]{3,2,1,0:T(8,128)}, f32[5,6,64,256]{3,2,1,0:T(8,128)S(1)}, u32[]{:S(2)}) copy-start(f32[5,6,64,256]{3,2,1,0:T(8,128)S(1)} %inner_layers.1.rest_13_) | copy-start | bytes 5898244
  30.8 5.3 %collective-permute-start.4 = (f32[264,128]{1,0:T(8,128)S(1)}, f32[264,128]{1,0:T(8,128)S(1)}, u32[]{:S(2)}, u32[]{:S(2)}) collective-permute-start(f32[264,128]{1,0:T(8,128)S(1)} %pick_ends.1), channel_id=1, source_target_pairs={{0,4},{4,0},{8,12},{12,8},{16,20},{20,16},{24,28},{28,24},{1,5},{5... | collective-permute-start | bytes 405512 | tf_op jit(solution)/shard_map/ppermute | solution.py:224
  36.8 9.0 %collective-permute-start.5 = (f32[264,128]{1,0:T(8,128)S(1)}, f32[264,128]{1,0:T(8,128)S(1)}, u32[]{:S(2)}, u32[]{:S(2)}) collective-permute-start(f32[264,128]{1,0:T(8,128)S(1)} %choose_ends.1.rest_6_), channel_id=1, source_target_pairs={{0,1},{1,0},{2,3},{3,2},{4,5},{5,4},{6,7},{7,6},{8,9},{9,8},{10,11... | collective-permute-start | bytes 405512 | tf_op jit(solution)/shard_map/ppermute | solution.py:714
  36.8 8.9 %collective-permute-start.6 = (f32[264,128]{1,0:T(8,128)S(1)}, f32[264,128]{1,0:T(8,128)S(1)}, u32[]{:S(2)}, u32[]{:S(2)}) collective-permute-start(f32[264,128]{1,0:T(8,128)S(1)} %choose_ends.1.rest_6_), channel_id=1, source_target_pairs={{1,2},{2,1},{5,6},{6,5},{9,10},{10,9},{13,14},{14,13},{17,18},{18,... | collective-permute-start | bytes 405512 | tf_op jit(solution)/shard_map/ppermute | solution.py:714
  37.7 1.7 %copy-start.3 = (f32[5,8,64,256]{3,2,1,0:T(8,128)S(1)}, f32[5,8,64,256]{3,2,1,0:T(8,128)}, u32[]{:S(2)}) copy-start(f32[5,8,64,256]{3,2,1,0:T(8,128)} %rest_10_.1) | copy-start | bytes 7864324
  39.5 6.3 %copy-start.4 = (f32[5,8,64,256]{3,2,1,0:T(8,128)S(1)}, f32[5,8,64,256]{3,2,1,0:T(8,128)}, u32[]{:S(2)}) copy-start(f32[5,8,64,256]{3,2,1,0:T(8,128)} %rest_10_.1) | copy-start | bytes 7864324
  39.5 6.3 %copy-start.6 = (f32[5,6,64,256]{3,2,1,0:T(8,128)S(1)}, f32[5,6,64,256]{3,2,1,0:T(8,128)}, u32[]{:S(2)}) copy-start(f32[5,6,64,256]{3,2,1,0:T(8,128)} %copy-done.5) | copy-start | bytes 5898244
  39.5 6.3 %copy-start.7 = (f32[2,5,64,128]{3,2,1,0:T(8,128)S(1)}, f32[2,5,64,128]{3,2,1,0:T(8,128)}, u32[]{:S(2)}) copy-start(f32[2,5,64,128]{3,2,1,0:T(8,128)} %get-tuple-element.16.rest_1_) | copy-start | bytes 983044
  39.5 6.4 %copy-start.8 = (f32[3,5,2,8,256]{4,3,2,1,0:T(8,128)S(1)}, f32[3,5,2,8,256]{4,3,2,1,0:T(8,128)}, u32[]{:S(2)}) copy-start(f32[3,5,2,8,256]{4,3,2,1,0:T(8,128)} %rest_15_.1) | copy-start | bytes 737284
  45.8 17.1 %copy-start.10 = (f32[8,8,256]{2,1,0:T(8,128)S(1)}, f32[8,8,256]{2,1,0:T(8,128)}, u32[]{:S(2)}) copy-start(f32[8,8,256]{2,1,0:T(8,128)} %weight.1) | copy-start | bytes 196612
  45.8 17.1 %copy-start.11 = (s32[8,8,256]{2,1,0:T(8,128)S(1)}, s32[8,8,256]{2,1,0:T(8,128)}, u32[]{:S(2)}) copy-start(s32[8,8,256]{2,1,0:T(8,128)} %ids.1) | copy-start | bytes 196612
  67.1 3.0 %collective-permute-start.7 = (f32[3,48,128]{2,1,0:T(8,128)S(1)}, f32[3,48,128]{2,1,0:T(8,128)S(1)}, u32[]{:S(2)}, u32[]{:S(2)}) collective-permute-start(f32[3,48,128]{2,1,0:T(8,128)S(1)} %constant_dynamic-slice_fusion), channel_id=1, source_target_pairs={{0,1},{1,0},{2,3},{3,2},{4,5},{5,4},{6,7},{7,6},{8,9},{9,8},{10,11... | collective-permute-start | bytes 221192 | tf_op jit(solution)/shard_map/ppermute | solution.py:701

commit v11 on v9

--- a/solution.py
+++ b/solution.py
@@ -46,73 +46,70 @@
 FREE = 16
 
 
-def ends_kernel(src, inv, coupling, tile, packet, cpl):
-    depth = tile.shape[2]
-    nvar = packet.shape[0] // depth + 1
-    tiles = [chord_tile([(s, field[:, s]) for s in range(field.shape[1])]) for field in (src, inv)]
-    for f in range(2):
-        tile[f] = tiles[f]
+def ends_kernel(src, inv, coupling, tile, packet, cpl, held, sems):
+    nvar, _, depth, _ = src.shape
+    order = [nvar - 1, *range(nvar - 1)]
+    loads = {}
+    for v in order:
+        for f, field in enumerate((src, inv)):
+            loads[f, v] = pltpu.make_async_copy(field.at[v], held.at[f, v], sems.at[f, v])
+            loads[f, v].start()
     lane = lane_iota((depth, LANES))
     place = lane & (HALF - 1)
     is_src = place - COLS * ((place * 43) >> 8) < 3
-    x, y = tiles[0][0], tiles[1][0]
-    both = jnp.where(
-        lane >= HALF,
-        jnp.where(is_src, pltpu.roll(x, LANES - 2, 1), pltpu.roll(y, 1, 1)),
-        jnp.where(is_src, x, pltpu.roll(y, 3, 1)),
-    )
-    both = pltpu.roll(both, LANES - COLS, 1)
-    step = pl.program_id(0)
     free = place >= HALF - FREE
-
-    @pl.when(step == 0)
-    def _():
-        for j in range(nvar - 1):
-            shift = (HALF - FREE - FREE * j) % LANES
-            packet[j * depth : (j + 1) * depth, :] = pltpu.roll(both, shift, 1) if shift else both
-        m = jnp.concatenate([coupling[u, v] for u in range(nvar) for v in range(nvar)], 0)
-        pair = lax.broadcasted_iota(jnp.int32, (nvar * nvar, LANES), 0)
-        own = bit(pair == (lane_iota((nvar * nvar, LANES)) & (HALF - 1)))
-        rows = lax.dot_general(
-            m, own, (((0,), (0,)), ((), ())), precision=lax.Precision.HIGHEST,
-            preferred_element_type=jnp.float32,
+    m = jnp.concatenate([coupling[u, v] for u in range(nvar) for v in range(nvar)], 0)
+    pair = lax.broadcasted_iota(jnp.int32, (nvar * nvar, LANES), 0)
+    own = bit(pair == (lane_iota((nvar * nvar, LANES)) & (HALF - 1)))
+    rows = lax.dot_general(
+        m, own, (((0,), (0,)), ((), ())), precision=lax.Precision.HIGHEST,
+        preferred_element_type=jnp.float32,
+    )
+    rows = jnp.concatenate([rows, jnp.zeros((8 - rows.shape[0], LANES), jnp.float32)], 0)
+    cpl[...] = rows
+    packet[(nvar - 1) * depth : (nvar - 1) * depth + 8, :] = rows
+    spread = None
+    for v in order:
+        pair = []
+        for f in range(2):
+            loads[f, v].wait()
+            field = held.at[f, v]
+            one = chord_tile([(s, field[s][None]) for s in range(field.shape[0])])[0]
+            tile[f, v] = one
+            pair.append(one)
+        x, y = pair
+        both = jnp.where(
+            lane >= HALF,
+            jnp.where(is_src, pltpu.roll(x, LANES - 2, 1), pltpu.roll(y, 1, 1)),
+            jnp.where(is_src, x, pltpu.roll(y, 3, 1)),
         )
-        rows = jnp.concatenate([rows, jnp.zeros((8 - rows.shape[0], LANES), jnp.float32)], 0)
-        cpl[...] = rows
-        packet[(nvar - 1) * depth : (nvar - 1) * depth + 8, :] = rows
-
-    @pl.when(step > 0)
-    def _():
-        at = pl.ds(pl.multiple_of((step - 1) * depth, depth), depth)
-        packet[at, :] = jnp.where(free, packet[at, :], both)
+        both = pltpu.roll(both, LANES - COLS, 1)
+        if spread is None:
+            spread = both
+            continue
+        shift = (HALF - FREE - FREE * v) % LANES
+        moved = pltpu.roll(spread, shift, 1) if shift else spread
+        packet[v * depth : (v + 1) * depth, :] = jnp.where(free, moved, both)
 
 
 def chord_ends(source, inv_diag, coupling):
     nvar, spans, depth, chord = source.shape
-
-    def var(step):
-        return jnp.where(step == 0, nvar - 1, step - 1)
-
-    field = pl.BlockSpec((1, spans, depth, chord), lambda i: (var(i), 0, 0, 0))
-    rows = (nvar - 1) * depth + 8
-    small = coupling.transpose(2, 3, 0, 1)
     return pl.pallas_call(
         ends_kernel,
-        grid=(nvar,),
-        in_specs=[field, field, pl.BlockSpec(small.shape, lambda i: (0, 0, 0, 0))],
-        out_specs=[
-            pl.BlockSpec((2, 1, depth, LANES), lambda i: (0, var(i), 0, 0)),
-            pl.BlockSpec((rows, LANES), lambda i: (0, 0)),
-            pl.BlockSpec((8, LANES), lambda i: (0, 0)),
-        ],
+        in_specs=[ANY, ANY, VMEM],
+        out_specs=[VMEM] * 3,
         out_shape=[
             jax.ShapeDtypeStruct((2, nvar, depth, LANES), jnp.float32),
-            jax.ShapeDtypeStruct((rows, LANES), jnp.float32),
+            jax.ShapeDtypeStruct(((nvar - 1) * depth + 8, LANES), jnp.float32),
             jax.ShapeDtypeStruct((8, LANES), jnp.float32),
         ],
-        compiler_params=pltpu.CompilerParams(vmem_limit_bytes=56 * MIB),
+        scratch_shapes=[
+            pltpu.VMEM((2, nvar, spans, depth, chord), jnp.float32),
+            pltpu.SemaphoreType.DMA((2, nvar)),
+        ],
+        compiler_params=pltpu.CompilerParams(vmem_limit_bytes=58 * MIB),
         name="chord_ends",
-    )(source, inv_diag, small)
+    )(source, inv_diag, coupling.transpose(2, 3, 0, 1))
 
 
 def layers_kernel(even, src, inv, inner, outer, held, sems):
@@ -545,7 +542,7 @@
 
 def inner_kernel(even, couplings, src_in, inv_in, out, *scratch):
     _, done = run_sweeps(
-        [(0, 3, 10, 2)], even, couplings, None, src_in, inv_in, None, None, None,
+        [(0, 3, 10, 3)], even, couplings, None, src_in, inv_in, None, None, None,
         lambda at: out.at[:, at - 4], scratch,
     )
     done()
@@ -588,7 +585,7 @@
         return p_outer.at[:, at - 1 if at < 4 else at - 7]
 
     result, done = run_sweeps(
-        [(1, 1, 12, 2), (2, 2, 11, 2)], even, cpl, ribbon, src_in, inv_in, inner, outer, p_in,
+        [(1, 1, 12, 5), (2, 2, 11, 4)], even, cpl, ribbon, src_in, inv_in, inner, outer, p_in,
         lambda at: out.at[:, at - DEEP], scratch,
     )
     layer = []

time: 83.4 us -> 82.1 us (0.984)
  Pallas kernels: 38.9 us -> 37.4 us
  transfers between devices with their start and end apart: 8 -> 8, of which waited for: 3 -> 4; matrix products, arithmetic and copies ran while one was open for 0% -> 0% of each run, Pallas kernels for 16% -> 16%
where the time goes in v11:
time: 82.1 us; the launch traced here: 81.8 us
  Pallas kernels  37.4 us (46%)
  blocking collectives  14.7 us (18%)
  starting transfers between devices  14.2 us (17%)
  waiting for transfers between devices  7.37 us (9%)
  local copies, waits for them, and re-layouts  6.68 us (8%)
  between operations  0.86 us (1%)
    all_to_all x1, blocking collectives, reduce_points(): lax.all_to_all(parts, ('blk', 'sub'), 0, 0, tiled=True, axis_index_groups...  14.7 us
    pallas_call x1, Pallas kernels, last_sweeps(): pl.pallas_call(last_kernel, grid=(1,), in_specs=[SMEM, whole(cpl), whole(...  14.5 us
    pallas_call x2, Pallas kernels, first_sweep(): pl.pallas_call(kernel, in_specs=[SMEM, VMEM] + [ANY] * (2 + len(halos)),...  9.7 us
    unnamed x29, local copies, waits for them, and re-layouts  6.61 us
    pallas_call x1, Pallas kernels, chord_ends(): pl.pallas_call(ends_kernel, in_specs=[ANY, ANY, VMEM], out_specs=[VMEM] *...  5.46 us
    ppermute x2, starting transfers between devices, route_ends(): lax.ppermute(held, 'blk', [(i, i ^ mask) for i in range(count)])  4.94 us
    pallas_call x1, Pallas kernels, scatter_points(): pl.pallas_call(scatter_kernel, in_specs=[VMEM, VMEM, VMEM], out_specs=VME...  4.17 us
    ppermute x1, waiting for transfers between devices, route_ends(): given = lax.ppermute(picked, 'blk', [(i, i ^ last) for i in range(count)])  3.68 us
  transfers between devices with their start and end apart: 8, of which 4 were waited for; matrix products, arithmetic and copies ran while one was open for 0% of the time, Pallas kernels for 16%

profile of v11, /device:TPU:0, one launch (start us, length us, event | category | flops | bytes accessed | tf_op | source)
XLA Modules:
  0.0 81.8 jit_solution(17713560739285866514)
XLA Ops:
  0.6 0.0 copy-start
  0.6 5.5 %chord_ends.1 = (f32[2,5,64,128]{3,2,1,0:T(8,128)}, f32[264,128]{1,0:T(8,128)}, f32[8,128]{1,0:T(8,128)}) custom-call(f32[5,8,64,256]{3,2,1,0:T(8,128)} %rest_9_.1, f32[5,8,64,256]{3,2,1,0:T(8,128)} %rest_10_.1, f32[5,5,1,6]{3,2,1,0:T(1,128)} %bitcast.10), custom_call_target="tpu_custom_call" | custom-call | tf_op jit(solution)/shard_map/chord_ends/pallas_call | solution.py:97
  6.1 4.1 %collective-permute-start = (f32[1,264,128]{2,1,0:T(8,128)}, f32[1,264,128]{2,1,0:T(8,128)S(1)}, u32[]{:S(2)}, u32[]{:S(2)}) collective-permute-start(f32[1,264,128]{2,1,0:T(8,128)} %bitcast.8), channel_id=1, source_target_pairs={{0,16},{4,20},{8,24},{12,28},{16,0},{20,4},{24,8},{28,12},{1,17},{... | collective-permute-start | bytes 405512 | tf_op jit(solution)/shard_map/ppermute | solution.py:208
  10.2 0.0 copy-done
  10.2 0.0 copy-start.1
  10.2 1.7 %copy-done.1 = f32[5,8,64,256]{3,2,1,0:T(8,128)S(1)} copy-done((f32[5,8,64,256]{3,2,1,0:T(8,128)S(1)}, f32[5,8,64,256]{3,2,1,0:T(8,128)}, u32[]{:S(2)}) %copy-start.1) | copy-done | bytes 2621464
  12.0 0.0 copy-start.12
  12.0 2.2 %span_layers.1 = (f32[5,5,64,256]{3,2,1,0:T(8,128)}, f32[5,5,64,256]{3,2,1,0:T(8,128)}) custom-call(s32[1]{0:T(128)} %bitcast.even, f32[5,8,64,256]{3,2,1,0:T(8,128)S(1)} %copy-done, f32[5,8,64,256]{3,2,1,0:T(8,128)S(1)} %copy-done.1), custom_call_target="tpu_custom_call" | custom-call | bytes 8388608 | tf_op jit(solution)/shard_map/span_layers/pallas_call | solution.py:147
  14.2 2.7 %collective-permute-done = f32[1,264,128]{2,1,0:T(8,128)S(1)} collective-permute-done((f32[1,264,128]{2,1,0:T(8,128)}, f32[1,264,128]{2,1,0:T(8,128)S(1)}, u32[]{:S(2)}, u32[]{:S(2)}) %collective-permute-start) | collective-permute-done | bytes 135200 | tf_op jit(solution)/shard_map/ppermute | solution.py:208
  16.9 1.8 %collective-permute-start.2 = (f32[5,5,64,256]{3,2,1,0:T(8,128)}, f32[5,5,64,256]{3,2,1,0:T(8,128)}, u32[]{:S(2)}, u32[]{:S(2)}) collective-permute-start(f32[5,5,64,256]{3,2,1,0:T(8,128)} %get-tuple-element.22), channel_id=1, source_target_pairs={{1,2},{2,1},{5,6},{6,5},{9,10},{10,9},{13,14},{14,13},{17,18},{18,... | collective-permute-start | bytes 4915208 | tf_op jit(solution)/shard_map/ppermute | solution.py:718
  18.7 1.8 %collective-permute-start.1 = (f32[5,5,64,256]{3,2,1,0:T(8,128)}, f32[5,5,64,256]{3,2,1,0:T(8,128)}, u32[]{:S(2)}, u32[]{:S(2)}) collective-permute-start(f32[5,5,64,256]{3,2,1,0:T(8,128)} %get-tuple-element.20), channel_id=1, source_target_pairs={{0,1},{1,0},{2,3},{3,2},{4,5},{5,4},{6,7},{7,6},{8,9},{9,8},{10,11... | collective-permute-start | bytes 4915208 | tf_op jit(solution)/shard_map/ppermute | solution.py:718
  20.6 0.0 copy-done.12
  20.6 0.8 %collective-permute-start.3 = (f32[2,264,128]{2,1,0:T(8,128)S(1)}, f32[2,264,128]{2,1,0:T(8,128)S(1)}, u32[]{:S(2)}, u32[]{:S(2)}) collective-permute-start(f32[2,264,128]{2,1,0:T(8,128)S(1)} %pad_maximum_fusion.held), channel_id=1, source_target_pairs={{0,8},{4,12},{8,0},{12,4},{16,24},{20,28},{24,16},{28,20},{1,9},{5... | collective-permute-start | bytes 811016 | tf_op jit(solution)/shard_map/ppermute | solution.py:208
  21.4 0.0 copy-done.13
  21.4 0.1 copy.12.faces
  21.5 0.0 copy-done.7
  21.5 1.7 %copy-done.2 = f32[5,8,64,256]{3,2,1,0:T(8,128)S(1)} copy-done((f32[5,8,64,256]{3,2,1,0:T(8,128)S(1)}, f32[5,8,64,256]{3,2,1,0:T(8,128)}, u32[]{:S(2)}) %copy-start.2) | copy-done | bytes 2621464
  23.3 4.5 %inner_layers.1.rest_13_ = f32[5,6,64,256]{3,2,1,0:T(8,128)S(1)} custom-call(s32[1]{0:T(128)} %bitcast.even, f32[8,128]{1,0:T(8,128)S(1)} %copy-done.7, f32[5,8,64,256]{3,2,1,0:T(8,128)S(1)} %copy-done, f32[5,8,64,256]{3,2,1,0:T(8,128)S(1)} %copy-done.2), custom_call_target="tpu_custom_call" | custom-call | flops 100000000 | bytes 4194304 | tf_op jit(solution)/shard_map/inner_layers/pallas_call | solution.py:561
  27.7 0.0 copy-start.5
  27.7 1.3 %copy-done.5 = f32[5,6,64,256]{3,2,1,0:T(8,128)} copy-done((f32[5,6,64,256]{3,2,1,0:T(8,128)}, f32[5,6,64,256]{3,2,1,0:T(8,128)S(1)}, u32[]{:S(2)}) %copy-start.5) | copy-done | bytes 1966104
  29.0 0.1 collective-permute-done.3.more
  29.1 0.6 pick_ends.1
  29.7 1.6 %collective-permute-start.4 = (f32[264,128]{1,0:T(8,128)S(1)}, f32[264,128]{1,0:T(8,128)S(1)}, u32[]{:S(2)}, u32[]{:S(2)}) collective-permute-start(f32[264,128]{1,0:T(8,128)S(1)} %pick_ends.1), channel_id=1, source_target_pairs={{0,4},{4,0},{8,12},{12,8},{16,20},{20,16},{24,28},{28,24},{1,5},{5... | collective-permute-start | bytes 405512 | tf_op jit(solution)/shard_map/ppermute | solution.py:224
  31.3 3.7 %collective-permute-done.4.given = f32[264,128]{1,0:T(8,128)S(1)} collective-permute-done((f32[264,128]{1,0:T(8,128)S(1)}, f32[264,128]{1,0:T(8,128)S(1)}, u32[]{:S(2)}, u32[]{:S(2)}) %collective-permute-start.4) | collective-permute-done | bytes 135200 | tf_op jit(solution)/shard_map/ppermute | solution.py:224
  35.0 0.7 choose_ends.1.rest_6_
  35.6 0.1 collective-permute-start.5
  35.7 0.8 %collective-permute-start.6 = (f32[264,128]{1,0:T(8,128)S(1)}, f32[264,128]{1,0:T(8,128)S(1)}, u32[]{:S(2)}, u32[]{:S(2)}) collective-permute-start(f32[264,128]{1,0:T(8,128)S(1)} %choose_ends.1.rest_6_), channel_id=1, source_target_pairs={{1,2},{2,1},{5,6},{6,5},{9,10},{10,9},{13,14},{14,13},{17,18},{18,... | collective-permute-start | bytes 405512 | tf_op jit(solution)/shard_map/ppermute | solution.py:718
  36.5 0.0 collective-permute-done.2.outer.rest_4_.rest_5_.rest_12_
  36.6 0.0 collective-permute-done.1.inner.rest_2_.rest_3_.rest_11_
  36.6 0.0 copy-start.3
  36.6 1.7 %copy-done.3 = f32[5,8,64,256]{3,2,1,0:T(8,128)S(1)} copy-done((f32[5,8,64,256]{3,2,1,0:T(8,128)S(1)}, f32[5,8,64,256]{3,2,1,0:T(8,128)}, u32[]{:S(2)}) %copy-start.3) | copy-done | bytes 2621464
  38.3 5.2 %outer_layers.1.rest_14_ = f32[5,6,64,256]{3,2,1,0:T(8,128)S(1)} custom-call(s32[1]{0:T(128)} %bitcast.even, f32[8,128]{1,0:T(8,128)S(1)} %copy-done.7, f32[5,8,64,256]{3,2,1,0:T(8,128)S(1)} %copy-done, f32[5,8,64,256]{3,2,1,0:T(8,128)S(1)} %copy-done.3, f32[5,5,64,256]{3,2,1,0:T(8,128)} %collective-permute-done.1.inner.rest_2_.rest_3_.rest_11_, ...), custom_call_target="tpu_custom_call" | custom-call | flops 100000000 | bytes 4194304 | tf_op jit(solution)/shard_map/outer_layers/pallas_call | solution.py:561
  43.6 0.0 collective-permute-done.5.rest_7_
  43.6 0.0 collective-permute-done.6.rest_8_
  43.6 0.0 copy-done.4
  43.6 0.0 copy-done.6
  43.6 0.0 copy-done.8
  43.6 0.0 copy-done.9
  43.6 0.0 copy-start.10
  43.6 0.0 copy-start.11
  43.7 14.5 %last_sweeps.1 = (f32[5,8,64,256]{3,2,1,0:T(8,128)}, f32[3,8,256]{2,1,0:T(8,128)S(1)}) custom-call(s32[1]{0:T(128)} %bitcast.even, f32[8,128]{1,0:T(8,128)S(1)} %copy-done.7, f32[2,5,64,128]{3,2,1,0:T(8,128)S(1)} %copy-done.8, f32[5,5,64,256]{3,2,1,0:T(8,128)} %collective-permute-done.1.inner.rest_2_.rest_3_.rest_11_, ...), custom_call_target="tpu_custom_call" | custom-call | flops 11000000512 | bytes 16777216 | tf_op jit(solution)/shard_map/last_sweeps/pallas_call | solution.py:616
  58.2 0.0 copy-done.10
  58.2 0.0 copy-done.11
  58.2 4.2 %scatter_points.1 = f32[3,48,256]{2,1,0:T(8,128)S(1)} custom-call(f32[3,8,256]{2,1,0:T(8,128)S(1)} %get-tuple-element.27.sens, f32[8,8,256]{2,1,0:T(8,128)S(1)} %copy-done.10, s32[8,8,256]{2,1,0:T(8,128)S(1)} %copy-done.11), custom_call_target="tpu_custom_call" | custom-call | flops 4000000000 | bytes 1048576 | tf_op jit(solution)/shard_map/scatter_points/pallas_call | solution.py:687
  62.4 3.1 %collective-permute-start.7 = (f32[3,48,128]{2,1,0:T(8,128)S(1)}, f32[3,48,128]{2,1,0:T(8,128)S(1)}, u32[]{:S(2)}, u32[]{:S(2)}) collective-permute-start(f32[3,48,128]{2,1,0:T(8,128)S(1)} %constant_dynamic-slice_fusion), channel_id=1, source_target_pairs={{0,1},{1,0},{2,3},{3,2},{4,5},{5,4},{6,7},{7,6},{8,9},{9,8},{10,11... | collective-permute-start | bytes 221192 | tf_op jit(solution)/shard_map/ppermute | solution.py:705
  65.5 0.9 %collective-permute-done.7 = f32[3,48,128]{2,1,0:T(8,128)S(1)} collective-permute-done((f32[3,48,128]{2,1,0:T(8,128)S(1)}, f32[3,48,128]{2,1,0:T(8,128)S(1)}, u32[]{:S(2)}, u32[]{:S(2)}) %collective-permute-start.7) | collective-permute-done | bytes 73760 | tf_op jit(solution)/shard_map/ppermute | solution.py:705
  66.5 14.7 %all_to_all.5 = f32[16,3,384]{2,1,0:T(4,128)S(1)} all-to-all(f32[16,3,384]{2,1,0:T(4,128)S(1)} %bitcast.7), channel_id=1, replica_groups={{0,2,4,6,8,10,12,14,16,18,20,22,24,26,28,30},{1,3,5,7,9,11,13,15,17,19,..., dimensions={0} | all-to-all | bytes 147456 | tf_op jit(solution)/shard_map/all_to_all | solution.py:709
  81.2 0.6 reduce_sum.9
  (12 shorter events, 0.1 us)
Async XLA Ops:
  0.6 9.6 %copy-start = (f32[5,8,64,256]{3,2,1,0:T(8,128)S(1)}, f32[5,8,64,256]{3,2,1,0:T(8,128)}, u32[]{:S(2)}) copy-start(f32[5,8,64,256]{3,2,1,0:T(8,128)} %rest_9_.1) | copy-start | bytes 7864324
  6.1 10.8 %collective-permute-start = (f32[1,264,128]{2,1,0:T(8,128)}, f32[1,264,128]{2,1,0:T(8,128)S(1)}, u32[]{:S(2)}, u32[]{:S(2)}) collective-permute-start(f32[1,264,128]{2,1,0:T(8,128)} %bitcast.8), channel_id=1, source_target_pairs={{0,16},{4,20},{8,24},{12,28},{16,0},{20,4},{24,8},{28,12},{1,17},{... | collective-permute-start | bytes 405512 | tf_op jit(solution)/shard_map/ppermute | solution.py:208
  10.2 1.7 %copy-start.1 = (f32[5,8,64,256]{3,2,1,0:T(8,128)S(1)}, f32[5,8,64,256]{3,2,1,0:T(8,128)}, u32[]{:S(2)}) copy-start(f32[5,8,64,256]{3,2,1,0:T(8,128)} %rest_10_.1) | copy-start | bytes 7864324
  12.0 8.6 %copy-start.12 = (f32[264,128]{1,0:T(8,128)S(1)}, f32[264,128]{1,0:T(8,128)}, u32[]{:S(2)}) copy-start(f32[264,128]{1,0:T(8,128)} %get-tuple-element.17) | copy-start | bytes 405508
  12.0 9.5 %copy-start.13 = (s32[8,2]{0,1:T(2,128)S(1)}, s32[8,2]{0,1:T(2,128)}, u32[]{:S(2)}) copy-start(s32[8,2]{0,1:T(2,128)} %param.10) | copy-start | bytes 196
  12.0 9.6 %copy-start.7 = (f32[8,128]{1,0:T(8,128)S(1)}, f32[8,128]{1,0:T(8,128)}, u32[]{:S(2)}) copy-start(f32[8,128]{1,0:T(8,128)} %get-tuple-element.15.couplings.rest_0_) | copy-start | bytes 12292
  16.9 19.6 %collective-permute-start.2 = (f32[5,5,64,256]{3,2,1,0:T(8,128)}, f32[5,5,64,256]{3,2,1,0:T(8,128)}, u32[]{:S(2)}, u32[]{:S(2)}) collective-permute-start(f32[5,5,64,256]{3,2,1,0:T(8,128)} %get-tuple-element.22), channel_id=1, source_target_pairs={{1,2},{2,1},{5,6},{6,5},{9,10},{10,9},{13,14},{14,13},{17,18},{18,... | collective-permute-start | bytes 4915208 | tf_op jit(solution)/shard_map/ppermute | solution.py:718
  18.7 17.8 %collective-permute-start.1 = (f32[5,5,64,256]{3,2,1,0:T(8,128)}, f32[5,5,64,256]{3,2,1,0:T(8,128)}, u32[]{:S(2)}, u32[]{:S(2)}) collective-permute-start(f32[5,5,64,256]{3,2,1,0:T(8,128)} %get-tuple-element.20), channel_id=1, source_target_pairs={{0,1},{1,0},{2,3},{3,2},{4,5},{5,4},{6,7},{7,6},{8,9},{9,8},{10,11... | collective-permute-start | bytes 4915208 | tf_op jit(solution)/shard_map/ppermute | solution.py:718
  20.6 8.5 %collective-permute-start.3 = (f32[2,264,128]{2,1,0:T(8,128)S(1)}, f32[2,264,128]{2,1,0:T(8,128)S(1)}, u32[]{:S(2)}, u32[]{:S(2)}) collective-permute-start(f32[2,264,128]{2,1,0:T(8,128)S(1)} %pad_maximum_fusion.held), channel_id=1, source_target_pairs={{0,8},{4,12},{8,0},{12,4},{16,24},{20,28},{24,16},{28,20},{1,9},{5... | collective-permute-start | bytes 811016 | tf_op jit(solution)/shard_map/ppermute | solution.py:208
  21.5 1.7 %copy-start.2 = (f32[5,8,64,256]{3,2,1,0:T(8,128)S(1)}, f32[5,8,64,256]{3,2,1,0:T(8,128)}, u32[]{:S(2)}) copy-start(f32[5,8,64,256]{3,2,1,0:T(8,128)} %rest_10_.1) | copy-start | bytes 7864324
  27.7 1.3 %copy-start.5 = (f32[5,6,64,256]{3,2,1,0:T(8,128)}, f32[5,6,64,256]{3,2,1,0:T(8,128)S(1)}, u32[]{:S(2)}) copy-start(f32[5,6,64,256]{3,2,1,0:T(8,128)S(1)} %inner_layers.1.rest_13_) | copy-start | bytes 5898244
  29.7 5.2 %collective-permute-start.4 = (f32[264,128]{1,0:T(8,128)S(1)}, f32[264,128]{1,0:T(8,128)S(1)}, u32[]{:S(2)}, u32[]{:S(2)}) collective-permute-start(f32[264,128]{1,0:T(8,128)S(1)} %pick_ends.1), channel_id=1, source_target_pairs={{0,4},{4,0},{8,12},{12,8},{16,20},{20,16},{24,28},{28,24},{1,5},{5... | collective-permute-start | bytes 405512 | tf_op jit(solution)/shard_map/ppermute | solution.py:224
  35.6 8.0 %collective-permute-start.5 = (f32[264,128]{1,0:T(8,128)S(1)}, f32[264,128]{1,0:T(8,128)S(1)}, u32[]{:S(2)}, u32[]{:S(2)}) collective-permute-start(f32[264,128]{1,0:T(8,128)S(1)} %choose_ends.1.rest_6_), channel_id=1, source_target_pairs={{0,1},{1,0},{2,3},{3,2},{4,5},{5,4},{6,7},{7,6},{8,9},{9,8},{10,11... | collective-permute-start | bytes 405512 | tf_op jit(solution)/shard_map/ppermute | solution.py:718
  35.7 7.9 %collective-permute-start.6 = (f32[264,128]{1,0:T(8,128)S(1)}, f32[264,128]{1,0:T(8,128)S(1)}, u32[]{:S(2)}, u32[]{:S(2)}) collective-permute-start(f32[264,128]{1,0:T(8,128)S(1)} %choose_ends.1.rest_6_), channel_id=1, source_target_pairs={{1,2},{2,1},{5,6},{6,5},{9,10},{10,9},{13,14},{14,13},{17,18},{18,... | collective-permute-start | bytes 405512 | tf_op jit(solution)/shard_map/ppermute | solution.py:718
  36.6 1.7 %copy-start.3 = (f32[5,8,64,256]{3,2,1,0:T(8,128)S(1)}, f32[5,8,64,256]{3,2,1,0:T(8,128)}, u32[]{:S(2)}) copy-start(f32[5,8,64,256]{3,2,1,0:T(8,128)} %rest_10_.1) | copy-start | bytes 7864324
  38.3 5.3 %copy-start.4 = (f32[5,8,64,256]{3,2,1,0:T(8,128)S(1)}, f32[5,8,64,256]{3,2,1,0:T(8,128)}, u32[]{:S(2)}) copy-start(f32[5,8,64,256]{3,2,1,0:T(8,128)} %rest_10_.1) | copy-start | bytes 7864324
  38.3 5.3 %copy-start.6 = (f32[5,6,64,256]{3,2,1,0:T(8,128)S(1)}, f32[5,6,64,256]{3,2,1,0:T(8,128)}, u32[]{:S(2)}) copy-start(f32[5,6,64,256]{3,2,1,0:T(8,128)} %copy-done.5) | copy-start | bytes 5898244
  38.3 5.3 %copy-start.8 = (f32[2,5,64,128]{3,2,1,0:T(8,128)S(1)}, f32[2,5,64,128]{3,2,1,0:T(8,128)}, u32[]{:S(2)}) copy-start(f32[2,5,64,128]{3,2,1,0:T(8,128)} %get-tuple-element.16.rest_1_) | copy-start | bytes 983044
  38.3 5.3 %copy-start.9 = (f32[3,5,2,8,256]{4,3,2,1,0:T(8,128)S(1)}, f32[3,5,2,8,256]{4,3,2,1,0:T(8,128)}, u32[]{:S(2)}) copy-start(f32[3,5,2,8,256]{4,3,2,1,0:T(8,128)} %rest_15_.1) | copy-start | bytes 737284
  43.6 14.6 %copy-start.10 = (f32[8,8,256]{2,1,0:T(8,128)S(1)}, f32[8,8,256]{2,1,0:T(8,128)}, u32[]{:S(2)}) copy-start(f32[8,8,256]{2,1,0:T(8,128)} %weight.1) | copy-start | bytes 196612
  43.6 14.6 %copy-start.11 = (s32[8,8,256]{2,1,0:T(8,128)S(1)}, s32[8,8,256]{2,1,0:T(8,128)}, u32[]{:S(2)}) copy-start(s32[8,8,256]{2,1,0:T(8,128)} %ids.1) | copy-start | bytes 196612
  62.4 4.0 %collective-permute-start.7 = (f32[3,48,128]{2,1,0:T(8,128)S(1)}, f32[3,48,128]{2,1,0:T(8,128)S(1)}, u32[]{:S(2)}, u32[]{:S(2)}) collective-permute-start(f32[3,48,128]{2,1,0:T(8,128)S(1)} %constant_dynamic-slice_fusion), channel_id=1, source_target_pairs={{0,1},{1,0},{2,3},{3,2},{4,5},{5,4},{6,7},{7,6},{8,9},{9,8},{10,11... | collective-permute-start | bytes 221192 | tf_op jit(solution)/shard_map/ppermute | solution.py:705
